TPU v7x, 32 devices: a whole 2x2x4 slice. The times are simulated.
32 devices in a mesh: grp: 8 (over z, y), blk: 4 (over x, core).
Axes of the slice: x: 2, y: 2, z: 4, core: 2. Of those that a mesh axis runs over, the one named last changes fastest.
Arguments:
- embeddings: bfloat16 [24576, 768], P(('grp', 'blk'))
- send_slot: int32 [24576], P(('grp', 'blk')), may hold values from 0 to 1535, as said below
Outputs:
- similarity: float32 [24576], P(('grp', 'blk'))
Inputs may be any that keep to these rules, and one draw needn't show every extreme that they name: `send_slot`: within the 768 rows of one arrival block the values are distinct; value // 48 is the target device in the order grp then blk. Every arrival block uses every multiple of 48 and the value 1536 - 1, and in every draw one target device receives all 48 of its slots from every arrival block.
All inputs are finite; a program needn't handle non-finite values.
Results may differ from a plain program's by a relative error of at most 0.00052.
Values may be sent and summed in bfloat16 or wider, within the bound.
No kernel may reach another device: no remote copies, remote signals or barrier semaphores. Data moves between devices by JAX's collectives and lax.ppermute only.
A program may use at most 64 MiB of HBM per device.

v0:
```python
import jax
import jax.numpy as jnp
from jax import lax
from jax.sharding import PartitionSpec as P

sentinel = -3.0
epsilon = 1e-06


def normalize_rows(inputs):
    widened = inputs.astype(jnp.float32)
    return (
        widened * lax.rsqrt(jnp.sum(widened * widened, axis=-1, keepdims=True) + epsilon)
    ).astype(jnp.bfloat16)


def tile_best(own_rows, own_live, own_start, columns, column_live):
    block_size = 512
    block_count = own_rows.shape[0] // block_size
    row_blocks = own_rows.reshape(block_count, block_size, own_rows.shape[1])
    live_blocks = own_live.reshape(block_count, block_size)
    row_ids = (own_start + jnp.arange(own_rows.shape[0])).reshape(block_count, block_size)
    column_ids = jnp.arange(columns.shape[0])
    column_usable = column_live > 0

    def scan_block(column_best, operands):
        row_block, block_live, block_ids = operands
        scores = lax.dot_general(
            row_block, columns, (((1,), (1,)), ((), ())), preferred_element_type=jnp.float32
        )
        usable = column_usable[None, :] & (block_ids[:, None] != column_ids[None, :])
        row_best = jnp.max(jnp.where(usable, scores, sentinel), axis=1)
        usable_both = usable & (block_live[:, None] > 0)
        column_best = jnp.maximum(
            column_best, jnp.max(jnp.where(usable_both, scores, sentinel), axis=0)
        )
        return (column_best, row_best)

    start_best = jnp.full((columns.shape[0],), sentinel, jnp.float32)
    column_best, row_best = lax.scan(scan_block, start_best, (row_blocks, live_blocks, row_ids))
    return (row_best.reshape(-1), column_best)


def on_device(embeddings, send_slot):
    row_count, features = embeddings.shape
    group_count = lax.axis_size("grp")
    member_count = lax.axis_size("blk")
    device_count = group_count * member_count
    slot_count = 2 * row_count
    pair_slots = slot_count // device_count
    normed = normalize_rows(embeddings)
    outgoing = jnp.zeros((slot_count, features), jnp.bfloat16).at[send_slot].set(normed)
    live_marks = (
        jnp.zeros((slot_count,), jnp.bfloat16)
        .at[send_slot]
        .set(jnp.ones((row_count,), jnp.bfloat16))
    )
    arrived, arrived_live = (
        lax.all_to_all(
            outgoing.reshape(device_count, pair_slots, features),
            ("grp", "blk"),
            split_axis=0,
            concat_axis=0,
            tiled=True,
        ),
        lax.all_to_all(
            live_marks.reshape(device_count, pair_slots),
            ("grp", "blk"),
            split_axis=0,
            concat_axis=0,
            tiled=True,
        ),
    )
    arrived = arrived.reshape(slot_count, features)
    arrived_live = arrived_live.reshape(slot_count)
    member_index = lax.axis_index("blk")
    own_start = member_index * slot_count
    row_best = tile_best(
        arrived,
        arrived_live,
        own_start,
        lax.all_gather(arrived, "blk", axis=0, tiled=True),
        lax.all_gather(arrived_live, "blk", axis=0, tiled=True),
    )[0]
    similar = jnp.maximum(jnp.full((slot_count,), sentinel, jnp.float32), row_best)
    homeward = lax.all_to_all(
        similar.reshape(device_count, pair_slots),
        ("grp", "blk"),
        split_axis=0,
        concat_axis=0,
        tiled=True,
    )
    return homeward.reshape(slot_count)[send_slot]


def solution(mesh):
    in_specs = (P(("grp", "blk"), None), P(("grp", "blk")))
    out_specs = P(("grp", "blk"))
    return jax.shard_map(
        on_device, mesh=mesh, in_specs=in_specs, out_specs=out_specs, check_vma=False
    )
```

profile of v0, /device:TPU:0, one launch (start us, length us, event | category | flops | bytes accessed | tf_op | source)
XLA Modules:
  0.0 201.4 jit_solution(4772037789235571066)
XLA Ops:
  6.5 0.7 compare_select_fusion
  7.2 1.6 fusion.6
  8.8 10.0 %scatter_custom_fusion.1 = bf16[1536,768]{1,0:T(8,128)(2,1)S(1)} fusion(s32[768]{0:T(1024)S(1)} %compare_select_fusion, bf16[768,768]{1,0:T(8,128)(2,1)} %param.4, f32[768]{0:T(1024)S(1)} %add_rsqrt_fusion, bf16[]{:T(256)} %constant.21.clone.1), kind=kCustom, calls=%fused_computation.15 | custom fusion | flops 1769472 | bytes 3543042 | tf_op jit(solution)/shard_map/scatter | solution.py:52
  18.8 62.9 %all_to_all.21 = bf16[32,48,768]{2,1,0:T(8,128)(2,1)} all-to-all(bf16[32,48,768]{2,1,0:T(8,128)(2,1)S(1)} %bitcast.19), channel_id=1, replica_groups=mesh['grp'=8,'blk'=4] {'grp','blk'}, dimensions={0} | all-to-all | bytes 4718592 | tf_op jit(solution)/shard_map/all_to_all | solution.py:59
  81.8 8.6 %scatter_custom_fusion = bf16[1536]{0:T(1024)(128)(2,1)S(1)} fusion(s32[768]{0:T(1024)S(1)} %compare_select_fusion, bf16[768]{0:T(1024)(128)(2,1)S(1)} %broadcast.28, bf16[]{:T(256)} %constant.21.clone.1), kind=kCustom, calls=%fused_computation.24 | custom fusion | bytes 3074 | tf_op jit(solution)/shard_map/scatter | solution.py:56
  90.4 0.7 all_to_all.17
  91.1 2.6 %all-to-all-start = ((bf16[32,1,48]{2,1,0:T(2,128)(2,1)}), bf16[32,1,48]{2,1,0:T(2,128)(2,1)S(1)}, u32[]{:S(2)}, u32[]{:S(2)}) async-start(bf16[32,1,48]{2,1,0:T(2,128)(2,1)} %all_to_all.17), calls=%async_computation | async-start | bytes 32768 | tf_op jit(solution)/shard_map/all_to_all | solution.py:66
  93.7 7.1 %all-to-all-done = bf16[32,1,48]{2,1,0:T(2,128)(2,1)S(1)} async-done(((bf16[32,1,48]{2,1,0:T(2,128)(2,1)}), bf16[32,1,48]{2,1,0:T(2,128)(2,1)S(1)}, u32[]{:S(2)}, u32[]{:S(2)}) %all-to-all-start) | async-done | bytes 3104 | tf_op jit(solution)/shard_map/all_to_all | solution.py:66
  100.8 0.1 reduce
  100.9 0.1 reshape.78
  100.9 5.5 %all-gather = bf16[4,1,1536]{2,1,0:T(2,128)(2,1)S(1)} all-gather(bf16[1,1,1536]{2,1,0:T(2,128)(2,1)S(1)} %reshape.78), channel_id=1, replica_groups=mesh['grp'=8,'blk'=4] {'blk'}, dimensions={0}, use_global_device_ids=true | all-gather | bytes 15360 | tf_op jit(solution)/shard_map/all_gather | solution.py:83
  106.4 0.1 compare_reduce_fusion
  106.5 37.6 %all-gather.3.cloned.1.call-done = bf16[6144,768]{1,0:T(8,128)(2,1)} async-done(((bf16[1536,768]{1,0:T(8,128)(2,1)}), bf16[6144,768]{1,0:T(8,128)(2,1)}) %all-gather.3.cloned.1.call-update) | async-done | bytes 9437200 | tf_op jit(solution)/shard_map/all_gather | solution.py:82
  144.1 30.5 %while.11 = (s32[]{:T(128)}, f32[3,512]{1,0:T(4,128)S(1)}, pred[6144]{0:T(1024)(128)(4,1)S(1)}, s32[3,512]{1,0:T(4,128)S(1)}, bf16[3,512,768]{2,1,0:T(8,128)(2,1...) while((s32[]{:T(128)}, f32[3,512]{1,0:T(4,128)S(1)}, pred[6144]{0:T(1024)(128)(4,1)S(1)}, ...), condition=%wide.region_5.6_spmd.clone, body=%wide.region_3.5_spmd.clone.sunk | while | flops 4844420608 | bytes 10242153 | solution.py:40
  144.2 10.1 %select_reduce_fusion.2 = f32[512]{0:T(512)S(1)} fusion(bf16[6144,768]{1,0:T(8,128)(2,1)} %get-tuple-element.127, s32[512]{0:T(512)S(1)} %bitcast.21, pred[6144]{0:T(1024)(128)(4,1)S(1)} %get-tuple-element.124, bf16[3,512,768]{2,1,0:T(8,128)(2,1)} %get-tuple-element.126, s32[]{:T(128)S(6)} %copy.7), kind=kOutput, calls=%fused_computation.5.clone.1 | convolution fusion | flops 4844420608 | bytes 10233860 | tf_op jit(solution)/shard_map/while/body/eval_jaxpr/dot_general | solution.py:28
  154.3 10.1 %select_reduce_fusion.2 = f32[512]{0:T(512)S(1)} fusion(bf16[6144,768]{1,0:T(8,128)(2,1)} %get-tuple-element.127, s32[512]{0:T(512)S(1)} %bitcast.21, pred[6144]{0:T(1024)(128)(4,1)S(1)} %get-tuple-element.124, bf16[3,512,768]{2,1,0:T(8,128)(2,1)} %get-tuple-element.126, s32[]{:T(128)S(6)} %copy.7), kind=kOutput, calls=%fused_computation.5.clone.1 | convolution fusion | flops 4844420608 | bytes 10233860 | tf_op jit(solution)/shard_map/while/body/eval_jaxpr/dot_general | solution.py:28
  164.5 10.1 %select_reduce_fusion.2 = f32[512]{0:T(512)S(1)} fusion(bf16[6144,768]{1,0:T(8,128)(2,1)} %get-tuple-element.127, s32[512]{0:T(512)S(1)} %bitcast.21, pred[6144]{0:T(1024)(128)(4,1)S(1)} %get-tuple-element.124, bf16[3,512,768]{2,1,0:T(8,128)(2,1)} %get-tuple-element.126, s32[]{:T(128)S(6)} %copy.7), kind=kOutput, calls=%fused_computation.5.clone.1 | convolution fusion | flops 4844420608 | bytes 10233860 | tf_op jit(solution)/shard_map/while/body/eval_jaxpr/dot_general | solution.py:28
  174.7 0.7 max_broadcast_in_dim.15
  175.4 4.6 %all-to-all-start.2 = ((f32[32,1,48]{2,1,0:T(1,128)}), f32[32,1,48]{2,1,0:T(1,128)S(1)}, u32[]{:S(2)}, u32[]{:S(2)}) async-start(f32[32,1,48]{2,1,0:T(1,128)} %max_broadcast_in_dim.15), calls=%async_computation.2 | async-start | bytes 32768 | tf_op jit(solution)/shard_map/all_to_all | solution.py:86
  180.0 7.1 %all-to-all-done.2 = f32[32,1,48]{2,1,0:T(1,128)S(1)} async-done(((f32[32,1,48]{2,1,0:T(1,128)}), f32[32,1,48]{2,1,0:T(1,128)S(1)}, u32[]{:S(2)}, u32[]{:S(2)}) %all-to-all-start.2) | async-done | bytes 6176 | tf_op jit(solution)/shard_map/all_to_all | solution.py:86
  187.2 0.5 broadcast.43
  187.7 0.7 reduce.6
  188.4 0.1 reshape.50
  188.4 6.1 %gather_fusion = f32[768]{0:T(1024)} fusion(f32[1536]{0:T(1024)S(1)} %reshape.50, s32[1024]{0:T(1024)S(1)} %pad_clamp_fusion), kind=kCustom, calls=%fused_computation | custom fusion | bytes 9216 | tf_op jit(solution)/shard_map/gather | solution.py:93
  (15 shorter events, 0.2 us)
Async XLA Ops:
  6.5 137.6 %all-gather.3.cloned.1.call-start = ((), (), s32[]{:S(2)}) async-start(), calls=%async_computation.3 | async-start | bytes 11796480 | tf_op jit(solution)/shard_map/all_gather | solution.py:82
  91.1 9.7 %all-to-all-start = ((bf16[32,1,48]{2,1,0:T(2,128)(2,1)}), bf16[32,1,48]{2,1,0:T(2,128)(2,1)S(1)}, u32[]{:S(2)}, u32[]{:S(2)}) async-start(bf16[32,1,48]{2,1,0:T(2,128)(2,1)} %all_to_all.17), calls=%async_computation | async-start | bytes 32768 | tf_op jit(solution)/shard_map/all_to_all | solution.py:66
  175.4 11.8 %all-to-all-start.2 = ((f32[32,1,48]{2,1,0:T(1,128)}), f32[32,1,48]{2,1,0:T(1,128)S(1)}, u32[]{:S(2)}, u32[]{:S(2)}) async-start(f32[32,1,48]{2,1,0:T(1,128)} %max_broadcast_in_dim.15), calls=%async_computation.2 | async-start | bytes 32768 | tf_op jit(solution)/shard_map/all_to_all | solution.py:86
Sparse Core Ops, SparseCore 0:
  81.9 62.2 all-gather.2
where the time goes:
time: 202 us; the launch traced here: 201 us
  blocking collectives  68.4 us (34%)
  waiting for transfers between devices  51.9 us (26%)
  matrix products  30.3 us (15%)
  local copies, waits for them, and re-layouts  17 us (8%)
  between operations  13.5 us (7%)
  other arithmetic  13.1 us (6%)
  starting transfers between devices  7.16 us (4%)
    all_to_all x1, blocking collectives, on_device(): lax.all_to_all(outgoing.reshape(device_count, pair_slots, features), ('gr...  62.9 us
    all_gather x1, waiting for transfers between devices, on_device(): lax.all_gather(arrived, 'blk', axis=0, tiled=True)  37.6 us
    dot_general x3, matrix products, scan_block(): lax.dot_general(row_block, columns, (((1,), (1,)), ((), ())), preferred_e...  30.3 us
    scatter x1, other arithmetic, on_device(): jnp.zeros((slot_count, features), jnp.bfloat16).at[send_slot].set(normed)  10 us
    scatter x1, local copies, waits for them, and re-layouts, on_device(): live_marks = jnp.zeros((slot_count,), jnp.bfloat16).at[send_slot].set(jnp...  8.62 us
    all_to_all x1, waiting for transfers between devices, on_device(): lax.all_to_all(similar.reshape(device_count, pair_slots), ('grp', 'blk'),...  7.13 us
    all_to_all x1, waiting for transfers between devices, on_device(): lax.all_to_all(live_marks.reshape(device_count, pair_slots), ('grp', 'blk...  7.12 us
    gather x1, local copies, waits for them, and re-layouts, on_device(): return homeward.reshape(slot_count)[send_slot]  6.14 us
  transfers between devices with their start and end apart: 3, of which 3 were waited for; matrix products, arithmetic and copies ran while one was open for 4% of the time, Pallas kernels for 0%

commit v1 on v0

v1 whole, which is shorter than its diff:
```python
import functools

import jax
import jax.numpy as jnp
from jax import lax
from jax.experimental import pallas as pl
from jax.experimental.pallas import tpu as pltpu
from jax.sharding import PartitionSpec as P

sentinel = -3.0
epsilon = 1e-06
dead_mark = 2.0
dead_bias = -8.0
lanes = 128


def chunk_sizes(capacity):
    count = 4 if capacity % 64 == 0 else 3
    return (capacity // count,) * count


def head_kernel(capacity, chunks, groups, slot_ref, x_ref, *out_refs):
    rows = x_ref.shape[0]
    wide = x_ref[...].astype(jnp.float32)
    normed = (
        wide * lax.rsqrt(jnp.sum(wide * wide, axis=-1, keepdims=True) + epsilon)
    ).astype(jnp.bfloat16)
    slots = slot_ref[...]
    first = 0
    for size, out_ref in zip(chunks, out_refs):
        place = lax.broadcasted_iota(jnp.int32, (groups, size, 1), 1)
        group = lax.broadcasted_iota(jnp.int32, (groups, size, 1), 0)
        wanted = (group * capacity + place + first).reshape(groups * size, 1)
        hit = wanted == slots
        pick = jnp.where(hit, 1.0, 0.0)
        live = jnp.max(pick, axis=1, keepdims=True)
        placed = jnp.dot(pick.astype(jnp.bfloat16), normed, preferred_element_type=jnp.float32)
        lane = lax.broadcasted_iota(jnp.int32, (1, placed.shape[1]), 1)
        mark = jnp.where(lane == 0, dead_mark, 0.0)
        placed = placed + (1.0 - live) * mark
        out_ref[...] = placed.astype(jnp.bfloat16)
        first += size


def head(embeddings, send_slot, capacity, chunks, groups):
    rows, features = embeddings.shape
    return pl.pallas_call(
        functools.partial(head_kernel, capacity, chunks, groups),
        out_shape=[
            jax.ShapeDtypeStruct((groups * size, features), jnp.bfloat16) for size in chunks
        ],
        compiler_params=pltpu.CompilerParams(vmem_limit_bytes=40 * 2**20),
        name="place_rows",
    )(send_slot.reshape(1, rows), embeddings)


def lane_fold(values):
    best = values[:, :lanes]
    for start in range(lanes, values.shape[1], lanes):
        best = jnp.maximum(best, values[:, start : start + lanes])
    return best


def gram_kernel(step, last, tile, me_ref, *refs):
    owns = refs[: step + 1]
    x_ref = refs[step + 1]
    states = refs[step + 2 : 2 * step + 2]
    outs = refs[2 * step + 2 :]
    row_outs = outs[: step + 1]
    col_out = outs[step + 1]
    index = pl.program_id(0)

    @pl.when(index == 0)
    def _():
        for state, out in zip(states, row_outs):
            out[...] = state[...]
        row_outs[step][...] = jnp.full(row_outs[step].shape, sentinel, jnp.float32)

    x = x_ref[...]
    features = x.shape[1]
    unit = jnp.where(lax.broadcasted_iota(jnp.int32, (16, features), 1) == 0, 1.0, 0.0)
    nt = (((1,), (1,)), ((), ()))
    marks = lax.dot_general(unit.astype(jnp.bfloat16), x, nt, preferred_element_type=jnp.float32)
    col_bias = jnp.where(marks[0:1, :] > 1.5, dead_bias, 0.0)
    col_best = jnp.full((1, tile), sentinel, jnp.float32)
    for j in range(step + 1):
        count = owns[j].shape[0]
        block = 128
        for start in range(0, count, block):
            own = owns[j][start : start + block, :]
            scores = lax.dot_general(own, x, nt, preferred_element_type=jnp.float32)
            usable = scores + col_bias
            if j == step:
                rows = lax.broadcasted_iota(jnp.int32, (block, tile), 0)
                cols = lax.broadcasted_iota(jnp.int32, (block, tile), 1)
                offset = index * tile - (me_ref[0] * count + start)
                usable = jnp.where(rows - cols == offset, dead_bias, usable)
            else:
                row_bias = jnp.where(own[:, 0:1].astype(jnp.float32) > 1.5, dead_bias, 0.0)
                col_best = jnp.maximum(
                    col_best, jnp.max(scores + row_bias, axis=0, keepdims=True)
                )
            row_outs[j][start : start + block, :] = jnp.maximum(
                row_outs[j][start : start + block, :], lane_fold(usable)
            )
    col_out[...] = col_best


def gram_step(step, last, me, owns, gathered, states):
    total, features = gathered.shape
    tile = 512
    while total % tile:
        tile -= 128
    const = lambda i, me_ref: (0, 0)
    counts = [own.shape[0] for own in owns]
    row_specs = [pl.BlockSpec((count, lanes), const) for count in counts]
    results = pl.pallas_call(
        functools.partial(gram_kernel, step, last, tile),
        grid_spec=pltpu.PrefetchScalarGridSpec(
            num_scalar_prefetch=1,
            grid=(total // tile,),
            in_specs=[pl.BlockSpec((count, features), const) for count in counts]
            + [pl.BlockSpec((tile, features), lambda i, me_ref: (i, 0))]
            + row_specs[:-1],
            out_specs=row_specs + [pl.BlockSpec((1, tile), lambda i, me_ref: (0, i))],
        ),
        out_shape=[jax.ShapeDtypeStruct((count, lanes), jnp.float32) for count in counts]
        + [jax.ShapeDtypeStruct((1, total), jnp.float32)],
        compiler_params=pltpu.CompilerParams(vmem_limit_bytes=40 * 2**20),
        cost_estimate=pl.CostEstimate(
            flops=2 * sum(counts) * total * features,
            bytes_accessed=2 * features * (sum(counts) + total),
            transcendentals=0,
        ),
        name="gram_step",
    )(me, *owns, gathered, *states)
    return list(results[:-1]), results[-1]


def tail_kernel(capacity, members, slot_ref, part_ref, out_ref, table):
    groups = part_ref.shape[0] // members
    width = table.shape[1]
    table[...] = jnp.full(table.shape, sentinel, jnp.float32)
    for g in range(groups):
        table[g : g + 1, :capacity] = jnp.max(
            part_ref[g * members : (g + 1) * members, :], axis=0, keepdims=True
        )
    rows = out_ref.shape[1]
    lane = lax.broadcasted_iota(jnp.int32, (lanes, lanes), 1)
    for start in range(0, rows, lanes):
        slot = jnp.broadcast_to(slot_ref[0:1, start : start + lanes], (lanes, lanes)).T
        best = jnp.full((lanes, lanes), sentinel, jnp.float32)
        for g in range(groups):
            for c in range(0, width, lanes):
                entry = table[g : g + 1, c : c + lanes]
                best = jnp.maximum(
                    best, jnp.where(slot - (g * capacity + c) == lane, entry, sentinel)
                )
        out_ref[0:1, start : start + lanes] = jnp.max(best.T, axis=0, keepdims=True)


def tail(partials, send_slot, capacity, members):
    rows = send_slot.shape[0]
    groups = partials.shape[0] // members
    width = -(-capacity // lanes) * lanes
    return pl.pallas_call(
        functools.partial(tail_kernel, capacity, members),
        out_shape=jax.ShapeDtypeStruct((1, rows), jnp.float32),
        scratch_shapes=[pltpu.VMEM((groups, width), jnp.float32)],
        name="pick_rows",
    )(send_slot.reshape(1, rows), partials).reshape(rows)


def on_device(embeddings, send_slot):
    row_count, features = embeddings.shape
    groups = lax.axis_size("grp")
    members = lax.axis_size("blk")
    slot_count = 2 * row_count
    capacity = slot_count // groups
    chunks = chunk_sizes(capacity)
    me = lax.axis_index("blk").astype(jnp.int32)
    placed = head(embeddings, send_slot, capacity, chunks, groups)
    owns, states, cols = [], [], []
    for step, size in enumerate(chunks):
        own = lax.all_to_all(
            placed[step].reshape(groups, size, features), "grp", 0, 0, tiled=True
        ).reshape(groups * size, features)
        gathered = lax.all_gather(own, "blk", axis=0, tiled=True)
        owns.append(own)
        states, col = gram_step(
            step, step == len(chunks) - 1, me.reshape(1), owns, gathered, states
        )
        cols.append(col)
    pieces = []
    for size, state, col in zip(chunks, states, cols):
        row = jnp.max(state, axis=1).reshape(1, groups, size)
        col = col.reshape(members, groups, size)
        is_me = (jnp.arange(members) == me)[:, None, None]
        pieces.append(jnp.where(is_me, jnp.maximum(row, col), col))
    best = jnp.concatenate(pieces, axis=2).transpose(1, 0, 2)
    homeward = lax.all_to_all(
        best.reshape(groups * members, capacity), ("grp", "blk"), 0, 0, tiled=True
    )
    return tail(homeward, send_slot, capacity, members)


def solution(mesh):
    in_specs = (P(("grp", "blk"), None), P(("grp", "blk")))
    out_specs = P(("grp", "blk"))
    return jax.shard_map(
        on_device, mesh=mesh, in_specs=in_specs, out_specs=out_specs, check_vma=False
    )
```

time: 202 us -> 173 us (0.86)
  waiting for transfers between devices: 51.9 us -> 18.4 us
  Pallas kernels: 0 us -> 31.9 us
  matrix products: 30.3 us -> 0 us
  blocking collectives: 68.4 us -> 92.8 us
  other arithmetic: 13.1 us -> 2.14 us
  starting transfers between devices: 7.16 us -> 0.13 us
  local copies, waits for them, and re-layouts: 17 us -> 13.2 us
    pallas_call x0 -> x6, Pallas kernels: none -> 31.9 us  [the longest x4 27.1 us: gram_step(): pl.pallas_call(functools.partial(gram_kernel, step, last, tile), grid_spe...]
    dot_general x3 -> x0, matrix products: 30.3 us -> none  [scan_block(): lax.dot_general(row_block, columns, (((1,), (1,)), ((), ())), preferred_e...]
    all_to_all x1 -> x5, blocking collectives: 62.9 us -> 92.8 us  [the longest x4 81.2 us: on_device(): lax.all_to_all(placed[step].reshape(groups, size, features), 'grp', 0, 0,...]
    all_gather x1 -> x4, waiting for transfers between devices: 37.6 us -> 18.4 us  [on_device(): gathered = lax.all_gather(own, 'blk', axis=0, tiled=True)]
    all_to_all x2 -> x0, waiting for transfers between devices: 14.2 us -> none  [the longest x1 7.13 us: on_device(): lax.all_to_all(similar.reshape(device_count, pair_slots), ('grp', 'blk'),...]
    unnamed x1 -> x29, local copies, waits for them, and re-layouts: 0.09 us -> 11.8 us
    scatter x1 -> x0, other arithmetic: 10 us -> none  [on_device(): jnp.zeros((slot_count, features), jnp.bfloat16).at[send_slot].set(normed)]
    scatter x1 -> x0, local copies, waits for them, and re-layouts: 8.62 us -> none  [on_device(): live_marks = jnp.zeros((slot_count,), jnp.bfloat16).at[send_slot].set(jnp...]
  transfers between devices with their start and end apart: 3 -> 4, of which waited for: 3 -> 2; matrix products, arithmetic and copies ran while one was open for 4% -> 0% of each run, Pallas kernels for 0% -> 10%
where the time goes in v1:
time: 173 us; the launch traced here: 172 us
  blocking collectives  92.8 us (54%)
  Pallas kernels  31.9 us (18%)
  waiting for transfers between devices  18.4 us (11%)
  between operations  13.3 us (8%)
  local copies, waits for them, and re-layouts  13.2 us (8%)
  other arithmetic  2.14 us (1%)
    all_to_all x4, blocking collectives, on_device(): lax.all_to_all(placed[step].reshape(groups, size, features), 'grp', 0, 0,...  81.2 us
    pallas_call x4, Pallas kernels, gram_step(): pl.pallas_call(functools.partial(gram_kernel, step, last, tile), grid_spe...  27.1 us
    all_gather x4, waiting for transfers between devices, on_device(): gathered = lax.all_gather(own, 'blk', axis=0, tiled=True)  18.4 us
    unnamed x29, local copies, waits for them, and re-layouts  11.8 us
    all_to_all x1, blocking collectives, on_device(): lax.all_to_all(best.reshape(groups * members, capacity), ('grp', 'blk'),...  11.7 us
  transfers between devices with their start and end apart: 4, of which 2 were waited for; matrix products, arithmetic and copies ran while one was open for 0% of the time, Pallas kernels for 10%

profile of v1, /device:TPU:0, one launch (start us, length us, event | category | flops | bytes accessed | tf_op | source)
XLA Modules:
  0.0 172.0 jit_solution(15832532021368372728)
XLA Ops:
  6.5 0.7 reshape.65.slot_ref
  7.2 1.3 copy-done.4
  8.5 2.5 %place_rows.1 = (bf16[384,768]{1,0:T(8,128)(2,1)S(1)}, bf16[384,768]{1,0:T(8,128)(2,1)S(1)}, bf16[384,768]{1,0:T(8,128)(2,1)S(1)}, bf16[384,768]{1,0:T(8,128)(2,1)S(1)}) custom-call(s32[1,768]{1,0:T(1,128)S(1)} %reshape.65.slot_ref, bf16[768,768]{1,0:T(8,128)(2,1)S(1)} %copy-done.4), custom_call_target="tpu_custom_call" | custom-call | tf_op jit(solution)/shard_map/place_rows/pallas_call | solution.py:47
  11.0 23.7 %all_to_all.31 = bf16[8,48,768]{2,1,0:T(8,128)(2,1)} all-to-all(bf16[8,48,768]{2,1,0:T(8,128)(2,1)S(1)} %bitcast.31), channel_id=1, replica_groups=mesh['grp'=8,'blk'=4] {'grp'}, dimensions={0} | all-to-all | bytes 1179648 | tf_op jit(solution)/shard_map/all_to_all | solution.py:185
  34.8 19.3 %all_to_all.32 = bf16[8,48,768]{2,1,0:T(8,128)(2,1)} all-to-all(bf16[8,48,768]{2,1,0:T(8,128)(2,1)S(1)} %bitcast.30), channel_id=1, replica_groups=mesh['grp'=8,'blk'=4] {'grp'}, dimensions={0} | all-to-all | bytes 1179648 | tf_op jit(solution)/shard_map/all_to_all | solution.py:185
  54.1 19.1 %all_to_all.33 = bf16[8,48,768]{2,1,0:T(8,128)(2,1)} all-to-all(bf16[8,48,768]{2,1,0:T(8,128)(2,1)S(1)} %bitcast.29), channel_id=1, replica_groups=mesh['grp'=8,'blk'=4] {'grp'}, dimensions={0} | all-to-all | bytes 1179648 | tf_op jit(solution)/shard_map/all_to_all | solution.py:185
  73.3 19.1 %all_to_all.34 = bf16[8,48,768]{2,1,0:T(8,128)(2,1)} all-to-all(bf16[8,48,768]{2,1,0:T(8,128)(2,1)S(1)} %bitcast.28), channel_id=1, replica_groups=mesh['grp'=8,'blk'=4] {'grp'}, dimensions={0} | all-to-all | bytes 1179648 | tf_op jit(solution)/shard_map/all_to_all | solution.py:185
  92.5 1.7 %copy-done.6 = bf16[1536,768]{1,0:T(8,128)(2,1)S(1)} copy-done((bf16[1536,768]{1,0:T(8,128)(2,1)S(1)}, bf16[1536,768]{1,0:T(8,128)(2,1)}, u32[]{:S(2)}) %copy-start.6) | copy-done | bytes 2359320
  94.2 3.4 %gram_step.4 = (f32[384,128]{1,0:T(8,128)S(1)}, f32[1,1536]{1,0:T(1,128)S(1)}) custom-call(s32[1]{0:T(128)} %bitcast.me_ref, bf16[384,768]{1,0:T(8,128)(2,1)S(1)} %bitcast.15, bf16[1536,768]{1,0:T(8,128)(2,1)S(1)} %copy-done.6), custom_call_target="tpu_custom_call" | custom-call | flops 905969664 | bytes 2949120 | tf_op jit(solution)/shard_map/gram_step/pallas_call | solution.py:117
  97.6 1.7 copy-done.8
  99.3 5.6 %gram_step.5 = (f32[384,128]{1,0:T(8,128)S(1)}, f32[384,128]{1,0:T(8,128)S(1)}, f32[1,1536]{1,0:T(1,128)S(1)}) custom-call(s32[1]{0:T(128)} %bitcast.me_ref, bf16[384,768]{1,0:T(8,128)(2,1)S(1)} %bitcast.16, bf16[384,768]{1,0:T(8,128)(2,1)S(1)} %bitcast.20, bf16[1536,768]{1,0:T(8,128)(2,1)S(1)} %copy-done.8, f32[384,128]{1,0:T(8,128)S(1)} %get-tuple-element.27.refs_3_), custom_call_target="tpu_custom_call" | custom-call | flops 1811939328 | bytes 3538944 | tf_op jit(solution)/shard_map/gram_step/pallas_call | solution.py:117
  104.9 3.8 %all-gather.7.cloned.1.call-done.refs_3_ = bf16[1536,768]{1,0:T(8,128)(2,1)} async-done(((bf16[384,768]{1,0:T(8,128)(2,1)}), bf16[1536,768]{1,0:T(8,128)(2,1)}) %all-gather.7.cloned.1.call-update) | async-done | bytes 2359312 | tf_op jit(solution)/shard_map/all_gather | solution.py:188
  108.7 1.7 copy-done.9
  110.3 7.9 %gram_step.6 = (f32[384,128]{1,0:T(8,128)S(1)}, f32[384,128]{1,0:T(8,128)S(1)}, f32[384,128]{1,0:T(8,128)S(1)}, f32[1,1536]{1,0:T(1,128)S(1)}) custom-call(s32[1]{0:T(128)} %bitcast.me_ref, bf16[384,768]{1,0:T(8,128)(2,1)S(1)} %bitcast.17, bf16[384,768]{1,0:T(8,128)(2,1)S(1)} %bitcast.21, bf16[384,768]{1,0:T(8,128)(2,1)S(1)} %bitcast.24, ...), custom_call_target="tpu_custom_call" | custom-call | flops 2717908992 | bytes 4128768 | tf_op jit(solution)/shard_map/gram_step/pallas_call | solution.py:117
  118.3 0.7 copy-done.10
  119.0 0.7 copy-done.12
  119.7 14.5 %all-gather.5.cloned.1.call-done.refs_4_ = bf16[1536,768]{1,0:T(8,128)(2,1)} async-done(((bf16[384,768]{1,0:T(8,128)(2,1)}), bf16[1536,768]{1,0:T(8,128)(2,1)}) %all-gather.5.cloned.1.call-update) | async-done | bytes 2359312 | tf_op jit(solution)/shard_map/all_gather | solution.py:188
  134.2 1.7 copy-done.7
  135.9 0.9 copy-done.11
  136.8 0.9 copy-done.13
  137.7 10.2 %gram_step.7 = (f32[384,128]{1,0:T(8,128)S(1)}, f32[384,128]{1,0:T(8,128)S(1)}, f32[384,128]{1,0:T(8,128)S(1)}, f32[384,128]{1,0:T(8,128)S(1)}, f32[1,1536]{1,0:T(1,128)S(1)}) custom-call(s32[1]{0:T(128)} %bitcast.me_ref, bf16[384,768]{1,0:T(8,128)(2,1)S(1)} %bitcast.18, bf16[384,768]{1,0:T(8,128)(2,1)S(1)} %bitcast.22, bf16[384,768]{1,0:T(8,128)(2,1)S(1)} %bitcast.25, ...), custom_call_target="tpu_custom_call" | custom-call | flops 3623878656 | bytes 4718592 | tf_op jit(solution)/shard_map/gram_step/pallas_call | solution.py:117
  149.6 11.7 %all_to_all.35 = f32[32,1,192]{2,1,0:T(1,128)S(1)} all-to-all(f32[32,1,192]{2,1,0:T(1,128)S(1)} %all_to_all.23), channel_id=1, replica_groups=mesh['grp'=8,'blk'=4] {'grp','blk'}, dimensions={0} | all-to-all | bytes 49152 | tf_op jit(solution)/shard_map/all_to_all | solution.py:201
  161.8 2.3 %pick_rows.1 = f32[1,768]{1,0:T(1,128)} custom-call(s32[1,768]{1,0:T(1,128)} %copy-done.5, f32[32,192]{1,0:T(8,128)} %bitcast.32), custom_call_target="tpu_custom_call" | custom-call | tf_op jit(solution)/shard_map/pick_rows/pallas_call | solution.py:166
  164.1 1.3 reduce.4
  (51 shorter events, 2.4 us)
Async XLA Ops:
  6.5 85.9 %all-gather.11.cloned.1.call-start = ((), (), s32[]{:S(2)}) async-start(), calls=%async_computation.8 | async-start | bytes 2949120 | tf_op jit(solution)/shard_map/all_gather | solution.py:188
  7.2 1.3 copy-start.4
  8.5 45.6 %copy-start.5 = (s32[1,768]{1,0:T(1,128)}, s32[1,768]{1,0:T(1,128)S(1)}, u32[]{:S(2)}) copy-start(s32[1,768]{1,0:T(1,128)S(1)} %reshape.65.slot_ref) | copy-start | bytes 9220
  34.7 62.8 %all-gather.9.cloned.1.call-start = ((), (), s32[]{:S(2)}) async-start(), calls=%async_computation.7 | async-start | bytes 2949120 | tf_op jit(solution)/shard_map/all_gather | solution.py:188
  54.1 38.4 %copy-start = (bf16[8,48,768]{2,1,0:T(8,128)(2,1)S(1)}, bf16[8,48,768]{2,1,0:T(8,128)(2,1)}, u32[]{:S(2)}) copy-start(bf16[8,48,768]{2,1,0:T(8,128)(2,1)} %all_to_all.31) | copy-start | bytes 1769476
  54.1 54.6 %all-gather.7.cloned.1.call-start = ((), (), s32[]{:S(2)}) async-start(), calls=%async_computation.6 | async-start | bytes 2949120 | tf_op jit(solution)/shard_map/all_gather | solution.py:188
  73.3 60.9 %all-gather.5.cloned.1.call-start = ((), (), s32[]{:S(2)}) async-start(), calls=%async_computation.5 | async-start | bytes 2949120 | tf_op jit(solution)/shard_map/all_gather | solution.py:188
  73.3 24.3 %copy-start.1 = (bf16[8,48,768]{2,1,0:T(8,128)(2,1)S(1)}, bf16[8,48,768]{2,1,0:T(8,128)(2,1)}, u32[]{:S(2)}) copy-start(bf16[8,48,768]{2,1,0:T(8,128)(2,1)} %all_to_all.32) | copy-start | bytes 1769476
  92.5 1.7 %copy-start.6 = (bf16[1536,768]{1,0:T(8,128)(2,1)S(1)}, bf16[1536,768]{1,0:T(8,128)(2,1)}, u32[]{:S(2)}) copy-start(bf16[1536,768]{1,0:T(8,128)(2,1)} %all-gather.11.cloned.1.call-done.refs_1_) | copy-start | bytes 7077892
  97.6 1.7 copy-start.8
  99.3 9.4 %copy-start.2 = (bf16[8,48,768]{2,1,0:T(8,128)(2,1)S(1)}, bf16[8,48,768]{2,1,0:T(8,128)(2,1)}, u32[]{:S(2)}) copy-start(bf16[8,48,768]{2,1,0:T(8,128)(2,1)} %all_to_all.33) | copy-start | bytes 1769476
  108.7 1.7 copy-start.9
  110.3 23.9 %copy-start.3 = (bf16[8,48,768]{2,1,0:T(8,128)(2,1)S(1)}, bf16[8,48,768]{2,1,0:T(8,128)(2,1)}, u32[]{:S(2)}) copy-start(bf16[8,48,768]{2,1,0:T(8,128)(2,1)} %all_to_all.34) | copy-start | bytes 1769476
  118.3 0.7 copy-start.10
  119.0 0.7 copy-start.12
  134.2 1.7 copy-start.7
  135.9 0.9 copy-start.11
  136.8 0.9 copy-start.13
Sparse Core Ops, SparseCore 0:
  34.9 22.4 all-gather.10
  58.9 24.0 all-gather.8
  84.6 24.0 all-gather.6
  110.1 24.0 all-gather.4

commit v2 on v1

v2 whole, which is shorter than its diff:
```python
import functools

import jax
import jax.numpy as jnp
from jax import lax
from jax.experimental import pallas as pl
from jax.experimental.pallas import tpu as pltpu
from jax.sharding import PartitionSpec as P

sentinel = -3.0
epsilon = 1e-06
dead_mark = 2.0
dead_bias = -8.0
lanes = 128
smem = pl.BlockSpec(memory_space=pltpu.SMEM)
vmem = pl.BlockSpec(memory_space=pltpu.VMEM)


def chunk_sizes(capacity):
    count = 4 if capacity % 64 == 0 else 3
    return (capacity // count,) * count


def swap(value, axis, size, bit):
    return lax.ppermute(value, axis, [(i, i ^ bit) for i in range(size)])


def head_kernel(capacity, chunks, groups, me_ref, slot_ref, x_ref, *out_refs):
    wide = x_ref[...].astype(jnp.float32)
    normed = (
        wide * lax.rsqrt(jnp.sum(wide * wide, axis=-1, keepdims=True) + epsilon)
    ).astype(jnp.bfloat16)
    slots = jnp.concatenate([slot_ref[q : q + 1, :] for q in range(slot_ref.shape[0])], axis=1)
    first = 0
    for step, size in enumerate(chunks):
        place = lax.broadcasted_iota(jnp.int32, (groups, size, 1), 1)
        group = lax.broadcasted_iota(jnp.int32, (groups, size, 1), 0) ^ me_ref[0]
        wanted = (group * capacity + place + first).reshape(groups * size, 1)
        pick = jnp.where(wanted == slots, 1.0, 0.0)
        live = jnp.max(pick, axis=1, keepdims=True)
        placed = jnp.dot(pick.astype(jnp.bfloat16), normed, preferred_element_type=jnp.float32)
        lane = lax.broadcasted_iota(jnp.int32, (1, placed.shape[1]), 1)
        mark = jnp.where(lane == 0, dead_mark, 0.0)
        placed = (placed + (1.0 - live) * mark).astype(jnp.bfloat16)
        for r in range(groups):
            out_refs[step * groups + r][...] = placed[r * size : (r + 1) * size, :]
        first += size


def head(me, embeddings, slots, capacity, chunks, groups):
    rows, features = embeddings.shape
    return pl.pallas_call(
        functools.partial(head_kernel, capacity, chunks, groups),
        in_specs=[smem, vmem, vmem],
        out_specs=[vmem] * (groups * len(chunks)),
        out_shape=[
            jax.ShapeDtypeStruct((size, features), jnp.bfloat16)
            for size in chunks
            for _ in range(groups)
        ],
        compiler_params=pltpu.CompilerParams(vmem_limit_bytes=32 * 2**20),
        name="place_rows",
    )(me, slots, embeddings)


def lane_fold(values):
    best = values[:, :lanes]
    for start in range(lanes, values.shape[1], lanes):
        best = jnp.maximum(best, values[:, start : start + lanes])
    return best


def gram_body(own_refs, piece_refs, row_refs, col_ref, stack, tile):
    step = len(own_refs) - 1
    count = own_refs[step].shape[0]
    for p, piece_ref in enumerate(piece_refs):
        stack[p * count : (p + 1) * count, :] = piece_ref[...]
    row_refs[step][...] = jnp.full(row_refs[step].shape, sentinel, jnp.float32)
    nt = (((1,), (1,)), ((), ()))

    @pl.loop(0, stack.shape[0] // tile)
    def _(n):
        first = pl.multiple_of(n * tile, tile)
        x = stack[pl.ds(first, tile), :]
        marks = x[:, :lanes].astype(jnp.float32).T[0:1, :]
        col_bias = jnp.where(marks > 1.5, dead_bias, 0.0)
        col_best = jnp.full((1, tile), sentinel, jnp.float32)
        for j in range(step + 1):
            own = own_refs[j][...]
            scores = lax.dot_general(own, x, nt, preferred_element_type=jnp.float32)
            usable = scores + col_bias
            if j == step:
                rows = lax.broadcasted_iota(jnp.int32, usable.shape, 0)
                cols = lax.broadcasted_iota(jnp.int32, usable.shape, 1)
                usable = jnp.where(rows - cols == first, dead_bias, usable)
            else:
                row_bias = jnp.where(own[:, 0:1].astype(jnp.float32) > 1.5, dead_bias, 0.0)
                col_best = jnp.maximum(
                    col_best, jnp.max(scores + row_bias, axis=0, keepdims=True)
                )
            row_refs[j][...] = jnp.maximum(row_refs[j][...], lane_fold(usable))
        col_ref[0:1, pl.ds(first, tile)] = col_best


def gram_kernel(step, pieces, tile, *refs):
    owns = refs[: step + 1]
    others = refs[step + 1 : step + pieces]
    refs = refs[step + pieces :]
    states, refs = refs[:step], refs[step:]
    rows, col, stack = refs[: step + 1], refs[step + 1], refs[step + 2]
    for state, row in zip(states, rows):
        row[...] = state[...]
    gram_body(owns, (owns[step],) + others, rows, col, stack, tile)


def gram_last_kernel(step, relatives, chunks, groups, tile, me_ref, *refs):
    pieces = len(relatives)
    owns = refs[: step + 1]
    others = refs[step + 1 : step + pieces]
    refs = refs[step + pieces :]
    states, refs = refs[:step], refs[step:]
    cols, refs = refs[:step], refs[step:]
    out_ref, stack, col, table = refs[:4]
    rows = refs[4:]
    for state, row in zip(states, rows):
        row[...] = state[...]
    gram_body(owns, (owns[step],) + others, rows, col, stack, tile)
    first = 0
    for k, size in enumerate(chunks):
        col_k = (cols[k] if k < step else col)[0:1, :]
        row_k = jnp.max(rows[k][...].T, axis=0, keepdims=True)
        count = groups * size
        for p, relative in enumerate(relatives):
            for r in range(groups):
                start = p * count + r * size
                best = col_k[:, start : start + size]
                if p == 0:
                    best = jnp.maximum(best, row_k[:, r * size : (r + 1) * size])
                row = r * pieces + p
                table[row : row + 1, first : first + size] = best
        first += size
    for r in range(groups):
        for p, relative in enumerate(relatives):
            row = r * pieces + p
            target = (me_ref[0] ^ r) * pieces + (me_ref[1] ^ relative)
            out_ref[pl.ds(target, 1), :] = table[row : row + 1, :]


def gram_step(step, me, owns, others, states, cols, relatives, chunks, groups):
    pieces = len(relatives)
    count, features = owns[step].shape
    total = pieces * count
    counts = [own.shape[0] for own in owns]
    tile = 256
    row_shapes = [(c, lanes) for c in counts]
    stack = pltpu.VMEM((total, features), jnp.bfloat16)
    params = dict(
        compiler_params=pltpu.CompilerParams(vmem_limit_bytes=24 * 2**20),
        cost_estimate=pl.CostEstimate(
            flops=2 * sum(counts) * total * features,
            bytes_accessed=2 * features * (sum(counts) + total),
            transcendentals=0,
        ),
    )
    if step < len(chunks) - 1:
        results = pl.pallas_call(
            functools.partial(gram_kernel, step, pieces, tile),
            in_specs=[vmem] * (step + pieces + step),
            out_specs=[vmem] * (step + 2),
            out_shape=[jax.ShapeDtypeStruct(s, jnp.float32) for s in row_shapes]
            + [jax.ShapeDtypeStruct((1, total), jnp.float32)],
            scratch_shapes=[stack],
            name="gram_step",
            **params,
        )(*owns, *others, *states)
        return list(results[:-1]), cols + [results[-1]]
    return pl.pallas_call(
        functools.partial(gram_last_kernel, step, relatives, chunks, groups, tile),
        in_specs=[smem] + [vmem] * (step + pieces + 2 * step),
        out_specs=vmem,
        out_shape=jax.ShapeDtypeStruct((groups * pieces, sum(chunks)), jnp.float32),
        scratch_shapes=[
            stack,
            pltpu.VMEM((1, total), jnp.float32),
            pltpu.VMEM((groups * pieces, sum(chunks)), jnp.float32),
        ]
        + [pltpu.VMEM(s, jnp.float32) for s in row_shapes],
        name="gram_last",
        **params,
    )(me, *owns, *others, *states, *cols)


def tail_kernel(capacity, members, slot_ref, part_ref, out_ref, table):
    groups = part_ref.shape[0] // members
    width = table.shape[1]
    table[...] = jnp.full(table.shape, sentinel, jnp.float32)
    for g in range(groups):
        table[g : g + 1, :capacity] = jnp.max(
            part_ref[g * members : (g + 1) * members, :], axis=0, keepdims=True
        )
    lane = lax.broadcasted_iota(jnp.int32, (lanes, lanes), 1)
    for q in range(out_ref.shape[0]):
        slot = jnp.broadcast_to(slot_ref[q : q + 1, :], (lanes, lanes)).T
        best = jnp.full((lanes, lanes), sentinel, jnp.float32)
        for g in range(groups):
            for c in range(0, width, lanes):
                entry = table[g : g + 1, c : c + lanes]
                best = jnp.maximum(
                    best, jnp.where(slot - (g * capacity + c) == lane, entry, sentinel)
                )
        out_ref[q : q + 1, :] = jnp.max(best.T, axis=0, keepdims=True)


def tail(partials, slots, capacity, members):
    groups = partials.shape[0] // members
    width = -(-capacity // lanes) * lanes
    return pl.pallas_call(
        functools.partial(tail_kernel, capacity, members),
        in_specs=[vmem, vmem],
        out_specs=vmem,
        out_shape=jax.ShapeDtypeStruct(slots.shape, jnp.float32),
        scratch_shapes=[pltpu.VMEM((groups, width), jnp.float32)],
        name="pick_rows",
    )(slots, partials)


def on_device(embeddings, send_slot):
    row_count, features = embeddings.shape
    groups = lax.axis_size("grp")
    members = lax.axis_size("blk")
    slot_count = 2 * row_count
    capacity = slot_count // groups
    chunks = chunk_sizes(capacity)
    me = jnp.stack([lax.axis_index("grp"), lax.axis_index("blk")]).astype(jnp.int32)
    slots = send_slot.reshape(row_count // lanes, lanes)
    placed = head(me, embeddings, slots, capacity, chunks, groups)
    owns, states, cols = [], [], []
    for step, size in enumerate(chunks):
        mine = placed[step * groups : (step + 1) * groups]
        arrived = {0: mine[0]}
        for r in reversed(range(1, groups)):
            arrived[r] = swap(mine[r], "grp", groups, r)
        own = jnp.concatenate([arrived[r] for r in range(groups)], axis=0)
        pieces, relatives = [own], [0]
        bit = members // 2
        while bit:
            pieces = pieces + [swap(piece, "blk", members, bit) for piece in pieces]
            relatives = relatives + [relative ^ bit for relative in relatives]
            bit //= 2
        owns.append(own)
        result = gram_step(
            step, me, owns, pieces[1:], states, cols, relatives, chunks, groups
        )
        if step < len(chunks) - 1:
            states, cols = result
    homeward = lax.all_to_all(result, ("grp", "blk"), 0, 0, tiled=True)
    return tail(homeward, slots, capacity, members).reshape(row_count)


def solution(mesh):
    in_specs = (P(("grp", "blk"), None), P(("grp", "blk")))
    out_specs = P(("grp", "blk"))
    return jax.shard_map(
        on_device, mesh=mesh, in_specs=in_specs, out_specs=out_specs, check_vma=False
    )
```

time: 173 us -> 140 us (0.81)
  blocking collectives: 92.8 us -> 10.6 us
  starting transfers between devices: 0.13 us -> 50.2 us
  waiting for transfers between devices: 18.4 us -> 52.9 us
  between operations: 13.3 us -> 0.31 us
  local copies, waits for them, and re-layouts: 13.2 us -> 2.79 us
  Pallas kernels: 31.9 us -> 22.9 us
  other arithmetic: 2.14 us -> 0.07 us
    all_to_all x5 -> x1, blocking collectives: 92.8 us -> 10.6 us  [on_device(): homeward = lax.all_to_all(result, ('grp', 'blk'), 0, 0, tiled=True)]
    ppermute x0 -> x40, waiting for transfers between devices: none -> 52.9 us  [swap(): return lax.ppermute(value, axis, [(i, i ^ bit) for i in range(size)])]
    ppermute x0 -> x40, starting transfers between devices: none -> 50.2 us  [swap(): return lax.ppermute(value, axis, [(i, i ^ bit) for i in range(size)])]
    all_gather x4 -> x0, waiting for transfers between devices: 18.4 us -> none  [on_device(): gathered = lax.all_gather(own, 'blk', axis=0, tiled=True)]
    pallas_call x5, Pallas kernels: 29.4 us -> 19.8 us  [the longest x3 10.3 us: gram_step(): pl.pallas_call(functools.partial(gram_kernel, step, pieces, tile), in_spe...]
    unnamed x29 -> x33, local copies, waits for them, and re-layouts: 11.8 us -> 2.73 us
  transfers between devices with their start and end apart: 4 -> 40, of which waited for: 2 -> 9; matrix products, arithmetic and copies ran while one was open for 0% -> 0% of each run, Pallas kernels for 10% -> 7%
where the time goes in v2:
time: 140 us
  waiting for transfers between devices  52.9 us (38%)
  starting transfers between devices  50.2 us (36%)
  Pallas kernels  22.9 us (16%)
  blocking collectives  10.6 us (8%)
  local copies, waits for them, and re-layouts  2.79 us (2%)
    ppermute x40, waiting for transfers between devices, swap(): return lax.ppermute(value, axis, [(i, i ^ bit) for i in range(size)])  52.9 us
    ppermute x40, starting transfers between devices, swap(): return lax.ppermute(value, axis, [(i, i ^ bit) for i in range(size)])  50.2 us
    all_to_all x1, blocking collectives, on_device(): homeward = lax.all_to_all(result, ('grp', 'blk'), 0, 0, tiled=True)  10.6 us
    pallas_call x3, Pallas kernels, gram_step(): pl.pallas_call(functools.partial(gram_kernel, step, pieces, tile), in_spe...  10.3 us
    pallas_call x1, Pallas kernels, gram_step(): pl.pallas_call(functools.partial(gram_last_kernel, step, relatives, chunk...  7.11 us
    pallas_call x1, Pallas kernels, head(): pl.pallas_call(functools.partial(head_kernel, capacity, chunks, groups),...  3.1 us
  transfers between devices with their start and end apart: 40, of which 9 were waited for; matrix products, arithmetic and copies ran while one was open for 0% of the time, Pallas kernels for 7%

profile of v2, /device:TPU:0, one launch (start us, length us, event | category | flops | bytes accessed | tf_op | source)
XLA Modules:
  0.0 139.8 jit_solution(3975472942914589207)
XLA Ops:
  2.0 3.1 %place_rows.1 = (bf16[48,768]{1,0:T(8,128)(2,1)S(1)}, bf16[48,768]{1,0:T(8,128)(2,1)S(1)}, bf16[48,768]{1,0:T(8,128)(2,1)S(1)}, bf16[48,768]{1,0:T(8,128)(2,1)S(...) custom-call(s32[2]{0:T(128)S(1)} %pad_add_fusion.me_ref, ...), custom_call_target="tpu_custom_call" | custom-call | tf_op jit(solution)/shard_map/place_rows/pallas_call | solution.py:52
  5.1 3.0 %collective-permute-start = (bf16[48,768]{1,0:T(8,128)(2,1)S(1)}, bf16[48,768]{1,0:T(8,128)(2,1)S(1)}, u32[]{:S(2)}, u32[]{:S(2)}) collective-permute-start(bf16[48,768]{1,0:T(8,128)(2,1)S(1)} %get-tuple-element.47), channel_id=1, source_target_pairs={{0,4},{4,0},{8,12},{12,8},{16,20},{20,16},{24,28},{28,24},{1,5},{5... | collective-permute-start | bytes 221192 | tf_op jit(solution)/shard_map/ppermute | solution.py:25
  9.8 3.0 %collective-permute-start.3 = (bf16[48,768]{1,0:T(8,128)(2,1)S(1)}, bf16[48,768]{1,0:T(8,128)(2,1)S(1)}, u32[]{:S(2)}, u32[]{:S(2)}) collective-permute-start(bf16[48,768]{1,0:T(8,128)(2,1)S(1)} %get-tuple-element.50), channel_id=1, source_target_pairs={{0,16},{4,20},{8,24},{12,28},{16,0},{20,4},{24,8},{28,12},{1,17},{... | collective-permute-start | bytes 221192 | tf_op jit(solution)/shard_map/ppermute | solution.py:25
  14.1 3.7 %collective-permute-start.5 = (bf16[48,768]{1,0:T(8,128)(2,1)S(1)}, bf16[48,768]{1,0:T(8,128)(2,1)S(1)}, u32[]{:S(2)}, u32[]{:S(2)}) collective-permute-start(bf16[48,768]{1,0:T(8,128)(2,1)S(1)} %get-tuple-element.52), channel_id=1, source_target_pairs={{0,24},{4,28},{8,16},{12,20},{16,8},{20,12},{24,0},{28,4},{1,25},{... | collective-permute-start | bytes 221192 | tf_op jit(solution)/shard_map/ppermute | solution.py:25
  20.5 3.5 %collective-permute-done.4 = bf16[48,768]{1,0:T(8,128)(2,1)S(1)} collective-permute-done((bf16[48,768]{1,0:T(8,128)(2,1)S(1)}, bf16[48,768]{1,0:T(8,128)(2,1)S(1)}, u32[]{:S(2)}, u32[]{:S(2)}) %collective-permute-start.4) | collective-permute-done | bytes 73760 | tf_op jit(solution)/shard_map/ppermute | solution.py:25
  24.6 3.4 %collective-permute-start.10 = (bf16[48,768]{1,0:T(8,128)(2,1)S(1)}, bf16[48,768]{1,0:T(8,128)(2,1)S(1)}, u32[]{:S(2)}, u32[]{:S(2)}) collective-permute-start(bf16[48,768]{1,0:T(8,128)(2,1)S(1)} %get-tuple-element.58), channel_id=1, source_target_pairs={{0,16},{4,20},{8,24},{12,28},{16,0},{20,4},{24,8},{28,12},{1,17},{... | collective-permute-start | bytes 221192 | tf_op jit(solution)/shard_map/ppermute | solution.py:25
  31.1 3.1 %collective-permute-start.13 = (bf16[48,768]{1,0:T(8,128)(2,1)S(1)}, bf16[48,768]{1,0:T(8,128)(2,1)S(1)}, u32[]{:S(2)}, u32[]{:S(2)}) collective-permute-start(bf16[48,768]{1,0:T(8,128)(2,1)S(1)} %get-tuple-element.61), channel_id=1, source_target_pairs={{0,28},{4,24},{8,20},{12,16},{16,12},{20,8},{24,4},{28,0},{1,29},{... | collective-permute-start | bytes 221192 | tf_op jit(solution)/shard_map/ppermute | solution.py:25
  34.6 4.0 %collective-permute-done.11 = bf16[48,768]{1,0:T(8,128)(2,1)S(1)} collective-permute-done((bf16[48,768]{1,0:T(8,128)(2,1)S(1)}, bf16[48,768]{1,0:T(8,128)(2,1)S(1)}, u32[]{:S(2)}, u32[]{:S(2)}) %collective-permute-start.11) | collective-permute-done | bytes 73760 | tf_op jit(solution)/shard_map/ppermute | solution.py:25
  38.7 3.4 %collective-permute-start.17 = (bf16[48,768]{1,0:T(8,128)(2,1)S(1)}, bf16[48,768]{1,0:T(8,128)(2,1)S(1)}, u32[]{:S(2)}, u32[]{:S(2)}) collective-permute-start(bf16[48,768]{1,0:T(8,128)(2,1)S(1)} %get-tuple-element.66), channel_id=1, source_target_pairs={{0,16},{4,20},{8,24},{12,28},{16,0},{20,4},{24,8},{28,12},{1,17},{... | collective-permute-start | bytes 221192 | tf_op jit(solution)/shard_map/ppermute | solution.py:25
  45.0 2.7 %collective-permute-start.20 = (bf16[48,768]{1,0:T(8,128)(2,1)S(1)}, bf16[48,768]{1,0:T(8,128)(2,1)S(1)}, u32[]{:S(2)}, u32[]{:S(2)}) collective-permute-start(bf16[48,768]{1,0:T(8,128)(2,1)S(1)} %get-tuple-element.69), channel_id=1, source_target_pairs={{0,28},{4,24},{8,20},{12,16},{16,12},{20,8},{24,4},{28,0},{1,29},{... | collective-permute-start | bytes 221192 | tf_op jit(solution)/shard_map/ppermute | solution.py:25
  48.8 4.0 %collective-permute-done.18 = bf16[48,768]{1,0:T(8,128)(2,1)S(1)} collective-permute-done((bf16[48,768]{1,0:T(8,128)(2,1)S(1)}, bf16[48,768]{1,0:T(8,128)(2,1)S(1)}, u32[]{:S(2)}, u32[]{:S(2)}) %collective-permute-start.18) | collective-permute-done | bytes 73760 | tf_op jit(solution)/shard_map/ppermute | solution.py:25
  52.8 3.1 %collective-permute-start.24 = (bf16[48,768]{1,0:T(8,128)(2,1)S(1)}, bf16[48,768]{1,0:T(8,128)(2,1)S(1)}, u32[]{:S(2)}, u32[]{:S(2)}) collective-permute-start(bf16[48,768]{1,0:T(8,128)(2,1)S(1)} %get-tuple-element.74), channel_id=1, source_target_pairs={{0,16},{4,20},{8,24},{12,28},{16,0},{20,4},{24,8},{28,12},{1,17},{... | collective-permute-start | bytes 221192 | tf_op jit(solution)/shard_map/ppermute | solution.py:25
  59.5 2.6 %collective-permute-start.26 = (bf16[48,768]{1,0:T(8,128)(2,1)S(1)}, bf16[48,768]{1,0:T(8,128)(2,1)S(1)}, u32[]{:S(2)}, u32[]{:S(2)}) collective-permute-start(bf16[48,768]{1,0:T(8,128)(2,1)S(1)} %get-tuple-element.76), channel_id=1, source_target_pairs={{0,24},{4,28},{8,16},{12,20},{16,8},{20,12},{24,0},{28,4},{1,25},{... | collective-permute-start | bytes 221192 | tf_op jit(solution)/shard_map/ppermute | solution.py:25
  66.5 2.8 %collective-permute-done.27 = bf16[48,768]{1,0:T(8,128)(2,1)S(1)} collective-permute-done((bf16[48,768]{1,0:T(8,128)(2,1)S(1)}, bf16[48,768]{1,0:T(8,128)(2,1)S(1)}, u32[]{:S(2)}, u32[]{:S(2)}) %collective-permute-start.27) | collective-permute-done | bytes 73760 | tf_op jit(solution)/shard_map/ppermute | solution.py:25
  69.8 4.4 %collective-permute-done.37.refs_1_ = bf16[384,768]{1,0:T(8,128)(2,1)S(1)} collective-permute-done((bf16[384,768]{1,0:T(8,128)(2,1)S(1)}, bf16[384,768]{1,0:T(8,128)(2,1)S(1)}, u32[]{:S(2)}, u32[]{:S(2)}) %collective-permute-start.37) | collective-permute-done | bytes 589856 | tf_op jit(solution)/shard_map/ppermute | solution.py:25
  75.6 11.2 %collective-permute-done.34.refs_2_ = bf16[384,768]{1,0:T(8,128)(2,1)S(1)} collective-permute-done((bf16[384,768]{1,0:T(8,128)(2,1)S(1)}, bf16[384,768]{1,0:T(8,128)(2,1)S(1)}, u32[]{:S(2)}, u32[]{:S(2)}) %collective-permute-start.34) | collective-permute-done | bytes 589856 | tf_op jit(solution)/shard_map/ppermute | solution.py:25
  87.4 12.1 %collective-permute-done.31.refs_3_ = bf16[384,768]{1,0:T(8,128)(2,1)S(1)} collective-permute-done((bf16[384,768]{1,0:T(8,128)(2,1)S(1)}, bf16[384,768]{1,0:T(8,128)(2,1)S(1)}, u32[]{:S(2)}, u32[]{:S(2)}) %collective-permute-start.31) | collective-permute-done | bytes 589856 | tf_op jit(solution)/shard_map/ppermute | solution.py:25
  99.5 8.7 %collective-permute-done.28.refs_4_ = bf16[384,768]{1,0:T(8,128)(2,1)S(1)} collective-permute-done((bf16[384,768]{1,0:T(8,128)(2,1)S(1)}, bf16[384,768]{1,0:T(8,128)(2,1)S(1)}, u32[]{:S(2)}, u32[]{:S(2)}) %collective-permute-start.28) | collective-permute-done | bytes 589856 | tf_op jit(solution)/shard_map/ppermute | solution.py:25
  108.7 2.4 %gram_step.3 = (f32[384,128]{1,0:T(8,128)S(1)}, f32[1,1536]{1,0:T(1,128)S(1)}) custom-call(bf16[384,768]{1,0:T(8,128)(2,1)S(1)} %constant_dynamic-update-slice_fusion.refs_0_, bf16[384,768]{1,0:T(8,128)(2,1)S(1)} %collective-permute-done.37.refs_1_, bf16[384,768]{1,0:T(8,128)(2,1)S(1)} %collective-permute-done.38.refs_2_, ...), custom_call_target="tpu_custom_call" | custom-call | flops 905969664 | bytes 2949120 | tf_op jit(solution)/shard_map/gram_step/pallas_call | solution.py:166
  111.1 3.5 %gram_step.4 = (f32[384,128]{1,0:T(8,128)S(1)}, f32[384,128]{1,0:T(8,128)S(1)}, f32[1,1536]{1,0:T(1,128)S(1)}) custom-call(bf16[384,768]{1,0:T(8,128)(2,1)S(1)} %constant_dynamic-update-slice_fusion.refs_0_, bf16[384,768]{1,0:T(8,128)(2,1)S(1)} %constant_dynamic-update-slice_fusion.8.refs_1_, bf16[384,768]{1,0:T(8,128)(2,1)S(1)} %collective-permute-done.34.refs_2_, ...), custom_call_target="tpu_custom_call" | custom-call | flops 1811939328 | bytes 3538944 | tf_op jit(solution)/shard_map/gram_step/pallas_call | solution.py:166
  114.7 4.4 %gram_step.5 = (f32[384,128]{1,0:T(8,128)S(1)}, f32[384,128]{1,0:T(8,128)S(1)}, f32[384,128]{1,0:T(8,128)S(1)}, f32[1,1536]{1,0:T(1,128)S(1)}) custom-call(bf16[384,768]{1,0:T(8,128)(2,1)S(1)} %constant_dynamic-update-slice_fusion.refs_0_, bf16[384,768]{1,0:T(8,128)(2,1)S(1)} %constant_dynamic-update-slice_fusion.8.refs_1_, ...), custom_call_target="tpu_custom_call" | custom-call | flops 2717908992 | bytes 4128768 | tf_op jit(solution)/shard_map/gram_step/pallas_call | solution.py:166
  119.1 7.1 %gram_last.1 = f32[32,192]{1,0:T(8,128)S(1)} custom-call(s32[2]{0:T(128)S(1)} %pad_add_fusion.me_ref, bf16[384,768]{1,0:T(8,128)(2,1)S(1)} %constant_dynamic-update-slice_fusion.refs_0_, bf16[384,768]{1,0:T(8,128)(2,1)S(1)} %constant_dynamic-update-slice_fusion.8.refs_1_, bf16[384,768]{1,0:T(8,128)(2,1)S(1)} %constant_dynamic-update-slice_fusion.16.refs_2_, ...), custom_call_target="tpu_custom_call" | custom-call | flops 3623878656 | bytes 4718592 | tf_op jit(solution)/shard_map/gram_last/pallas_call | solution.py:177
  126.3 10.6 %all_to_all.11 = f32[32,1,192]{2,1,0:T(1,128)S(1)} all-to-all(f32[32,1,192]{2,1,0:T(1,128)S(1)} %copy.3), channel_id=1, replica_groups=mesh['grp'=8,'blk'=4] {'grp','blk'}, dimensions={0} | all-to-all | bytes 49152 | tf_op jit(solution)/shard_map/all_to_all | solution.py:256
  137.5 2.3 %pick_rows.1 = f32[6,128]{1,0:T(8,128)} custom-call(s32[6,128]{1,0:T(8,128)} %bitcast.9, f32[32,192]{1,0:T(8,128)} %bitcast.11), custom_call_target="tpu_custom_call" | custom-call | tf_op jit(solution)/shard_map/pick_rows/pallas_call | solution.py:217
  (102 shorter events, 27.2 us)
Async XLA Ops:
  12.7 11.3 %collective-permute-start.4 = (bf16[48,768]{1,0:T(8,128)(2,1)S(1)}, bf16[48,768]{1,0:T(8,128)(2,1)S(1)}, u32[]{:S(2)}, u32[]{:S(2)}) collective-permute-start(bf16[48,768]{1,0:T(8,128)(2,1)S(1)} %get-tuple-element.51), channel_id=1, source_target_pairs={{0,20},{4,16},{8,28},{12,24},{16,4},{20,0},{24,12},{28,8},{1,21},{... | collective-permute-start | bytes 221192 | tf_op jit(solution)/shard_map/ppermute | solution.py:25
  14.1 10.5 %collective-permute-start.5 = (bf16[48,768]{1,0:T(8,128)(2,1)S(1)}, bf16[48,768]{1,0:T(8,128)(2,1)S(1)}, u32[]{:S(2)}, u32[]{:S(2)}) collective-permute-start(bf16[48,768]{1,0:T(8,128)(2,1)S(1)} %get-tuple-element.52), channel_id=1, source_target_pairs={{0,24},{4,28},{8,16},{12,20},{16,8},{20,12},{24,0},{28,4},{1,25},{... | collective-permute-start | bytes 221192 | tf_op jit(solution)/shard_map/ppermute | solution.py:25
  17.8 10.3 %collective-permute-start.6 = (bf16[48,768]{1,0:T(8,128)(2,1)S(1)}, bf16[48,768]{1,0:T(8,128)(2,1)S(1)}, u32[]{:S(2)}, u32[]{:S(2)}) collective-permute-start(bf16[48,768]{1,0:T(8,128)(2,1)S(1)} %get-tuple-element.53), channel_id=1, source_target_pairs={{0,28},{4,24},{8,20},{12,16},{16,12},{20,8},{24,4},{28,0},{1,29},{... | collective-permute-start | bytes 221192 | tf_op jit(solution)/shard_map/ppermute | solution.py:25
  17.9 11.1 %collective-permute-start.7 = (bf16[48,768]{1,0:T(8,128)(2,1)S(1)}, bf16[48,768]{1,0:T(8,128)(2,1)S(1)}, u32[]{:S(2)}, u32[]{:S(2)}) collective-permute-start(bf16[48,768]{1,0:T(8,128)(2,1)S(1)} %get-tuple-element.55), channel_id=1, source_target_pairs={{0,4},{4,0},{8,12},{12,8},{16,20},{20,16},{24,28},{28,24},{1,5},{5... | collective-permute-start | bytes 221192 | tf_op jit(solution)/shard_map/ppermute | solution.py:25
  19.6 11.5 %collective-permute-start.8 = (bf16[48,768]{1,0:T(8,128)(2,1)S(1)}, bf16[48,768]{1,0:T(8,128)(2,1)S(1)}, u32[]{:S(2)}, u32[]{:S(2)}) collective-permute-start(bf16[48,768]{1,0:T(8,128)(2,1)S(1)} %get-tuple-element.56), channel_id=1, source_target_pairs={{0,8},{4,12},{8,0},{12,4},{16,24},{20,28},{24,16},{28,20},{1,9},{5... | collective-permute-start | bytes 221192 | tf_op jit(solution)/shard_map/ppermute | solution.py:25
  24.0 10.3 %collective-permute-start.9 = (bf16[48,768]{1,0:T(8,128)(2,1)S(1)}, bf16[48,768]{1,0:T(8,128)(2,1)S(1)}, u32[]{:S(2)}, u32[]{:S(2)}) collective-permute-start(bf16[48,768]{1,0:T(8,128)(2,1)S(1)} %get-tuple-element.57), channel_id=1, source_target_pairs={{0,12},{4,8},{8,4},{12,0},{16,28},{20,24},{24,20},{28,16},{1,13},{... | collective-permute-start | bytes 221192 | tf_op jit(solution)/shard_map/ppermute | solution.py:25
  28.1 10.5 %collective-permute-start.11 = (bf16[48,768]{1,0:T(8,128)(2,1)S(1)}, bf16[48,768]{1,0:T(8,128)(2,1)S(1)}, u32[]{:S(2)}, u32[]{:S(2)}) collective-permute-start(bf16[48,768]{1,0:T(8,128)(2,1)S(1)} %get-tuple-element.59), channel_id=1, source_target_pairs={{0,20},{4,16},{8,28},{12,24},{16,4},{20,0},{24,12},{28,8},{1,21},{... | collective-permute-start | bytes 221192 | tf_op jit(solution)/shard_map/ppermute | solution.py:25
  31.1 11.0 %collective-permute-start.13 = (bf16[48,768]{1,0:T(8,128)(2,1)S(1)}, bf16[48,768]{1,0:T(8,128)(2,1)S(1)}, u32[]{:S(2)}, u32[]{:S(2)}) collective-permute-start(bf16[48,768]{1,0:T(8,128)(2,1)S(1)} %get-tuple-element.61), channel_id=1, source_target_pairs={{0,28},{4,24},{8,20},{12,16},{16,12},{20,8},{24,4},{28,0},{1,29},{... | collective-permute-start | bytes 221192 | tf_op jit(solution)/shard_map/ppermute | solution.py:25
  34.5 10.5 %collective-permute-start.15 = (bf16[48,768]{1,0:T(8,128)(2,1)S(1)}, bf16[48,768]{1,0:T(8,128)(2,1)S(1)}, u32[]{:S(2)}, u32[]{:S(2)}) collective-permute-start(bf16[48,768]{1,0:T(8,128)(2,1)S(1)} %get-tuple-element.64), channel_id=1, source_target_pairs={{0,8},{4,12},{8,0},{12,4},{16,24},{20,28},{24,16},{28,20},{1,9},{5... | collective-permute-start | bytes 221192 | tf_op jit(solution)/shard_map/ppermute | solution.py:25
  42.1 10.6 %collective-permute-start.18 = (bf16[48,768]{1,0:T(8,128)(2,1)S(1)}, bf16[48,768]{1,0:T(8,128)(2,1)S(1)}, u32[]{:S(2)}, u32[]{:S(2)}) collective-permute-start(bf16[48,768]{1,0:T(8,128)(2,1)S(1)} %get-tuple-element.67), channel_id=1, source_target_pairs={{0,20},{4,16},{8,28},{12,24},{16,4},{20,0},{24,12},{28,8},{1,21},{... | collective-permute-start | bytes 221192 | tf_op jit(solution)/shard_map/ppermute | solution.py:25
  45.0 10.9 %collective-permute-start.20 = (bf16[48,768]{1,0:T(8,128)(2,1)S(1)}, bf16[48,768]{1,0:T(8,128)(2,1)S(1)}, u32[]{:S(2)}, u32[]{:S(2)}) collective-permute-start(bf16[48,768]{1,0:T(8,128)(2,1)S(1)} %get-tuple-element.69), channel_id=1, source_target_pairs={{0,28},{4,24},{8,20},{12,16},{16,12},{20,8},{24,4},{28,0},{1,29},{... | collective-permute-start | bytes 221192 | tf_op jit(solution)/shard_map/ppermute | solution.py:25
  48.7 10.7 %collective-permute-start.22 = (bf16[48,768]{1,0:T(8,128)(2,1)S(1)}, bf16[48,768]{1,0:T(8,128)(2,1)S(1)}, u32[]{:S(2)}, u32[]{:S(2)}) collective-permute-start(bf16[48,768]{1,0:T(8,128)(2,1)S(1)} %get-tuple-element.72), channel_id=1, source_target_pairs={{0,8},{4,12},{8,0},{12,4},{16,24},{20,28},{24,16},{28,20},{1,9},{5... | collective-permute-start | bytes 221192 | tf_op jit(solution)/shard_map/ppermute | solution.py:25
  57.9 16.3 %collective-permute-start.37 = (bf16[384,768]{1,0:T(8,128)(2,1)S(1)}, bf16[384,768]{1,0:T(8,128)(2,1)S(1)}, u32[]{:S(2)}, u32[]{:S(2)}) collective-permute-start(bf16[384,768]{1,0:T(8,128)(2,1)S(1)} %constant_dynamic-update-slice_fusion.refs_0_), channel_id=1, source_target_pairs={{0,2},{1,3},{2,0},{3,1},{4,6},{5,7},{6,4},{7,5},{8,10},{9,11},{10,... | collective-permute-start | bytes 1769480 | tf_op jit(solution)/shard_map/ppermute | solution.py:25
  59.4 16.3 %collective-permute-start.38 = (bf16[384,768]{1,0:T(8,128)(2,1)S(1)}, bf16[384,768]{1,0:T(8,128)(2,1)S(1)}, u32[]{:S(2)}, u32[]{:S(2)}) collective-permute-start(bf16[384,768]{1,0:T(8,128)(2,1)S(1)} %constant_dynamic-update-slice_fusion.refs_0_), channel_id=1, source_target_pairs={{0,1},{1,0},{2,3},{3,2},{4,5},{5,4},{6,7},{7,6},{8,9},{9,8},{10,11... | collective-permute-start | bytes 1769480 | tf_op jit(solution)/shard_map/ppermute | solution.py:25
  63.3 23.5 %collective-permute-start.34 = (bf16[384,768]{1,0:T(8,128)(2,1)S(1)}, bf16[384,768]{1,0:T(8,128)(2,1)S(1)}, u32[]{:S(2)}, u32[]{:S(2)}) collective-permute-start(bf16[384,768]{1,0:T(8,128)(2,1)S(1)} %constant_dynamic-update-slice_fusion.8.refs_1_), channel_id=1, source_target_pairs={{0,2},{1,3},{2,0},{3,1},{4,6},{5,7},{6,4},{7,5},{8,10},{9,11},{10,... | collective-permute-start | bytes 1769480 | tf_op jit(solution)/shard_map/ppermute | solution.py:25
  66.5 20.4 %collective-permute-start.35 = (bf16[384,768]{1,0:T(8,128)(2,1)S(1)}, bf16[384,768]{1,0:T(8,128)(2,1)S(1)}, u32[]{:S(2)}, u32[]{:S(2)}) collective-permute-start(bf16[384,768]{1,0:T(8,128)(2,1)S(1)} %constant_dynamic-update-slice_fusion.8.refs_1_), channel_id=1, source_target_pairs={{0,1},{1,0},{2,3},{3,2},{4,5},{5,4},{6,7},{7,6},{8,9},{9,8},{10,11... | collective-permute-start | bytes 1769480 | tf_op jit(solution)/shard_map/ppermute | solution.py:25
  69.3 30.2 %collective-permute-start.31 = (bf16[384,768]{1,0:T(8,128)(2,1)S(1)}, bf16[384,768]{1,0:T(8,128)(2,1)S(1)}, u32[]{:S(2)}, u32[]{:S(2)}) collective-permute-start(bf16[384,768]{1,0:T(8,128)(2,1)S(1)} %constant_dynamic-update-slice_fusion.16.refs_2_), channel_id=1, source_target_pairs={{0,2},{1,3},{2,0},{3,1},{4,6},{5,7},{6,4},{7,5},{8,10},{9,11},{10,... | collective-permute-start | bytes 1769480 | tf_op jit(solution)/shard_map/ppermute | solution.py:25
  74.2 34.0 %collective-permute-start.28 = (bf16[384,768]{1,0:T(8,128)(2,1)S(1)}, bf16[384,768]{1,0:T(8,128)(2,1)S(1)}, u32[]{:S(2)}, u32[]{:S(2)}) collective-permute-start(bf16[384,768]{1,0:T(8,128)(2,1)S(1)} %constant_dynamic-update-slice_fusion.24.refs_3_), channel_id=1, source_target_pairs={{0,2},{1,3},{2,0},{3,1},{4,6},{5,7},{6,4},{7,5},{8,10},{9,11},{10,... | collective-permute-start | bytes 1769480 | tf_op jit(solution)/shard_map/ppermute | solution.py:25
  75.6 32.6 %collective-permute-start.39 = (bf16[384,768]{1,0:T(8,128)(2,1)S(1)}, bf16[384,768]{1,0:T(8,128)(2,1)S(1)}, u32[]{:S(2)}, u32[]{:S(2)}) collective-permute-start(bf16[384,768]{1,0:T(8,128)(2,1)S(1)} %collective-permute-done.37.refs_1_), channel_id=1, source_target_pairs={{0,1},{1,0},{2,3},{3,2},{4,5},{5,4},{6,7},{7,6},{8,9},{9,8},{10,11... | collective-permute-start | bytes 1769480 | tf_op jit(solution)/shard_map/ppermute | solution.py:25
  86.9 24.3 %collective-permute-start.36 = (bf16[384,768]{1,0:T(8,128)(2,1)S(1)}, bf16[384,768]{1,0:T(8,128)(2,1)S(1)}, u32[]{:S(2)}, u32[]{:S(2)}) collective-permute-start(bf16[384,768]{1,0:T(8,128)(2,1)S(1)} %collective-permute-done.34.refs_2_), channel_id=1, source_target_pairs={{0,1},{1,0},{2,3},{3,2},{4,5},{5,4},{6,7},{7,6},{8,9},{9,8},{10,11... | collective-permute-start | bytes 1769480 | tf_op jit(solution)/shard_map/ppermute | solution.py:25
  86.9 27.8 %collective-permute-start.32 = (bf16[384,768]{1,0:T(8,128)(2,1)S(1)}, bf16[384,768]{1,0:T(8,128)(2,1)S(1)}, u32[]{:S(2)}, u32[]{:S(2)}) collective-permute-start(bf16[384,768]{1,0:T(8,128)(2,1)S(1)} %constant_dynamic-update-slice_fusion.16.refs_2_), channel_id=1, source_target_pairs={{0,1},{1,0},{2,3},{3,2},{4,5},{5,4},{6,7},{7,6},{8,9},{9,8},{10,11... | collective-permute-start | bytes 1769480 | tf_op jit(solution)/shard_map/ppermute | solution.py:25
  99.5 15.2 %collective-permute-start.33 = (bf16[384,768]{1,0:T(8,128)(2,1)S(1)}, bf16[384,768]{1,0:T(8,128)(2,1)S(1)}, u32[]{:S(2)}, u32[]{:S(2)}) collective-permute-start(bf16[384,768]{1,0:T(8,128)(2,1)S(1)} %collective-permute-done.31.refs_3_), channel_id=1, source_target_pairs={{0,1},{1,0},{2,3},{3,2},{4,5},{5,4},{6,7},{7,6},{8,9},{9,8},{10,11... | collective-permute-start | bytes 1769480 | tf_op jit(solution)/shard_map/ppermute | solution.py:25
  108.2 10.9 %collective-permute-start.29 = (bf16[384,768]{1,0:T(8,128)(2,1)S(1)}, bf16[384,768]{1,0:T(8,128)(2,1)S(1)}, u32[]{:S(2)}, u32[]{:S(2)}) collective-permute-start(bf16[384,768]{1,0:T(8,128)(2,1)S(1)} %constant_dynamic-update-slice_fusion.24.refs_3_), channel_id=1, source_target_pairs={{0,1},{1,0},{2,3},{3,2},{4,5},{5,4},{6,7},{7,6},{8,9},{9,8},{10,11... | collective-permute-start | bytes 1769480 | tf_op jit(solution)/shard_map/ppermute | solution.py:25
  108.2 10.9 %collective-permute-start.30 = (bf16[384,768]{1,0:T(8,128)(2,1)S(1)}, bf16[384,768]{1,0:T(8,128)(2,1)S(1)}, u32[]{:S(2)}, u32[]{:S(2)}) collective-permute-start(bf16[384,768]{1,0:T(8,128)(2,1)S(1)} %collective-permute-done.28.refs_4_), channel_id=1, source_target_pairs={{0,1},{1,0},{2,3},{3,2},{4,5},{5,4},{6,7},{7,6},{8,9},{9,8},{10,11... | collective-permute-start | bytes 1769480 | tf_op jit(solution)/shard_map/ppermute | solution.py:25
  (18 other events, 143.4 us)

commit v3 on v2

--- a/solution.py
+++ b/solution.py
@@ -21,6 +21,10 @@
     return (capacity // count,) * count
 
 
+def after(value, *earlier):
+    return lax.optimization_barrier((value,) + earlier)[0]
+
+
 def swap(value, axis, size, bit):
     return lax.ppermute(value, axis, [(i, i ^ bit) for i in range(size)])
 
@@ -31,10 +35,11 @@
         wide * lax.rsqrt(jnp.sum(wide * wide, axis=-1, keepdims=True) + epsilon)
     ).astype(jnp.bfloat16)
     slots = jnp.concatenate([slot_ref[q : q + 1, :] for q in range(slot_ref.shape[0])], axis=1)
-    first = 0
+    first, high = 0, groups // 2
     for step, size in enumerate(chunks):
         place = lax.broadcasted_iota(jnp.int32, (groups, size, 1), 1)
-        group = lax.broadcasted_iota(jnp.int32, (groups, size, 1), 0) ^ me_ref[0]
+        order = lax.broadcasted_iota(jnp.int32, (groups, size, 1), 0)
+        group = (order % high * 2 + order // high) ^ me_ref[0]
         wanted = (group * capacity + place + first).reshape(groups * size, 1)
         pick = jnp.where(wanted == slots, 1.0, 0.0)
         live = jnp.max(pick, axis=1, keepdims=True)
@@ -42,8 +47,8 @@
         lane = lax.broadcasted_iota(jnp.int32, (1, placed.shape[1]), 1)
         mark = jnp.where(lane == 0, dead_mark, 0.0)
         placed = (placed + (1.0 - live) * mark).astype(jnp.bfloat16)
-        for r in range(groups):
-            out_refs[step * groups + r][...] = placed[r * size : (r + 1) * size, :]
+        out_refs[2 * step][...] = placed[: high * size, :]
+        out_refs[2 * step + 1][...] = placed[high * size :, :]
         first += size
 
 
@@ -52,11 +57,11 @@
     return pl.pallas_call(
         functools.partial(head_kernel, capacity, chunks, groups),
         in_specs=[smem, vmem, vmem],
-        out_specs=[vmem] * (groups * len(chunks)),
+        out_specs=[vmem] * (2 * len(chunks)),
         out_shape=[
-            jax.ShapeDtypeStruct((size, features), jnp.bfloat16)
+            jax.ShapeDtypeStruct((groups // 2 * size, features), jnp.bfloat16)
             for size in chunks
-            for _ in range(groups)
+            for _ in range(2)
         ],
         compiler_params=pltpu.CompilerParams(vmem_limit_bytes=32 * 2**20),
         name="place_rows",
@@ -72,9 +77,10 @@
 
 def gram_body(own_refs, piece_refs, row_refs, col_ref, stack, tile):
     step = len(own_refs) - 1
-    count = own_refs[step].shape[0]
-    for p, piece_ref in enumerate(piece_refs):
-        stack[p * count : (p + 1) * count, :] = piece_ref[...]
+    start = 0
+    for piece_ref in piece_refs:
+        stack[start : start + piece_ref.shape[0], :] = piece_ref[...]
+        start += piece_ref.shape[0]
     row_refs[step][...] = jnp.full(row_refs[step].shape, sentinel, jnp.float32)
     nt = (((1,), (1,)), ((), ()))
 
@@ -102,29 +108,25 @@
         col_ref[0:1, pl.ds(first, tile)] = col_best
 
 
-def gram_kernel(step, pieces, tile, *refs):
-    owns = refs[: step + 1]
-    others = refs[step + 1 : step + pieces]
-    refs = refs[step + pieces :]
+def gram_kernel(step, tile, *refs):
+    owns, pieces, refs = refs[: step + 1], refs[step + 1 : step + 3], refs[step + 3 :]
     states, refs = refs[:step], refs[step:]
     rows, col, stack = refs[: step + 1], refs[step + 1], refs[step + 2]
     for state, row in zip(states, rows):
         row[...] = state[...]
-    gram_body(owns, (owns[step],) + others, rows, col, stack, tile)
+    gram_body(owns, pieces, rows, col, stack, tile)
 
 
 def gram_last_kernel(step, relatives, chunks, groups, tile, me_ref, *refs):
-    pieces = len(relatives)
-    owns = refs[: step + 1]
-    others = refs[step + 1 : step + pieces]
-    refs = refs[step + pieces :]
+    members = len(relatives)
+    owns, pieces, refs = refs[: step + 1], refs[step + 1 : step + 3], refs[step + 3 :]
     states, refs = refs[:step], refs[step:]
     cols, refs = refs[:step], refs[step:]
     out_ref, stack, col, table = refs[:4]
     rows = refs[4:]
     for state, row in zip(states, rows):
         row[...] = state[...]
-    gram_body(owns, (owns[step],) + others, rows, col, stack, tile)
+    gram_body(owns, pieces, rows, col, stack, tile)
     first = 0
     for k, size in enumerate(chunks):
         col_k = (cols[k] if k < step else col)[0:1, :]
@@ -136,20 +138,20 @@
                 best = col_k[:, start : start + size]
                 if p == 0:
                     best = jnp.maximum(best, row_k[:, r * size : (r + 1) * size])
-                row = r * pieces + p
+                row = r * members + p
                 table[row : row + 1, first : first + size] = best
         first += size
     for r in range(groups):
         for p, relative in enumerate(relatives):
-            row = r * pieces + p
-            target = (me_ref[0] ^ r) * pieces + (me_ref[1] ^ relative)
+            row = r * members + p
+            target = (me_ref[0] ^ r) * members + (me_ref[1] ^ relative)
             out_ref[pl.ds(target, 1), :] = table[row : row + 1, :]
 
 
-def gram_step(step, me, owns, others, states, cols, relatives, chunks, groups):
-    pieces = len(relatives)
-    count, features = owns[step].shape
-    total = pieces * count
+def gram_step(step, me, owns, pieces, states, cols, relatives, chunks, groups):
+    members = len(relatives)
+    features = owns[step].shape[1]
+    total = members * owns[step].shape[0]
     counts = [own.shape[0] for own in owns]
     tile = 256
     row_shapes = [(c, lanes) for c in counts]
@@ -164,30 +166,30 @@
     )
     if step < len(chunks) - 1:
         results = pl.pallas_call(
-            functools.partial(gram_kernel, step, pieces, tile),
-            in_specs=[vmem] * (step + pieces + step),
+            functools.partial(gram_kernel, step, tile),
+            in_specs=[vmem] * (step + 3 + step),
             out_specs=[vmem] * (step + 2),
             out_shape=[jax.ShapeDtypeStruct(s, jnp.float32) for s in row_shapes]
             + [jax.ShapeDtypeStruct((1, total), jnp.float32)],
             scratch_shapes=[stack],
             name="gram_step",
             **params,
-        )(*owns, *others, *states)
+        )(*owns, *pieces, *states)
         return list(results[:-1]), cols + [results[-1]]
     return pl.pallas_call(
         functools.partial(gram_last_kernel, step, relatives, chunks, groups, tile),
-        in_specs=[smem] + [vmem] * (step + pieces + 2 * step),
+        in_specs=[smem] + [vmem] * (step + 3 + 2 * step),
         out_specs=vmem,
-        out_shape=jax.ShapeDtypeStruct((groups * pieces, sum(chunks)), jnp.float32),
+        out_shape=jax.ShapeDtypeStruct((groups * members, sum(chunks)), jnp.float32),
         scratch_shapes=[
             stack,
             pltpu.VMEM((1, total), jnp.float32),
-            pltpu.VMEM((groups * pieces, sum(chunks)), jnp.float32),
+            pltpu.VMEM((groups * members, sum(chunks)), jnp.float32),
         ]
         + [pltpu.VMEM(s, jnp.float32) for s in row_shapes],
         name="gram_last",
         **params,
-    )(me, *owns, *others, *states, *cols)
+    )(me, *owns, *pieces, *states, *cols)
 
 
 def tail_kernel(capacity, members, slot_ref, part_ref, out_ref, table):
@@ -234,25 +236,32 @@
     me = jnp.stack([lax.axis_index("grp"), lax.axis_index("blk")]).astype(jnp.int32)
     slots = send_slot.reshape(row_count // lanes, lanes)
     placed = head(me, embeddings, slots, capacity, chunks, groups)
-    owns, states, cols = [], [], []
+    high = groups // 2
+    near, owns, across, done, states, cols = [], [], [], [], [], []
     for step, size in enumerate(chunks):
-        mine = placed[step * groups : (step + 1) * groups]
-        arrived = {0: mine[0]}
-        for r in reversed(range(1, groups)):
-            arrived[r] = swap(mine[r], "grp", groups, r)
-        own = jnp.concatenate([arrived[r] for r in range(groups)], axis=0)
-        pieces, relatives = [own], [0]
-        bit = members // 2
-        while bit:
-            pieces = pieces + [swap(piece, "blk", members, bit) for piece in pieces]
-            relatives = relatives + [relative ^ bit for relative in relatives]
-            bit //= 2
+        keep, send = placed[2 * step : 2 * step + 2]
+        near.append(swap(after(send, *near[: max(step - 1, 0)][-1:]), "grp", groups, 1))
+        arrived = []
+        for z in range(high):
+            span = slice(z * size, (z + 1) * size)
+            pair = jnp.concatenate([keep[span], near[step][span]], axis=0)
+            if z > 0:
+                earlier = owns[step - 2 : step - 1] if step >= 2 else []
+                earlier = earlier + (across[step - 3 : step - 2] if step >= 3 else [])
+                pair = swap(after(pair, *earlier), "grp", groups, 2 * z)
+            arrived.append(pair)
+        own = jnp.concatenate(arrived, axis=0)
         owns.append(own)
+        earlier = done[step - 2 : step - 1] if step >= 2 else []
+        across.append(swap(after(own, *earlier), "blk", members, 2))
+        pair = jnp.concatenate([own, across[step]], axis=0)
+        other = swap(pair, "blk", members, 1)
         result = gram_step(
-            step, me, owns, pieces[1:], states, cols, relatives, chunks, groups
+            step, me, owns, (pair, other), states, cols, (0, 2, 1, 3), chunks, groups
         )
         if step < len(chunks) - 1:
             states, cols = result
+            done.append(cols[-1])
     homeward = lax.all_to_all(result, ("grp", "blk"), 0, 0, tiled=True)
     return tail(homeward, slots, capacity, members).reshape(row_count)
 

time: 140 us -> 134 us (0.957)
  starting transfers between devices: 50.2 us -> 43.9 us
  waiting for transfers between devices: 52.9 us -> 46.7 us
  blocking collectives: 10.6 us -> 16.4 us
    ppermute x40 -> x24, starting transfers between devices: 50.2 us -> 43.9 us  [swap(): return lax.ppermute(value, axis, [(i, i ^ bit) for i in range(size)])]
    ppermute x40 -> x24, waiting for transfers between devices: 52.9 us -> 46.7 us  [swap(): return lax.ppermute(value, axis, [(i, i ^ bit) for i in range(size)])]
    all_to_all x1, blocking collectives: 10.6 us -> 16.4 us  [on_device(): homeward = lax.all_to_all(result, ('grp', 'blk'), 0, 0, tiled=True)]
    unnamed x33 -> x24, local copies, waits for them, and re-layouts: 2.73 us -> 3.01 us
  transfers between devices with their start and end apart: 40 -> 24, of which waited for: 9 -> 10; matrix products, arithmetic and copies ran while one was open for 0% -> 1% of each run, Pallas kernels for 7% -> 8%
where the time goes in v3:
time: 134 us
  waiting for transfers between devices  46.7 us (35%)
  starting transfers between devices  43.9 us (33%)
  Pallas kernels  22.9 us (17%)
  blocking collectives  16.4 us (12%)
  local copies, waits for them, and re-layouts  3.21 us (2%)
    ppermute x24, waiting for transfers between devices, swap(): return lax.ppermute(value, axis, [(i, i ^ bit) for i in range(size)])  46.7 us
    ppermute x24, starting transfers between devices, swap(): return lax.ppermute(value, axis, [(i, i ^ bit) for i in range(size)])  43.9 us
    all_to_all x1, blocking collectives, on_device(): homeward = lax.all_to_all(result, ('grp', 'blk'), 0, 0, tiled=True)  16.4 us
    pallas_call x3, Pallas kernels, gram_step(): pl.pallas_call(functools.partial(gram_kernel, step, tile), in_specs=[vmem...  10.3 us
    pallas_call x1, Pallas kernels, gram_step(): pl.pallas_call(functools.partial(gram_last_kernel, step, relatives, chunk...  7.17 us
    pallas_call x1, Pallas kernels, head(): pl.pallas_call(functools.partial(head_kernel, capacity, chunks, groups),...  3.08 us
    unnamed x24, local copies, waits for them, and re-layouts  3.01 us
  transfers between devices with their start and end apart: 24, of which 10 were waited for; matrix products, arithmetic and copies ran while one was open for 1% of the time, Pallas kernels for 8%

profile of v3, /device:TPU:0, one launch (start us, length us, event | category | flops | bytes accessed | tf_op | source)
XLA Modules:
  0.0 133.7 jit_solution(10512780735605154987)
XLA Ops:
  2.0 3.1 %place_rows.1 = (bf16[192,768]{1,0:T(8,128)(2,1)S(1)}, bf16[192,768]{1,0:T(8,128)(2,1)S(1)}, bf16[192,768]{1,0:T(8,128)(2,1)S(1)}, bf16[192,768]{1,0:T(8,128)(2,...) custom-call(s32[2]{0:T(128)S(1)} %pad_add_fusion.me_ref, ...), custom_call_target="tpu_custom_call" | custom-call | tf_op jit(solution)/shard_map/place_rows/pallas_call | solution.py:57
  5.1 3.0 %collective-permute-start = (bf16[192,768]{1,0:T(8,128)(2,1)S(1)}, bf16[192,768]{1,0:T(8,128)(2,1)S(1)}, u32[]{:S(2)}, u32[]{:S(2)}) collective-permute-start(bf16[192,768]{1,0:T(8,128)(2,1)S(1)} %get-tuple-element.33), channel_id=1, source_target_pairs={{0,4},{4,0},{8,12},{12,8},{16,20},{20,16},{24,28},{28,24},{1,5},{5... | collective-permute-start | bytes 884744 | tf_op jit(solution)/shard_map/ppermute | solution.py:29
  8.4 7.6 %collective-permute-done = bf16[192,768]{1,0:T(8,128)(2,1)S(1)} collective-permute-done((bf16[192,768]{1,0:T(8,128)(2,1)S(1)}, bf16[192,768]{1,0:T(8,128)(2,1)S(1)}, u32[]{:S(2)}, u32[]{:S(2)}) %collective-permute-start) | collective-permute-done | bytes 294944 | tf_op jit(solution)/shard_map/ppermute | solution.py:29
  16.0 2.2 %collective-permute-start.1 = (bf16[96,768]{1,0:T(8,128)(2,1)S(1)}, bf16[96,768]{1,0:T(8,128)(2,1)S(1)}, u32[]{:S(2)}, u32[]{:S(2)}) collective-permute-start(bf16[96,768]{1,0:T(8,128)(2,1)S(1)} %pad_maximum_fusion), channel_id=1, source_target_pairs={{0,8},{4,12},{8,0},{12,4},{16,24},{20,28},{24,16},{28,20},{1,9},{5... | collective-permute-start | bytes 442376 | tf_op jit(solution)/shard_map/ppermute | solution.py:29
  18.2 2.7 %collective-permute-start.2 = (bf16[96,768]{1,0:T(8,128)(2,1)S(1)}, bf16[96,768]{1,0:T(8,128)(2,1)S(1)}, u32[]{:S(2)}, u32[]{:S(2)}) collective-permute-start(bf16[96,768]{1,0:T(8,128)(2,1)S(1)} %pad_maximum_fusion.1), channel_id=1, source_target_pairs={{0,16},{4,20},{8,24},{12,28},{16,0},{20,4},{24,8},{28,12},{1,17},{... | collective-permute-start | bytes 442376 | tf_op jit(solution)/shard_map/ppermute | solution.py:29
  24.6 2.5 %collective-permute-start.6 = (bf16[96,768]{1,0:T(8,128)(2,1)S(1)}, bf16[96,768]{1,0:T(8,128)(2,1)S(1)}, u32[]{:S(2)}, u32[]{:S(2)}) collective-permute-start(bf16[96,768]{1,0:T(8,128)(2,1)S(1)} %pad_maximum_fusion.4), channel_id=1, source_target_pairs={{0,16},{4,20},{8,24},{12,28},{16,0},{20,4},{24,8},{28,12},{1,17},{... | collective-permute-start | bytes 442376 | tf_op jit(solution)/shard_map/ppermute | solution.py:29
  27.1 5.2 %collective-permute-done.2 = bf16[96,768]{1,0:T(8,128)(2,1)S(1)} collective-permute-done((bf16[96,768]{1,0:T(8,128)(2,1)S(1)}, bf16[96,768]{1,0:T(8,128)(2,1)S(1)}, u32[]{:S(2)}, u32[]{:S(2)}) %collective-permute-start.2) | collective-permute-done | bytes 147488 | tf_op jit(solution)/shard_map/ppermute | solution.py:29
  32.4 2.5 %collective-permute-start.7 = (bf16[96,768]{1,0:T(8,128)(2,1)S(1)}, bf16[96,768]{1,0:T(8,128)(2,1)S(1)}, u32[]{:S(2)}, u32[]{:S(2)}) collective-permute-start(bf16[96,768]{1,0:T(8,128)(2,1)S(1)} %pad_maximum_fusion.5), channel_id=1, source_target_pairs={{0,24},{4,28},{8,16},{12,20},{16,8},{20,12},{24,0},{28,4},{1,25},{... | collective-permute-start | bytes 442376 | tf_op jit(solution)/shard_map/ppermute | solution.py:29
  38.1 5.0 %collective-permute-done.6 = bf16[96,768]{1,0:T(8,128)(2,1)S(1)} collective-permute-done((bf16[96,768]{1,0:T(8,128)(2,1)S(1)}, bf16[96,768]{1,0:T(8,128)(2,1)S(1)}, u32[]{:S(2)}, u32[]{:S(2)}) %collective-permute-start.6) | collective-permute-done | bytes 147488 | tf_op jit(solution)/shard_map/ppermute | solution.py:29
  44.7 2.6 %collective-permute-start.11 = (bf16[96,768]{1,0:T(8,128)(2,1)S(1)}, bf16[96,768]{1,0:T(8,128)(2,1)S(1)}, u32[]{:S(2)}, u32[]{:S(2)}) collective-permute-start(bf16[96,768]{1,0:T(8,128)(2,1)S(1)} %pad_maximum_fusion.8), channel_id=1, source_target_pairs={{0,24},{4,28},{8,16},{12,20},{16,8},{20,12},{24,0},{28,4},{1,25},{... | collective-permute-start | bytes 442376 | tf_op jit(solution)/shard_map/ppermute | solution.py:29
  47.3 2.8 %collective-permute-start.10 = (bf16[96,768]{1,0:T(8,128)(2,1)S(1)}, bf16[96,768]{1,0:T(8,128)(2,1)S(1)}, u32[]{:S(2)}, u32[]{:S(2)}) collective-permute-start(bf16[96,768]{1,0:T(8,128)(2,1)S(1)} %get-tuple-element.40), channel_id=1, source_target_pairs={{0,16},{4,20},{8,24},{12,28},{16,0},{20,4},{24,8},{28,12},{1,17},{... | collective-permute-start | bytes 442376 | tf_op jit(solution)/shard_map/ppermute | solution.py:29
  50.6 7.8 %collective-permute-start.9 = (bf16[96,768]{1,0:T(8,128)(2,1)S(1)}, bf16[96,768]{1,0:T(8,128)(2,1)S(1)}, u32[]{:S(2)}, u32[]{:S(2)}) collective-permute-start(bf16[96,768]{1,0:T(8,128)(2,1)S(1)} %get-tuple-element.39), channel_id=1, source_target_pairs={{0,8},{4,12},{8,0},{12,4},{16,24},{20,28},{24,16},{28,20},{1,9},{5... | collective-permute-start | bytes 442376 | tf_op jit(solution)/shard_map/ppermute | solution.py:29
  59.8 1.8 %collective-permute-done.9 = bf16[96,768]{1,0:T(8,128)(2,1)S(1)} collective-permute-done((bf16[96,768]{1,0:T(8,128)(2,1)S(1)}, bf16[96,768]{1,0:T(8,128)(2,1)S(1)}, u32[]{:S(2)}, u32[]{:S(2)}) %collective-permute-start.9) | collective-permute-done | bytes 147488 | tf_op jit(solution)/shard_map/ppermute | solution.py:29
  61.6 4.0 %collective-permute-start.14 = (bf16[96,768]{1,0:T(8,128)(2,1)S(1)}, bf16[96,768]{1,0:T(8,128)(2,1)S(1)}, u32[]{:S(2)}, u32[]{:S(2)}) collective-permute-start(bf16[96,768]{1,0:T(8,128)(2,1)S(1)} %get-tuple-element.45), channel_id=1, source_target_pairs={{0,8},{4,12},{8,0},{12,4},{16,24},{20,28},{24,16},{28,20},{1,9},{5... | collective-permute-start | bytes 442376 | tf_op jit(solution)/shard_map/ppermute | solution.py:29
  68.3 3.5 %collective-permute-done.14 = bf16[96,768]{1,0:T(8,128)(2,1)S(1)} collective-permute-done((bf16[96,768]{1,0:T(8,128)(2,1)S(1)}, bf16[96,768]{1,0:T(8,128)(2,1)S(1)}, u32[]{:S(2)}, u32[]{:S(2)}) %collective-permute-start.14) | collective-permute-done | bytes 147488 | tf_op jit(solution)/shard_map/ppermute | solution.py:29
  71.8 7.8 %collective-permute-done.15 = bf16[96,768]{1,0:T(8,128)(2,1)S(1)} collective-permute-done((bf16[96,768]{1,0:T(8,128)(2,1)S(1)}, bf16[96,768]{1,0:T(8,128)(2,1)S(1)}, u32[]{:S(2)}, u32[]{:S(2)}) %collective-permute-start.15) | collective-permute-done | bytes 147488 | tf_op jit(solution)/shard_map/ppermute | solution.py:29
  79.7 2.4 %gram_step.3 = (f32[384,128]{1,0:T(8,128)S(1)}, f32[1,1536]{1,0:T(1,128)S(1)}) custom-call(bf16[384,768]{1,0:T(8,128)(2,1)S(1)} %get-tuple-element.106.refs_0_, bf16[768,768]{1,0:T(8,128)(2,1)S(1)} %constant_dynamic-update-slice_fusion.26.refs_1_, bf16[768,768]{1,0:T(8,128)(2,1)S(1)} %collective-permute-done.19.refs_2_), custom_call_target="tpu_custom_call" | custom-call | flops 905969664 | bytes 2949120 | tf_op jit(solution)/shard_map/gram_step/pallas_call | solution.py:168
  83.7 3.5 %gram_step.4 = (f32[384,128]{1,0:T(8,128)S(1)}, f32[384,128]{1,0:T(8,128)S(1)}, f32[1,1536]{1,0:T(1,128)S(1)}) custom-call(bf16[384,768]{1,0:T(8,128)(2,1)S(1)} %get-tuple-element.106.refs_0_, bf16[384,768]{1,0:T(8,128)(2,1)S(1)} %get-tuple-element.112.refs_1_, bf16[768,768]{1,0:T(8,128)(2,1)S(1)} %constant_dynamic-update-slice_fusion.20.refs_2_, ...), custom_call_target="tpu_custom_call" | custom-call | flops 1811939328 | bytes 3538944 | tf_op jit(solution)/shard_map/gram_step/pallas_call | solution.py:168
  87.8 8.4 %collective-permute-done.22 = bf16[384,768]{1,0:T(8,128)(2,1)S(1)} collective-permute-done((bf16[384,768]{1,0:T(8,128)(2,1)S(1)}, bf16[384,768]{1,0:T(8,128)(2,1)S(1)}, u32[]{:S(2)}, u32[]{:S(2)}) %collective-permute-start.22) | collective-permute-done | bytes 589856 | tf_op jit(solution)/shard_map/ppermute | solution.py:29
  96.3 6.2 %collective-permute-done.20 = bf16[384,768]{1,0:T(8,128)(2,1)S(1)} collective-permute-done((bf16[384,768]{1,0:T(8,128)(2,1)S(1)}, bf16[384,768]{1,0:T(8,128)(2,1)S(1)}, u32[]{:S(2)}, u32[]{:S(2)}) %collective-permute-start.20) | collective-permute-done | bytes 589856 | tf_op jit(solution)/shard_map/ppermute | solution.py:29
  102.6 4.4 %gram_step.5 = (f32[384,128]{1,0:T(8,128)S(1)}, f32[384,128]{1,0:T(8,128)S(1)}, f32[384,128]{1,0:T(8,128)S(1)}, f32[1,1536]{1,0:T(1,128)S(1)}) custom-call(bf16[384,768]{1,0:T(8,128)(2,1)S(1)} %get-tuple-element.106.refs_0_, bf16[384,768]{1,0:T(8,128)(2,1)S(1)} %get-tuple-element.112.refs_1_, bf16[384,768]{1,0:T(8,128)(2,1)S(1)} %get-tuple-element.52.refs_2_, ...), custom_call_target="tpu_custom_call" | custom-call | flops 2717908992 | bytes 4128768 | tf_op jit(solution)/shard_map/gram_step/pallas_call | solution.py:168
  107.1 7.2 %gram_last.1 = f32[32,192]{1,0:T(8,128)S(1)} custom-call(s32[2]{0:T(128)S(1)} %pad_add_fusion.me_ref, bf16[384,768]{1,0:T(8,128)(2,1)S(1)} %get-tuple-element.106.refs_0_, bf16[384,768]{1,0:T(8,128)(2,1)S(1)} %get-tuple-element.112.refs_1_, bf16[384,768]{1,0:T(8,128)(2,1)S(1)} %get-tuple-element.52.refs_2_, bf16[384,768]{1,0:T(8,128)(2,1)S(1)} %get-tuple-element.50.refs_3_, ...), custom_call_target="tpu_custom_call" | custom-call | flops 3623878656 | bytes 4718592 | tf_op jit(solution)/shard_map/gram_last/pallas_call | solution.py:179
  114.3 16.4 %all_to_all.11 = f32[32,1,192]{2,1,0:T(1,128)S(1)} all-to-all(f32[32,1,192]{2,1,0:T(1,128)S(1)} %copy.3), channel_id=1, replica_groups=mesh['grp'=8,'blk'=4] {'grp','blk'}, dimensions={0} | all-to-all | bytes 49152 | tf_op jit(solution)/shard_map/all_to_all | solution.py:265
  131.3 2.3 %pick_rows.1 = f32[6,128]{1,0:T(8,128)} custom-call(s32[6,128]{1,0:T(8,128)} %bitcast.9, f32[32,192]{1,0:T(8,128)} %bitcast.11), custom_call_target="tpu_custom_call" | custom-call | tf_op jit(solution)/shard_map/pick_rows/pallas_call | solution.py:219
  (71 shorter events, 18.4 us)
Async XLA Ops:
  5.1 10.9 %collective-permute-start = (bf16[192,768]{1,0:T(8,128)(2,1)S(1)}, bf16[192,768]{1,0:T(8,128)(2,1)S(1)}, u32[]{:S(2)}, u32[]{:S(2)}) collective-permute-start(bf16[192,768]{1,0:T(8,128)(2,1)S(1)} %get-tuple-element.33), channel_id=1, source_target_pairs={{0,4},{4,0},{8,12},{12,8},{16,20},{20,16},{24,28},{28,24},{1,5},{5... | collective-permute-start | bytes 884744 | tf_op jit(solution)/shard_map/ppermute | solution.py:29
  8.2 14.6 %collective-permute-start.4 = (bf16[192,768]{1,0:T(8,128)(2,1)S(1)}, bf16[192,768]{1,0:T(8,128)(2,1)S(1)}, u32[]{:S(2)}, u32[]{:S(2)}) collective-permute-start(bf16[192,768]{1,0:T(8,128)(2,1)S(1)} %get-tuple-element.35), channel_id=1, source_target_pairs={{0,4},{4,0},{8,12},{12,8},{16,20},{20,16},{24,28},{28,24},{1,5},{5... | collective-permute-start | bytes 884744 | tf_op jit(solution)/shard_map/ppermute | solution.py:29
  16.0 8.5 %collective-permute-start.1 = (bf16[96,768]{1,0:T(8,128)(2,1)S(1)}, bf16[96,768]{1,0:T(8,128)(2,1)S(1)}, u32[]{:S(2)}, u32[]{:S(2)}) collective-permute-start(bf16[96,768]{1,0:T(8,128)(2,1)S(1)} %pad_maximum_fusion), channel_id=1, source_target_pairs={{0,8},{4,12},{8,0},{12,4},{16,24},{20,28},{24,16},{28,20},{1,9},{5... | collective-permute-start | bytes 442376 | tf_op jit(solution)/shard_map/ppermute | solution.py:29
  18.2 14.1 %collective-permute-start.2 = (bf16[96,768]{1,0:T(8,128)(2,1)S(1)}, bf16[96,768]{1,0:T(8,128)(2,1)S(1)}, u32[]{:S(2)}, u32[]{:S(2)}) collective-permute-start(bf16[96,768]{1,0:T(8,128)(2,1)S(1)} %pad_maximum_fusion.1), channel_id=1, source_target_pairs={{0,16},{4,20},{8,24},{12,28},{16,0},{20,4},{24,8},{28,12},{1,17},{... | collective-permute-start | bytes 442376 | tf_op jit(solution)/shard_map/ppermute | solution.py:29
  20.9 14.0 %collective-permute-start.3 = (bf16[96,768]{1,0:T(8,128)(2,1)S(1)}, bf16[96,768]{1,0:T(8,128)(2,1)S(1)}, u32[]{:S(2)}, u32[]{:S(2)}) collective-permute-start(bf16[96,768]{1,0:T(8,128)(2,1)S(1)} %pad_maximum_fusion.2), channel_id=1, source_target_pairs={{0,24},{4,28},{8,16},{12,20},{16,8},{20,12},{24,0},{28,4},{1,25},{... | collective-permute-start | bytes 442376 | tf_op jit(solution)/shard_map/ppermute | solution.py:29
  21.0 23.7 %collective-permute-start.8 = (bf16[192,768]{1,0:T(8,128)(2,1)S(1)}, bf16[192,768]{1,0:T(8,128)(2,1)S(1)}, u32[]{:S(2)}, u32[]{:S(2)}) collective-permute-start(bf16[192,768]{1,0:T(8,128)(2,1)S(1)} %get-tuple-element.38), channel_id=1, source_target_pairs={{0,4},{4,0},{8,12},{12,8},{16,20},{20,16},{24,28},{28,24},{1,5},{5... | collective-permute-start | bytes 884744 | tf_op jit(solution)/shard_map/ppermute | solution.py:29
  22.8 13.7 %collective-permute-start.5 = (bf16[96,768]{1,0:T(8,128)(2,1)S(1)}, bf16[96,768]{1,0:T(8,128)(2,1)S(1)}, u32[]{:S(2)}, u32[]{:S(2)}) collective-permute-start(bf16[96,768]{1,0:T(8,128)(2,1)S(1)} %pad_maximum_fusion.3), channel_id=1, source_target_pairs={{0,8},{4,12},{8,0},{12,4},{16,24},{20,28},{24,16},{28,20},{1,9},{5... | collective-permute-start | bytes 442376 | tf_op jit(solution)/shard_map/ppermute | solution.py:29
  24.6 18.4 %collective-permute-start.6 = (bf16[96,768]{1,0:T(8,128)(2,1)S(1)}, bf16[96,768]{1,0:T(8,128)(2,1)S(1)}, u32[]{:S(2)}, u32[]{:S(2)}) collective-permute-start(bf16[96,768]{1,0:T(8,128)(2,1)S(1)} %pad_maximum_fusion.4), channel_id=1, source_target_pairs={{0,16},{4,20},{8,24},{12,28},{16,0},{20,4},{24,8},{28,12},{1,17},{... | collective-permute-start | bytes 442376 | tf_op jit(solution)/shard_map/ppermute | solution.py:29
  32.4 10.7 %collective-permute-start.7 = (bf16[96,768]{1,0:T(8,128)(2,1)S(1)}, bf16[96,768]{1,0:T(8,128)(2,1)S(1)}, u32[]{:S(2)}, u32[]{:S(2)}) collective-permute-start(bf16[96,768]{1,0:T(8,128)(2,1)S(1)} %pad_maximum_fusion.5), channel_id=1, source_target_pairs={{0,24},{4,28},{8,16},{12,20},{16,8},{20,12},{24,0},{28,4},{1,25},{... | collective-permute-start | bytes 442376 | tf_op jit(solution)/shard_map/ppermute | solution.py:29
  34.9 24.3 %collective-permute-start.12 = (bf16[192,768]{1,0:T(8,128)(2,1)S(1)}, bf16[192,768]{1,0:T(8,128)(2,1)S(1)}, u32[]{:S(2)}, u32[]{:S(2)}) collective-permute-start(bf16[192,768]{1,0:T(8,128)(2,1)S(1)} %get-tuple-element.44), channel_id=1, source_target_pairs={{0,4},{4,0},{8,12},{12,8},{16,20},{20,16},{24,28},{28,24},{1,5},{5... | collective-permute-start | bytes 884744 | tf_op jit(solution)/shard_map/ppermute | solution.py:29
  36.5 14.1 %collective-permute-start.13 = (bf16[384,768]{1,0:T(8,128)(2,1)S(1)}, bf16[384,768]{1,0:T(8,128)(2,1)S(1)}, u32[]{:S(2)}, u32[]{:S(2)}) collective-permute-start(bf16[384,768]{1,0:T(8,128)(2,1)S(1)} %get-tuple-element.106.refs_0_), channel_id=1, source_target_pairs={{0,2},{1,3},{2,0},{3,1},{4,6},{5,7},{6,4},{7,5},{8,10},{9,11},{10,... | collective-permute-start | bytes 1769480 | tf_op jit(solution)/shard_map/ppermute | solution.py:29
  43.1 16.0 %collective-permute-start.17 = (bf16[384,768]{1,0:T(8,128)(2,1)S(1)}, bf16[384,768]{1,0:T(8,128)(2,1)S(1)}, u32[]{:S(2)}, u32[]{:S(2)}) collective-permute-start(bf16[384,768]{1,0:T(8,128)(2,1)S(1)} %get-tuple-element.112.refs_1_), channel_id=1, source_target_pairs={{0,2},{1,3},{2,0},{3,1},{4,6},{5,7},{6,4},{7,5},{8,10},{9,11},{10,... | collective-permute-start | bytes 1769480 | tf_op jit(solution)/shard_map/ppermute | solution.py:29
  44.7 22.0 %collective-permute-start.11 = (bf16[96,768]{1,0:T(8,128)(2,1)S(1)}, bf16[96,768]{1,0:T(8,128)(2,1)S(1)}, u32[]{:S(2)}, u32[]{:S(2)}) collective-permute-start(bf16[96,768]{1,0:T(8,128)(2,1)S(1)} %pad_maximum_fusion.8), channel_id=1, source_target_pairs={{0,24},{4,28},{8,16},{12,20},{16,8},{20,12},{24,0},{28,4},{1,25},{... | collective-permute-start | bytes 442376 | tf_op jit(solution)/shard_map/ppermute | solution.py:29
  47.3 18.3 %collective-permute-start.10 = (bf16[96,768]{1,0:T(8,128)(2,1)S(1)}, bf16[96,768]{1,0:T(8,128)(2,1)S(1)}, u32[]{:S(2)}, u32[]{:S(2)}) collective-permute-start(bf16[96,768]{1,0:T(8,128)(2,1)S(1)} %get-tuple-element.40), channel_id=1, source_target_pairs={{0,16},{4,20},{8,24},{12,28},{16,0},{20,4},{24,8},{28,12},{1,17},{... | collective-permute-start | bytes 442376 | tf_op jit(solution)/shard_map/ppermute | solution.py:29
  50.6 11.0 %collective-permute-start.9 = (bf16[96,768]{1,0:T(8,128)(2,1)S(1)}, bf16[96,768]{1,0:T(8,128)(2,1)S(1)}, u32[]{:S(2)}, u32[]{:S(2)}) collective-permute-start(bf16[96,768]{1,0:T(8,128)(2,1)S(1)} %get-tuple-element.39), channel_id=1, source_target_pairs={{0,8},{4,12},{8,0},{12,4},{16,24},{20,28},{24,16},{28,20},{1,9},{5... | collective-permute-start | bytes 442376 | tf_op jit(solution)/shard_map/ppermute | solution.py:29
  59.1 20.6 %collective-permute-start.19 = (bf16[768,768]{1,0:T(8,128)(2,1)S(1)}, bf16[768,768]{1,0:T(8,128)(2,1)S(1)}, u32[]{:S(2)}, u32[]{:S(2)}) collective-permute-start(bf16[768,768]{1,0:T(8,128)(2,1)S(1)} %constant_dynamic-update-slice_fusion.26.refs_1_), channel_id=1, source_target_pairs={{0,1},{1,0},{2,3},{3,2},{4,5},{5,4},{6,7},{7,6},{8,9},{9,8},{10,11... | collective-permute-start | bytes 3538952 | tf_op jit(solution)/shard_map/ppermute | solution.py:29
  59.1 24.6 %collective-permute-start.18 = (bf16[768,768]{1,0:T(8,128)(2,1)S(1)}, bf16[768,768]{1,0:T(8,128)(2,1)S(1)}, u32[]{:S(2)}, u32[]{:S(2)}) collective-permute-start(bf16[768,768]{1,0:T(8,128)(2,1)S(1)} %constant_dynamic-update-slice_fusion.20.refs_2_), channel_id=1, source_target_pairs={{0,1},{1,0},{2,3},{3,2},{4,5},{5,4},{6,7},{7,6},{8,9},{9,8},{10,11... | collective-permute-start | bytes 3538952 | tf_op jit(solution)/shard_map/ppermute | solution.py:29
  61.6 10.2 %collective-permute-start.14 = (bf16[96,768]{1,0:T(8,128)(2,1)S(1)}, bf16[96,768]{1,0:T(8,128)(2,1)S(1)}, u32[]{:S(2)}, u32[]{:S(2)}) collective-permute-start(bf16[96,768]{1,0:T(8,128)(2,1)S(1)} %get-tuple-element.45), channel_id=1, source_target_pairs={{0,8},{4,12},{8,0},{12,4},{16,24},{20,28},{24,16},{28,20},{1,9},{5... | collective-permute-start | bytes 442376 | tf_op jit(solution)/shard_map/ppermute | solution.py:29
  65.6 14.0 %collective-permute-start.15 = (bf16[96,768]{1,0:T(8,128)(2,1)S(1)}, bf16[96,768]{1,0:T(8,128)(2,1)S(1)}, u32[]{:S(2)}, u32[]{:S(2)}) collective-permute-start(bf16[96,768]{1,0:T(8,128)(2,1)S(1)} %get-tuple-element.46), channel_id=1, source_target_pairs={{0,16},{4,20},{8,24},{12,28},{16,0},{20,4},{24,8},{28,12},{1,17},{... | collective-permute-start | bytes 442376 | tf_op jit(solution)/shard_map/ppermute | solution.py:29
  66.8 16.9 %collective-permute-start.16 = (bf16[96,768]{1,0:T(8,128)(2,1)S(1)}, bf16[96,768]{1,0:T(8,128)(2,1)S(1)}, u32[]{:S(2)}, u32[]{:S(2)}) collective-permute-start(bf16[96,768]{1,0:T(8,128)(2,1)S(1)} %pad_maximum_fusion.11), channel_id=1, source_target_pairs={{0,24},{4,28},{8,16},{12,20},{16,8},{20,12},{24,0},{28,4},{1,25},{... | collective-permute-start | bytes 442376 | tf_op jit(solution)/shard_map/ppermute | solution.py:29
  82.1 14.1 %collective-permute-start.22 = (bf16[384,768]{1,0:T(8,128)(2,1)S(1)}, bf16[384,768]{1,0:T(8,128)(2,1)S(1)}, u32[]{:S(2)}, u32[]{:S(2)}) collective-permute-start(bf16[384,768]{1,0:T(8,128)(2,1)S(1)} %get-tuple-element.52.refs_2_), channel_id=1, source_target_pairs={{0,2},{1,3},{2,0},{3,1},{4,6},{5,7},{6,4},{7,5},{8,10},{9,11},{10,... | collective-permute-start | bytes 1769480 | tf_op jit(solution)/shard_map/ppermute | solution.py:29
  87.2 15.3 %collective-permute-start.20 = (bf16[384,768]{1,0:T(8,128)(2,1)S(1)}, bf16[384,768]{1,0:T(8,128)(2,1)S(1)}, u32[]{:S(2)}, u32[]{:S(2)}) collective-permute-start(bf16[384,768]{1,0:T(8,128)(2,1)S(1)} %get-tuple-element.50.refs_3_), channel_id=1, source_target_pairs={{0,2},{1,3},{2,0},{3,1},{4,6},{5,7},{6,4},{7,5},{8,10},{9,11},{10,... | collective-permute-start | bytes 1769480 | tf_op jit(solution)/shard_map/ppermute | solution.py:29
  96.2 6.4 %collective-permute-start.23 = (bf16[768,768]{1,0:T(8,128)(2,1)S(1)}, bf16[768,768]{1,0:T(8,128)(2,1)S(1)}, u32[]{:S(2)}, u32[]{:S(2)}) collective-permute-start(bf16[768,768]{1,0:T(8,128)(2,1)S(1)} %constant_dynamic-update-slice_fusion.38.refs_3_), channel_id=1, source_target_pairs={{0,1},{1,0},{2,3},{3,2},{4,5},{5,4},{6,7},{7,6},{8,9},{9,8},{10,11... | collective-permute-start | bytes 3538952 | tf_op jit(solution)/shard_map/ppermute | solution.py:29
  102.6 4.5 %collective-permute-start.21 = (bf16[768,768]{1,0:T(8,128)(2,1)S(1)}, bf16[768,768]{1,0:T(8,128)(2,1)S(1)}, u32[]{:S(2)}, u32[]{:S(2)}) collective-permute-start(bf16[768,768]{1,0:T(8,128)(2,1)S(1)} %constant_dynamic-update-slice_fusion.32.refs_4_), channel_id=1, source_target_pairs={{0,1},{1,0},{2,3},{3,2},{4,5},{5,4},{6,7},{7,6},{8,9},{9,8},{10,11... | collective-permute-start | bytes 3538952 | tf_op jit(solution)/shard_map/ppermute | solution.py:29
  (2 other events, 2.0 us)

commit v4 on v3

--- a/solution.py
+++ b/solution.py
@@ -39,7 +39,8 @@
     for step, size in enumerate(chunks):
         place = lax.broadcasted_iota(jnp.int32, (groups, size, 1), 1)
         order = lax.broadcasted_iota(jnp.int32, (groups, size, 1), 0)
-        group = (order % high * 2 + order // high) ^ me_ref[0]
+        relative = order if step == 0 else order % high * 2 + order // high
+        group = relative ^ me_ref[0]
         wanted = (group * capacity + place + first).reshape(groups * size, 1)
         pick = jnp.where(wanted == slots, 1.0, 0.0)
         live = jnp.max(pick, axis=1, keepdims=True)
@@ -236,32 +237,82 @@
     me = jnp.stack([lax.axis_index("grp"), lax.axis_index("blk")]).astype(jnp.int32)
     slots = send_slot.reshape(row_count // lanes, lanes)
     placed = head(me, embeddings, slots, capacity, chunks, groups)
-    high = groups // 2
-    near, owns, across, done, states, cols = [], [], [], [], [], []
-    for step, size in enumerate(chunks):
-        keep, send = placed[2 * step : 2 * step + 2]
-        near.append(swap(after(send, *near[: max(step - 1, 0)][-1:]), "grp", groups, 1))
-        arrived = []
-        for z in range(high):
-            span = slice(z * size, (z + 1) * size)
-            pair = jnp.concatenate([keep[span], near[step][span]], axis=0)
-            if z > 0:
-                earlier = owns[step - 2 : step - 1] if step >= 2 else []
-                earlier = earlier + (across[step - 3 : step - 2] if step >= 3 else [])
-                pair = swap(after(pair, *earlier), "grp", groups, 2 * z)
-            arrived.append(pair)
-        own = jnp.concatenate(arrived, axis=0)
-        owns.append(own)
-        earlier = done[step - 2 : step - 1] if step >= 2 else []
-        across.append(swap(after(own, *earlier), "blk", members, 2))
-        pair = jnp.concatenate([own, across[step]], axis=0)
-        other = swap(pair, "blk", members, 1)
+    count, high = len(chunks), groups // 2
+    last = count - 1
+
+    sent, owns, done, states, cols = {}, {}, {}, [], []
+    pairs, window = {}, []
+
+    def send(key, value, axis, size, bit, *earlier):
+        earlier = earlier + tuple(window[-5:-4])
+        sent[key] = swap(after(value, *earlier) if earlier else value, axis, size, bit)
+        window.append(sent[key])
+
+    def rows(value, index, size):
+        return value[index * size : (index + 1) * size]
+
+    def block(step, z):
+        size = chunks[step]
+        return jnp.concatenate(
+            [rows(placed[2 * step], z, size), rows(sent["y", step], z, size)], axis=0
+        )
+
+    def start(kind, step, bit=0):
+        size = chunks[step]
+        if kind == "d":
+            value = rows(placed[2 * bit // groups], bit % high, size)
+            send((kind, step, bit), value, "grp", groups, bit)
+        elif kind == "y":
+            send((kind, step), placed[2 * step + 1], "grp", groups, 1)
+        elif kind == "z":
+            send((kind, step, bit), block(step, bit), "grp", groups, 2 * bit)
+        elif kind == "x":
+            if step == 0:
+                parts = [rows(placed[0], 0, size)]
+                parts += [sent["d", 0, r] for r in range(1, groups)]
+            else:
+                parts = [block(step, 0)] + [sent["z", step, z] for z in range(1, high)]
+            owns[step] = jnp.concatenate(parts, axis=0)
+            earlier = [sent["x", step - 1]] if step >= 1 else []
+            earlier += [done[step - 2]] if step >= 2 else []
+            send((kind, step), owns[step], "blk", members, 2, *earlier)
+        elif kind == "c":
+            pairs[step] = jnp.concatenate([owns[step], sent["x", step]], axis=0)
+            earlier = [done[step - 1]] if step == last else []
+            send((kind, step), pairs[step], "blk", members, 1, *earlier)
+
+    def gram(step):
+        nonlocal states, cols
         result = gram_step(
-            step, me, owns, (pair, other), states, cols, (0, 2, 1, 3), chunks, groups
+            step,
+            me,
+            [owns[j] for j in range(step + 1)],
+            (pairs[step], sent["c", step]),
+            states,
+            cols,
+            (0, 2, 1, 3),
+            chunks,
+            groups,
         )
-        if step < len(chunks) - 1:
-            states, cols = result
-            done.append(cols[-1])
+        if step == last:
+            return result
+        states, cols = result
+        done[step] = cols[-1]
+
+    direct = [("d", 0, r) for r in reversed(range(1, groups))]
+    order = direct[:4] + [("y", 1)] + direct[4:]
+    for step in range(1, count):
+        stages = [("z", step, z) for z in reversed(range(1, high))]
+        order += stages[:2] + ([("y", step + 1)] if step < last else [])
+        order += [("x", step - 1)] + stages[2:]
+        order += [("c", step - 1), ("gram", step - 1)]
+    order += [("x", last), ("c", last)]
+    for item in order:
+        if item[0] == "gram":
+            gram(item[1])
+        else:
+            start(*item)
+    result = gram(last)
     homeward = lax.all_to_all(result, ("grp", "blk"), 0, 0, tiled=True)
     return tail(homeward, slots, capacity, members).reshape(row_count)
 

time: 134 us -> 134 us (level)
  waiting for transfers between devices: 46.7 us -> 53.2 us
  blocking collectives: 16.4 us -> 11 us
    ppermute x24 -> x27, waiting for transfers between devices: 46.7 us -> 53.2 us  [swap(): return lax.ppermute(value, axis, [(i, i ^ bit) for i in range(size)])]
    all_to_all x1, blocking collectives: 16.4 us -> 11 us  [on_device(): homeward = lax.all_to_all(result, ('grp', 'blk'), 0, 0, tiled=True)]
    ppermute x24 -> x27, starting transfers between devices: 43.9 us -> 42.6 us  [swap(): return lax.ppermute(value, axis, [(i, i ^ bit) for i in range(size)])]
    unnamed x24 -> x27, local copies, waits for them, and re-layouts: 3.01 us -> 3.01 us
  transfers between devices with their start and end apart: 24 -> 27, of which waited for: 10 -> 12; matrix products, arithmetic and copies ran while one was open for 1% -> 1% of each run, Pallas kernels for 8% -> 4%
where the time goes in v4:
time: 134 us; the launch traced here: 133 us
  waiting for transfers between devices  53.2 us (40%)
  starting transfers between devices  42.6 us (32%)
  Pallas kernels  22.9 us (17%)
  blocking collectives  11 us (8%)
  local copies, waits for them, and re-layouts  3.22 us (2%)
    ppermute x27, waiting for transfers between devices, swap(): return lax.ppermute(value, axis, [(i, i ^ bit) for i in range(size)])  53.2 us
    ppermute x27, starting transfers between devices, swap(): return lax.ppermute(value, axis, [(i, i ^ bit) for i in range(size)])  42.6 us
    all_to_all x1, blocking collectives, on_device(): homeward = lax.all_to_all(result, ('grp', 'blk'), 0, 0, tiled=True)  11 us
    pallas_call x3, Pallas kernels, gram_step(): pl.pallas_call(functools.partial(gram_kernel, step, tile), in_specs=[vmem...  10.4 us
    pallas_call x1, Pallas kernels, gram_step(): pl.pallas_call(functools.partial(gram_last_kernel, step, relatives, chunk...  7.11 us
    pallas_call x1, Pallas kernels, head(): pl.pallas_call(functools.partial(head_kernel, capacity, chunks, groups),...  3.08 us
    unnamed x27, local copies, waits for them, and re-layouts  3.01 us
  transfers between devices with their start and end apart: 27, of which 12 were waited for; matrix products, arithmetic and copies ran while one was open for 1% of the time, Pallas kernels for 4%

profile of v4, /device:TPU:0, one launch (start us, length us, event | category | flops | bytes accessed | tf_op | source)
XLA Modules:
  0.0 133.5 jit_solution(12722135723878022124)
XLA Ops:
  2.0 3.1 %place_rows.1 = (bf16[192,768]{1,0:T(8,128)(2,1)S(1)}, bf16[192,768]{1,0:T(8,128)(2,1)S(1)}, bf16[192,768]{1,0:T(8,128)(2,1)S(1)}, bf16[192,768]{1,0:T(8,128)(2,...) custom-call(s32[2]{0:T(128)S(1)} %pad_add_fusion.me_ref, ...), custom_call_target="tpu_custom_call" | custom-call | tf_op jit(solution)/shard_map/place_rows/pallas_call | solution.py:58
  5.2 5.1 %collective-permute-start = (bf16[48,768]{1,0:T(8,128)(2,1)S(1)}, bf16[48,768]{1,0:T(8,128)(2,1)S(1)}, u32[]{:S(2)}, u32[]{:S(2)}) collective-permute-start(bf16[48,768]{1,0:T(8,128)(2,1)S(1)} %get-tuple-element.121), channel_id=1, source_target_pairs={{0,20},{4,16},{8,28},{12,24},{16,4},{20,0},{24,12},{28,8},{1,21},{... | collective-permute-start | bytes 221192 | tf_op jit(solution)/shard_map/ppermute | solution.py:29
  11.6 2.4 %collective-permute-start.4 = (bf16[48,768]{1,0:T(8,128)(2,1)S(1)}, bf16[48,768]{1,0:T(8,128)(2,1)S(1)}, u32[]{:S(2)}, u32[]{:S(2)}) collective-permute-start(bf16[48,768]{1,0:T(8,128)(2,1)S(1)} %get-tuple-element.119), channel_id=1, source_target_pairs={{0,28},{4,24},{8,20},{12,16},{16,12},{20,8},{24,4},{28,0},{1,29},{... | collective-permute-start | bytes 221192 | tf_op jit(solution)/shard_map/ppermute | solution.py:29
  15.1 4.3 %collective-permute-start.1 = (bf16[48,768]{1,0:T(8,128)(2,1)S(1)}, bf16[48,768]{1,0:T(8,128)(2,1)S(1)}, u32[]{:S(2)}, u32[]{:S(2)}) collective-permute-start(bf16[48,768]{1,0:T(8,128)(2,1)S(1)} %get-tuple-element.46), channel_id=1, source_target_pairs={{0,4},{4,0},{8,12},{12,8},{16,20},{20,16},{24,28},{28,24},{1,5},{5... | collective-permute-start | bytes 221192 | tf_op jit(solution)/shard_map/ppermute | solution.py:29
  19.4 5.0 %collective-permute-start.3 = (bf16[48,768]{1,0:T(8,128)(2,1)S(1)}, bf16[48,768]{1,0:T(8,128)(2,1)S(1)}, u32[]{:S(2)}, u32[]{:S(2)}) collective-permute-start(bf16[48,768]{1,0:T(8,128)(2,1)S(1)} %get-tuple-element.47), channel_id=1, source_target_pairs={{0,8},{4,12},{8,0},{12,4},{16,24},{20,28},{24,16},{28,20},{1,9},{5... | collective-permute-start | bytes 221192 | tf_op jit(solution)/shard_map/ppermute | solution.py:29
  27.3 2.4 %collective-permute-done.5 = bf16[48,768]{1,0:T(8,128)(2,1)S(1)} collective-permute-done((bf16[48,768]{1,0:T(8,128)(2,1)S(1)}, bf16[48,768]{1,0:T(8,128)(2,1)S(1)}, u32[]{:S(2)}, u32[]{:S(2)}) %collective-permute-start.5) | collective-permute-done | bytes 73760 | tf_op jit(solution)/shard_map/ppermute | solution.py:29
  31.4 2.6 %collective-permute-start.10 = (bf16[96,768]{1,0:T(8,128)(2,1)S(1)}, bf16[96,768]{1,0:T(8,128)(2,1)S(1)}, u32[]{:S(2)}, u32[]{:S(2)}) collective-permute-start(bf16[96,768]{1,0:T(8,128)(2,1)S(1)} %pad_maximum_fusion.2), channel_id=1, source_target_pairs={{0,24},{4,28},{8,16},{12,20},{16,8},{20,12},{24,0},{28,4},{1,25},{... | collective-permute-start | bytes 442376 | tf_op jit(solution)/shard_map/ppermute | solution.py:29
  36.0 6.1 %collective-permute-done.12 = bf16[384,768]{1,0:T(8,128)(2,1)S(1)} collective-permute-done((bf16[384,768]{1,0:T(8,128)(2,1)S(1)}, bf16[384,768]{1,0:T(8,128)(2,1)S(1)}, u32[]{:S(2)}, u32[]{:S(2)}) %collective-permute-start.12) | collective-permute-done | bytes 589856 | tf_op jit(solution)/shard_map/ppermute | solution.py:29
  42.3 2.2 %collective-permute-start.11 = (bf16[192,768]{1,0:T(8,128)(2,1)S(1)}, bf16[192,768]{1,0:T(8,128)(2,1)S(1)}, u32[]{:S(2)}, u32[]{:S(2)}) collective-permute-start(bf16[192,768]{1,0:T(8,128)(2,1)S(1)} %get-tuple-element.56), channel_id=1, source_target_pairs={{0,4},{4,0},{8,12},{12,8},{16,20},{20,16},{24,28},{28,24},{1,5},{5... | collective-permute-start | bytes 884744 | tf_op jit(solution)/shard_map/ppermute | solution.py:29
  47.9 4.2 %collective-permute-done.11 = bf16[192,768]{1,0:T(8,128)(2,1)S(1)} collective-permute-done((bf16[192,768]{1,0:T(8,128)(2,1)S(1)}, bf16[192,768]{1,0:T(8,128)(2,1)S(1)}, u32[]{:S(2)}, u32[]{:S(2)}) %collective-permute-start.11) | collective-permute-done | bytes 294944 | tf_op jit(solution)/shard_map/ppermute | solution.py:29
  53.7 3.2 %collective-permute-start.16 = (bf16[96,768]{1,0:T(8,128)(2,1)S(1)}, bf16[96,768]{1,0:T(8,128)(2,1)S(1)}, u32[]{:S(2)}, u32[]{:S(2)}) collective-permute-start(bf16[96,768]{1,0:T(8,128)(2,1)S(1)} %pad_maximum_fusion.5), channel_id=1, source_target_pairs={{0,24},{4,28},{8,16},{12,20},{16,8},{20,12},{24,0},{28,4},{1,25},{... | collective-permute-start | bytes 442376 | tf_op jit(solution)/shard_map/ppermute | solution.py:29
  57.6 2.8 %collective-permute-done.21 = bf16[384,768]{1,0:T(8,128)(2,1)S(1)} collective-permute-done((bf16[384,768]{1,0:T(8,128)(2,1)S(1)}, bf16[384,768]{1,0:T(8,128)(2,1)S(1)}, u32[]{:S(2)}, u32[]{:S(2)}) %collective-permute-start.21) | collective-permute-done | bytes 589856 | tf_op jit(solution)/shard_map/ppermute | solution.py:29
  60.4 4.4 %collective-permute-done.16 = bf16[96,768]{1,0:T(8,128)(2,1)S(1)} collective-permute-done((bf16[96,768]{1,0:T(8,128)(2,1)S(1)}, bf16[96,768]{1,0:T(8,128)(2,1)S(1)}, u32[]{:S(2)}, u32[]{:S(2)}) %collective-permute-start.16) | collective-permute-done | bytes 147488 | tf_op jit(solution)/shard_map/ppermute | solution.py:29
  64.8 2.4 %gram_step.3 = (f32[384,128]{1,0:T(8,128)S(1)}, f32[1,1536]{1,0:T(1,128)S(1)}) custom-call(bf16[384,768]{1,0:T(8,128)(2,1)S(1)} %get-tuple-element.57.refs_0_, bf16[768,768]{1,0:T(8,128)(2,1)S(1)} %constant_dynamic-update-slice_fusion.13.refs_1_, bf16[768,768]{1,0:T(8,128)(2,1)S(1)} %collective-permute-done.13.refs_2_), custom_call_target="tpu_custom_call" | custom-call | flops 905969664 | bytes 2949120 | tf_op jit(solution)/shard_map/gram_step/pallas_call | solution.py:169
  70.4 3.5 %collective-permute-start.18 = (bf16[96,768]{1,0:T(8,128)(2,1)S(1)}, bf16[96,768]{1,0:T(8,128)(2,1)S(1)}, u32[]{:S(2)}, u32[]{:S(2)}) collective-permute-start(bf16[96,768]{1,0:T(8,128)(2,1)S(1)} %pad_maximum_fusion.6), channel_id=1, source_target_pairs={{0,8},{4,12},{8,0},{12,4},{16,24},{20,28},{24,16},{28,20},{1,9},{5... | collective-permute-start | bytes 442376 | tf_op jit(solution)/shard_map/ppermute | solution.py:29
  74.6 8.5 %collective-permute-done.22 = bf16[384,768]{1,0:T(8,128)(2,1)S(1)} collective-permute-done((bf16[384,768]{1,0:T(8,128)(2,1)S(1)}, bf16[384,768]{1,0:T(8,128)(2,1)S(1)}, u32[]{:S(2)}, u32[]{:S(2)}) %collective-permute-start.22) | collective-permute-done | bytes 589856 | tf_op jit(solution)/shard_map/ppermute | solution.py:29
  83.3 2.7 %collective-permute-done.19 = bf16[96,768]{1,0:T(8,128)(2,1)S(1)} collective-permute-done((bf16[96,768]{1,0:T(8,128)(2,1)S(1)}, bf16[96,768]{1,0:T(8,128)(2,1)S(1)}, u32[]{:S(2)}, u32[]{:S(2)}) %collective-permute-start.19) | collective-permute-done | bytes 147488 | tf_op jit(solution)/shard_map/ppermute | solution.py:29
  86.1 3.5 %gram_step.4 = (f32[384,128]{1,0:T(8,128)S(1)}, f32[384,128]{1,0:T(8,128)S(1)}, f32[1,1536]{1,0:T(1,128)S(1)}) custom-call(bf16[384,768]{1,0:T(8,128)(2,1)S(1)} %get-tuple-element.57.refs_0_, bf16[384,768]{1,0:T(8,128)(2,1)S(1)} %get-tuple-element.68.refs_1_, bf16[768,768]{1,0:T(8,128)(2,1)S(1)} %constant_dynamic-update-slice_fusion.32.refs_2_, ...), custom_call_target="tpu_custom_call" | custom-call | flops 1811939328 | bytes 3538944 | tf_op jit(solution)/shard_map/gram_step/pallas_call | solution.py:169
  90.4 14.5 %collective-permute-done.24 = bf16[384,768]{1,0:T(8,128)(2,1)S(1)} collective-permute-done((bf16[384,768]{1,0:T(8,128)(2,1)S(1)}, bf16[384,768]{1,0:T(8,128)(2,1)S(1)}, u32[]{:S(2)}, u32[]{:S(2)}) %collective-permute-start.24) | collective-permute-done | bytes 589856 | tf_op jit(solution)/shard_map/ppermute | solution.py:29
  105.0 4.5 %gram_step.5 = (f32[384,128]{1,0:T(8,128)S(1)}, f32[384,128]{1,0:T(8,128)S(1)}, f32[384,128]{1,0:T(8,128)S(1)}, f32[1,1536]{1,0:T(1,128)S(1)}) custom-call(bf16[384,768]{1,0:T(8,128)(2,1)S(1)} %get-tuple-element.57.refs_0_, bf16[384,768]{1,0:T(8,128)(2,1)S(1)} %get-tuple-element.68.refs_1_, bf16[384,768]{1,0:T(8,128)(2,1)S(1)} %get-tuple-element.70.refs_2_, ...), custom_call_target="tpu_custom_call" | custom-call | flops 2717908992 | bytes 4128768 | tf_op jit(solution)/shard_map/gram_step/pallas_call | solution.py:169
  109.5 2.8 %collective-permute-done.26.refs_5_ = bf16[768,768]{1,0:T(8,128)(2,1)S(1)} collective-permute-done((bf16[768,768]{1,0:T(8,128)(2,1)S(1)}, bf16[768,768]{1,0:T(8,128)(2,1)S(1)}, u32[]{:S(2)}, u32[]{:S(2)}) %collective-permute-start.26) | collective-permute-done | bytes 1179680 | tf_op jit(solution)/shard_map/ppermute | solution.py:29
  112.4 7.1 %gram_last.1 = f32[32,192]{1,0:T(8,128)S(1)} custom-call(s32[2]{0:T(128)S(1)} %pad_add_fusion.me_ref, bf16[384,768]{1,0:T(8,128)(2,1)S(1)} %get-tuple-element.57.refs_0_, bf16[384,768]{1,0:T(8,128)(2,1)S(1)} %get-tuple-element.68.refs_1_, bf16[384,768]{1,0:T(8,128)(2,1)S(1)} %get-tuple-element.70.refs_2_, bf16[384,768]{1,0:T(8,128)(2,1)S(1)} %get-tuple-element.74.refs_3_, ...), custom_call_target="tpu_custom_call" | custom-call | flops 3623878656 | bytes 4718592 | tf_op jit(solution)/shard_map/gram_last/pallas_call | solution.py:180
  119.5 11.0 %all_to_all.11 = f32[32,1,192]{2,1,0:T(1,128)S(1)} all-to-all(f32[32,1,192]{2,1,0:T(1,128)S(1)} %copy.3), channel_id=1, replica_groups=mesh['grp'=8,'blk'=4] {'grp','blk'}, dimensions={0} | all-to-all | bytes 49152 | tf_op jit(solution)/shard_map/all_to_all | solution.py:316
  131.1 2.3 %pick_rows.1 = f32[6,128]{1,0:T(8,128)} custom-call(s32[6,128]{1,0:T(8,128)} %bitcast.9, f32[32,192]{1,0:T(8,128)} %bitcast.11), custom_call_target="tpu_custom_call" | custom-call | tf_op jit(solution)/shard_map/pick_rows/pallas_call | solution.py:220
  (80 shorter events, 22.6 us)
Async XLA Ops:
  5.2 10.0 %collective-permute-start = (bf16[48,768]{1,0:T(8,128)(2,1)S(1)}, bf16[48,768]{1,0:T(8,128)(2,1)S(1)}, u32[]{:S(2)}, u32[]{:S(2)}) collective-permute-start(bf16[48,768]{1,0:T(8,128)(2,1)S(1)} %get-tuple-element.121), channel_id=1, source_target_pairs={{0,20},{4,16},{8,28},{12,24},{16,4},{20,0},{24,12},{28,8},{1,21},{... | collective-permute-start | bytes 221192 | tf_op jit(solution)/shard_map/ppermute | solution.py:29
  10.2 9.2 %collective-permute-start.2 = (bf16[48,768]{1,0:T(8,128)(2,1)S(1)}, bf16[48,768]{1,0:T(8,128)(2,1)S(1)}, u32[]{:S(2)}, u32[]{:S(2)}) collective-permute-start(bf16[48,768]{1,0:T(8,128)(2,1)S(1)} %get-tuple-element.120), channel_id=1, source_target_pairs={{0,24},{4,28},{8,16},{12,20},{16,8},{20,12},{24,0},{28,4},{1,25},{... | collective-permute-start | bytes 221192 | tf_op jit(solution)/shard_map/ppermute | solution.py:29
  11.6 12.9 %collective-permute-start.4 = (bf16[48,768]{1,0:T(8,128)(2,1)S(1)}, bf16[48,768]{1,0:T(8,128)(2,1)S(1)}, u32[]{:S(2)}, u32[]{:S(2)}) collective-permute-start(bf16[48,768]{1,0:T(8,128)(2,1)S(1)} %get-tuple-element.119), channel_id=1, source_target_pairs={{0,28},{4,24},{8,20},{12,16},{16,12},{20,8},{24,4},{28,0},{1,29},{... | collective-permute-start | bytes 221192 | tf_op jit(solution)/shard_map/ppermute | solution.py:29
  15.1 10.3 %collective-permute-start.1 = (bf16[48,768]{1,0:T(8,128)(2,1)S(1)}, bf16[48,768]{1,0:T(8,128)(2,1)S(1)}, u32[]{:S(2)}, u32[]{:S(2)}) collective-permute-start(bf16[48,768]{1,0:T(8,128)(2,1)S(1)} %get-tuple-element.46), channel_id=1, source_target_pairs={{0,4},{4,0},{8,12},{12,8},{16,20},{20,16},{24,28},{28,24},{1,5},{5... | collective-permute-start | bytes 221192 | tf_op jit(solution)/shard_map/ppermute | solution.py:29
  19.4 10.3 %collective-permute-start.6 = (bf16[48,768]{1,0:T(8,128)(2,1)S(1)}, bf16[48,768]{1,0:T(8,128)(2,1)S(1)}, u32[]{:S(2)}, u32[]{:S(2)}) collective-permute-start(bf16[48,768]{1,0:T(8,128)(2,1)S(1)} %get-tuple-element.118), channel_id=1, source_target_pairs={{0,16},{4,20},{8,24},{12,28},{16,0},{20,4},{24,8},{28,12},{1,17},{... | collective-permute-start | bytes 221192 | tf_op jit(solution)/shard_map/ppermute | solution.py:29
  19.4 11.9 %collective-permute-start.7 = (bf16[192,768]{1,0:T(8,128)(2,1)S(1)}, bf16[192,768]{1,0:T(8,128)(2,1)S(1)}, u32[]{:S(2)}, u32[]{:S(2)}) collective-permute-start(bf16[192,768]{1,0:T(8,128)(2,1)S(1)} %get-tuple-element.50), channel_id=1, source_target_pairs={{0,4},{4,0},{8,12},{12,8},{16,20},{20,16},{24,28},{28,24},{1,5},{5... | collective-permute-start | bytes 884744 | tf_op jit(solution)/shard_map/ppermute | solution.py:29
  29.8 12.4 %collective-permute-start.12 = (bf16[384,768]{1,0:T(8,128)(2,1)S(1)}, bf16[384,768]{1,0:T(8,128)(2,1)S(1)}, u32[]{:S(2)}, u32[]{:S(2)}) collective-permute-start(bf16[384,768]{1,0:T(8,128)(2,1)S(1)} %get-tuple-element.57.refs_0_), channel_id=1, source_target_pairs={{0,2},{1,3},{2,0},{3,1},{4,6},{5,7},{6,4},{7,5},{8,10},{9,11},{10,... | collective-permute-start | bytes 1769480 | tf_op jit(solution)/shard_map/ppermute | solution.py:29
  31.4 10.8 %collective-permute-start.10 = (bf16[96,768]{1,0:T(8,128)(2,1)S(1)}, bf16[96,768]{1,0:T(8,128)(2,1)S(1)}, u32[]{:S(2)}, u32[]{:S(2)}) collective-permute-start(bf16[96,768]{1,0:T(8,128)(2,1)S(1)} %pad_maximum_fusion.2), channel_id=1, source_target_pairs={{0,24},{4,28},{8,16},{12,20},{16,8},{20,12},{24,0},{28,4},{1,25},{... | collective-permute-start | bytes 442376 | tf_op jit(solution)/shard_map/ppermute | solution.py:29
  34.0 10.5 %collective-permute-start.8 = (bf16[96,768]{1,0:T(8,128)(2,1)S(1)}, bf16[96,768]{1,0:T(8,128)(2,1)S(1)}, u32[]{:S(2)}, u32[]{:S(2)}) collective-permute-start(bf16[96,768]{1,0:T(8,128)(2,1)S(1)} %pad_maximum_fusion), channel_id=1, source_target_pairs={{0,8},{4,12},{8,0},{12,4},{16,24},{20,28},{24,16},{28,20},{1,9},{5... | collective-permute-start | bytes 442376 | tf_op jit(solution)/shard_map/ppermute | solution.py:29
  34.1 12.1 %collective-permute-start.9 = (bf16[96,768]{1,0:T(8,128)(2,1)S(1)}, bf16[96,768]{1,0:T(8,128)(2,1)S(1)}, u32[]{:S(2)}, u32[]{:S(2)}) collective-permute-start(bf16[96,768]{1,0:T(8,128)(2,1)S(1)} %pad_maximum_fusion.1), channel_id=1, source_target_pairs={{0,16},{4,20},{8,24},{12,28},{16,0},{20,4},{24,8},{28,12},{1,17},{... | collective-permute-start | bytes 442376 | tf_op jit(solution)/shard_map/ppermute | solution.py:29
  42.2 15.1 %collective-permute-start.13 = (bf16[768,768]{1,0:T(8,128)(2,1)S(1)}, bf16[768,768]{1,0:T(8,128)(2,1)S(1)}, u32[]{:S(2)}, u32[]{:S(2)}) collective-permute-start(bf16[768,768]{1,0:T(8,128)(2,1)S(1)} %constant_dynamic-update-slice_fusion.13.refs_1_), channel_id=1, source_target_pairs={{0,1},{1,0},{2,3},{3,2},{4,5},{5,4},{6,7},{7,6},{8,9},{9,8},{10,11... | collective-permute-start | bytes 3538952 | tf_op jit(solution)/shard_map/ppermute | solution.py:29
  42.3 9.8 %collective-permute-start.11 = (bf16[192,768]{1,0:T(8,128)(2,1)S(1)}, bf16[192,768]{1,0:T(8,128)(2,1)S(1)}, u32[]{:S(2)}, u32[]{:S(2)}) collective-permute-start(bf16[192,768]{1,0:T(8,128)(2,1)S(1)} %get-tuple-element.56), channel_id=1, source_target_pairs={{0,4},{4,0},{8,12},{12,8},{16,20},{20,16},{24,28},{28,24},{1,5},{5... | collective-permute-start | bytes 884744 | tf_op jit(solution)/shard_map/ppermute | solution.py:29
  46.3 14.1 %collective-permute-start.21 = (bf16[384,768]{1,0:T(8,128)(2,1)S(1)}, bf16[384,768]{1,0:T(8,128)(2,1)S(1)}, u32[]{:S(2)}, u32[]{:S(2)}) collective-permute-start(bf16[384,768]{1,0:T(8,128)(2,1)S(1)} %get-tuple-element.68.refs_1_), channel_id=1, source_target_pairs={{0,2},{1,3},{2,0},{3,1},{4,6},{5,7},{6,4},{7,5},{8,10},{9,11},{10,... | collective-permute-start | bytes 1769480 | tf_op jit(solution)/shard_map/ppermute | solution.py:29
  52.1 15.2 %collective-permute-start.15 = (bf16[96,768]{1,0:T(8,128)(2,1)S(1)}, bf16[96,768]{1,0:T(8,128)(2,1)S(1)}, u32[]{:S(2)}, u32[]{:S(2)}) collective-permute-start(bf16[96,768]{1,0:T(8,128)(2,1)S(1)} %pad_maximum_fusion.4), channel_id=1, source_target_pairs={{0,16},{4,20},{8,24},{12,28},{16,0},{20,4},{24,8},{28,12},{1,17},{... | collective-permute-start | bytes 442376 | tf_op jit(solution)/shard_map/ppermute | solution.py:29
  53.7 11.0 %collective-permute-start.16 = (bf16[96,768]{1,0:T(8,128)(2,1)S(1)}, bf16[96,768]{1,0:T(8,128)(2,1)S(1)}, u32[]{:S(2)}, u32[]{:S(2)}) collective-permute-start(bf16[96,768]{1,0:T(8,128)(2,1)S(1)} %pad_maximum_fusion.5), channel_id=1, source_target_pairs={{0,24},{4,28},{8,16},{12,20},{16,8},{20,12},{24,0},{28,4},{1,25},{... | collective-permute-start | bytes 442376 | tf_op jit(solution)/shard_map/ppermute | solution.py:29
  57.0 11.7 %collective-permute-start.17 = (bf16[192,768]{1,0:T(8,128)(2,1)S(1)}, bf16[192,768]{1,0:T(8,128)(2,1)S(1)}, u32[]{:S(2)}, u32[]{:S(2)}) collective-permute-start(bf16[192,768]{1,0:T(8,128)(2,1)S(1)} %get-tuple-element.64), channel_id=1, source_target_pairs={{0,4},{4,0},{8,12},{12,8},{16,20},{20,16},{24,28},{28,24},{1,5},{5... | collective-permute-start | bytes 884744 | tf_op jit(solution)/shard_map/ppermute | solution.py:29
  57.3 9.9 %collective-permute-start.14 = (bf16[96,768]{1,0:T(8,128)(2,1)S(1)}, bf16[96,768]{1,0:T(8,128)(2,1)S(1)}, u32[]{:S(2)}, u32[]{:S(2)}) collective-permute-start(bf16[96,768]{1,0:T(8,128)(2,1)S(1)} %pad_maximum_fusion.3), channel_id=1, source_target_pairs={{0,8},{4,12},{8,0},{12,4},{16,24},{20,28},{24,16},{28,20},{1,9},{5... | collective-permute-start | bytes 442376 | tf_op jit(solution)/shard_map/ppermute | solution.py:29
  64.8 18.4 %collective-permute-start.23 = (bf16[768,768]{1,0:T(8,128)(2,1)S(1)}, bf16[768,768]{1,0:T(8,128)(2,1)S(1)}, u32[]{:S(2)}, u32[]{:S(2)}) collective-permute-start(bf16[768,768]{1,0:T(8,128)(2,1)S(1)} %constant_dynamic-update-slice_fusion.32.refs_2_), channel_id=1, source_target_pairs={{0,1},{1,0},{2,3},{3,2},{4,5},{5,4},{6,7},{7,6},{8,9},{9,8},{10,11... | collective-permute-start | bytes 3538952 | tf_op jit(solution)/shard_map/ppermute | solution.py:29
  67.3 15.8 %collective-permute-start.22 = (bf16[384,768]{1,0:T(8,128)(2,1)S(1)}, bf16[384,768]{1,0:T(8,128)(2,1)S(1)}, u32[]{:S(2)}, u32[]{:S(2)}) collective-permute-start(bf16[384,768]{1,0:T(8,128)(2,1)S(1)} %get-tuple-element.70.refs_2_), channel_id=1, source_target_pairs={{0,2},{1,3},{2,0},{3,1},{4,6},{5,7},{6,4},{7,5},{8,10},{9,11},{10,... | collective-permute-start | bytes 1769480 | tf_op jit(solution)/shard_map/ppermute | solution.py:29
  68.7 17.4 %collective-permute-start.20 = (bf16[96,768]{1,0:T(8,128)(2,1)S(1)}, bf16[96,768]{1,0:T(8,128)(2,1)S(1)}, u32[]{:S(2)}, u32[]{:S(2)}) collective-permute-start(bf16[96,768]{1,0:T(8,128)(2,1)S(1)} %pad_maximum_fusion.8), channel_id=1, source_target_pairs={{0,24},{4,28},{8,16},{12,20},{16,8},{20,12},{24,0},{28,4},{1,25},{... | collective-permute-start | bytes 442376 | tf_op jit(solution)/shard_map/ppermute | solution.py:29
  70.4 12.9 %collective-permute-start.18 = (bf16[96,768]{1,0:T(8,128)(2,1)S(1)}, bf16[96,768]{1,0:T(8,128)(2,1)S(1)}, u32[]{:S(2)}, u32[]{:S(2)}) collective-permute-start(bf16[96,768]{1,0:T(8,128)(2,1)S(1)} %pad_maximum_fusion.6), channel_id=1, source_target_pairs={{0,8},{4,12},{8,0},{12,4},{16,24},{20,28},{24,16},{28,20},{1,9},{5... | collective-permute-start | bytes 442376 | tf_op jit(solution)/shard_map/ppermute | solution.py:29
  73.9 12.1 %collective-permute-start.19 = (bf16[96,768]{1,0:T(8,128)(2,1)S(1)}, bf16[96,768]{1,0:T(8,128)(2,1)S(1)}, u32[]{:S(2)}, u32[]{:S(2)}) collective-permute-start(bf16[96,768]{1,0:T(8,128)(2,1)S(1)} %pad_maximum_fusion.7), channel_id=1, source_target_pairs={{0,16},{4,20},{8,24},{12,28},{16,0},{20,4},{24,8},{28,12},{1,17},{... | collective-permute-start | bytes 442376 | tf_op jit(solution)/shard_map/ppermute | solution.py:29
  83.2 21.8 %collective-permute-start.25 = (bf16[768,768]{1,0:T(8,128)(2,1)S(1)}, bf16[768,768]{1,0:T(8,128)(2,1)S(1)}, u32[]{:S(2)}, u32[]{:S(2)}) collective-permute-start(bf16[768,768]{1,0:T(8,128)(2,1)S(1)} %constant_dynamic-update-slice_fusion.44.refs_3_), channel_id=1, source_target_pairs={{0,1},{1,0},{2,3},{3,2},{4,5},{5,4},{6,7},{7,6},{8,9},{9,8},{10,11... | collective-permute-start | bytes 3538952 | tf_op jit(solution)/shard_map/ppermute | solution.py:29
  89.6 15.3 %collective-permute-start.24 = (bf16[384,768]{1,0:T(8,128)(2,1)S(1)}, bf16[384,768]{1,0:T(8,128)(2,1)S(1)}, u32[]{:S(2)}, u32[]{:S(2)}) collective-permute-start(bf16[384,768]{1,0:T(8,128)(2,1)S(1)} %get-tuple-element.74.refs_3_), channel_id=1, source_target_pairs={{0,2},{1,3},{2,0},{3,1},{4,6},{5,7},{6,4},{7,5},{8,10},{9,11},{10,... | collective-permute-start | bytes 1769480 | tf_op jit(solution)/shard_map/ppermute | solution.py:29
  (5 other events, 17.9 us)

commit v5 on v4

--- a/solution.py
+++ b/solution.py
@@ -17,8 +17,7 @@
 
 
 def chunk_sizes(capacity):
-    count = 4 if capacity % 64 == 0 else 3
-    return (capacity // count,) * count
+    return (capacity // 3,) * 3
 
 
 def after(value, *earlier):
@@ -39,8 +38,7 @@
     for step, size in enumerate(chunks):
         place = lax.broadcasted_iota(jnp.int32, (groups, size, 1), 1)
         order = lax.broadcasted_iota(jnp.int32, (groups, size, 1), 0)
-        relative = order if step == 0 else order % high * 2 + order // high
-        group = relative ^ me_ref[0]
+        group = (order % high * 2 + order // high) ^ me_ref[0]
         wanted = (group * capacity + place + first).reshape(groups * size, 1)
         pick = jnp.where(wanted == slots, 1.0, 0.0)
         live = jnp.max(pick, axis=1, keepdims=True)
@@ -240,13 +238,7 @@
     count, high = len(chunks), groups // 2
     last = count - 1
 
-    sent, owns, done, states, cols = {}, {}, {}, [], []
-    pairs, window = {}, []
-
-    def send(key, value, axis, size, bit, *earlier):
-        earlier = earlier + tuple(window[-5:-4])
-        sent[key] = swap(after(value, *earlier) if earlier else value, axis, size, bit)
-        window.append(sent[key])
+    sent, owns, done, states, cols, pairs = {}, {}, {}, [], [], {}
 
     def rows(value, index, size):
         return value[index * size : (index + 1) * size]
@@ -257,32 +249,38 @@
             [rows(placed[2 * step], z, size), rows(sent["y", step], z, size)], axis=0
         )
 
-    def start(kind, step, bit=0):
-        size = chunks[step]
-        if kind == "d":
-            value = rows(placed[2 * bit // groups], bit % high, size)
-            send((kind, step, bit), value, "grp", groups, bit)
-        elif kind == "y":
-            send((kind, step), placed[2 * step + 1], "grp", groups, 1)
-        elif kind == "z":
-            send((kind, step, bit), block(step, bit), "grp", groups, 2 * bit)
-        elif kind == "x":
-            if step == 0:
-                parts = [rows(placed[0], 0, size)]
-                parts += [sent["d", 0, r] for r in range(1, groups)]
-            else:
-                parts = [block(step, 0)] + [sent["z", step, z] for z in range(1, high)]
-            owns[step] = jnp.concatenate(parts, axis=0)
-            earlier = [sent["x", step - 1]] if step >= 1 else []
-            earlier += [done[step - 2]] if step >= 2 else []
-            send((kind, step), owns[step], "blk", members, 2, *earlier)
-        elif kind == "c":
-            pairs[step] = jnp.concatenate([owns[step], sent["x", step]], axis=0)
-            earlier = [done[step - 1]] if step == last else []
-            send((kind, step), pairs[step], "blk", members, 1, *earlier)
+    def send(key, value, axis, size, bit, *earlier):
+        held = [sent[name] for name in earlier if name in sent]
+        held += [done[name[1]] for name in earlier if name[0] == "gram" and name[1] in done]
+        sent[key] = swap(after(value, *held) if held else value, axis, size, bit)
+
+    def send_y(step):
+        if step < count:
+            send(("y", step), placed[2 * step + 1], "grp", groups, 1, ("y", step - 1))
+
+    def send_z(step, z):
+        early = [("z", step - 1, z)]
+        if z == high - 1:
+            early += [("x", step - 2, 0)]
+        send(("z", step, z), block(step, z), "grp", groups, 2 * z, *early)
+
+    def send_x(step):
+        parts = [block(step, 0)] + [sent["z", step, z] for z in range(1, high)]
+        owns[step] = jnp.concatenate(parts, axis=0)
+        cuts = 1 if step == 0 else 2
+        half = owns[step].shape[0] // cuts
+        for cut in range(cuts):
+            early = [("x", step - 1, 0), ("x", step - 1, 1)] if cut == 0 else [("gram", step - 1)]
+            value = rows(owns[step], cut, half)
+            send(("x", step, cut), value, "blk", members, 2, *early)
+            if cut == 0 and step >= 1:
+                gram(step - 1)
 
     def gram(step):
         nonlocal states, cols
+        across = [sent[name] for name in sent if name[:2] == ("x", step)]
+        pairs[step] = jnp.concatenate([owns[step]] + across, axis=0)
+        send(("c", step), pairs[step], "blk", members, 1)
         result = gram_step(
             step,
             me,
@@ -299,19 +297,21 @@
         states, cols = result
         done[step] = cols[-1]
 
-    direct = [("d", 0, r) for r in reversed(range(1, groups))]
-    order = direct[:4] + [("y", 1)] + direct[4:]
+    far = [high // 2] + [z for z in reversed(range(1, high)) if z != high // 2]
+    send_y(0)
+    for z in far[:2]:
+        send_z(0, z)
+    send_y(1)
+    for z in far[2:]:
+        send_z(0, z)
     for step in range(1, count):
-        stages = [("z", step, z) for z in reversed(range(1, high))]
-        order += stages[:2] + ([("y", step + 1)] if step < last else [])
-        order += [("x", step - 1)] + stages[2:]
-        order += [("c", step - 1), ("gram", step - 1)]
-    order += [("x", last), ("c", last)]
-    for item in order:
-        if item[0] == "gram":
-            gram(item[1])
-        else:
-            start(*item)
+        for z in far[:2]:
+            send_z(step, z)
+        send_x(step - 1)
+        for z in far[2:]:
+            send_z(step, z)
+        send_y(step + 1)
+    send_x(last)
     result = gram(last)
     homeward = lax.all_to_all(result, ("grp", "blk"), 0, 0, tiled=True)
     return tail(homeward, slots, capacity, members).reshape(row_count)

time: 134 us -> 182 us (1.36)
  waiting for transfers between devices: 53.2 us -> 110 us
  starting transfers between devices: 42.6 us -> 31.4 us
  blocking collectives: 11 us -> 14.1 us
    ppermute x27 -> x20, waiting for transfers between devices: 53.2 us -> 110 us  [swap(): return lax.ppermute(value, axis, [(i, i ^ bit) for i in range(size)])]
    ppermute x27 -> x20, starting transfers between devices: 42.6 us -> 31.4 us  [swap(): return lax.ppermute(value, axis, [(i, i ^ bit) for i in range(size)])]
    all_to_all x1, blocking collectives: 11 us -> 14.1 us  [on_device(): homeward = lax.all_to_all(result, ('grp', 'blk'), 0, 0, tiled=True)]
    pallas_call x3 -> x2, Pallas kernels: 10.4 us -> 8.98 us  [gram_step(): pl.pallas_call(functools.partial(gram_kernel, step, tile), in_specs=[vmem...]
  transfers between devices with their start and end apart: 27 -> 20, of which waited for: 12 -> 15; matrix products, arithmetic and copies ran while one was open for 1% -> 0% of each run, Pallas kernels for 4% -> 5%
where the time goes in v5:
time: 182 us
  waiting for transfers between devices  110 us (60%)
  starting transfers between devices  31.4 us (17%)
  Pallas kernels  22.8 us (13%)
  blocking collectives  14.1 us (8%)
  local copies, waits for them, and re-layouts  3.22 us (2%)
    ppermute x20, waiting for transfers between devices, swap(): return lax.ppermute(value, axis, [(i, i ^ bit) for i in range(size)])  110 us
    ppermute x20, starting transfers between devices, swap(): return lax.ppermute(value, axis, [(i, i ^ bit) for i in range(size)])  31.4 us
    all_to_all x1, blocking collectives, on_device(): homeward = lax.all_to_all(result, ('grp', 'blk'), 0, 0, tiled=True)  14.1 us
    pallas_call x2, Pallas kernels, gram_step(): pl.pallas_call(functools.partial(gram_kernel, step, tile), in_specs=[vmem...  8.98 us
    pallas_call x1, Pallas kernels, gram_step(): pl.pallas_call(functools.partial(gram_last_kernel, step, relatives, chunk...  8.4 us
  transfers between devices with their start and end apart: 20, of which 15 were waited for; matrix products, arithmetic and copies ran while one was open for 0% of the time, Pallas kernels for 5%

profile of v5, /device:TPU:0, one launch (start us, length us, event | category | flops | bytes accessed | tf_op | source)
XLA Modules:
  0.0 181.9 jit_solution(237563322023146342)
XLA Ops:
  2.0 3.1 %place_rows.1 = (bf16[256,768]{1,0:T(8,128)(2,1)S(1)}, bf16[256,768]{1,0:T(8,128)(2,1)S(1)}, bf16[256,768]{1,0:T(8,128)(2,1)S(1)}, bf16[256,768]{1,0:T(8,128)(2,...) custom-call(s32[2]{0:T(128)S(1)} %pad_add_fusion.me_ref, s32[6,128]{1,0:T(8,128)S(1)} %bitcast.10, ...), custom_call_target="tpu_custom_call" | custom-call | tf_op jit(solution)/shard_map/place_rows/pallas_call | solution.py:56
  5.2 3.0 %collective-permute-start = (bf16[256,768]{1,0:T(8,128)(2,1)S(1)}, bf16[256,768]{1,0:T(8,128)(2,1)S(1)}, u32[]{:S(2)}, u32[]{:S(2)}) collective-permute-start(bf16[256,768]{1,0:T(8,128)(2,1)S(1)} %get-tuple-element.29), channel_id=1, source_target_pairs={{0,4},{4,0},{8,12},{12,8},{16,20},{20,16},{24,28},{28,24},{1,5},{5... | collective-permute-start | bytes 1179656 | tf_op jit(solution)/shard_map/ppermute | solution.py:28
  8.2 9.1 %collective-permute-done = bf16[256,768]{1,0:T(8,128)(2,1)S(1)} collective-permute-done((bf16[256,768]{1,0:T(8,128)(2,1)S(1)}, bf16[256,768]{1,0:T(8,128)(2,1)S(1)}, u32[]{:S(2)}, u32[]{:S(2)}) %collective-permute-start) | collective-permute-done | bytes 393248 | tf_op jit(solution)/shard_map/ppermute | solution.py:28
  19.2 2.7 %collective-permute-start.2 = (bf16[128,768]{1,0:T(8,128)(2,1)S(1)}, bf16[128,768]{1,0:T(8,128)(2,1)S(1)}, u32[]{:S(2)}, u32[]{:S(2)}) collective-permute-start(bf16[128,768]{1,0:T(8,128)(2,1)S(1)} %pad_maximum_fusion.5), channel_id=1, source_target_pairs={{0,16},{4,20},{8,24},{12,28},{16,0},{20,4},{24,8},{28,12},{1,17},{... | collective-permute-start | bytes 589832 | tf_op jit(solution)/shard_map/ppermute | solution.py:28
  22.0 4.2 %collective-permute-done.1 = bf16[128,768]{1,0:T(8,128)(2,1)S(1)} collective-permute-done((bf16[128,768]{1,0:T(8,128)(2,1)S(1)}, bf16[128,768]{1,0:T(8,128)(2,1)S(1)}, u32[]{:S(2)}, u32[]{:S(2)}) %collective-permute-start.1) | collective-permute-done | bytes 196640 | tf_op jit(solution)/shard_map/ppermute | solution.py:28
  26.2 10.1 %collective-permute-done.2 = bf16[128,768]{1,0:T(8,128)(2,1)S(1)} collective-permute-done((bf16[128,768]{1,0:T(8,128)(2,1)S(1)}, bf16[128,768]{1,0:T(8,128)(2,1)S(1)}, u32[]{:S(2)}, u32[]{:S(2)}) %collective-permute-start.2) | collective-permute-done | bytes 196640 | tf_op jit(solution)/shard_map/ppermute | solution.py:28
  37.9 13.6 %collective-permute-done.11 = bf16[512,768]{1,0:T(8,128)(2,1)S(1)} collective-permute-done((bf16[512,768]{1,0:T(8,128)(2,1)S(1)}, bf16[512,768]{1,0:T(8,128)(2,1)S(1)}, u32[]{:S(2)}, u32[]{:S(2)}) %collective-permute-start.11) | collective-permute-done | bytes 786464 | tf_op jit(solution)/shard_map/ppermute | solution.py:28
  53.3 9.9 %collective-permute-done.4 = bf16[256,768]{1,0:T(8,128)(2,1)S(1)} collective-permute-done((bf16[256,768]{1,0:T(8,128)(2,1)S(1)}, bf16[256,768]{1,0:T(8,128)(2,1)S(1)}, u32[]{:S(2)}, u32[]{:S(2)}) %collective-permute-start.4) | collective-permute-done | bytes 393248 | tf_op jit(solution)/shard_map/ppermute | solution.py:28
  63.3 6.5 %collective-permute-start.6 = (bf16[128,768]{1,0:T(8,128)(2,1)S(1)}, bf16[128,768]{1,0:T(8,128)(2,1)S(1)}, u32[]{:S(2)}, u32[]{:S(2)}) collective-permute-start(bf16[128,768]{1,0:T(8,128)(2,1)S(1)} %pad_maximum_fusion.8), channel_id=1, source_target_pairs={{0,16},{4,20},{8,24},{12,28},{16,0},{20,4},{24,8},{28,12},{1,17},{... | collective-permute-start | bytes 589832 | tf_op jit(solution)/shard_map/ppermute | solution.py:28
  70.5 12.9 %collective-permute-done.6 = bf16[128,768]{1,0:T(8,128)(2,1)S(1)} collective-permute-done((bf16[128,768]{1,0:T(8,128)(2,1)S(1)}, bf16[128,768]{1,0:T(8,128)(2,1)S(1)}, u32[]{:S(2)}, u32[]{:S(2)}) %collective-permute-start.6) | collective-permute-done | bytes 196640 | tf_op jit(solution)/shard_map/ppermute | solution.py:28
  86.0 3.5 %gram_step.2 = (f32[512,128]{1,0:T(8,128)S(1)}, f32[1,2048]{1,0:T(1,128)S(1)}) custom-call(bf16[512,768]{1,0:T(8,128)(2,1)S(1)} %get-tuple-element.92.refs_0_, bf16[1024,768]{1,0:T(8,128)(2,1)S(1)} %constant_dynamic-update-slice_fusion.13.refs_1_, bf16[1024,768]{1,0:T(8,128)(2,1)S(1)} %collective-permute-done.14.refs_2_), custom_call_target="tpu_custom_call" | custom-call | flops 1610612736 | bytes 3932160 | tf_op jit(solution)/shard_map/gram_step/pallas_call | solution.py:167
  90.2 6.4 %collective-permute-done.13 = bf16[256,768]{1,0:T(8,128)(2,1)S(1)} collective-permute-done((bf16[256,768]{1,0:T(8,128)(2,1)S(1)}, bf16[256,768]{1,0:T(8,128)(2,1)S(1)}, u32[]{:S(2)}, u32[]{:S(2)}) %collective-permute-start.13) | collective-permute-done | bytes 393248 | tf_op jit(solution)/shard_map/ppermute | solution.py:28
  96.5 5.7 %collective-permute-done.15 = bf16[256,768]{1,0:T(8,128)(2,1)S(1)} collective-permute-done((bf16[256,768]{1,0:T(8,128)(2,1)S(1)}, bf16[256,768]{1,0:T(8,128)(2,1)S(1)}, u32[]{:S(2)}, u32[]{:S(2)}) %collective-permute-start.15) | collective-permute-done | bytes 393248 | tf_op jit(solution)/shard_map/ppermute | solution.py:28
  104.0 9.9 %collective-permute-done.8 = bf16[256,768]{1,0:T(8,128)(2,1)S(1)} collective-permute-done((bf16[256,768]{1,0:T(8,128)(2,1)S(1)}, bf16[256,768]{1,0:T(8,128)(2,1)S(1)}, u32[]{:S(2)}, u32[]{:S(2)}) %collective-permute-start.8) | collective-permute-done | bytes 393248 | tf_op jit(solution)/shard_map/ppermute | solution.py:28
  114.0 4.8 %collective-permute-start.9 = (bf16[128,768]{1,0:T(8,128)(2,1)S(1)}, bf16[128,768]{1,0:T(8,128)(2,1)S(1)}, u32[]{:S(2)}, u32[]{:S(2)}) collective-permute-start(bf16[128,768]{1,0:T(8,128)(2,1)S(1)} %pad_maximum_fusion.10), channel_id=1, source_target_pairs={{0,8},{4,12},{8,0},{12,4},{16,24},{20,28},{24,16},{28,20},{1,9},{5... | collective-permute-start | bytes 589832 | tf_op jit(solution)/shard_map/ppermute | solution.py:28
  118.9 2.4 %collective-permute-start.12 = (bf16[128,768]{1,0:T(8,128)(2,1)S(1)}, bf16[128,768]{1,0:T(8,128)(2,1)S(1)}, u32[]{:S(2)}, u32[]{:S(2)}) collective-permute-start(bf16[128,768]{1,0:T(8,128)(2,1)S(1)} %pad_maximum_fusion.12), channel_id=1, source_target_pairs={{0,24},{4,28},{8,16},{12,20},{16,8},{20,12},{24,0},{28,4},{1,25},{... | collective-permute-start | bytes 589832 | tf_op jit(solution)/shard_map/ppermute | solution.py:28
  121.3 4.2 %collective-permute-done.9 = bf16[128,768]{1,0:T(8,128)(2,1)S(1)} collective-permute-done((bf16[128,768]{1,0:T(8,128)(2,1)S(1)}, bf16[128,768]{1,0:T(8,128)(2,1)S(1)}, u32[]{:S(2)}, u32[]{:S(2)}) %collective-permute-start.9) | collective-permute-done | bytes 196640 | tf_op jit(solution)/shard_map/ppermute | solution.py:28
  125.6 10.0 %collective-permute-done.10 = bf16[128,768]{1,0:T(8,128)(2,1)S(1)} collective-permute-done((bf16[128,768]{1,0:T(8,128)(2,1)S(1)}, bf16[128,768]{1,0:T(8,128)(2,1)S(1)}, u32[]{:S(2)}, u32[]{:S(2)}) %collective-permute-start.10) | collective-permute-done | bytes 196640 | tf_op jit(solution)/shard_map/ppermute | solution.py:28
  137.1 5.5 %gram_step.3 = (f32[512,128]{1,0:T(8,128)S(1)}, f32[512,128]{1,0:T(8,128)S(1)}, f32[1,2048]{1,0:T(1,128)S(1)}) custom-call(bf16[512,768]{1,0:T(8,128)(2,1)S(1)} %get-tuple-element.92.refs_0_, bf16[512,768]{1,0:T(8,128)(2,1)S(1)} %get-tuple-element.86.refs_1_, bf16[1024,768]{1,0:T(8,128)(2,1)S(1)} %constant_dynamic-update-slice_fusion.17.refs_2_, ...), custom_call_target="tpu_custom_call" | custom-call | flops 3221225472 | bytes 4718592 | tf_op jit(solution)/shard_map/gram_step/pallas_call | solution.py:167
  143.3 2.7 %collective-permute-done.16 = bf16[256,768]{1,0:T(8,128)(2,1)S(1)} collective-permute-done((bf16[256,768]{1,0:T(8,128)(2,1)S(1)}, bf16[256,768]{1,0:T(8,128)(2,1)S(1)}, u32[]{:S(2)}, u32[]{:S(2)}) %collective-permute-start.16) | collective-permute-done | bytes 393248 | tf_op jit(solution)/shard_map/ppermute | solution.py:28
  146.1 6.8 %collective-permute-done.18 = bf16[256,768]{1,0:T(8,128)(2,1)S(1)} collective-permute-done((bf16[256,768]{1,0:T(8,128)(2,1)S(1)}, bf16[256,768]{1,0:T(8,128)(2,1)S(1)}, u32[]{:S(2)}, u32[]{:S(2)}) %collective-permute-start.18) | collective-permute-done | bytes 393248 | tf_op jit(solution)/shard_map/ppermute | solution.py:28
  153.0 3.4 %collective-permute-done.19.refs_4_ = bf16[1024,768]{1,0:T(8,128)(2,1)S(1)} collective-permute-done((bf16[1024,768]{1,0:T(8,128)(2,1)S(1)}, bf16[1024,768]{1,0:T(8,128)(2,1)S(1)}, u32[]{:S(2)}, u32[]{:S(2)}) %collective-permute-start.19) | collective-permute-done | bytes 1572896 | tf_op jit(solution)/shard_map/ppermute | solution.py:28
  156.4 8.4 %gram_last.1 = f32[32,192]{1,0:T(8,128)S(1)} custom-call(s32[2]{0:T(128)S(1)} %pad_add_fusion.me_ref, bf16[512,768]{1,0:T(8,128)(2,1)S(1)} %get-tuple-element.92.refs_0_, bf16[512,768]{1,0:T(8,128)(2,1)S(1)} %get-tuple-element.86.refs_1_, bf16[512,768]{1,0:T(8,128)(2,1)S(1)} %get-tuple-element.98.refs_2_, ...), custom_call_target="tpu_custom_call" | custom-call | flops 4831838208 | bytes 5505024 | tf_op jit(solution)/shard_map/gram_last/pallas_call | solution.py:178
  164.8 14.1 %all_to_all.11 = f32[32,1,192]{2,1,0:T(1,128)S(1)} all-to-all(f32[32,1,192]{2,1,0:T(1,128)S(1)} %copy.3), channel_id=1, replica_groups=mesh['grp'=8,'blk'=4] {'grp','blk'}, dimensions={0} | all-to-all | bytes 49152 | tf_op jit(solution)/shard_map/all_to_all | solution.py:316
  (62 shorter events, 18.8 us)
Async XLA Ops:
  0.1 1.3 copy-start
  1.3 0.7 copy-start.1
  5.2 12.1 %collective-permute-start = (bf16[256,768]{1,0:T(8,128)(2,1)S(1)}, bf16[256,768]{1,0:T(8,128)(2,1)S(1)}, u32[]{:S(2)}, u32[]{:S(2)}) collective-permute-start(bf16[256,768]{1,0:T(8,128)(2,1)S(1)} %get-tuple-element.29), channel_id=1, source_target_pairs={{0,4},{4,0},{8,12},{12,8},{16,20},{20,16},{24,28},{28,24},{1,5},{5... | collective-permute-start | bytes 1179656 | tf_op jit(solution)/shard_map/ppermute | solution.py:28
  17.4 8.8 %collective-permute-start.1 = (bf16[128,768]{1,0:T(8,128)(2,1)S(1)}, bf16[128,768]{1,0:T(8,128)(2,1)S(1)}, u32[]{:S(2)}, u32[]{:S(2)}) collective-permute-start(bf16[128,768]{1,0:T(8,128)(2,1)S(1)} %pad_maximum_fusion.4), channel_id=1, source_target_pairs={{0,8},{4,12},{8,0},{12,4},{16,24},{20,28},{24,16},{28,20},{1,9},{5... | collective-permute-start | bytes 589832 | tf_op jit(solution)/shard_map/ppermute | solution.py:28
  19.2 17.0 %collective-permute-start.2 = (bf16[128,768]{1,0:T(8,128)(2,1)S(1)}, bf16[128,768]{1,0:T(8,128)(2,1)S(1)}, u32[]{:S(2)}, u32[]{:S(2)}) collective-permute-start(bf16[128,768]{1,0:T(8,128)(2,1)S(1)} %pad_maximum_fusion.5), channel_id=1, source_target_pairs={{0,16},{4,20},{8,24},{12,28},{16,0},{20,4},{24,8},{28,12},{1,17},{... | collective-permute-start | bytes 589832 | tf_op jit(solution)/shard_map/ppermute | solution.py:28
  21.9 14.4 %collective-permute-start.3 = (bf16[128,768]{1,0:T(8,128)(2,1)S(1)}, bf16[128,768]{1,0:T(8,128)(2,1)S(1)}, u32[]{:S(2)}, u32[]{:S(2)}) collective-permute-start(bf16[128,768]{1,0:T(8,128)(2,1)S(1)} %pad_maximum_fusion.6), channel_id=1, source_target_pairs={{0,24},{4,28},{8,16},{12,20},{16,8},{20,12},{24,0},{28,4},{1,25},{... | collective-permute-start | bytes 589832 | tf_op jit(solution)/shard_map/ppermute | solution.py:28
  36.4 15.1 %collective-permute-start.11 = (bf16[512,768]{1,0:T(8,128)(2,1)S(1)}, bf16[512,768]{1,0:T(8,128)(2,1)S(1)}, u32[]{:S(2)}, u32[]{:S(2)}) collective-permute-start(bf16[512,768]{1,0:T(8,128)(2,1)S(1)} %get-tuple-element.92.refs_0_), channel_id=1, source_target_pairs={{0,2},{1,3},{2,0},{3,1},{4,6},{5,7},{6,4},{7,5},{8,10},{9,11},{10,... | collective-permute-start | bytes 2359304 | tf_op jit(solution)/shard_map/ppermute | solution.py:28
  51.6 34.4 %collective-permute-start.14 = (bf16[1024,768]{1,0:T(8,128)(2,1)S(1)}, bf16[1024,768]{1,0:T(8,128)(2,1)S(1)}, u32[]{:S(2)}, u32[]{:S(2)}) collective-permute-start(bf16[1024,768]{1,0:T(8,128)(2,1)S(1)} %constant_dynamic-update-slice_fusion.13.refs_1_), channel_id=1, source_target_pairs={{0,1},{1,0},{2,3},{3,2},{4,5},{5,4},{6,7},{7,6},{8,9},{9,8},{10,11... | collective-permute-start | bytes 4718600 | tf_op jit(solution)/shard_map/ppermute | solution.py:28
  51.6 11.5 %collective-permute-start.4 = (bf16[256,768]{1,0:T(8,128)(2,1)S(1)}, bf16[256,768]{1,0:T(8,128)(2,1)S(1)}, u32[]{:S(2)}, u32[]{:S(2)}) collective-permute-start(bf16[256,768]{1,0:T(8,128)(2,1)S(1)} %get-tuple-element.32), channel_id=1, source_target_pairs={{0,4},{4,0},{8,12},{12,8},{16,20},{20,16},{24,28},{28,24},{1,5},{5... | collective-permute-start | bytes 1179656 | tf_op jit(solution)/shard_map/ppermute | solution.py:28
  63.3 20.1 %collective-permute-start.6 = (bf16[128,768]{1,0:T(8,128)(2,1)S(1)}, bf16[128,768]{1,0:T(8,128)(2,1)S(1)}, u32[]{:S(2)}, u32[]{:S(2)}) collective-permute-start(bf16[128,768]{1,0:T(8,128)(2,1)S(1)} %pad_maximum_fusion.8), channel_id=1, source_target_pairs={{0,16},{4,20},{8,24},{12,28},{16,0},{20,4},{24,8},{28,12},{1,17},{... | collective-permute-start | bytes 589832 | tf_op jit(solution)/shard_map/ppermute | solution.py:28
  69.8 13.6 %collective-permute-start.7 = (bf16[128,768]{1,0:T(8,128)(2,1)S(1)}, bf16[128,768]{1,0:T(8,128)(2,1)S(1)}, u32[]{:S(2)}, u32[]{:S(2)}) collective-permute-start(bf16[128,768]{1,0:T(8,128)(2,1)S(1)} %pad_maximum_fusion.9), channel_id=1, source_target_pairs={{0,24},{4,28},{8,16},{12,20},{16,8},{20,12},{24,0},{28,4},{1,25},{... | collective-permute-start | bytes 589832 | tf_op jit(solution)/shard_map/ppermute | solution.py:28
  70.4 14.0 %collective-permute-start.5 = (bf16[128,768]{1,0:T(8,128)(2,1)S(1)}, bf16[128,768]{1,0:T(8,128)(2,1)S(1)}, u32[]{:S(2)}, u32[]{:S(2)}) collective-permute-start(bf16[128,768]{1,0:T(8,128)(2,1)S(1)} %pad_maximum_fusion.7), channel_id=1, source_target_pairs={{0,8},{4,12},{8,0},{12,4},{16,24},{20,28},{24,16},{28,20},{1,9},{5... | collective-permute-start | bytes 589832 | tf_op jit(solution)/shard_map/ppermute | solution.py:28
  84.4 12.1 %collective-permute-start.13 = (bf16[256,768]{1,0:T(8,128)(2,1)S(1)}, bf16[256,768]{1,0:T(8,128)(2,1)S(1)}, u32[]{:S(2)}, u32[]{:S(2)}) collective-permute-start(bf16[256,768]{1,0:T(8,128)(2,1)S(1)} %pad_maximum_fusion.1), channel_id=1, source_target_pairs={{0,2},{1,3},{2,0},{3,1},{4,6},{5,7},{6,4},{7,5},{8,10},{9,11},{10,... | collective-permute-start | bytes 1179656 | tf_op jit(solution)/shard_map/ppermute | solution.py:28
  89.5 12.8 %collective-permute-start.15 = (bf16[256,768]{1,0:T(8,128)(2,1)S(1)}, bf16[256,768]{1,0:T(8,128)(2,1)S(1)}, u32[]{:S(2)}, u32[]{:S(2)}) collective-permute-start(bf16[256,768]{1,0:T(8,128)(2,1)S(1)} %pad_maximum_fusion.2), channel_id=1, source_target_pairs={{0,2},{1,3},{2,0},{3,1},{4,6},{5,7},{6,4},{7,5},{8,10},{9,11},{10,... | collective-permute-start | bytes 1179656 | tf_op jit(solution)/shard_map/ppermute | solution.py:28
  102.3 34.9 %collective-permute-start.17 = (bf16[1024,768]{1,0:T(8,128)(2,1)S(1)}, bf16[1024,768]{1,0:T(8,128)(2,1)S(1)}, u32[]{:S(2)}, u32[]{:S(2)}) collective-permute-start(bf16[1024,768]{1,0:T(8,128)(2,1)S(1)} %constant_dynamic-update-slice_fusion.17.refs_2_), channel_id=1, source_target_pairs={{0,1},{1,0},{2,3},{3,2},{4,5},{5,4},{6,7},{7,6},{8,9},{9,8},{10,11... | collective-permute-start | bytes 4718600 | tf_op jit(solution)/shard_map/ppermute | solution.py:28
  102.4 11.5 %collective-permute-start.8 = (bf16[256,768]{1,0:T(8,128)(2,1)S(1)}, bf16[256,768]{1,0:T(8,128)(2,1)S(1)}, u32[]{:S(2)}, u32[]{:S(2)}) collective-permute-start(bf16[256,768]{1,0:T(8,128)(2,1)S(1)} %get-tuple-element.38), channel_id=1, source_target_pairs={{0,4},{4,0},{8,12},{12,8},{16,20},{20,16},{24,28},{28,24},{1,5},{5... | collective-permute-start | bytes 1179656 | tf_op jit(solution)/shard_map/ppermute | solution.py:28
  114.0 11.6 %collective-permute-start.9 = (bf16[128,768]{1,0:T(8,128)(2,1)S(1)}, bf16[128,768]{1,0:T(8,128)(2,1)S(1)}, u32[]{:S(2)}, u32[]{:S(2)}) collective-permute-start(bf16[128,768]{1,0:T(8,128)(2,1)S(1)} %pad_maximum_fusion.10), channel_id=1, source_target_pairs={{0,8},{4,12},{8,0},{12,4},{16,24},{20,28},{24,16},{28,20},{1,9},{5... | collective-permute-start | bytes 589832 | tf_op jit(solution)/shard_map/ppermute | solution.py:28
  118.8 16.7 %collective-permute-start.10 = (bf16[128,768]{1,0:T(8,128)(2,1)S(1)}, bf16[128,768]{1,0:T(8,128)(2,1)S(1)}, u32[]{:S(2)}, u32[]{:S(2)}) collective-permute-start(bf16[128,768]{1,0:T(8,128)(2,1)S(1)} %pad_maximum_fusion.11), channel_id=1, source_target_pairs={{0,16},{4,20},{8,24},{12,28},{16,0},{20,4},{24,8},{28,12},{1,17},{... | collective-permute-start | bytes 589832 | tf_op jit(solution)/shard_map/ppermute | solution.py:28
  118.9 16.6 %collective-permute-start.12 = (bf16[128,768]{1,0:T(8,128)(2,1)S(1)}, bf16[128,768]{1,0:T(8,128)(2,1)S(1)}, u32[]{:S(2)}, u32[]{:S(2)}) collective-permute-start(bf16[128,768]{1,0:T(8,128)(2,1)S(1)} %pad_maximum_fusion.12), channel_id=1, source_target_pairs={{0,24},{4,28},{8,16},{12,20},{16,8},{20,12},{24,0},{28,4},{1,25},{... | collective-permute-start | bytes 589832 | tf_op jit(solution)/shard_map/ppermute | solution.py:28
  135.6 10.5 %collective-permute-start.16 = (bf16[256,768]{1,0:T(8,128)(2,1)S(1)}, bf16[256,768]{1,0:T(8,128)(2,1)S(1)}, u32[]{:S(2)}, u32[]{:S(2)}) collective-permute-start(bf16[256,768]{1,0:T(8,128)(2,1)S(1)} %pad_maximum_fusion), channel_id=1, source_target_pairs={{0,2},{1,3},{2,0},{3,1},{4,6},{5,7},{6,4},{7,5},{8,10},{9,11},{10,... | collective-permute-start | bytes 1179656 | tf_op jit(solution)/shard_map/ppermute | solution.py:28
  142.6 10.3 %collective-permute-start.18 = (bf16[256,768]{1,0:T(8,128)(2,1)S(1)}, bf16[256,768]{1,0:T(8,128)(2,1)S(1)}, u32[]{:S(2)}, u32[]{:S(2)}) collective-permute-start(bf16[256,768]{1,0:T(8,128)(2,1)S(1)} %pad_maximum_fusion.3), channel_id=1, source_target_pairs={{0,2},{1,3},{2,0},{3,1},{4,6},{5,7},{6,4},{7,5},{8,10},{9,11},{10,... | collective-permute-start | bytes 1179656 | tf_op jit(solution)/shard_map/ppermute | solution.py:28
  152.9 3.5 %collective-permute-start.19 = (bf16[1024,768]{1,0:T(8,128)(2,1)S(1)}, bf16[1024,768]{1,0:T(8,128)(2,1)S(1)}, u32[]{:S(2)}, u32[]{:S(2)}) collective-permute-start(bf16[1024,768]{1,0:T(8,128)(2,1)S(1)} %constant_dynamic-update-slice_fusion.24.refs_3_), channel_id=1, source_target_pairs={{0,1},{1,0},{2,3},{3,2},{4,5},{5,4},{6,7},{7,6},{8,9},{9,8},{10,11... | collective-permute-start | bytes 4718600 | tf_op jit(solution)/shard_map/ppermute | solution.py:28

commit v6 on v5

--- a/solution.py
+++ b/solution.py
@@ -17,7 +17,8 @@
 
 
 def chunk_sizes(capacity):
-    return (capacity // 3,) * 3
+    count = 4 if capacity % 64 == 0 else 3
+    return (capacity // count,) * count
 
 
 def after(value, *earlier):
@@ -107,13 +108,17 @@
         col_ref[0:1, pl.ds(first, tile)] = col_best
 
 
-def gram_kernel(step, tile, *refs):
-    owns, pieces, refs = refs[: step + 1], refs[step + 1 : step + 3], refs[step + 3 :]
-    states, refs = refs[:step], refs[step:]
-    rows, col, stack = refs[: step + 1], refs[step + 1], refs[step + 2]
+def gram_kernel(first, step, tile, *refs):
+    news = step + 1 - first
+    owns, refs = refs[: step + 1], refs[step + 1 :]
+    pieces, refs = refs[: 2 * news], refs[2 * news :]
+    states, refs = refs[:first], refs[first:]
+    rows, cols, stack = refs[: step + 1], refs[step + 1 : -1], refs[-1]
     for state, row in zip(states, rows):
         row[...] = state[...]
-    gram_body(owns, pieces, rows, col, stack, tile)
+    for k in range(news):
+        now = first + k + 1
+        gram_body(owns[:now], pieces[2 * k : 2 * k + 2], rows[:now], cols[k], stack, tile)
 
 
 def gram_last_kernel(step, relatives, chunks, groups, tile, me_ref, *refs):
@@ -147,11 +152,13 @@
             out_ref[pl.ds(target, 1), :] = table[row : row + 1, :]
 
 
-def gram_step(step, me, owns, pieces, states, cols, relatives, chunks, groups):
+def gram_step(first, me, owns, pieces, states, cols, relatives, chunks, groups):
+    step = len(owns) - 1
     members = len(relatives)
-    features = owns[step].shape[1]
-    total = members * owns[step].shape[0]
+    features = owns[0].shape[1]
     counts = [own.shape[0] for own in owns]
+    totals = [members * count for count in counts[first:]]
+    total = max(totals)
     tile = 256
     row_shapes = [(c, lanes) for c in counts]
     stack = pltpu.VMEM((total, features), jnp.bfloat16)
@@ -165,16 +172,16 @@
     )
     if step < len(chunks) - 1:
         results = pl.pallas_call(
-            functools.partial(gram_kernel, step, tile),
-            in_specs=[vmem] * (step + 3 + step),
-            out_specs=[vmem] * (step + 2),
+            functools.partial(gram_kernel, first, step, tile),
+            in_specs=[vmem] * (step + 1 + len(pieces) + first),
+            out_specs=[vmem] * (step + 1 + len(totals)),
             out_shape=[jax.ShapeDtypeStruct(s, jnp.float32) for s in row_shapes]
-            + [jax.ShapeDtypeStruct((1, total), jnp.float32)],
+            + [jax.ShapeDtypeStruct((1, count), jnp.float32) for count in totals],
             scratch_shapes=[stack],
             name="gram_step",
             **params,
         )(*owns, *pieces, *states)
-        return list(results[:-1]), cols + [results[-1]]
+        return list(results[: step + 1]), cols + list(results[step + 1 :])
     return pl.pallas_call(
         functools.partial(gram_last_kernel, step, relatives, chunks, groups, tile),
         in_specs=[smem] + [vmem] * (step + 3 + 2 * step),
@@ -238,7 +245,7 @@
     count, high = len(chunks), groups // 2
     last = count - 1
 
-    sent, owns, done, states, cols, pairs = {}, {}, {}, [], [], {}
+    sent, owns, done, pairs = {}, {}, {}, {}
 
     def rows(value, index, size):
         return value[index * size : (index + 1) * size]
@@ -250,69 +257,63 @@
         )
 
     def send(key, value, axis, size, bit, *earlier):
-        held = [sent[name] for name in earlier if name in sent]
-        held += [done[name[1]] for name in earlier if name[0] == "gram" and name[1] in done]
+        held = [done[name] if name in done else sent[name] for name in earlier]
         sent[key] = swap(after(value, *held) if held else value, axis, size, bit)
 
-    def send_y(step):
-        if step < count:
-            send(("y", step), placed[2 * step + 1], "grp", groups, 1, ("y", step - 1))
-
     def send_z(step, z):
-        early = [("z", step - 1, z)]
-        if z == high - 1:
+        early = [("z", step - 1, z)] if step >= 1 else []
+        if step >= 2 and z != high // 2:
             early += [("x", step - 2, 0)]
         send(("z", step, z), block(step, z), "grp", groups, 2 * z, *early)
 
-    def send_x(step):
+    def collect(step):
         parts = [block(step, 0)] + [sent["z", step, z] for z in range(1, high)]
         owns[step] = jnp.concatenate(parts, axis=0)
-        cuts = 1 if step == 0 else 2
-        half = owns[step].shape[0] // cuts
-        for cut in range(cuts):
-            early = [("x", step - 1, 0), ("x", step - 1, 1)] if cut == 0 else [("gram", step - 1)]
-            value = rows(owns[step], cut, half)
-            send(("x", step, cut), value, "blk", members, 2, *early)
-            if cut == 0 and step >= 1:
-                gram(step - 1)
-
-    def gram(step):
-        nonlocal states, cols
-        across = [sent[name] for name in sent if name[:2] == ("x", step)]
+
+    def send_x(step):
+        collect(step)
+        early = [("x", step - 1, 0)] if step >= 1 else []
+        early += [("y", step + 2)] if step + 2 < count else []
+        send(("x", step, 0), owns[step], "blk", members, 2, *early)
+
+    def send_c(step):
+        across = [sent[name] for name in list(sent) if name[:2] == ("x", step)]
         pairs[step] = jnp.concatenate([owns[step]] + across, axis=0)
         send(("c", step), pairs[step], "blk", members, 1)
-        result = gram_step(
-            step,
-            me,
-            [owns[j] for j in range(step + 1)],
-            (pairs[step], sent["c", step]),
-            states,
-            cols,
-            (0, 2, 1, 3),
-            chunks,
-            groups,
+
+    def gram(first, step, states, cols):
+        pieces = []
+        for k in range(first, step + 1):
+            pieces += [pairs[k], sent["c", k]]
+        mine = [owns[k] for k in range(step + 1)]
+        return gram_step(
+            first, me, mine, pieces, states, cols, (0, 2, 1, 3), chunks, groups
         )
-        if step == last:
-            return result
-        states, cols = result
-        done[step] = cols[-1]
 
     far = [high // 2] + [z for z in reversed(range(1, high)) if z != high // 2]
-    send_y(0)
-    for z in far[:2]:
-        send_z(0, z)
-    send_y(1)
-    for z in far[2:]:
+    for step in range(count):
+        send(("y", step), placed[2 * step + 1], "grp", groups, 1)
+    for z in far:
         send_z(0, z)
     for step in range(1, count):
-        for z in far[:2]:
+        for z in far:
             send_z(step, z)
         send_x(step - 1)
-        for z in far[2:]:
-            send_z(step, z)
-        send_y(step + 1)
-    send_x(last)
-    result = gram(last)
+        send_c(step - 1)
+    collect(last)
+    total = owns[last].shape[0]
+    third = total // 48 * 16
+    states, cols = gram(0, last - 2, [], [])
+    done["gram", 0] = cols[-1]
+    states, cols = gram(last - 1, last - 1, states, cols)
+    done["gram", 1] = cols[-1]
+    early = [("x", last - 1, 0)] + [("c", k) for k in range(last - 1)]
+    send(("x", last, 0), owns[last][:third], "blk", members, 2, *early)
+    early = [("gram", 0), ("c", last - 1)]
+    send(("x", last, 1), owns[last][third : 2 * third], "blk", members, 2, *early)
+    send(("x", last, 2), owns[last][2 * third :], "blk", members, 2, ("gram", 1))
+    send_c(last)
+    result = gram(last, last, states, cols)
     homeward = lax.all_to_all(result, ("grp", "blk"), 0, 0, tiled=True)
     return tail(homeward, slots, capacity, members).reshape(row_count)
 

time: 182 us -> 137 us (0.75)
  waiting for transfers between devices: 110 us -> 60.8 us
  starting transfers between devices: 31.4 us -> 37.8 us
  blocking collectives: 14.1 us -> 11.8 us
    ppermute x20 -> x26, waiting for transfers between devices: 110 us -> 60.8 us  [swap(): return lax.ppermute(value, axis, [(i, i ^ bit) for i in range(size)])]
    ppermute x20 -> x26, starting transfers between devices: 31.4 us -> 37.8 us  [swap(): return lax.ppermute(value, axis, [(i, i ^ bit) for i in range(size)])]
    all_to_all x1, blocking collectives: 14.1 us -> 11.8 us  [on_device(): homeward = lax.all_to_all(result, ('grp', 'blk'), 0, 0, tiled=True)]
  transfers between devices with their start and end apart: 20 -> 26, of which waited for: 15 -> 13; matrix products, arithmetic and copies ran while one was open for 0% -> 1% of each run, Pallas kernels for 5% -> 7%
where the time goes in v6:
time: 137 us
  waiting for transfers between devices  60.8 us (44%)
  starting transfers between devices  37.8 us (28%)
  Pallas kernels  22.6 us (16%)
  blocking collectives  11.8 us (9%)
  local copies, waits for them, and re-layouts  3.22 us (2%)
    ppermute x26, waiting for transfers between devices, swap(): return lax.ppermute(value, axis, [(i, i ^ bit) for i in range(size)])  60.8 us
    ppermute x26, starting transfers between devices, swap(): return lax.ppermute(value, axis, [(i, i ^ bit) for i in range(size)])  37.8 us
    all_to_all x1, blocking collectives, on_device(): homeward = lax.all_to_all(result, ('grp', 'blk'), 0, 0, tiled=True)  11.8 us
    pallas_call x2, Pallas kernels, gram_step(): pl.pallas_call(functools.partial(gram_kernel, first, step, tile), in_spec...  10.1 us
    pallas_call x1, Pallas kernels, gram_step(): pl.pallas_call(functools.partial(gram_last_kernel, step, relatives, chunk...  7.05 us
    pallas_call x1, Pallas kernels, head(): pl.pallas_call(functools.partial(head_kernel, capacity, chunks, groups),...  3.08 us
    unnamed x24, local copies, waits for them, and re-layouts  3.02 us
  transfers between devices with their start and end apart: 26, of which 13 were waited for; matrix products, arithmetic and copies ran while one was open for 1% of the time, Pallas kernels for 7%

profile of v6, /device:TPU:0, one launch (start us, length us, event | category | flops | bytes accessed | tf_op | source)
XLA Modules:
  0.0 136.7 jit_solution(11411326532531129304)
XLA Ops:
  2.0 3.1 %place_rows.1 = (bf16[192,768]{1,0:T(8,128)(2,1)S(1)}, bf16[192,768]{1,0:T(8,128)(2,1)S(1)}, bf16[192,768]{1,0:T(8,128)(2,1)S(1)}, bf16[192,768]{1,0:T(8,128)(2,...) custom-call(s32[2]{0:T(128)S(1)} %pad_add_fusion.me_ref, ...), custom_call_target="tpu_custom_call" | custom-call | tf_op jit(solution)/shard_map/place_rows/pallas_call | solution.py:57
  5.1 3.0 %collective-permute-start = (bf16[192,768]{1,0:T(8,128)(2,1)S(1)}, bf16[192,768]{1,0:T(8,128)(2,1)S(1)}, u32[]{:S(2)}, u32[]{:S(2)}) collective-permute-start(bf16[192,768]{1,0:T(8,128)(2,1)S(1)} %get-tuple-element.37), channel_id=1, source_target_pairs={{0,4},{4,0},{8,12},{12,8},{16,20},{20,16},{24,28},{28,24},{1,5},{5... | collective-permute-start | bytes 884744 | tf_op jit(solution)/shard_map/ppermute | solution.py:29
  8.2 1.9 %collective-permute-start.8 = (bf16[192,768]{1,0:T(8,128)(2,1)S(1)}, bf16[192,768]{1,0:T(8,128)(2,1)S(1)}, u32[]{:S(2)}, u32[]{:S(2)}) collective-permute-start(bf16[192,768]{1,0:T(8,128)(2,1)S(1)} %get-tuple-element.44), channel_id=1, source_target_pairs={{0,4},{4,0},{8,12},{12,8},{16,20},{20,16},{24,28},{28,24},{1,5},{5... | collective-permute-start | bytes 884744 | tf_op jit(solution)/shard_map/ppermute | solution.py:29
  10.4 5.6 %collective-permute-done = bf16[192,768]{1,0:T(8,128)(2,1)S(1)} collective-permute-done((bf16[192,768]{1,0:T(8,128)(2,1)S(1)}, bf16[192,768]{1,0:T(8,128)(2,1)S(1)}, u32[]{:S(2)}, u32[]{:S(2)}) %collective-permute-start) | collective-permute-done | bytes 294944 | tf_op jit(solution)/shard_map/ppermute | solution.py:29
  16.0 2.2 %collective-permute-start.1 = (bf16[96,768]{1,0:T(8,128)(2,1)S(1)}, bf16[96,768]{1,0:T(8,128)(2,1)S(1)}, u32[]{:S(2)}, u32[]{:S(2)}) collective-permute-start(bf16[96,768]{1,0:T(8,128)(2,1)S(1)} %pad_maximum_fusion.4), channel_id=1, source_target_pairs={{0,8},{4,12},{8,0},{12,4},{16,24},{20,28},{24,16},{28,20},{1,9},{5... | collective-permute-start | bytes 442376 | tf_op jit(solution)/shard_map/ppermute | solution.py:29
  18.2 2.7 %collective-permute-start.2 = (bf16[96,768]{1,0:T(8,128)(2,1)S(1)}, bf16[96,768]{1,0:T(8,128)(2,1)S(1)}, u32[]{:S(2)}, u32[]{:S(2)}) collective-permute-start(bf16[96,768]{1,0:T(8,128)(2,1)S(1)} %pad_maximum_fusion.5), channel_id=1, source_target_pairs={{0,16},{4,20},{8,24},{12,28},{16,0},{20,4},{24,8},{28,12},{1,17},{... | collective-permute-start | bytes 442376 | tf_op jit(solution)/shard_map/ppermute | solution.py:29
  22.3 4.1 %collective-permute-start.3 = (bf16[96,768]{1,0:T(8,128)(2,1)S(1)}, bf16[96,768]{1,0:T(8,128)(2,1)S(1)}, u32[]{:S(2)}, u32[]{:S(2)}) collective-permute-start(bf16[96,768]{1,0:T(8,128)(2,1)S(1)} %pad_maximum_fusion.6), channel_id=1, source_target_pairs={{0,24},{4,28},{8,16},{12,20},{16,8},{20,12},{24,0},{28,4},{1,25},{... | collective-permute-start | bytes 442376 | tf_op jit(solution)/shard_map/ppermute | solution.py:29
  26.5 2.1 %collective-permute-done.8 = bf16[192,768]{1,0:T(8,128)(2,1)S(1)} collective-permute-done((bf16[192,768]{1,0:T(8,128)(2,1)S(1)}, bf16[192,768]{1,0:T(8,128)(2,1)S(1)}, u32[]{:S(2)}, u32[]{:S(2)}) %collective-permute-start.8) | collective-permute-done | bytes 294944 | tf_op jit(solution)/shard_map/ppermute | solution.py:29
  28.7 2.2 %collective-permute-start.5 = (bf16[96,768]{1,0:T(8,128)(2,1)S(1)}, bf16[96,768]{1,0:T(8,128)(2,1)S(1)}, u32[]{:S(2)}, u32[]{:S(2)}) collective-permute-start(bf16[96,768]{1,0:T(8,128)(2,1)S(1)} %pad_maximum_fusion.7), channel_id=1, source_target_pairs={{0,8},{4,12},{8,0},{12,4},{16,24},{20,28},{24,16},{28,20},{1,9},{5... | collective-permute-start | bytes 442376 | tf_op jit(solution)/shard_map/ppermute | solution.py:29
  32.6 3.0 %collective-permute-start.6 = (bf16[96,768]{1,0:T(8,128)(2,1)S(1)}, bf16[96,768]{1,0:T(8,128)(2,1)S(1)}, u32[]{:S(2)}, u32[]{:S(2)}) collective-permute-start(bf16[96,768]{1,0:T(8,128)(2,1)S(1)} %pad_maximum_fusion.8), channel_id=1, source_target_pairs={{0,16},{4,20},{8,24},{12,28},{16,0},{20,4},{24,8},{28,12},{1,17},{... | collective-permute-start | bytes 442376 | tf_op jit(solution)/shard_map/ppermute | solution.py:29
  36.9 9.6 %collective-permute-done.6 = bf16[96,768]{1,0:T(8,128)(2,1)S(1)} collective-permute-done((bf16[96,768]{1,0:T(8,128)(2,1)S(1)}, bf16[96,768]{1,0:T(8,128)(2,1)S(1)}, u32[]{:S(2)}, u32[]{:S(2)}) %collective-permute-start.6) | collective-permute-done | bytes 147488 | tf_op jit(solution)/shard_map/ppermute | solution.py:29
  46.6 2.4 %collective-permute-start.10 = (bf16[96,768]{1,0:T(8,128)(2,1)S(1)}, bf16[96,768]{1,0:T(8,128)(2,1)S(1)}, u32[]{:S(2)}, u32[]{:S(2)}) collective-permute-start(bf16[96,768]{1,0:T(8,128)(2,1)S(1)} %pad_maximum_fusion.10), channel_id=1, source_target_pairs={{0,8},{4,12},{8,0},{12,4},{16,24},{20,28},{24,16},{28,20},{1,9},{5... | collective-permute-start | bytes 442376 | tf_op jit(solution)/shard_map/ppermute | solution.py:29
  53.4 8.4 %collective-permute-done.11 = bf16[96,768]{1,0:T(8,128)(2,1)S(1)} collective-permute-done((bf16[96,768]{1,0:T(8,128)(2,1)S(1)}, bf16[96,768]{1,0:T(8,128)(2,1)S(1)}, u32[]{:S(2)}, u32[]{:S(2)}) %collective-permute-start.11) | collective-permute-done | bytes 147488 | tf_op jit(solution)/shard_map/ppermute | solution.py:29
  64.2 11.4 %collective-permute-done.18 = bf16[384,768]{1,0:T(8,128)(2,1)S(1)} collective-permute-done((bf16[384,768]{1,0:T(8,128)(2,1)S(1)}, bf16[384,768]{1,0:T(8,128)(2,1)S(1)}, u32[]{:S(2)}, u32[]{:S(2)}) %collective-permute-start.18) | collective-permute-done | bytes 589856 | tf_op jit(solution)/shard_map/ppermute | solution.py:29
  75.9 3.2 %collective-permute-start.15 = (bf16[96,768]{1,0:T(8,128)(2,1)S(1)}, bf16[96,768]{1,0:T(8,128)(2,1)S(1)}, u32[]{:S(2)}, u32[]{:S(2)}) collective-permute-start(bf16[96,768]{1,0:T(8,128)(2,1)S(1)} %pad_maximum_fusion.13), channel_id=1, source_target_pairs={{0,8},{4,12},{8,0},{12,4},{16,24},{20,28},{24,16},{28,20},{1,9},{5... | collective-permute-start | bytes 442376 | tf_op jit(solution)/shard_map/ppermute | solution.py:29
  79.9 6.3 %collective-permute-done.15 = bf16[96,768]{1,0:T(8,128)(2,1)S(1)} collective-permute-done((bf16[96,768]{1,0:T(8,128)(2,1)S(1)}, bf16[96,768]{1,0:T(8,128)(2,1)S(1)}, u32[]{:S(2)}, u32[]{:S(2)}) %collective-permute-start.15) | collective-permute-done | bytes 147488 | tf_op jit(solution)/shard_map/ppermute | solution.py:29
  89.6 4.2 %collective-permute-done.17 = bf16[96,768]{1,0:T(8,128)(2,1)S(1)} collective-permute-done((bf16[96,768]{1,0:T(8,128)(2,1)S(1)}, bf16[96,768]{1,0:T(8,128)(2,1)S(1)}, u32[]{:S(2)}, u32[]{:S(2)}) %collective-permute-start.17) | collective-permute-done | bytes 147488 | tf_op jit(solution)/shard_map/ppermute | solution.py:29
  94.7 5.8 %gram_step.2 = (f32[384,128]{1,0:T(8,128)S(1)}, f32[384,128]{1,0:T(8,128)S(1)}, f32[1,1536]{1,0:T(1,128)S(1)}, f32[1,1536]{1,0:T(1,128)S(1)}) custom-call(bf16[384,768]{1,0:T(8,128)(2,1)S(1)} %get-tuple-element.45.refs_0_, bf16[384,768]{1,0:T(8,128)(2,1)S(1)} %get-tuple-element.51.refs_1_, bf16[768,768]{1,0:T(8,128)(2,1)S(1)} %constant_dynamic-update-slice_fusion.20.refs_2_, ...), custom_call_target="tpu_custom_call" | custom-call | flops 1811939328 | bytes 3538944 | tf_op jit(solution)/shard_map/gram_step/pallas_call | solution.py:174
  101.8 4.4 %gram_step.3 = (f32[384,128]{1,0:T(8,128)S(1)}, f32[384,128]{1,0:T(8,128)S(1)}, f32[384,128]{1,0:T(8,128)S(1)}, f32[1,1536]{1,0:T(1,128)S(1)}) custom-call(bf16[384,768]{1,0:T(8,128)(2,1)S(1)} %get-tuple-element.45.refs_0_, bf16[384,768]{1,0:T(8,128)(2,1)S(1)} %get-tuple-element.51.refs_1_, bf16[384,768]{1,0:T(8,128)(2,1)S(1)} %get-tuple-element.55.refs_2_, ...), custom_call_target="tpu_custom_call" | custom-call | flops 2717908992 | bytes 4128768 | tf_op jit(solution)/shard_map/gram_step/pallas_call | solution.py:174
  107.0 4.9 %collective-permute-done.24 = bf16[128,768]{1,0:T(8,128)(2,1)S(1)} collective-permute-done((bf16[128,768]{1,0:T(8,128)(2,1)S(1)}, bf16[128,768]{1,0:T(8,128)(2,1)S(1)}, u32[]{:S(2)}, u32[]{:S(2)}) %collective-permute-start.24) | collective-permute-done | bytes 196640 | tf_op jit(solution)/shard_map/ppermute | solution.py:29
  112.1 2.8 %collective-permute-done.25.refs_5_ = bf16[768,768]{1,0:T(8,128)(2,1)S(1)} collective-permute-done((bf16[768,768]{1,0:T(8,128)(2,1)S(1)}, bf16[768,768]{1,0:T(8,128)(2,1)S(1)}, u32[]{:S(2)}, u32[]{:S(2)}) %collective-permute-start.25) | collective-permute-done | bytes 1179680 | tf_op jit(solution)/shard_map/ppermute | solution.py:29
  114.9 7.0 %gram_last.1 = f32[32,192]{1,0:T(8,128)S(1)} custom-call(s32[2]{0:T(128)S(1)} %pad_add_fusion.me_ref, bf16[384,768]{1,0:T(8,128)(2,1)S(1)} %get-tuple-element.45.refs_0_, bf16[384,768]{1,0:T(8,128)(2,1)S(1)} %get-tuple-element.51.refs_1_, bf16[384,768]{1,0:T(8,128)(2,1)S(1)} %get-tuple-element.55.refs_2_, bf16[384,768]{1,0:T(8,128)(2,1)S(1)} %get-tuple-element.131.refs_3_, ...), custom_call_target="tpu_custom_call" | custom-call | flops 3623878656 | bytes 4718592 | tf_op jit(solution)/shard_map/gram_last/pallas_call | solution.py:185
  122.0 11.8 %all_to_all.11 = f32[32,1,192]{2,1,0:T(1,128)S(1)} all-to-all(f32[32,1,192]{2,1,0:T(1,128)S(1)} %copy.3), channel_id=1, replica_groups=mesh['grp'=8,'blk'=4] {'grp','blk'}, dimensions={0} | all-to-all | bytes 49152 | tf_op jit(solution)/shard_map/all_to_all | solution.py:317
  134.4 2.3 %pick_rows.1 = f32[6,128]{1,0:T(8,128)} custom-call(s32[6,128]{1,0:T(8,128)} %bitcast.9, f32[32,192]{1,0:T(8,128)} %bitcast.11), custom_call_target="tpu_custom_call" | custom-call | tf_op jit(solution)/shard_map/pick_rows/pallas_call | solution.py:225
  (78 shorter events, 21.7 us)
Async XLA Ops:
  5.1 10.9 %collective-permute-start = (bf16[192,768]{1,0:T(8,128)(2,1)S(1)}, bf16[192,768]{1,0:T(8,128)(2,1)S(1)}, u32[]{:S(2)}, u32[]{:S(2)}) collective-permute-start(bf16[192,768]{1,0:T(8,128)(2,1)S(1)} %get-tuple-element.37), channel_id=1, source_target_pairs={{0,4},{4,0},{8,12},{12,8},{16,20},{20,16},{24,28},{28,24},{1,5},{5... | collective-permute-start | bytes 884744 | tf_op jit(solution)/shard_map/ppermute | solution.py:29
  8.2 14.2 %collective-permute-start.4 = (bf16[192,768]{1,0:T(8,128)(2,1)S(1)}, bf16[192,768]{1,0:T(8,128)(2,1)S(1)}, u32[]{:S(2)}, u32[]{:S(2)}) collective-permute-start(bf16[192,768]{1,0:T(8,128)(2,1)S(1)} %get-tuple-element.39), channel_id=1, source_target_pairs={{0,4},{4,0},{8,12},{12,8},{16,20},{20,16},{24,28},{28,24},{1,5},{5... | collective-permute-start | bytes 884744 | tf_op jit(solution)/shard_map/ppermute | solution.py:29
  8.2 20.4 %collective-permute-start.8 = (bf16[192,768]{1,0:T(8,128)(2,1)S(1)}, bf16[192,768]{1,0:T(8,128)(2,1)S(1)}, u32[]{:S(2)}, u32[]{:S(2)}) collective-permute-start(bf16[192,768]{1,0:T(8,128)(2,1)S(1)} %get-tuple-element.44), channel_id=1, source_target_pairs={{0,4},{4,0},{8,12},{12,8},{16,20},{20,16},{24,28},{28,24},{1,5},{5... | collective-permute-start | bytes 884744 | tf_op jit(solution)/shard_map/ppermute | solution.py:29
  10.2 38.9 %collective-permute-start.13 = (bf16[192,768]{1,0:T(8,128)(2,1)S(1)}, bf16[192,768]{1,0:T(8,128)(2,1)S(1)}, u32[]{:S(2)}, u32[]{:S(2)}) collective-permute-start(bf16[192,768]{1,0:T(8,128)(2,1)S(1)} %get-tuple-element.50), channel_id=1, source_target_pairs={{0,4},{4,0},{8,12},{12,8},{16,20},{20,16},{24,28},{28,24},{1,5},{5... | collective-permute-start | bytes 884744 | tf_op jit(solution)/shard_map/ppermute | solution.py:29
  16.0 12.7 %collective-permute-start.1 = (bf16[96,768]{1,0:T(8,128)(2,1)S(1)}, bf16[96,768]{1,0:T(8,128)(2,1)S(1)}, u32[]{:S(2)}, u32[]{:S(2)}) collective-permute-start(bf16[96,768]{1,0:T(8,128)(2,1)S(1)} %pad_maximum_fusion.4), channel_id=1, source_target_pairs={{0,8},{4,12},{8,0},{12,4},{16,24},{20,28},{24,16},{28,20},{1,9},{5... | collective-permute-start | bytes 442376 | tf_op jit(solution)/shard_map/ppermute | solution.py:29
  18.2 12.7 %collective-permute-start.2 = (bf16[96,768]{1,0:T(8,128)(2,1)S(1)}, bf16[96,768]{1,0:T(8,128)(2,1)S(1)}, u32[]{:S(2)}, u32[]{:S(2)}) collective-permute-start(bf16[96,768]{1,0:T(8,128)(2,1)S(1)} %pad_maximum_fusion.5), channel_id=1, source_target_pairs={{0,16},{4,20},{8,24},{12,28},{16,0},{20,4},{24,8},{28,12},{1,17},{... | collective-permute-start | bytes 442376 | tf_op jit(solution)/shard_map/ppermute | solution.py:29
  22.3 8.7 %collective-permute-start.3 = (bf16[96,768]{1,0:T(8,128)(2,1)S(1)}, bf16[96,768]{1,0:T(8,128)(2,1)S(1)}, u32[]{:S(2)}, u32[]{:S(2)}) collective-permute-start(bf16[96,768]{1,0:T(8,128)(2,1)S(1)} %pad_maximum_fusion.6), channel_id=1, source_target_pairs={{0,24},{4,28},{8,16},{12,20},{16,8},{20,12},{24,0},{28,4},{1,25},{... | collective-permute-start | bytes 442376 | tf_op jit(solution)/shard_map/ppermute | solution.py:29
  28.7 8.2 %collective-permute-start.5 = (bf16[96,768]{1,0:T(8,128)(2,1)S(1)}, bf16[96,768]{1,0:T(8,128)(2,1)S(1)}, u32[]{:S(2)}, u32[]{:S(2)}) collective-permute-start(bf16[96,768]{1,0:T(8,128)(2,1)S(1)} %pad_maximum_fusion.7), channel_id=1, source_target_pairs={{0,8},{4,12},{8,0},{12,4},{16,24},{20,28},{24,16},{28,20},{1,9},{5... | collective-permute-start | bytes 442376 | tf_op jit(solution)/shard_map/ppermute | solution.py:29
  31.0 15.6 %collective-permute-start.9 = (bf16[384,768]{1,0:T(8,128)(2,1)S(1)}, bf16[384,768]{1,0:T(8,128)(2,1)S(1)}, u32[]{:S(2)}, u32[]{:S(2)}) collective-permute-start(bf16[384,768]{1,0:T(8,128)(2,1)S(1)} %get-tuple-element.45.refs_0_), channel_id=1, source_target_pairs={{0,2},{1,3},{2,0},{3,1},{4,6},{5,7},{6,4},{7,5},{8,10},{9,11},{10,... | collective-permute-start | bytes 1769480 | tf_op jit(solution)/shard_map/ppermute | solution.py:29
  32.6 14.0 %collective-permute-start.6 = (bf16[96,768]{1,0:T(8,128)(2,1)S(1)}, bf16[96,768]{1,0:T(8,128)(2,1)S(1)}, u32[]{:S(2)}, u32[]{:S(2)}) collective-permute-start(bf16[96,768]{1,0:T(8,128)(2,1)S(1)} %pad_maximum_fusion.8), channel_id=1, source_target_pairs={{0,16},{4,20},{8,24},{12,28},{16,0},{20,4},{24,8},{28,12},{1,17},{... | collective-permute-start | bytes 442376 | tf_op jit(solution)/shard_map/ppermute | solution.py:29
  35.5 11.0 %collective-permute-start.7 = (bf16[96,768]{1,0:T(8,128)(2,1)S(1)}, bf16[96,768]{1,0:T(8,128)(2,1)S(1)}, u32[]{:S(2)}, u32[]{:S(2)}) collective-permute-start(bf16[96,768]{1,0:T(8,128)(2,1)S(1)} %pad_maximum_fusion.9), channel_id=1, source_target_pairs={{0,24},{4,28},{8,16},{12,20},{16,8},{20,12},{24,0},{28,4},{1,25},{... | collective-permute-start | bytes 442376 | tf_op jit(solution)/shard_map/ppermute | solution.py:29
  46.6 6.8 %collective-permute-start.10 = (bf16[96,768]{1,0:T(8,128)(2,1)S(1)}, bf16[96,768]{1,0:T(8,128)(2,1)S(1)}, u32[]{:S(2)}, u32[]{:S(2)}) collective-permute-start(bf16[96,768]{1,0:T(8,128)(2,1)S(1)} %pad_maximum_fusion.10), channel_id=1, source_target_pairs={{0,8},{4,12},{8,0},{12,4},{16,24},{20,28},{24,16},{28,20},{1,9},{5... | collective-permute-start | bytes 442376 | tf_op jit(solution)/shard_map/ppermute | solution.py:29
  49.1 13.8 %collective-permute-start.14 = (bf16[384,768]{1,0:T(8,128)(2,1)S(1)}, bf16[384,768]{1,0:T(8,128)(2,1)S(1)}, u32[]{:S(2)}, u32[]{:S(2)}) collective-permute-start(bf16[384,768]{1,0:T(8,128)(2,1)S(1)} %get-tuple-element.51.refs_1_), channel_id=1, source_target_pairs={{0,2},{1,3},{2,0},{3,1},{4,6},{5,7},{6,4},{7,5},{8,10},{9,11},{10,... | collective-permute-start | bytes 1769480 | tf_op jit(solution)/shard_map/ppermute | solution.py:29
  49.6 12.2 %collective-permute-start.11 = (bf16[96,768]{1,0:T(8,128)(2,1)S(1)}, bf16[96,768]{1,0:T(8,128)(2,1)S(1)}, u32[]{:S(2)}, u32[]{:S(2)}) collective-permute-start(bf16[96,768]{1,0:T(8,128)(2,1)S(1)} %pad_maximum_fusion.11), channel_id=1, source_target_pairs={{0,16},{4,20},{8,24},{12,28},{16,0},{20,4},{24,8},{28,12},{1,17},{... | collective-permute-start | bytes 442376 | tf_op jit(solution)/shard_map/ppermute | solution.py:29
  50.4 11.4 %collective-permute-start.12 = (bf16[96,768]{1,0:T(8,128)(2,1)S(1)}, bf16[96,768]{1,0:T(8,128)(2,1)S(1)}, u32[]{:S(2)}, u32[]{:S(2)}) collective-permute-start(bf16[96,768]{1,0:T(8,128)(2,1)S(1)} %pad_maximum_fusion.12), channel_id=1, source_target_pairs={{0,24},{4,28},{8,16},{12,20},{16,8},{20,12},{24,0},{28,4},{1,25},{... | collective-permute-start | bytes 442376 | tf_op jit(solution)/shard_map/ppermute | solution.py:29
  62.8 12.8 %collective-permute-start.18 = (bf16[384,768]{1,0:T(8,128)(2,1)S(1)}, bf16[384,768]{1,0:T(8,128)(2,1)S(1)}, u32[]{:S(2)}, u32[]{:S(2)}) collective-permute-start(bf16[384,768]{1,0:T(8,128)(2,1)S(1)} %get-tuple-element.55.refs_2_), channel_id=1, source_target_pairs={{0,2},{1,3},{2,0},{3,1},{4,6},{5,7},{6,4},{7,5},{8,10},{9,11},{10,... | collective-permute-start | bytes 1769480 | tf_op jit(solution)/shard_map/ppermute | solution.py:29
  63.6 30.3 %collective-permute-start.19 = (bf16[768,768]{1,0:T(8,128)(2,1)S(1)}, bf16[768,768]{1,0:T(8,128)(2,1)S(1)}, u32[]{:S(2)}, u32[]{:S(2)}) collective-permute-start(bf16[768,768]{1,0:T(8,128)(2,1)S(1)} %constant_dynamic-update-slice_fusion.20.refs_2_), channel_id=1, source_target_pairs={{0,1},{1,0},{2,3},{3,2},{4,5},{5,4},{6,7},{7,6},{8,9},{9,8},{10,11... | collective-permute-start | bytes 3538952 | tf_op jit(solution)/shard_map/ppermute | solution.py:29
  63.7 30.2 %collective-permute-start.20 = (bf16[768,768]{1,0:T(8,128)(2,1)S(1)}, bf16[768,768]{1,0:T(8,128)(2,1)S(1)}, u32[]{:S(2)}, u32[]{:S(2)}) collective-permute-start(bf16[768,768]{1,0:T(8,128)(2,1)S(1)} %constant_dynamic-update-slice_fusion.26.refs_4_), channel_id=1, source_target_pairs={{0,1},{1,0},{2,3},{3,2},{4,5},{5,4},{6,7},{7,6},{8,9},{9,8},{10,11... | collective-permute-start | bytes 3538952 | tf_op jit(solution)/shard_map/ppermute | solution.py:29
  75.7 24.7 %collective-permute-start.22 = (bf16[768,768]{1,0:T(8,128)(2,1)S(1)}, bf16[768,768]{1,0:T(8,128)(2,1)S(1)}, u32[]{:S(2)}, u32[]{:S(2)}) collective-permute-start(bf16[768,768]{1,0:T(8,128)(2,1)S(1)} %constant_dynamic-update-slice_fusion.32.refs_3_), channel_id=1, source_target_pairs={{0,1},{1,0},{2,3},{3,2},{4,5},{5,4},{6,7},{7,6},{8,9},{9,8},{10,11... | collective-permute-start | bytes 3538952 | tf_op jit(solution)/shard_map/ppermute | solution.py:29
  75.9 10.4 %collective-permute-start.15 = (bf16[96,768]{1,0:T(8,128)(2,1)S(1)}, bf16[96,768]{1,0:T(8,128)(2,1)S(1)}, u32[]{:S(2)}, u32[]{:S(2)}) collective-permute-start(bf16[96,768]{1,0:T(8,128)(2,1)S(1)} %pad_maximum_fusion.13), channel_id=1, source_target_pairs={{0,8},{4,12},{8,0},{12,4},{16,24},{20,28},{24,16},{28,20},{1,9},{5... | collective-permute-start | bytes 442376 | tf_op jit(solution)/shard_map/ppermute | solution.py:29
  79.0 10.5 %collective-permute-start.16 = (bf16[96,768]{1,0:T(8,128)(2,1)S(1)}, bf16[96,768]{1,0:T(8,128)(2,1)S(1)}, u32[]{:S(2)}, u32[]{:S(2)}) collective-permute-start(bf16[96,768]{1,0:T(8,128)(2,1)S(1)} %pad_maximum_fusion.14), channel_id=1, source_target_pairs={{0,16},{4,20},{8,24},{12,28},{16,0},{20,4},{24,8},{28,12},{1,17},{... | collective-permute-start | bytes 442376 | tf_op jit(solution)/shard_map/ppermute | solution.py:29
  86.2 7.6 %collective-permute-start.17 = (bf16[96,768]{1,0:T(8,128)(2,1)S(1)}, bf16[96,768]{1,0:T(8,128)(2,1)S(1)}, u32[]{:S(2)}, u32[]{:S(2)}) collective-permute-start(bf16[96,768]{1,0:T(8,128)(2,1)S(1)} %pad_maximum_fusion.15), channel_id=1, source_target_pairs={{0,24},{4,28},{8,16},{12,20},{16,8},{20,12},{24,0},{28,4},{1,25},{... | collective-permute-start | bytes 442376 | tf_op jit(solution)/shard_map/ppermute | solution.py:29
  93.9 13.1 %collective-permute-start.21 = (bf16[128,768]{1,0:T(8,128)(2,1)S(1)}, bf16[128,768]{1,0:T(8,128)(2,1)S(1)}, u32[]{:S(2)}, u32[]{:S(2)}) collective-permute-start(bf16[128,768]{1,0:T(8,128)(2,1)S(1)} %get-tuple-element.56), channel_id=1, source_target_pairs={{0,2},{1,3},{2,0},{3,1},{4,6},{5,7},{6,4},{7,5},{8,10},{9,11},{10,... | collective-permute-start | bytes 589832 | tf_op jit(solution)/shard_map/ppermute | solution.py:29
  100.4 6.6 %collective-permute-start.23 = (bf16[128,768]{1,0:T(8,128)(2,1)S(1)}, bf16[128,768]{1,0:T(8,128)(2,1)S(1)}, u32[]{:S(2)}, u32[]{:S(2)}) collective-permute-start(bf16[128,768]{1,0:T(8,128)(2,1)S(1)} %get-tuple-element.58), channel_id=1, source_target_pairs={{0,2},{1,3},{2,0},{3,1},{4,6},{5,7},{6,4},{7,5},{8,10},{9,11},{10,... | collective-permute-start | bytes 589832 | tf_op jit(solution)/shard_map/ppermute | solution.py:29
  (4 other events, 10.6 us)

commit v7 on v6

--- a/solution.py
+++ b/solution.py
@@ -276,10 +276,10 @@
         early += [("y", step + 2)] if step + 2 < count else []
         send(("x", step, 0), owns[step], "blk", members, 2, *early)
 
-    def send_c(step):
+    def send_c(step, *early):
         across = [sent[name] for name in list(sent) if name[:2] == ("x", step)]
         pairs[step] = jnp.concatenate([owns[step]] + across, axis=0)
-        send(("c", step), pairs[step], "blk", members, 1)
+        send(("c", step), pairs[step], "blk", members, 1, *early)
 
     def gram(first, step, states, cols):
         pieces = []
@@ -299,19 +299,19 @@
         for z in far:
             send_z(step, z)
         send_x(step - 1)
-        send_c(step - 1)
+        send_c(step - 1, *([("z", last, z) for z in far] if step == last else []))
     collect(last)
     total = owns[last].shape[0]
-    third = total // 48 * 16
+    cut, end = total * 208 // 384 // 16 * 16, total * 352 // 384 // 16 * 16
     states, cols = gram(0, last - 2, [], [])
     done["gram", 0] = cols[-1]
     states, cols = gram(last - 1, last - 1, states, cols)
     done["gram", 1] = cols[-1]
     early = [("x", last - 1, 0)] + [("c", k) for k in range(last - 1)]
-    send(("x", last, 0), owns[last][:third], "blk", members, 2, *early)
+    send(("x", last, 0), owns[last][:cut], "blk", members, 2, *early)
     early = [("gram", 0), ("c", last - 1)]
-    send(("x", last, 1), owns[last][third : 2 * third], "blk", members, 2, *early)
-    send(("x", last, 2), owns[last][2 * third :], "blk", members, 2, ("gram", 1))
+    send(("x", last, 1), owns[last][cut:end], "blk", members, 2, *early)
+    send(("x", last, 2), owns[last][end:], "blk", members, 2, ("gram", 1))
     send_c(last)
     result = gram(last, last, states, cols)
     homeward = lax.all_to_all(result, ("grp", "blk"), 0, 0, tiled=True)

time: 137 us -> 127 us (0.927)
  waiting for transfers between devices: 60.8 us -> 52.9 us
  starting transfers between devices: 37.8 us -> 35.8 us
    ppermute x26, waiting for transfers between devices: 60.8 us -> 52.9 us  [swap(): return lax.ppermute(value, axis, [(i, i ^ bit) for i in range(size)])]
    ppermute x26, starting transfers between devices: 37.8 us -> 35.8 us  [swap(): return lax.ppermute(value, axis, [(i, i ^ bit) for i in range(size)])]
  transfers between devices with their start and end apart: 26 -> 26, of which waited for: 13 -> 13; matrix products, arithmetic and copies ran while one was open for 1% -> 1% of each run, Pallas kernels for 7% -> 8%
where the time goes in v7:
time: 127 us; the launch traced here: 126 us
  waiting for transfers between devices  52.9 us (42%)
  starting transfers between devices  35.8 us (28%)
  Pallas kernels  22.6 us (18%)
  blocking collectives  11.3 us (9%)
  local copies, waits for them, and re-layouts  3.23 us (3%)
    ppermute x26, waiting for transfers between devices, swap(): return lax.ppermute(value, axis, [(i, i ^ bit) for i in range(size)])  52.9 us
    ppermute x26, starting transfers between devices, swap(): return lax.ppermute(value, axis, [(i, i ^ bit) for i in range(size)])  35.8 us
    all_to_all x1, blocking collectives, on_device(): homeward = lax.all_to_all(result, ('grp', 'blk'), 0, 0, tiled=True)  11.3 us
    pallas_call x2, Pallas kernels, gram_step(): pl.pallas_call(functools.partial(gram_kernel, first, step, tile), in_spec...  10.2 us
    pallas_call x1, Pallas kernels, gram_step(): pl.pallas_call(functools.partial(gram_last_kernel, step, relatives, chunk...  7.04 us
    pallas_call x1, Pallas kernels, head(): pl.pallas_call(functools.partial(head_kernel, capacity, chunks, groups),...  3.08 us
    unnamed x24, local copies, waits for them, and re-layouts  3.04 us
  transfers between devices with their start and end apart: 26, of which 13 were waited for; matrix products, arithmetic and copies ran while one was open for 1% of the time, Pallas kernels for 8%

profile of v7, /device:TPU:0, one launch (start us, length us, event | category | flops | bytes accessed | tf_op | source)
XLA Modules:
  0.0 126.4 jit_solution(2014096111616856427)
XLA Ops:
  2.0 3.1 %place_rows.1 = (bf16[192,768]{1,0:T(8,128)(2,1)S(1)}, bf16[192,768]{1,0:T(8,128)(2,1)S(1)}, bf16[192,768]{1,0:T(8,128)(2,1)S(1)}, bf16[192,768]{1,0:T(8,128)(2,...) custom-call(s32[2]{0:T(128)S(1)} %pad_add_fusion.me_ref, ...), custom_call_target="tpu_custom_call" | custom-call | tf_op jit(solution)/shard_map/place_rows/pallas_call | solution.py:57
  5.1 3.0 %collective-permute-start = (bf16[192,768]{1,0:T(8,128)(2,1)S(1)}, bf16[192,768]{1,0:T(8,128)(2,1)S(1)}, u32[]{:S(2)}, u32[]{:S(2)}) collective-permute-start(bf16[192,768]{1,0:T(8,128)(2,1)S(1)} %get-tuple-element.38), channel_id=1, source_target_pairs={{0,4},{4,0},{8,12},{12,8},{16,20},{20,16},{24,28},{28,24},{1,5},{5... | collective-permute-start | bytes 884744 | tf_op jit(solution)/shard_map/ppermute | solution.py:29
  8.2 1.9 %collective-permute-start.8 = (bf16[192,768]{1,0:T(8,128)(2,1)S(1)}, bf16[192,768]{1,0:T(8,128)(2,1)S(1)}, u32[]{:S(2)}, u32[]{:S(2)}) collective-permute-start(bf16[192,768]{1,0:T(8,128)(2,1)S(1)} %get-tuple-element.45), channel_id=1, source_target_pairs={{0,4},{4,0},{8,12},{12,8},{16,20},{20,16},{24,28},{28,24},{1,5},{5... | collective-permute-start | bytes 884744 | tf_op jit(solution)/shard_map/ppermute | solution.py:29
  10.4 5.6 %collective-permute-done = bf16[192,768]{1,0:T(8,128)(2,1)S(1)} collective-permute-done((bf16[192,768]{1,0:T(8,128)(2,1)S(1)}, bf16[192,768]{1,0:T(8,128)(2,1)S(1)}, u32[]{:S(2)}, u32[]{:S(2)}) %collective-permute-start) | collective-permute-done | bytes 294944 | tf_op jit(solution)/shard_map/ppermute | solution.py:29
  16.0 2.2 %collective-permute-start.1 = (bf16[96,768]{1,0:T(8,128)(2,1)S(1)}, bf16[96,768]{1,0:T(8,128)(2,1)S(1)}, u32[]{:S(2)}, u32[]{:S(2)}) collective-permute-start(bf16[96,768]{1,0:T(8,128)(2,1)S(1)} %pad_maximum_fusion.4), channel_id=1, source_target_pairs={{0,8},{4,12},{8,0},{12,4},{16,24},{20,28},{24,16},{28,20},{1,9},{5... | collective-permute-start | bytes 442376 | tf_op jit(solution)/shard_map/ppermute | solution.py:29
  18.2 2.7 %collective-permute-start.2 = (bf16[96,768]{1,0:T(8,128)(2,1)S(1)}, bf16[96,768]{1,0:T(8,128)(2,1)S(1)}, u32[]{:S(2)}, u32[]{:S(2)}) collective-permute-start(bf16[96,768]{1,0:T(8,128)(2,1)S(1)} %pad_maximum_fusion.5), channel_id=1, source_target_pairs={{0,16},{4,20},{8,24},{12,28},{16,0},{20,4},{24,8},{28,12},{1,17},{... | collective-permute-start | bytes 442376 | tf_op jit(solution)/shard_map/ppermute | solution.py:29
  22.3 4.1 %collective-permute-start.3 = (bf16[96,768]{1,0:T(8,128)(2,1)S(1)}, bf16[96,768]{1,0:T(8,128)(2,1)S(1)}, u32[]{:S(2)}, u32[]{:S(2)}) collective-permute-start(bf16[96,768]{1,0:T(8,128)(2,1)S(1)} %pad_maximum_fusion.6), channel_id=1, source_target_pairs={{0,24},{4,28},{8,16},{12,20},{16,8},{20,12},{24,0},{28,4},{1,25},{... | collective-permute-start | bytes 442376 | tf_op jit(solution)/shard_map/ppermute | solution.py:29
  26.5 2.1 %collective-permute-done.8 = bf16[192,768]{1,0:T(8,128)(2,1)S(1)} collective-permute-done((bf16[192,768]{1,0:T(8,128)(2,1)S(1)}, bf16[192,768]{1,0:T(8,128)(2,1)S(1)}, u32[]{:S(2)}, u32[]{:S(2)}) %collective-permute-start.8) | collective-permute-done | bytes 294944 | tf_op jit(solution)/shard_map/ppermute | solution.py:29
  28.7 2.2 %collective-permute-start.5 = (bf16[96,768]{1,0:T(8,128)(2,1)S(1)}, bf16[96,768]{1,0:T(8,128)(2,1)S(1)}, u32[]{:S(2)}, u32[]{:S(2)}) collective-permute-start(bf16[96,768]{1,0:T(8,128)(2,1)S(1)} %pad_maximum_fusion.7), channel_id=1, source_target_pairs={{0,8},{4,12},{8,0},{12,4},{16,24},{20,28},{24,16},{28,20},{1,9},{5... | collective-permute-start | bytes 442376 | tf_op jit(solution)/shard_map/ppermute | solution.py:29
  32.6 3.0 %collective-permute-start.6 = (bf16[96,768]{1,0:T(8,128)(2,1)S(1)}, bf16[96,768]{1,0:T(8,128)(2,1)S(1)}, u32[]{:S(2)}, u32[]{:S(2)}) collective-permute-start(bf16[96,768]{1,0:T(8,128)(2,1)S(1)} %pad_maximum_fusion.8), channel_id=1, source_target_pairs={{0,16},{4,20},{8,24},{12,28},{16,0},{20,4},{24,8},{28,12},{1,17},{... | collective-permute-start | bytes 442376 | tf_op jit(solution)/shard_map/ppermute | solution.py:29
  36.9 9.6 %collective-permute-done.6 = bf16[96,768]{1,0:T(8,128)(2,1)S(1)} collective-permute-done((bf16[96,768]{1,0:T(8,128)(2,1)S(1)}, bf16[96,768]{1,0:T(8,128)(2,1)S(1)}, u32[]{:S(2)}, u32[]{:S(2)}) %collective-permute-start.6) | collective-permute-done | bytes 147488 | tf_op jit(solution)/shard_map/ppermute | solution.py:29
  46.6 2.4 %collective-permute-start.10 = (bf16[96,768]{1,0:T(8,128)(2,1)S(1)}, bf16[96,768]{1,0:T(8,128)(2,1)S(1)}, u32[]{:S(2)}, u32[]{:S(2)}) collective-permute-start(bf16[96,768]{1,0:T(8,128)(2,1)S(1)} %pad_maximum_fusion.10), channel_id=1, source_target_pairs={{0,8},{4,12},{8,0},{12,4},{16,24},{20,28},{24,16},{28,20},{1,9},{5... | collective-permute-start | bytes 442376 | tf_op jit(solution)/shard_map/ppermute | solution.py:29
  53.4 8.4 %collective-permute-done.11 = bf16[96,768]{1,0:T(8,128)(2,1)S(1)} collective-permute-done((bf16[96,768]{1,0:T(8,128)(2,1)S(1)}, bf16[96,768]{1,0:T(8,128)(2,1)S(1)}, u32[]{:S(2)}, u32[]{:S(2)}) %collective-permute-start.11) | collective-permute-done | bytes 147488 | tf_op jit(solution)/shard_map/ppermute | solution.py:29
  63.7 2.5 %collective-permute-start.16 = (bf16[96,768]{1,0:T(8,128)(2,1)S(1)}, bf16[96,768]{1,0:T(8,128)(2,1)S(1)}, u32[]{:S(2)}, u32[]{:S(2)}) collective-permute-start(bf16[96,768]{1,0:T(8,128)(2,1)S(1)} %pad_maximum_fusion.14), channel_id=1, source_target_pairs={{0,16},{4,20},{8,24},{12,28},{16,0},{20,4},{24,8},{28,12},{1,17},{... | collective-permute-start | bytes 442376 | tf_op jit(solution)/shard_map/ppermute | solution.py:29
  66.4 9.3 %collective-permute-done.18 = bf16[384,768]{1,0:T(8,128)(2,1)S(1)} collective-permute-done((bf16[384,768]{1,0:T(8,128)(2,1)S(1)}, bf16[384,768]{1,0:T(8,128)(2,1)S(1)}, u32[]{:S(2)}, u32[]{:S(2)}) %collective-permute-start.18) | collective-permute-done | bytes 589856 | tf_op jit(solution)/shard_map/ppermute | solution.py:29
  77.4 5.3 %collective-permute-done.17 = bf16[96,768]{1,0:T(8,128)(2,1)S(1)} collective-permute-done((bf16[96,768]{1,0:T(8,128)(2,1)S(1)}, bf16[96,768]{1,0:T(8,128)(2,1)S(1)}, u32[]{:S(2)}, u32[]{:S(2)}) %collective-permute-start.17) | collective-permute-done | bytes 147488 | tf_op jit(solution)/shard_map/ppermute | solution.py:29
  83.7 5.8 %gram_step.2 = (f32[384,128]{1,0:T(8,128)S(1)}, f32[384,128]{1,0:T(8,128)S(1)}, f32[1,1536]{1,0:T(1,128)S(1)}, f32[1,1536]{1,0:T(1,128)S(1)}) custom-call(bf16[384,768]{1,0:T(8,128)(2,1)S(1)} %get-tuple-element.46.refs_0_, bf16[384,768]{1,0:T(8,128)(2,1)S(1)} %get-tuple-element.52.refs_1_, bf16[768,768]{1,0:T(8,128)(2,1)S(1)} %constant_dynamic-update-slice_fusion.20.refs_2_, ...), custom_call_target="tpu_custom_call" | custom-call | flops 1811939328 | bytes 3538944 | tf_op jit(solution)/shard_map/gram_step/pallas_call | solution.py:174
  89.5 3.3 %collective-permute-done.21 = bf16[208,768]{1,0:T(8,128)(2,1)S(1)} collective-permute-done((bf16[208,768]{1,0:T(8,128)(2,1)S(1)}, bf16[208,768]{1,0:T(8,128)(2,1)S(1)}, u32[]{:S(2)}, u32[]{:S(2)}) %collective-permute-start.21) | collective-permute-done | bytes 319520 | tf_op jit(solution)/shard_map/ppermute | solution.py:29
  93.7 4.4 %gram_step.3 = (f32[384,128]{1,0:T(8,128)S(1)}, f32[384,128]{1,0:T(8,128)S(1)}, f32[384,128]{1,0:T(8,128)S(1)}, f32[1,1536]{1,0:T(1,128)S(1)}) custom-call(bf16[384,768]{1,0:T(8,128)(2,1)S(1)} %get-tuple-element.46.refs_0_, bf16[384,768]{1,0:T(8,128)(2,1)S(1)} %get-tuple-element.52.refs_1_, bf16[384,768]{1,0:T(8,128)(2,1)S(1)} %get-tuple-element.56.refs_2_, ...), custom_call_target="tpu_custom_call" | custom-call | flops 2717908992 | bytes 4128768 | tf_op jit(solution)/shard_map/gram_step/pallas_call | solution.py:174
  100.0 2.2 %collective-permute-done.24 = bf16[32,768]{1,0:T(8,128)(2,1)S(1)} collective-permute-done((bf16[32,768]{1,0:T(8,128)(2,1)S(1)}, bf16[32,768]{1,0:T(8,128)(2,1)S(1)}, u32[]{:S(2)}, u32[]{:S(2)}) %collective-permute-start.24) | collective-permute-done | bytes 49184 | tf_op jit(solution)/shard_map/ppermute | solution.py:29
  102.3 2.8 %collective-permute-done.25.refs_5_ = bf16[768,768]{1,0:T(8,128)(2,1)S(1)} collective-permute-done((bf16[768,768]{1,0:T(8,128)(2,1)S(1)}, bf16[768,768]{1,0:T(8,128)(2,1)S(1)}, u32[]{:S(2)}, u32[]{:S(2)}) %collective-permute-start.25) | collective-permute-done | bytes 1179680 | tf_op jit(solution)/shard_map/ppermute | solution.py:29
  105.1 7.0 %gram_last.1 = f32[32,192]{1,0:T(8,128)S(1)} custom-call(s32[2]{0:T(128)S(1)} %pad_add_fusion.me_ref, bf16[384,768]{1,0:T(8,128)(2,1)S(1)} %get-tuple-element.46.refs_0_, bf16[384,768]{1,0:T(8,128)(2,1)S(1)} %get-tuple-element.52.refs_1_, bf16[384,768]{1,0:T(8,128)(2,1)S(1)} %get-tuple-element.56.refs_2_, bf16[384,768]{1,0:T(8,128)(2,1)S(1)} %get-tuple-element.130.refs_3_, ...), custom_call_target="tpu_custom_call" | custom-call | flops 3623878656 | bytes 4718592 | tf_op jit(solution)/shard_map/gram_last/pallas_call | solution.py:185
  112.2 11.3 %all_to_all.11 = f32[32,1,192]{2,1,0:T(1,128)S(1)} all-to-all(f32[32,1,192]{2,1,0:T(1,128)S(1)} %copy.3), channel_id=1, replica_groups=mesh['grp'=8,'blk'=4] {'grp','blk'}, dimensions={0} | all-to-all | bytes 49152 | tf_op jit(solution)/shard_map/all_to_all | solution.py:317
  124.1 2.3 %pick_rows.1 = f32[6,128]{1,0:T(8,128)} custom-call(s32[6,128]{1,0:T(8,128)} %bitcast.9, f32[32,192]{1,0:T(8,128)} %bitcast.11), custom_call_target="tpu_custom_call" | custom-call | tf_op jit(solution)/shard_map/pick_rows/pallas_call | solution.py:225
  (80 shorter events, 19.3 us)
Async XLA Ops:
  5.1 10.9 %collective-permute-start = (bf16[192,768]{1,0:T(8,128)(2,1)S(1)}, bf16[192,768]{1,0:T(8,128)(2,1)S(1)}, u32[]{:S(2)}, u32[]{:S(2)}) collective-permute-start(bf16[192,768]{1,0:T(8,128)(2,1)S(1)} %get-tuple-element.38), channel_id=1, source_target_pairs={{0,4},{4,0},{8,12},{12,8},{16,20},{20,16},{24,28},{28,24},{1,5},{5... | collective-permute-start | bytes 884744 | tf_op jit(solution)/shard_map/ppermute | solution.py:29
  8.2 14.2 %collective-permute-start.4 = (bf16[192,768]{1,0:T(8,128)(2,1)S(1)}, bf16[192,768]{1,0:T(8,128)(2,1)S(1)}, u32[]{:S(2)}, u32[]{:S(2)}) collective-permute-start(bf16[192,768]{1,0:T(8,128)(2,1)S(1)} %get-tuple-element.40), channel_id=1, source_target_pairs={{0,4},{4,0},{8,12},{12,8},{16,20},{20,16},{24,28},{28,24},{1,5},{5... | collective-permute-start | bytes 884744 | tf_op jit(solution)/shard_map/ppermute | solution.py:29
  8.2 20.4 %collective-permute-start.8 = (bf16[192,768]{1,0:T(8,128)(2,1)S(1)}, bf16[192,768]{1,0:T(8,128)(2,1)S(1)}, u32[]{:S(2)}, u32[]{:S(2)}) collective-permute-start(bf16[192,768]{1,0:T(8,128)(2,1)S(1)} %get-tuple-element.45), channel_id=1, source_target_pairs={{0,4},{4,0},{8,12},{12,8},{16,20},{20,16},{24,28},{28,24},{1,5},{5... | collective-permute-start | bytes 884744 | tf_op jit(solution)/shard_map/ppermute | solution.py:29
  10.2 38.9 %collective-permute-start.13 = (bf16[192,768]{1,0:T(8,128)(2,1)S(1)}, bf16[192,768]{1,0:T(8,128)(2,1)S(1)}, u32[]{:S(2)}, u32[]{:S(2)}) collective-permute-start(bf16[192,768]{1,0:T(8,128)(2,1)S(1)} %get-tuple-element.51), channel_id=1, source_target_pairs={{0,4},{4,0},{8,12},{12,8},{16,20},{20,16},{24,28},{28,24},{1,5},{5... | collective-permute-start | bytes 884744 | tf_op jit(solution)/shard_map/ppermute | solution.py:29
  16.0 12.7 %collective-permute-start.1 = (bf16[96,768]{1,0:T(8,128)(2,1)S(1)}, bf16[96,768]{1,0:T(8,128)(2,1)S(1)}, u32[]{:S(2)}, u32[]{:S(2)}) collective-permute-start(bf16[96,768]{1,0:T(8,128)(2,1)S(1)} %pad_maximum_fusion.4), channel_id=1, source_target_pairs={{0,8},{4,12},{8,0},{12,4},{16,24},{20,28},{24,16},{28,20},{1,9},{5... | collective-permute-start | bytes 442376 | tf_op jit(solution)/shard_map/ppermute | solution.py:29
  18.2 12.7 %collective-permute-start.2 = (bf16[96,768]{1,0:T(8,128)(2,1)S(1)}, bf16[96,768]{1,0:T(8,128)(2,1)S(1)}, u32[]{:S(2)}, u32[]{:S(2)}) collective-permute-start(bf16[96,768]{1,0:T(8,128)(2,1)S(1)} %pad_maximum_fusion.5), channel_id=1, source_target_pairs={{0,16},{4,20},{8,24},{12,28},{16,0},{20,4},{24,8},{28,12},{1,17},{... | collective-permute-start | bytes 442376 | tf_op jit(solution)/shard_map/ppermute | solution.py:29
  22.3 8.7 %collective-permute-start.3 = (bf16[96,768]{1,0:T(8,128)(2,1)S(1)}, bf16[96,768]{1,0:T(8,128)(2,1)S(1)}, u32[]{:S(2)}, u32[]{:S(2)}) collective-permute-start(bf16[96,768]{1,0:T(8,128)(2,1)S(1)} %pad_maximum_fusion.6), channel_id=1, source_target_pairs={{0,24},{4,28},{8,16},{12,20},{16,8},{20,12},{24,0},{28,4},{1,25},{... | collective-permute-start | bytes 442376 | tf_op jit(solution)/shard_map/ppermute | solution.py:29
  28.7 8.2 %collective-permute-start.5 = (bf16[96,768]{1,0:T(8,128)(2,1)S(1)}, bf16[96,768]{1,0:T(8,128)(2,1)S(1)}, u32[]{:S(2)}, u32[]{:S(2)}) collective-permute-start(bf16[96,768]{1,0:T(8,128)(2,1)S(1)} %pad_maximum_fusion.7), channel_id=1, source_target_pairs={{0,8},{4,12},{8,0},{12,4},{16,24},{20,28},{24,16},{28,20},{1,9},{5... | collective-permute-start | bytes 442376 | tf_op jit(solution)/shard_map/ppermute | solution.py:29
  31.0 15.6 %collective-permute-start.9 = (bf16[384,768]{1,0:T(8,128)(2,1)S(1)}, bf16[384,768]{1,0:T(8,128)(2,1)S(1)}, u32[]{:S(2)}, u32[]{:S(2)}) collective-permute-start(bf16[384,768]{1,0:T(8,128)(2,1)S(1)} %get-tuple-element.46.refs_0_), channel_id=1, source_target_pairs={{0,2},{1,3},{2,0},{3,1},{4,6},{5,7},{6,4},{7,5},{8,10},{9,11},{10,... | collective-permute-start | bytes 1769480 | tf_op jit(solution)/shard_map/ppermute | solution.py:29
  32.6 14.0 %collective-permute-start.6 = (bf16[96,768]{1,0:T(8,128)(2,1)S(1)}, bf16[96,768]{1,0:T(8,128)(2,1)S(1)}, u32[]{:S(2)}, u32[]{:S(2)}) collective-permute-start(bf16[96,768]{1,0:T(8,128)(2,1)S(1)} %pad_maximum_fusion.8), channel_id=1, source_target_pairs={{0,16},{4,20},{8,24},{12,28},{16,0},{20,4},{24,8},{28,12},{1,17},{... | collective-permute-start | bytes 442376 | tf_op jit(solution)/shard_map/ppermute | solution.py:29
  35.5 11.0 %collective-permute-start.7 = (bf16[96,768]{1,0:T(8,128)(2,1)S(1)}, bf16[96,768]{1,0:T(8,128)(2,1)S(1)}, u32[]{:S(2)}, u32[]{:S(2)}) collective-permute-start(bf16[96,768]{1,0:T(8,128)(2,1)S(1)} %pad_maximum_fusion.9), channel_id=1, source_target_pairs={{0,24},{4,28},{8,16},{12,20},{16,8},{20,12},{24,0},{28,4},{1,25},{... | collective-permute-start | bytes 442376 | tf_op jit(solution)/shard_map/ppermute | solution.py:29
  46.6 6.8 %collective-permute-start.10 = (bf16[96,768]{1,0:T(8,128)(2,1)S(1)}, bf16[96,768]{1,0:T(8,128)(2,1)S(1)}, u32[]{:S(2)}, u32[]{:S(2)}) collective-permute-start(bf16[96,768]{1,0:T(8,128)(2,1)S(1)} %pad_maximum_fusion.10), channel_id=1, source_target_pairs={{0,8},{4,12},{8,0},{12,4},{16,24},{20,28},{24,16},{28,20},{1,9},{5... | collective-permute-start | bytes 442376 | tf_op jit(solution)/shard_map/ppermute | solution.py:29
  49.1 13.8 %collective-permute-start.14 = (bf16[384,768]{1,0:T(8,128)(2,1)S(1)}, bf16[384,768]{1,0:T(8,128)(2,1)S(1)}, u32[]{:S(2)}, u32[]{:S(2)}) collective-permute-start(bf16[384,768]{1,0:T(8,128)(2,1)S(1)} %get-tuple-element.52.refs_1_), channel_id=1, source_target_pairs={{0,2},{1,3},{2,0},{3,1},{4,6},{5,7},{6,4},{7,5},{8,10},{9,11},{10,... | collective-permute-start | bytes 1769480 | tf_op jit(solution)/shard_map/ppermute | solution.py:29
  49.6 12.2 %collective-permute-start.11 = (bf16[96,768]{1,0:T(8,128)(2,1)S(1)}, bf16[96,768]{1,0:T(8,128)(2,1)S(1)}, u32[]{:S(2)}, u32[]{:S(2)}) collective-permute-start(bf16[96,768]{1,0:T(8,128)(2,1)S(1)} %pad_maximum_fusion.11), channel_id=1, source_target_pairs={{0,16},{4,20},{8,24},{12,28},{16,0},{20,4},{24,8},{28,12},{1,17},{... | collective-permute-start | bytes 442376 | tf_op jit(solution)/shard_map/ppermute | solution.py:29
  50.4 11.4 %collective-permute-start.12 = (bf16[96,768]{1,0:T(8,128)(2,1)S(1)}, bf16[96,768]{1,0:T(8,128)(2,1)S(1)}, u32[]{:S(2)}, u32[]{:S(2)}) collective-permute-start(bf16[96,768]{1,0:T(8,128)(2,1)S(1)} %pad_maximum_fusion.12), channel_id=1, source_target_pairs={{0,24},{4,28},{8,16},{12,20},{16,8},{20,12},{24,0},{28,4},{1,25},{... | collective-permute-start | bytes 442376 | tf_op jit(solution)/shard_map/ppermute | solution.py:29
  52.2 30.6 %collective-permute-start.19 = (bf16[768,768]{1,0:T(8,128)(2,1)S(1)}, bf16[768,768]{1,0:T(8,128)(2,1)S(1)}, u32[]{:S(2)}, u32[]{:S(2)}) collective-permute-start(bf16[768,768]{1,0:T(8,128)(2,1)S(1)} %constant_dynamic-update-slice_fusion.20.refs_2_), channel_id=1, source_target_pairs={{0,1},{1,0},{2,3},{3,2},{4,5},{5,4},{6,7},{7,6},{8,9},{9,8},{10,11... | collective-permute-start | bytes 3538952 | tf_op jit(solution)/shard_map/ppermute | solution.py:29
  62.8 12.8 %collective-permute-start.18 = (bf16[384,768]{1,0:T(8,128)(2,1)S(1)}, bf16[384,768]{1,0:T(8,128)(2,1)S(1)}, u32[]{:S(2)}, u32[]{:S(2)}) collective-permute-start(bf16[384,768]{1,0:T(8,128)(2,1)S(1)} %get-tuple-element.56.refs_2_), channel_id=1, source_target_pairs={{0,2},{1,3},{2,0},{3,1},{4,6},{5,7},{6,4},{7,5},{8,10},{9,11},{10,... | collective-permute-start | bytes 1769480 | tf_op jit(solution)/shard_map/ppermute | solution.py:29
  63.6 19.2 %collective-permute-start.20 = (bf16[768,768]{1,0:T(8,128)(2,1)S(1)}, bf16[768,768]{1,0:T(8,128)(2,1)S(1)}, u32[]{:S(2)}, u32[]{:S(2)}) collective-permute-start(bf16[768,768]{1,0:T(8,128)(2,1)S(1)} %constant_dynamic-update-slice_fusion.26.refs_4_), channel_id=1, source_target_pairs={{0,1},{1,0},{2,3},{3,2},{4,5},{5,4},{6,7},{7,6},{8,9},{9,8},{10,11... | collective-permute-start | bytes 3538952 | tf_op jit(solution)/shard_map/ppermute | solution.py:29
  63.7 13.6 %collective-permute-start.16 = (bf16[96,768]{1,0:T(8,128)(2,1)S(1)}, bf16[96,768]{1,0:T(8,128)(2,1)S(1)}, u32[]{:S(2)}, u32[]{:S(2)}) collective-permute-start(bf16[96,768]{1,0:T(8,128)(2,1)S(1)} %pad_maximum_fusion.14), channel_id=1, source_target_pairs={{0,16},{4,20},{8,24},{12,28},{16,0},{20,4},{24,8},{28,12},{1,17},{... | collective-permute-start | bytes 442376 | tf_op jit(solution)/shard_map/ppermute | solution.py:29
  66.2 11.1 %collective-permute-start.15 = (bf16[96,768]{1,0:T(8,128)(2,1)S(1)}, bf16[96,768]{1,0:T(8,128)(2,1)S(1)}, u32[]{:S(2)}, u32[]{:S(2)}) collective-permute-start(bf16[96,768]{1,0:T(8,128)(2,1)S(1)} %pad_maximum_fusion.13), channel_id=1, source_target_pairs={{0,8},{4,12},{8,0},{12,4},{16,24},{20,28},{24,16},{28,20},{1,9},{5... | collective-permute-start | bytes 442376 | tf_op jit(solution)/shard_map/ppermute | solution.py:29
  75.7 7.0 %collective-permute-start.17 = (bf16[96,768]{1,0:T(8,128)(2,1)S(1)}, bf16[96,768]{1,0:T(8,128)(2,1)S(1)}, u32[]{:S(2)}, u32[]{:S(2)}) collective-permute-start(bf16[96,768]{1,0:T(8,128)(2,1)S(1)} %pad_maximum_fusion.15), channel_id=1, source_target_pairs={{0,24},{4,28},{8,16},{12,20},{16,8},{20,12},{24,0},{28,4},{1,25},{... | collective-permute-start | bytes 442376 | tf_op jit(solution)/shard_map/ppermute | solution.py:29
  82.7 10.2 %collective-permute-start.22 = (bf16[768,768]{1,0:T(8,128)(2,1)S(1)}, bf16[768,768]{1,0:T(8,128)(2,1)S(1)}, u32[]{:S(2)}, u32[]{:S(2)}) collective-permute-start(bf16[768,768]{1,0:T(8,128)(2,1)S(1)} %constant_dynamic-update-slice_fusion.32.refs_3_), channel_id=1, source_target_pairs={{0,1},{1,0},{2,3},{3,2},{4,5},{5,4},{6,7},{7,6},{8,9},{9,8},{10,11... | collective-permute-start | bytes 3538952 | tf_op jit(solution)/shard_map/ppermute | solution.py:29
  82.8 10.0 %collective-permute-start.21 = (bf16[208,768]{1,0:T(8,128)(2,1)S(1)}, bf16[208,768]{1,0:T(8,128)(2,1)S(1)}, u32[]{:S(2)}, u32[]{:S(2)}) collective-permute-start(bf16[208,768]{1,0:T(8,128)(2,1)S(1)} %pad_maximum_fusion), channel_id=1, source_target_pairs={{0,2},{1,3},{2,0},{3,1},{4,6},{5,7},{6,4},{7,5},{8,10},{9,11},{10,... | collective-permute-start | bytes 958472 | tf_op jit(solution)/shard_map/ppermute | solution.py:29
  92.9 7.1 %collective-permute-start.23 = (bf16[144,768]{1,0:T(8,128)(2,1)S(1)}, bf16[144,768]{1,0:T(8,128)(2,1)S(1)}, u32[]{:S(2)}, u32[]{:S(2)}) collective-permute-start(bf16[144,768]{1,0:T(8,128)(2,1)S(1)} %pad_maximum_fusion.3), channel_id=1, source_target_pairs={{0,2},{1,3},{2,0},{3,1},{4,6},{5,7},{6,4},{7,5},{8,10},{9,11},{10,... | collective-permute-start | bytes 663560 | tf_op jit(solution)/shard_map/ppermute | solution.py:29
  (4 other events, 9.0 us)

commit v8 on v7

--- a/solution.py
+++ b/solution.py
@@ -29,43 +29,85 @@
     return lax.ppermute(value, axis, [(i, i ^ bit) for i in range(size)])
 
 
-def head_kernel(capacity, chunks, groups, me_ref, slot_ref, x_ref, *out_refs):
+def place(me, slots, normed, capacity, first, size, groups, low):
+    shape = (groups // 2, size, 1)
+    spot = lax.broadcasted_iota(jnp.int32, shape, 1) + first
+    group = (lax.broadcasted_iota(jnp.int32, shape, 0) * 2 + low) ^ me
+    wanted = (group * capacity + spot).reshape(groups // 2 * size, 1)
+    pick = jnp.where(wanted == slots, 1.0, 0.0)
+    live = jnp.max(pick, axis=1, keepdims=True)
+    placed = jnp.dot(pick.astype(jnp.bfloat16), normed, preferred_element_type=jnp.float32)
+    lane = lax.broadcasted_iota(jnp.int32, (1, placed.shape[1]), 1)
+    mark = jnp.where(lane == 0, dead_mark, 0.0)
+    return (placed + (1.0 - live) * mark).astype(jnp.bfloat16)
+
+
+def flat(slot_ref):
+    return jnp.concatenate([slot_ref[q : q + 1, :] for q in range(slot_ref.shape[0])], axis=1)
+
+
+def first_kernel(capacity, chunks, groups, me_ref, slot_ref, x_ref, normed_ref, send_ref):
     wide = x_ref[...].astype(jnp.float32)
-    normed = (
+    normed_ref[...] = (
         wide * lax.rsqrt(jnp.sum(wide * wide, axis=-1, keepdims=True) + epsilon)
     ).astype(jnp.bfloat16)
-    slots = jnp.concatenate([slot_ref[q : q + 1, :] for q in range(slot_ref.shape[0])], axis=1)
-    first, high = 0, groups // 2
+    send_ref[...] = place(
+        me_ref[0], flat(slot_ref), normed_ref[...], capacity, 0, chunks[0], groups, 1
+    )
+
+
+def rest_kernel(capacity, chunks, groups, me_ref, slot_ref, normed_ref, *out_refs):
+    keeps, send_ref = out_refs[:-1], out_refs[-1]
+    slots, normed = flat(slot_ref), normed_ref[...]
+    first, row = 0, 0
     for step, size in enumerate(chunks):
-        place = lax.broadcasted_iota(jnp.int32, (groups, size, 1), 1)
-        order = lax.broadcasted_iota(jnp.int32, (groups, size, 1), 0)
-        group = (order % high * 2 + order // high) ^ me_ref[0]
-        wanted = (group * capacity + place + first).reshape(groups * size, 1)
-        pick = jnp.where(wanted == slots, 1.0, 0.0)
-        live = jnp.max(pick, axis=1, keepdims=True)
-        placed = jnp.dot(pick.astype(jnp.bfloat16), normed, preferred_element_type=jnp.float32)
-        lane = lax.broadcasted_iota(jnp.int32, (1, placed.shape[1]), 1)
-        mark = jnp.where(lane == 0, dead_mark, 0.0)
-        placed = (placed + (1.0 - live) * mark).astype(jnp.bfloat16)
-        out_refs[2 * step][...] = placed[: high * size, :]
-        out_refs[2 * step + 1][...] = placed[high * size :, :]
+        if step > 0:
+            count = groups // 2 * size
+            send_ref[row : row + count, :] = place(
+                me_ref[0], slots, normed, capacity, first, size, groups, 1
+            )
+            row += count
+        first += size
+    first = 0
+    for step, size in enumerate(chunks):
+        keeps[step][...] = place(me_ref[0], slots, normed, capacity, first, size, groups, 0)
         first += size
 
 
 def head(me, embeddings, slots, capacity, chunks, groups):
     rows, features = embeddings.shape
-    return pl.pallas_call(
-        functools.partial(head_kernel, capacity, chunks, groups),
+    half = [groups // 2 * size for size in chunks]
+
+    def shape(count):
+        return jax.ShapeDtypeStruct((count, features), jnp.bfloat16)
+
+    def cost(count):
+        return pl.CostEstimate(
+            flops=2 * count * rows * features,
+            bytes_accessed=2 * (rows + count) * features,
+            transcendentals=0,
+        )
+
+    params = pltpu.CompilerParams(vmem_limit_bytes=24 * 2**20)
+    normed, first_send = pl.pallas_call(
+        functools.partial(first_kernel, capacity, chunks, groups),
         in_specs=[smem, vmem, vmem],
-        out_specs=[vmem] * (2 * len(chunks)),
-        out_shape=[
-            jax.ShapeDtypeStruct((groups // 2 * size, features), jnp.bfloat16)
-            for size in chunks
-            for _ in range(2)
-        ],
-        compiler_params=pltpu.CompilerParams(vmem_limit_bytes=32 * 2**20),
-        name="place_rows",
+        out_specs=[vmem, vmem],
+        out_shape=[shape(rows), shape(half[0])],
+        compiler_params=params,
+        cost_estimate=cost(half[0]),
+        name="place_first",
     )(me, slots, embeddings)
+    *keeps, rest_send = pl.pallas_call(
+        functools.partial(rest_kernel, capacity, chunks, groups),
+        in_specs=[smem, vmem, vmem],
+        out_specs=[vmem] * (len(chunks) + 1),
+        out_shape=[shape(count) for count in half] + [shape(sum(half[1:]))],
+        compiler_params=params,
+        cost_estimate=cost(2 * sum(half) - half[0]),
+        name="place_rest",
+    )(me, slots, normed)
+    return keeps, first_send, rest_send
 
 
 def lane_fold(values):
@@ -241,7 +283,7 @@
     chunks = chunk_sizes(capacity)
     me = jnp.stack([lax.axis_index("grp"), lax.axis_index("blk")]).astype(jnp.int32)
     slots = send_slot.reshape(row_count // lanes, lanes)
-    placed = head(me, embeddings, slots, capacity, chunks, groups)
+    keeps, first_send, rest_send = head(me, embeddings, slots, capacity, chunks, groups)
     count, high = len(chunks), groups // 2
     last = count - 1
 
@@ -252,8 +294,10 @@
 
     def block(step, z):
         size = chunks[step]
+        near = sent["y", 0] if step == 0 else sent["y", 1]
+        skip = sum(chunks[1:step]) * high
         return jnp.concatenate(
-            [rows(placed[2 * step], z, size), rows(sent["y", step], z, size)], axis=0
+            [rows(keeps[step], z, size), rows(near[skip:], z, size)], axis=0
         )
 
     def send(key, value, axis, size, bit, *earlier):
@@ -262,19 +306,24 @@
 
     def send_z(step, z):
         early = [("z", step - 1, z)] if step >= 1 else []
-        if step >= 2 and z != high // 2:
+        if step >= 2 and z == far[-1]:
             early += [("x", step - 2, 0)]
+        if step == last and step >= 3:
+            early += [("c", step - 2 if z == far[-1] else step - 3)]
         send(("z", step, z), block(step, z), "grp", groups, 2 * z, *early)
 
     def collect(step):
         parts = [block(step, 0)] + [sent["z", step, z] for z in range(1, high)]
         owns[step] = jnp.concatenate(parts, axis=0)
 
-    def send_x(step):
-        collect(step)
-        early = [("x", step - 1, 0)] if step >= 1 else []
-        early += [("y", step + 2)] if step + 2 < count else []
-        send(("x", step, 0), owns[step], "blk", members, 2, *early)
+    def send_x(step, cuts, between):
+        total = owns[step].shape[0]
+        cuts = [0] + [total * cut // 384 // 16 * 16 for cut in cuts] + [total]
+        parts = [name for name in sent if name[:2] == ("x", step - 1)]
+        for part in range(len(cuts) - 1):
+            value = owns[step][cuts[part] : cuts[part + 1]]
+            early = parts if part == 0 else between
+            send(("x", step, part), value, "blk", members, 2, *early)
 
     def send_c(step, *early):
         across = [sent[name] for name in list(sent) if name[:2] == ("x", step)]
@@ -290,28 +339,28 @@
             first, me, mine, pieces, states, cols, (0, 2, 1, 3), chunks, groups
         )
 
-    far = [high // 2] + [z for z in reversed(range(1, high)) if z != high // 2]
-    for step in range(count):
-        send(("y", step), placed[2 * step + 1], "grp", groups, 1)
+    far = [high // 2] + [z for z in range(1, high) if z != high // 2]
+    send(("y", 0), first_send, "grp", groups, 1)
+    send(("y", 1), rest_send, "grp", groups, 1)
     for z in far:
         send_z(0, z)
     for step in range(1, count):
-        for z in far:
-            send_z(step, z)
-        send_x(step - 1)
-        send_c(step - 1, *([("z", last, z) for z in far] if step == last else []))
+        collect(step - 1)
+        if step < last:
+            for z in far:
+                send_z(step, z)
+            send_x(step - 1, [], [])
+            send_c(step - 1)
+    for z in far:
+        send_z(last, z)
     collect(last)
-    total = owns[last].shape[0]
-    cut, end = total * 208 // 384 // 16 * 16, total * 352 // 384 // 16 * 16
     states, cols = gram(0, last - 2, [], [])
     done["gram", 0] = cols[-1]
+    send_x(last - 1, [256], [("gram", 0)])
+    send_c(last - 1, *[("z", last, z) for z in far])
     states, cols = gram(last - 1, last - 1, states, cols)
     done["gram", 1] = cols[-1]
-    early = [("x", last - 1, 0)] + [("c", k) for k in range(last - 1)]
-    send(("x", last, 0), owns[last][:cut], "blk", members, 2, *early)
-    early = [("gram", 0), ("c", last - 1)]
-    send(("x", last, 1), owns[last][cut:end], "blk", members, 2, *early)
-    send(("x", last, 2), owns[last][end:], "blk", members, 2, ("gram", 1))
+    send_x(last, [256], [("gram", 1)])
     send_c(last)
     result = gram(last, last, states, cols)
     homeward = lax.all_to_all(result, ("grp", "blk"), 0, 0, tiled=True)

time: 127 us -> 158 us (1.24)
  waiting for transfers between devices: 52.9 us -> 85.9 us
  starting transfers between devices: 35.8 us -> 32.3 us
    ppermute x26 -> x24, waiting for transfers between devices: 52.9 us -> 85.9 us  [swap(): return lax.ppermute(value, axis, [(i, i ^ bit) for i in range(size)])]
    ppermute x26 -> x24, starting transfers between devices: 35.8 us -> 32.3 us  [swap(): return lax.ppermute(value, axis, [(i, i ^ bit) for i in range(size)])]
    pallas_call x1 -> x2, Pallas kernels: 3.08 us -> 3.87 us  [the longest x1 2.61 us: head(): pl.pallas_call(functools.partial(rest_kernel, capacity, chunks, groups),...]
  transfers between devices with their start and end apart: 26 -> 24, of which waited for: 13 -> 16; matrix products, arithmetic and copies ran while one was open for 1% -> 1% of each run, Pallas kernels for 8% -> 6%
where the time goes in v8:
time: 158 us; the launch traced here: 157 us
  waiting for transfers between devices  85.9 us (54%)
  starting transfers between devices  32.3 us (20%)
  Pallas kernels  23.4 us (15%)
  blocking collectives  12 us (8%)
  local copies, waits for them, and re-layouts  3.23 us (2%)
    ppermute x24, waiting for transfers between devices, swap(): return lax.ppermute(value, axis, [(i, i ^ bit) for i in range(size)])  85.9 us
    ppermute x24, starting transfers between devices, swap(): return lax.ppermute(value, axis, [(i, i ^ bit) for i in range(size)])  32.3 us
    all_to_all x1, blocking collectives, on_device(): homeward = lax.all_to_all(result, ('grp', 'blk'), 0, 0, tiled=True)  12 us
    pallas_call x2, Pallas kernels, gram_step(): pl.pallas_call(functools.partial(gram_kernel, first, step, tile), in_spec...  10.2 us
    pallas_call x1, Pallas kernels, gram_step(): pl.pallas_call(functools.partial(gram_last_kernel, step, relatives, chunk...  7.05 us
  transfers between devices with their start and end apart: 24, of which 16 were waited for; matrix products, arithmetic and copies ran while one was open for 1% of the time, Pallas kernels for 6%

profile of v8, /device:TPU:0, one launch (start us, length us, event | category | flops | bytes accessed | tf_op | source)
XLA Modules:
  0.0 157.4 jit_solution(4389232672087612303)
XLA Ops:
  3.3 2.6 %place_rest.1 = (bf16[192,768]{1,0:T(8,128)(2,1)S(1)}, bf16[192,768]{1,0:T(8,128)(2,1)S(1)}, bf16[192,768]{1,0:T(8,128)(2,1)S(1)}, bf16[192,768]{1,0:T(8,128)(2,1)S(1)}, bf16[576,768]{1,0:T(8,128)(2,1)S(1)}) custom-call(s32[2]{0:T(128)S(1)} %pad_add_fusion.me_ref, s32[6,128]{1,0:T(8,128)S(1)} %bitcast.11, bf16[768,768]{1,0:T(8,128)(2,1)S(1)} %get-tuple-element.35.normed_ref), custom_call_target="tpu_custom_call" | custom-call | flops 1585446912 | bytes 3244032 | tf_op jit(solution)/shard_map/place_rest/pallas_call | solution.py:101
  5.9 3.0 %collective-permute-start.4 = (bf16[576,768]{1,0:T(8,128)(2,1)S(1)}, bf16[576,768]{1,0:T(8,128)(2,1)S(1)}, u32[]{:S(2)}, u32[]{:S(2)}) collective-permute-start(bf16[576,768]{1,0:T(8,128)(2,1)S(1)} %get-tuple-element.39), channel_id=1, source_target_pairs={{0,4},{4,0},{8,12},{12,8},{16,20},{20,16},{24,28},{28,24},{1,5},{5... | collective-permute-start | bytes 2654216 | tf_op jit(solution)/shard_map/ppermute | solution.py:29
  9.2 25.8 %collective-permute-done = bf16[192,768]{1,0:T(8,128)(2,1)S(1)} collective-permute-done((bf16[192,768]{1,0:T(8,128)(2,1)S(1)}, bf16[192,768]{1,0:T(8,128)(2,1)S(1)}, u32[]{:S(2)}, u32[]{:S(2)}) %collective-permute-start) | collective-permute-done | bytes 294944 | tf_op jit(solution)/shard_map/ppermute | solution.py:29
  35.0 1.9 %collective-permute-start.1 = (bf16[96,768]{1,0:T(8,128)(2,1)S(1)}, bf16[96,768]{1,0:T(8,128)(2,1)S(1)}, u32[]{:S(2)}, u32[]{:S(2)}) collective-permute-start(bf16[96,768]{1,0:T(8,128)(2,1)S(1)} %pad_maximum_fusion.8), channel_id=1, source_target_pairs={{0,8},{4,12},{8,0},{12,4},{16,24},{20,28},{24,16},{28,20},{1,9},{5... | collective-permute-start | bytes 442376 | tf_op jit(solution)/shard_map/ppermute | solution.py:29
  36.8 2.7 %collective-permute-start.2 = (bf16[96,768]{1,0:T(8,128)(2,1)S(1)}, bf16[96,768]{1,0:T(8,128)(2,1)S(1)}, u32[]{:S(2)}, u32[]{:S(2)}) collective-permute-start(bf16[96,768]{1,0:T(8,128)(2,1)S(1)} %pad_maximum_fusion.9), channel_id=1, source_target_pairs={{0,16},{4,20},{8,24},{12,28},{16,0},{20,4},{24,8},{28,12},{1,17},{... | collective-permute-start | bytes 442376 | tf_op jit(solution)/shard_map/ppermute | solution.py:29
  39.6 2.2 %collective-permute-done.1 = bf16[96,768]{1,0:T(8,128)(2,1)S(1)} collective-permute-done((bf16[96,768]{1,0:T(8,128)(2,1)S(1)}, bf16[96,768]{1,0:T(8,128)(2,1)S(1)}, u32[]{:S(2)}, u32[]{:S(2)}) %collective-permute-start.1) | collective-permute-done | bytes 147488 | tf_op jit(solution)/shard_map/ppermute | solution.py:29
  41.9 8.3 %collective-permute-done.2 = bf16[96,768]{1,0:T(8,128)(2,1)S(1)} collective-permute-done((bf16[96,768]{1,0:T(8,128)(2,1)S(1)}, bf16[96,768]{1,0:T(8,128)(2,1)S(1)}, u32[]{:S(2)}, u32[]{:S(2)}) %collective-permute-start.2) | collective-permute-done | bytes 147488 | tf_op jit(solution)/shard_map/ppermute | solution.py:29
  51.8 3.2 %collective-permute-start.6 = (bf16[96,768]{1,0:T(8,128)(2,1)S(1)}, bf16[96,768]{1,0:T(8,128)(2,1)S(1)}, u32[]{:S(2)}, u32[]{:S(2)}) collective-permute-start(bf16[96,768]{1,0:T(8,128)(2,1)S(1)} %pad_maximum_fusion.12), channel_id=1, source_target_pairs={{0,16},{4,20},{8,24},{12,28},{16,0},{20,4},{24,8},{28,12},{1,17},{... | collective-permute-start | bytes 442376 | tf_op jit(solution)/shard_map/ppermute | solution.py:29
  56.8 5.2 %collective-permute-done.5 = bf16[96,768]{1,0:T(8,128)(2,1)S(1)} collective-permute-done((bf16[96,768]{1,0:T(8,128)(2,1)S(1)}, bf16[96,768]{1,0:T(8,128)(2,1)S(1)}, u32[]{:S(2)}, u32[]{:S(2)}) %collective-permute-start.5) | collective-permute-done | bytes 147488 | tf_op jit(solution)/shard_map/ppermute | solution.py:29
  65.3 11.2 %collective-permute-done.15 = bf16[384,768]{1,0:T(8,128)(2,1)S(1)} collective-permute-done((bf16[384,768]{1,0:T(8,128)(2,1)S(1)}, bf16[384,768]{1,0:T(8,128)(2,1)S(1)}, u32[]{:S(2)}, u32[]{:S(2)}) %collective-permute-start.15) | collective-permute-done | bytes 589856 | tf_op jit(solution)/shard_map/ppermute | solution.py:29
  76.8 4.7 %collective-permute-start.8 = (bf16[96,768]{1,0:T(8,128)(2,1)S(1)}, bf16[96,768]{1,0:T(8,128)(2,1)S(1)}, u32[]{:S(2)}, u32[]{:S(2)}) collective-permute-start(bf16[96,768]{1,0:T(8,128)(2,1)S(1)} %pad_maximum_fusion.14), channel_id=1, source_target_pairs={{0,8},{4,12},{8,0},{12,4},{16,24},{20,28},{24,16},{28,20},{1,9},{5... | collective-permute-start | bytes 442376 | tf_op jit(solution)/shard_map/ppermute | solution.py:29
  81.6 2.4 %collective-permute-start.11 = (bf16[96,768]{1,0:T(8,128)(2,1)S(1)}, bf16[96,768]{1,0:T(8,128)(2,1)S(1)}, u32[]{:S(2)}, u32[]{:S(2)}) collective-permute-start(bf16[96,768]{1,0:T(8,128)(2,1)S(1)} %pad_maximum_fusion.16), channel_id=1, source_target_pairs={{0,24},{4,28},{8,16},{12,20},{16,8},{20,12},{24,0},{28,4},{1,25},{... | collective-permute-start | bytes 442376 | tf_op jit(solution)/shard_map/ppermute | solution.py:29
  84.0 2.8 %collective-permute-done.8 = bf16[96,768]{1,0:T(8,128)(2,1)S(1)} collective-permute-done((bf16[96,768]{1,0:T(8,128)(2,1)S(1)}, bf16[96,768]{1,0:T(8,128)(2,1)S(1)}, u32[]{:S(2)}, u32[]{:S(2)}) %collective-permute-start.8) | collective-permute-done | bytes 147488 | tf_op jit(solution)/shard_map/ppermute | solution.py:29
  86.8 8.4 %collective-permute-done.9 = bf16[96,768]{1,0:T(8,128)(2,1)S(1)} collective-permute-done((bf16[96,768]{1,0:T(8,128)(2,1)S(1)}, bf16[96,768]{1,0:T(8,128)(2,1)S(1)}, u32[]{:S(2)}, u32[]{:S(2)}) %collective-permute-start.9) | collective-permute-done | bytes 147488 | tf_op jit(solution)/shard_map/ppermute | solution.py:29
  96.1 5.8 %gram_step.2 = (f32[384,128]{1,0:T(8,128)S(1)}, f32[384,128]{1,0:T(8,128)S(1)}, f32[1,1536]{1,0:T(1,128)S(1)}, f32[1,1536]{1,0:T(1,128)S(1)}) custom-call(bf16[384,768]{1,0:T(8,128)(2,1)S(1)} %get-tuple-element.128.refs_0_, bf16[384,768]{1,0:T(8,128)(2,1)S(1)} %get-tuple-element.50.refs_1_, ...), custom_call_target="tpu_custom_call" | custom-call | flops 1811939328 | bytes 3538944 | tf_op jit(solution)/shard_map/gram_step/pallas_call | solution.py:216
  105.1 2.7 %collective-permute-start.17 = (bf16[96,768]{1,0:T(8,128)(2,1)S(1)}, bf16[96,768]{1,0:T(8,128)(2,1)S(1)}, u32[]{:S(2)}, u32[]{:S(2)}) collective-permute-start(bf16[96,768]{1,0:T(8,128)(2,1)S(1)} %pad_maximum_fusion.19), channel_id=1, source_target_pairs={{0,24},{4,28},{8,16},{12,20},{16,8},{20,12},{24,0},{28,4},{1,25},{... | collective-permute-start | bytes 442376 | tf_op jit(solution)/shard_map/ppermute | solution.py:29
  109.7 5.3 %collective-permute-done.14 = bf16[96,768]{1,0:T(8,128)(2,1)S(1)} collective-permute-done((bf16[96,768]{1,0:T(8,128)(2,1)S(1)}, bf16[96,768]{1,0:T(8,128)(2,1)S(1)}, u32[]{:S(2)}, u32[]{:S(2)}) %collective-permute-start.14) | collective-permute-done | bytes 147488 | tf_op jit(solution)/shard_map/ppermute | solution.py:29
  119.5 4.4 %gram_step.3 = (f32[384,128]{1,0:T(8,128)S(1)}, f32[384,128]{1,0:T(8,128)S(1)}, f32[384,128]{1,0:T(8,128)S(1)}, f32[1,1536]{1,0:T(1,128)S(1)}) custom-call(bf16[384,768]{1,0:T(8,128)(2,1)S(1)} %get-tuple-element.128.refs_0_, bf16[384,768]{1,0:T(8,128)(2,1)S(1)} %get-tuple-element.50.refs_1_, bf16[384,768]{1,0:T(8,128)(2,1)S(1)} %get-tuple-element.110.refs_2_, ...), custom_call_target="tpu_custom_call" | custom-call | flops 2717908992 | bytes 4128768 | tf_op jit(solution)/shard_map/gram_step/pallas_call | solution.py:216
  125.7 3.0 %collective-permute-done.20 = bf16[256,768]{1,0:T(8,128)(2,1)S(1)} collective-permute-done((bf16[256,768]{1,0:T(8,128)(2,1)S(1)}, bf16[256,768]{1,0:T(8,128)(2,1)S(1)}, u32[]{:S(2)}, u32[]{:S(2)}) %collective-permute-start.20) | collective-permute-done | bytes 393248 | tf_op jit(solution)/shard_map/ppermute | solution.py:29
  128.7 3.8 %collective-permute-done.22 = bf16[128,768]{1,0:T(8,128)(2,1)S(1)} collective-permute-done((bf16[128,768]{1,0:T(8,128)(2,1)S(1)}, bf16[128,768]{1,0:T(8,128)(2,1)S(1)}, u32[]{:S(2)}, u32[]{:S(2)}) %collective-permute-start.22) | collective-permute-done | bytes 196640 | tf_op jit(solution)/shard_map/ppermute | solution.py:29
  132.6 2.8 %collective-permute-done.23.refs_5_ = bf16[768,768]{1,0:T(8,128)(2,1)S(1)} collective-permute-done((bf16[768,768]{1,0:T(8,128)(2,1)S(1)}, bf16[768,768]{1,0:T(8,128)(2,1)S(1)}, u32[]{:S(2)}, u32[]{:S(2)}) %collective-permute-start.23) | collective-permute-done | bytes 1179680 | tf_op jit(solution)/shard_map/ppermute | solution.py:29
  135.4 7.0 %gram_last.1 = f32[32,192]{1,0:T(8,128)S(1)} custom-call(s32[2]{0:T(128)S(1)} %pad_add_fusion.me_ref, bf16[384,768]{1,0:T(8,128)(2,1)S(1)} %get-tuple-element.128.refs_0_, bf16[384,768]{1,0:T(8,128)(2,1)S(1)} %get-tuple-element.50.refs_1_, bf16[384,768]{1,0:T(8,128)(2,1)S(1)} %get-tuple-element.110.refs_2_, bf16[384,768]{1,0:T(8,128)(2,1)S(1)} %get-tuple-element.116.refs_3_, ...), custom_call_target="tpu_custom_call" | custom-call | flops 3623878656 | bytes 4718592 | tf_op jit(solution)/shard_map/gram_last/pallas_call | solution.py:227
  142.5 12.0 %all_to_all.11 = f32[32,1,192]{2,1,0:T(1,128)S(1)} all-to-all(f32[32,1,192]{2,1,0:T(1,128)S(1)} %copy.3), channel_id=1, replica_groups=mesh['grp'=8,'blk'=4] {'grp','blk'}, dimensions={0} | all-to-all | bytes 49152 | tf_op jit(solution)/shard_map/all_to_all | solution.py:366
  155.1 2.3 %pick_rows.1 = f32[6,128]{1,0:T(8,128)} custom-call(s32[6,128]{1,0:T(8,128)} %bitcast.9, f32[32,192]{1,0:T(8,128)} %bitcast.12), custom_call_target="tpu_custom_call" | custom-call | tf_op jit(solution)/shard_map/pick_rows/pallas_call | solution.py:267
  (78 shorter events, 23.5 us)
Async XLA Ops:
  5.9 45.9 %collective-permute-start.4 = (bf16[576,768]{1,0:T(8,128)(2,1)S(1)}, bf16[576,768]{1,0:T(8,128)(2,1)S(1)}, u32[]{:S(2)}, u32[]{:S(2)}) collective-permute-start(bf16[576,768]{1,0:T(8,128)(2,1)S(1)} %get-tuple-element.39), channel_id=1, source_target_pairs={{0,4},{4,0},{8,12},{12,8},{16,20},{20,16},{24,28},{28,24},{1,5},{5... | collective-permute-start | bytes 2654216 | tf_op jit(solution)/shard_map/ppermute | solution.py:29
  8.9 26.0 %collective-permute-start = (bf16[192,768]{1,0:T(8,128)(2,1)S(1)}, bf16[192,768]{1,0:T(8,128)(2,1)S(1)}, u32[]{:S(2)}, u32[]{:S(2)}) collective-permute-start(bf16[192,768]{1,0:T(8,128)(2,1)S(1)} %get-tuple-element.37), channel_id=1, source_target_pairs={{0,4},{4,0},{8,12},{12,8},{16,20},{20,16},{24,28},{28,24},{1,5},{5... | collective-permute-start | bytes 884744 | tf_op jit(solution)/shard_map/ppermute | solution.py:29
  35.0 6.9 %collective-permute-start.1 = (bf16[96,768]{1,0:T(8,128)(2,1)S(1)}, bf16[96,768]{1,0:T(8,128)(2,1)S(1)}, u32[]{:S(2)}, u32[]{:S(2)}) collective-permute-start(bf16[96,768]{1,0:T(8,128)(2,1)S(1)} %pad_maximum_fusion.8), channel_id=1, source_target_pairs={{0,8},{4,12},{8,0},{12,4},{16,24},{20,28},{24,16},{28,20},{1,9},{5... | collective-permute-start | bytes 442376 | tf_op jit(solution)/shard_map/ppermute | solution.py:29
  36.8 13.3 %collective-permute-start.2 = (bf16[96,768]{1,0:T(8,128)(2,1)S(1)}, bf16[96,768]{1,0:T(8,128)(2,1)S(1)}, u32[]{:S(2)}, u32[]{:S(2)}) collective-permute-start(bf16[96,768]{1,0:T(8,128)(2,1)S(1)} %pad_maximum_fusion.9), channel_id=1, source_target_pairs={{0,16},{4,20},{8,24},{12,28},{16,0},{20,4},{24,8},{28,12},{1,17},{... | collective-permute-start | bytes 442376 | tf_op jit(solution)/shard_map/ppermute | solution.py:29
  39.5 10.7 %collective-permute-start.3 = (bf16[96,768]{1,0:T(8,128)(2,1)S(1)}, bf16[96,768]{1,0:T(8,128)(2,1)S(1)}, u32[]{:S(2)}, u32[]{:S(2)}) collective-permute-start(bf16[96,768]{1,0:T(8,128)(2,1)S(1)} %pad_maximum_fusion.10), channel_id=1, source_target_pairs={{0,24},{4,28},{8,16},{12,20},{16,8},{20,12},{24,0},{28,4},{1,25},{... | collective-permute-start | bytes 442376 | tf_op jit(solution)/shard_map/ppermute | solution.py:29
  50.3 14.3 %collective-permute-start.10 = (bf16[384,768]{1,0:T(8,128)(2,1)S(1)}, bf16[384,768]{1,0:T(8,128)(2,1)S(1)}, u32[]{:S(2)}, u32[]{:S(2)}) collective-permute-start(bf16[384,768]{1,0:T(8,128)(2,1)S(1)} %get-tuple-element.128.refs_0_), channel_id=1, source_target_pairs={{0,2},{1,3},{2,0},{3,1},{4,6},{5,7},{6,4},{7,5},{8,10},{9,11},{10,... | collective-permute-start | bytes 1769480 | tf_op jit(solution)/shard_map/ppermute | solution.py:29
  51.8 11.1 %collective-permute-start.6 = (bf16[96,768]{1,0:T(8,128)(2,1)S(1)}, bf16[96,768]{1,0:T(8,128)(2,1)S(1)}, u32[]{:S(2)}, u32[]{:S(2)}) collective-permute-start(bf16[96,768]{1,0:T(8,128)(2,1)S(1)} %pad_maximum_fusion.12), channel_id=1, source_target_pairs={{0,16},{4,20},{8,24},{12,28},{16,0},{20,4},{24,8},{28,12},{1,17},{... | collective-permute-start | bytes 442376 | tf_op jit(solution)/shard_map/ppermute | solution.py:29
  55.0 6.9 %collective-permute-start.5 = (bf16[96,768]{1,0:T(8,128)(2,1)S(1)}, bf16[96,768]{1,0:T(8,128)(2,1)S(1)}, u32[]{:S(2)}, u32[]{:S(2)}) collective-permute-start(bf16[96,768]{1,0:T(8,128)(2,1)S(1)} %pad_maximum_fusion.11), channel_id=1, source_target_pairs={{0,8},{4,12},{8,0},{12,4},{16,24},{20,28},{24,16},{28,20},{1,9},{5... | collective-permute-start | bytes 442376 | tf_op jit(solution)/shard_map/ppermute | solution.py:29
  55.2 9.3 %collective-permute-start.7 = (bf16[96,768]{1,0:T(8,128)(2,1)S(1)}, bf16[96,768]{1,0:T(8,128)(2,1)S(1)}, u32[]{:S(2)}, u32[]{:S(2)}) collective-permute-start(bf16[96,768]{1,0:T(8,128)(2,1)S(1)} %pad_maximum_fusion.13), channel_id=1, source_target_pairs={{0,24},{4,28},{8,16},{12,20},{16,8},{20,12},{24,0},{28,4},{1,25},{... | collective-permute-start | bytes 442376 | tf_op jit(solution)/shard_map/ppermute | solution.py:29
  64.6 12.0 %collective-permute-start.15 = (bf16[384,768]{1,0:T(8,128)(2,1)S(1)}, bf16[384,768]{1,0:T(8,128)(2,1)S(1)}, u32[]{:S(2)}, u32[]{:S(2)}) collective-permute-start(bf16[384,768]{1,0:T(8,128)(2,1)S(1)} %get-tuple-element.50.refs_1_), channel_id=1, source_target_pairs={{0,2},{1,3},{2,0},{3,1},{4,6},{5,7},{6,4},{7,5},{8,10},{9,11},{10,... | collective-permute-start | bytes 1769480 | tf_op jit(solution)/shard_map/ppermute | solution.py:29
  65.3 30.9 %collective-permute-start.12 = (bf16[768,768]{1,0:T(8,128)(2,1)S(1)}, bf16[768,768]{1,0:T(8,128)(2,1)S(1)}, u32[]{:S(2)}, u32[]{:S(2)}) collective-permute-start(bf16[768,768]{1,0:T(8,128)(2,1)S(1)} %constant_dynamic-update-slice_fusion.15.refs_2_), channel_id=1, source_target_pairs={{0,1},{1,0},{2,3},{3,2},{4,5},{5,4},{6,7},{7,6},{8,9},{9,8},{10,11... | collective-permute-start | bytes 3538952 | tf_op jit(solution)/shard_map/ppermute | solution.py:29
  76.6 19.5 %collective-permute-start.16 = (bf16[768,768]{1,0:T(8,128)(2,1)S(1)}, bf16[768,768]{1,0:T(8,128)(2,1)S(1)}, u32[]{:S(2)}, u32[]{:S(2)}) collective-permute-start(bf16[768,768]{1,0:T(8,128)(2,1)S(1)} %constant_dynamic-update-slice_fusion.21.refs_4_), channel_id=1, source_target_pairs={{0,1},{1,0},{2,3},{3,2},{4,5},{5,4},{6,7},{7,6},{8,9},{9,8},{10,11... | collective-permute-start | bytes 3538952 | tf_op jit(solution)/shard_map/ppermute | solution.py:29
  76.8 10.0 %collective-permute-start.8 = (bf16[96,768]{1,0:T(8,128)(2,1)S(1)}, bf16[96,768]{1,0:T(8,128)(2,1)S(1)}, u32[]{:S(2)}, u32[]{:S(2)}) collective-permute-start(bf16[96,768]{1,0:T(8,128)(2,1)S(1)} %pad_maximum_fusion.14), channel_id=1, source_target_pairs={{0,8},{4,12},{8,0},{12,4},{16,24},{20,28},{24,16},{28,20},{1,9},{5... | collective-permute-start | bytes 442376 | tf_op jit(solution)/shard_map/ppermute | solution.py:29
  81.5 13.8 %collective-permute-start.9 = (bf16[96,768]{1,0:T(8,128)(2,1)S(1)}, bf16[96,768]{1,0:T(8,128)(2,1)S(1)}, u32[]{:S(2)}, u32[]{:S(2)}) collective-permute-start(bf16[96,768]{1,0:T(8,128)(2,1)S(1)} %pad_maximum_fusion.15), channel_id=1, source_target_pairs={{0,16},{4,20},{8,24},{12,28},{16,0},{20,4},{24,8},{28,12},{1,17},{... | collective-permute-start | bytes 442376 | tf_op jit(solution)/shard_map/ppermute | solution.py:29
  81.6 14.5 %collective-permute-start.11 = (bf16[96,768]{1,0:T(8,128)(2,1)S(1)}, bf16[96,768]{1,0:T(8,128)(2,1)S(1)}, u32[]{:S(2)}, u32[]{:S(2)}) collective-permute-start(bf16[96,768]{1,0:T(8,128)(2,1)S(1)} %pad_maximum_fusion.16), channel_id=1, source_target_pairs={{0,24},{4,28},{8,16},{12,20},{16,8},{20,12},{24,0},{28,4},{1,25},{... | collective-permute-start | bytes 442376 | tf_op jit(solution)/shard_map/ppermute | solution.py:29
  95.3 12.5 %collective-permute-start.18 = (bf16[256,768]{1,0:T(8,128)(2,1)S(1)}, bf16[256,768]{1,0:T(8,128)(2,1)S(1)}, u32[]{:S(2)}, u32[]{:S(2)}) collective-permute-start(bf16[256,768]{1,0:T(8,128)(2,1)S(1)} %pad_maximum_fusion), channel_id=1, source_target_pairs={{0,2},{1,3},{2,0},{3,1},{4,6},{5,7},{6,4},{7,5},{8,10},{9,11},{10,... | collective-permute-start | bytes 1179656 | tf_op jit(solution)/shard_map/ppermute | solution.py:29
  102.0 7.7 %collective-permute-start.19 = (bf16[128,768]{1,0:T(8,128)(2,1)S(1)}, bf16[128,768]{1,0:T(8,128)(2,1)S(1)}, u32[]{:S(2)}, u32[]{:S(2)}) collective-permute-start(bf16[128,768]{1,0:T(8,128)(2,1)S(1)} %pad_maximum_fusion.7), channel_id=1, source_target_pairs={{0,2},{1,3},{2,0},{3,1},{4,6},{5,7},{6,4},{7,5},{8,10},{9,11},{10,... | collective-permute-start | bytes 589832 | tf_op jit(solution)/shard_map/ppermute | solution.py:29
  103.4 11.6 %collective-permute-start.14 = (bf16[96,768]{1,0:T(8,128)(2,1)S(1)}, bf16[96,768]{1,0:T(8,128)(2,1)S(1)}, u32[]{:S(2)}, u32[]{:S(2)}) collective-permute-start(bf16[96,768]{1,0:T(8,128)(2,1)S(1)} %pad_maximum_fusion.18), channel_id=1, source_target_pairs={{0,16},{4,20},{8,24},{12,28},{16,0},{20,4},{24,8},{28,12},{1,17},{... | collective-permute-start | bytes 442376 | tf_op jit(solution)/shard_map/ppermute | solution.py:29
  104.3 10.6 %collective-permute-start.13 = (bf16[96,768]{1,0:T(8,128)(2,1)S(1)}, bf16[96,768]{1,0:T(8,128)(2,1)S(1)}, u32[]{:S(2)}, u32[]{:S(2)}) collective-permute-start(bf16[96,768]{1,0:T(8,128)(2,1)S(1)} %pad_maximum_fusion.17), channel_id=1, source_target_pairs={{0,8},{4,12},{8,0},{12,4},{16,24},{20,28},{24,16},{28,20},{1,9},{5... | collective-permute-start | bytes 442376 | tf_op jit(solution)/shard_map/ppermute | solution.py:29
  105.1 11.5 %collective-permute-start.17 = (bf16[96,768]{1,0:T(8,128)(2,1)S(1)}, bf16[96,768]{1,0:T(8,128)(2,1)S(1)}, u32[]{:S(2)}, u32[]{:S(2)}) collective-permute-start(bf16[96,768]{1,0:T(8,128)(2,1)S(1)} %pad_maximum_fusion.19), channel_id=1, source_target_pairs={{0,24},{4,28},{8,16},{12,20},{16,8},{20,12},{24,0},{28,4},{1,25},{... | collective-permute-start | bytes 442376 | tf_op jit(solution)/shard_map/ppermute | solution.py:29
  116.6 2.8 %collective-permute-start.21 = (bf16[768,768]{1,0:T(8,128)(2,1)S(1)}, bf16[768,768]{1,0:T(8,128)(2,1)S(1)}, u32[]{:S(2)}, u32[]{:S(2)}) collective-permute-start(bf16[768,768]{1,0:T(8,128)(2,1)S(1)} %constant_dynamic-update-slice_fusion.32.refs_3_), channel_id=1, source_target_pairs={{0,1},{1,0},{2,3},{3,2},{4,5},{5,4},{6,7},{7,6},{8,9},{9,8},{10,11... | collective-permute-start | bytes 3538952 | tf_op jit(solution)/shard_map/ppermute | solution.py:29
  116.7 12.0 %collective-permute-start.20 = (bf16[256,768]{1,0:T(8,128)(2,1)S(1)}, bf16[256,768]{1,0:T(8,128)(2,1)S(1)}, u32[]{:S(2)}, u32[]{:S(2)}) collective-permute-start(bf16[256,768]{1,0:T(8,128)(2,1)S(1)} %pad_maximum_fusion.3), channel_id=1, source_target_pairs={{0,2},{1,3},{2,0},{3,1},{4,6},{5,7},{6,4},{7,5},{8,10},{9,11},{10,... | collective-permute-start | bytes 1179656 | tf_op jit(solution)/shard_map/ppermute | solution.py:29
  123.8 8.7 %collective-permute-start.22 = (bf16[128,768]{1,0:T(8,128)(2,1)S(1)}, bf16[128,768]{1,0:T(8,128)(2,1)S(1)}, u32[]{:S(2)}, u32[]{:S(2)}) collective-permute-start(bf16[128,768]{1,0:T(8,128)(2,1)S(1)} %pad_maximum_fusion.6), channel_id=1, source_target_pairs={{0,2},{1,3},{2,0},{3,1},{4,6},{5,7},{6,4},{7,5},{8,10},{9,11},{10,... | collective-permute-start | bytes 589832 | tf_op jit(solution)/shard_map/ppermute | solution.py:29
  132.5 2.9 %collective-permute-start.23 = (bf16[768,768]{1,0:T(8,128)(2,1)S(1)}, bf16[768,768]{1,0:T(8,128)(2,1)S(1)}, u32[]{:S(2)}, u32[]{:S(2)}) collective-permute-start(bf16[768,768]{1,0:T(8,128)(2,1)S(1)} %constant_dynamic-update-slice_fusion.39.refs_4_), channel_id=1, source_target_pairs={{0,1},{1,0},{2,3},{3,2},{4,5},{5,4},{6,7},{7,6},{8,9},{9,8},{10,11... | collective-permute-start | bytes 3538952 | tf_op jit(solution)/shard_map/ppermute | solution.py:29
  (2 other events, 2.0 us)

commit v9 on v8

--- a/solution.py
+++ b/solution.py
@@ -294,7 +294,7 @@
 
     def block(step, z):
         size = chunks[step]
-        near = sent["y", 0] if step == 0 else sent["y", 1]
+        near = first_near if step == 0 else sent["y", 2]
         skip = sum(chunks[1:step]) * high
         return jnp.concatenate(
             [rows(keeps[step], z, size), rows(near[skip:], z, size)], axis=0
@@ -322,7 +322,7 @@
         parts = [name for name in sent if name[:2] == ("x", step - 1)]
         for part in range(len(cuts) - 1):
             value = owns[step][cuts[part] : cuts[part + 1]]
-            early = parts if part == 0 else between
+            early = parts if part == 0 else between[part - 1]
             send(("x", step, part), value, "blk", members, 2, *early)
 
     def send_c(step, *early):
@@ -340,27 +340,26 @@
         )
 
     far = [high // 2] + [z for z in range(1, high) if z != high // 2]
-    send(("y", 0), first_send, "grp", groups, 1)
-    send(("y", 1), rest_send, "grp", groups, 1)
+    cut = first_send.shape[0] // 32 * 16
+    done["rest"] = rest_send
+    send(("y", 0), first_send[:cut], "grp", groups, 1)
+    send(("y", 1), first_send[cut:], "grp", groups, 1, "rest")
+    send(("y", 2), rest_send, "grp", groups, 1, ("y", 0))
+    first_near = jnp.concatenate([sent["y", 0], sent["y", 1]], axis=0)
     for z in far:
         send_z(0, z)
     for step in range(1, count):
         collect(step - 1)
-        if step < last:
-            for z in far:
-                send_z(step, z)
-            send_x(step - 1, [], [])
-            send_c(step - 1)
-    for z in far:
-        send_z(last, z)
+        for z in far:
+            send_z(step, z)
+        send_x(step - 1, [], [])
+        send_c(step - 1, *[("z", step, z) for z in far])
     collect(last)
     states, cols = gram(0, last - 2, [], [])
     done["gram", 0] = cols[-1]
-    send_x(last - 1, [256], [("gram", 0)])
-    send_c(last - 1, *[("z", last, z) for z in far])
     states, cols = gram(last - 1, last - 1, states, cols)
     done["gram", 1] = cols[-1]
-    send_x(last, [256], [("gram", 1)])
+    send_x(last, [208, 352], [[("gram", 0), ("c", last - 1)], [("gram", 1)]])
     send_c(last)
     result = gram(last, last, states, cols)
     homeward = lax.all_to_all(result, ("grp", "blk"), 0, 0, tiled=True)

time: 158 us -> 123 us (0.78)
  waiting for transfers between devices: 85.9 us -> 52.2 us
    ppermute x24 -> x25, waiting for transfers between devices: 85.9 us -> 52.2 us  [swap(): return lax.ppermute(value, axis, [(i, i ^ bit) for i in range(size)])]
    ppermute x24 -> x25, starting transfers between devices: 32.3 us -> 31.9 us  [swap(): return lax.ppermute(value, axis, [(i, i ^ bit) for i in range(size)])]
  transfers between devices with their start and end apart: 24 -> 25, of which waited for: 16 -> 13; matrix products, arithmetic and copies ran while one was open for 1% -> 1% of each run, Pallas kernels for 6% -> 10%
where the time goes in v9:
time: 123 us
  waiting for transfers between devices  52.2 us (42%)
  starting transfers between devices  31.9 us (26%)
  Pallas kernels  23.5 us (19%)
  blocking collectives  11.5 us (9%)
  local copies, waits for them, and re-layouts  3.26 us (3%)
    ppermute x25, waiting for transfers between devices, swap(): return lax.ppermute(value, axis, [(i, i ^ bit) for i in range(size)])  52.2 us
    ppermute x25, starting transfers between devices, swap(): return lax.ppermute(value, axis, [(i, i ^ bit) for i in range(size)])  31.9 us
    all_to_all x1, blocking collectives, on_device(): homeward = lax.all_to_all(result, ('grp', 'blk'), 0, 0, tiled=True)  11.5 us
    pallas_call x2, Pallas kernels, gram_step(): pl.pallas_call(functools.partial(gram_kernel, first, step, tile), in_spec...  10.2 us
    pallas_call x1, Pallas kernels, gram_step(): pl.pallas_call(functools.partial(gram_last_kernel, step, relatives, chunk...  7.03 us
    unnamed x23, local copies, waits for them, and re-layouts  3.03 us
    pallas_call x1, Pallas kernels, head(): pl.pallas_call(functools.partial(rest_kernel, capacity, chunks, groups),...  2.61 us
  transfers between devices with their start and end apart: 25, of which 13 were waited for; matrix products, arithmetic and copies ran while one was open for 1% of the time, Pallas kernels for 10%

profile of v9, /device:TPU:0, one launch (start us, length us, event | category | flops | bytes accessed | tf_op | source)
XLA Modules:
  0.0 122.9 jit_solution(15092724027373199063)
XLA Ops:
  3.3 3.0 %collective-permute-start = (bf16[96,768]{1,0:T(8,128)(2,1)S(1)}, bf16[96,768]{1,0:T(8,128)(2,1)S(1)}, u32[]{:S(2)}, u32[]{:S(2)}) collective-permute-start(bf16[96,768]{1,0:T(8,128)(2,1)S(1)} %get-tuple-element.111), channel_id=1, source_target_pairs={{0,4},{4,0},{8,12},{12,8},{16,20},{20,16},{24,28},{28,24},{1,5},{5... | collective-permute-start | bytes 442376 | tf_op jit(solution)/shard_map/ppermute | solution.py:29
  6.4 2.6 %place_rest.1 = (bf16[192,768]{1,0:T(8,128)(2,1)S(1)}, bf16[192,768]{1,0:T(8,128)(2,1)S(1)}, bf16[192,768]{1,0:T(8,128)(2,1)S(1)}, bf16[192,768]{1,0:T(8,128)(2,1)S(1)}, bf16[576,768]{1,0:T(8,128)(2,1)S(1)}) custom-call(s32[2]{0:T(128)S(1)} %pad_add_fusion.me_ref, s32[6,128]{1,0:T(8,128)S(1)} %bitcast.11, bf16[768,768]{1,0:T(8,128)(2,1)S(1)} %get-tuple-element.39.normed_ref), custom_call_target="tpu_custom_call" | custom-call | flops 1585446912 | bytes 3244032 | tf_op jit(solution)/shard_map/place_rest/pallas_call | solution.py:101
  10.2 2.1 %collective-permute-start.5 = (bf16[576,768]{1,0:T(8,128)(2,1)S(1)}, bf16[576,768]{1,0:T(8,128)(2,1)S(1)}, u32[]{:S(2)}, u32[]{:S(2)}) collective-permute-start(bf16[576,768]{1,0:T(8,128)(2,1)S(1)} %get-tuple-element.45), channel_id=1, source_target_pairs={{0,4},{4,0},{8,12},{12,8},{16,20},{20,16},{24,28},{28,24},{1,5},{5... | collective-permute-start | bytes 2654216 | tf_op jit(solution)/shard_map/ppermute | solution.py:29
  13.8 2.0 %collective-permute-done.2 = bf16[96,768]{1,0:T(8,128)(2,1)S(1)} collective-permute-done((bf16[96,768]{1,0:T(8,128)(2,1)S(1)}, bf16[96,768]{1,0:T(8,128)(2,1)S(1)}, u32[]{:S(2)}, u32[]{:S(2)}) %collective-permute-start.2) | collective-permute-done | bytes 147488 | tf_op jit(solution)/shard_map/ppermute | solution.py:29
  15.9 2.6 %collective-permute-start.3 = (bf16[96,768]{1,0:T(8,128)(2,1)S(1)}, bf16[96,768]{1,0:T(8,128)(2,1)S(1)}, u32[]{:S(2)}, u32[]{:S(2)}) collective-permute-start(bf16[96,768]{1,0:T(8,128)(2,1)S(1)} %pad_maximum_fusion.5), channel_id=1, source_target_pairs={{0,16},{4,20},{8,24},{12,28},{16,0},{20,4},{24,8},{28,12},{1,17},{... | collective-permute-start | bytes 442376 | tf_op jit(solution)/shard_map/ppermute | solution.py:29
  20.0 7.8 %collective-permute-done.3 = bf16[96,768]{1,0:T(8,128)(2,1)S(1)} collective-permute-done((bf16[96,768]{1,0:T(8,128)(2,1)S(1)}, bf16[96,768]{1,0:T(8,128)(2,1)S(1)}, u32[]{:S(2)}, u32[]{:S(2)}) %collective-permute-start.3) | collective-permute-done | bytes 147488 | tf_op jit(solution)/shard_map/ppermute | solution.py:29
  29.3 4.0 %collective-permute-done.5 = bf16[576,768]{1,0:T(8,128)(2,1)S(1)} collective-permute-done((bf16[576,768]{1,0:T(8,128)(2,1)S(1)}, bf16[576,768]{1,0:T(8,128)(2,1)S(1)}, u32[]{:S(2)}, u32[]{:S(2)}) %collective-permute-start.5) | collective-permute-done | bytes 884768 | tf_op jit(solution)/shard_map/ppermute | solution.py:29
  35.1 2.7 %collective-permute-start.7 = (bf16[96,768]{1,0:T(8,128)(2,1)S(1)}, bf16[96,768]{1,0:T(8,128)(2,1)S(1)}, u32[]{:S(2)}, u32[]{:S(2)}) collective-permute-start(bf16[96,768]{1,0:T(8,128)(2,1)S(1)} %pad_maximum_fusion.8), channel_id=1, source_target_pairs={{0,16},{4,20},{8,24},{12,28},{16,0},{20,4},{24,8},{28,12},{1,17},{... | collective-permute-start | bytes 442376 | tf_op jit(solution)/shard_map/ppermute | solution.py:29
  38.0 2.2 %collective-permute-done.6 = bf16[96,768]{1,0:T(8,128)(2,1)S(1)} collective-permute-done((bf16[96,768]{1,0:T(8,128)(2,1)S(1)}, bf16[96,768]{1,0:T(8,128)(2,1)S(1)}, u32[]{:S(2)}, u32[]{:S(2)}) %collective-permute-start.6) | collective-permute-done | bytes 147488 | tf_op jit(solution)/shard_map/ppermute | solution.py:29
  40.3 7.8 %collective-permute-done.7 = bf16[96,768]{1,0:T(8,128)(2,1)S(1)} collective-permute-done((bf16[96,768]{1,0:T(8,128)(2,1)S(1)}, bf16[96,768]{1,0:T(8,128)(2,1)S(1)}, u32[]{:S(2)}, u32[]{:S(2)}) %collective-permute-start.7) | collective-permute-done | bytes 147488 | tf_op jit(solution)/shard_map/ppermute | solution.py:29
  49.7 2.6 %collective-permute-start.12 = (bf16[96,768]{1,0:T(8,128)(2,1)S(1)}, bf16[96,768]{1,0:T(8,128)(2,1)S(1)}, u32[]{:S(2)}, u32[]{:S(2)}) collective-permute-start(bf16[96,768]{1,0:T(8,128)(2,1)S(1)} %pad_maximum_fusion.12), channel_id=1, source_target_pairs={{0,24},{4,28},{8,16},{12,20},{16,8},{20,12},{24,0},{28,4},{1,25},{... | collective-permute-start | bytes 442376 | tf_op jit(solution)/shard_map/ppermute | solution.py:29
  52.3 2.7 %collective-permute-start.10 = (bf16[96,768]{1,0:T(8,128)(2,1)S(1)}, bf16[96,768]{1,0:T(8,128)(2,1)S(1)}, u32[]{:S(2)}, u32[]{:S(2)}) collective-permute-start(bf16[96,768]{1,0:T(8,128)(2,1)S(1)} %pad_maximum_fusion.11), channel_id=1, source_target_pairs={{0,16},{4,20},{8,24},{12,28},{16,0},{20,4},{24,8},{28,12},{1,17},{... | collective-permute-start | bytes 442376 | tf_op jit(solution)/shard_map/ppermute | solution.py:29
  55.4 3.5 %collective-permute-done.16 = bf16[384,768]{1,0:T(8,128)(2,1)S(1)} collective-permute-done((bf16[384,768]{1,0:T(8,128)(2,1)S(1)}, bf16[384,768]{1,0:T(8,128)(2,1)S(1)}, u32[]{:S(2)}, u32[]{:S(2)}) %collective-permute-start.16) | collective-permute-done | bytes 589856 | tf_op jit(solution)/shard_map/ppermute | solution.py:29
  59.0 4.4 %collective-permute-done.10 = bf16[96,768]{1,0:T(8,128)(2,1)S(1)} collective-permute-done((bf16[96,768]{1,0:T(8,128)(2,1)S(1)}, bf16[96,768]{1,0:T(8,128)(2,1)S(1)}, u32[]{:S(2)}, u32[]{:S(2)}) %collective-permute-start.10) | collective-permute-done | bytes 147488 | tf_op jit(solution)/shard_map/ppermute | solution.py:29
  64.1 2.4 %collective-permute-start.15 = (bf16[96,768]{1,0:T(8,128)(2,1)S(1)}, bf16[96,768]{1,0:T(8,128)(2,1)S(1)}, u32[]{:S(2)}, u32[]{:S(2)}) collective-permute-start(bf16[96,768]{1,0:T(8,128)(2,1)S(1)} %pad_maximum_fusion.14), channel_id=1, source_target_pairs={{0,16},{4,20},{8,24},{12,28},{16,0},{20,4},{24,8},{28,12},{1,17},{... | collective-permute-start | bytes 442376 | tf_op jit(solution)/shard_map/ppermute | solution.py:29
  68.6 10.7 %collective-permute-done.19 = bf16[384,768]{1,0:T(8,128)(2,1)S(1)} collective-permute-done((bf16[384,768]{1,0:T(8,128)(2,1)S(1)}, bf16[384,768]{1,0:T(8,128)(2,1)S(1)}, u32[]{:S(2)}, u32[]{:S(2)}) %collective-permute-start.19) | collective-permute-done | bytes 589856 | tf_op jit(solution)/shard_map/ppermute | solution.py:29
  80.1 5.9 %gram_step.2 = (f32[384,128]{1,0:T(8,128)S(1)}, f32[384,128]{1,0:T(8,128)S(1)}, f32[1,1536]{1,0:T(1,128)S(1)}, f32[1,1536]{1,0:T(1,128)S(1)}) custom-call(bf16[384,768]{1,0:T(8,128)(2,1)S(1)} %get-tuple-element.131.refs_0_, bf16[384,768]{1,0:T(8,128)(2,1)S(1)} %get-tuple-element.57.refs_1_, ...), custom_call_target="tpu_custom_call" | custom-call | flops 1811939328 | bytes 3538944 | tf_op jit(solution)/shard_map/gram_step/pallas_call | solution.py:216
  86.0 3.4 %collective-permute-done.20 = bf16[208,768]{1,0:T(8,128)(2,1)S(1)} collective-permute-done((bf16[208,768]{1,0:T(8,128)(2,1)S(1)}, bf16[208,768]{1,0:T(8,128)(2,1)S(1)}, u32[]{:S(2)}, u32[]{:S(2)}) %collective-permute-start.20) | collective-permute-done | bytes 319520 | tf_op jit(solution)/shard_map/ppermute | solution.py:29
  90.1 4.4 %gram_step.3 = (f32[384,128]{1,0:T(8,128)S(1)}, f32[384,128]{1,0:T(8,128)S(1)}, f32[384,128]{1,0:T(8,128)S(1)}, f32[1,1536]{1,0:T(1,128)S(1)}) custom-call(bf16[384,768]{1,0:T(8,128)(2,1)S(1)} %get-tuple-element.131.refs_0_, bf16[384,768]{1,0:T(8,128)(2,1)S(1)} %get-tuple-element.57.refs_1_, bf16[384,768]{1,0:T(8,128)(2,1)S(1)} %get-tuple-element.60.refs_2_, ...), custom_call_target="tpu_custom_call" | custom-call | flops 2717908992 | bytes 4128768 | tf_op jit(solution)/shard_map/gram_step/pallas_call | solution.py:216
  96.6 2.0 %collective-permute-done.23 = bf16[32,768]{1,0:T(8,128)(2,1)S(1)} collective-permute-done((bf16[32,768]{1,0:T(8,128)(2,1)S(1)}, bf16[32,768]{1,0:T(8,128)(2,1)S(1)}, u32[]{:S(2)}, u32[]{:S(2)}) %collective-permute-start.23) | collective-permute-done | bytes 49184 | tf_op jit(solution)/shard_map/ppermute | solution.py:29
  98.6 2.8 %collective-permute-done.24.refs_5_ = bf16[768,768]{1,0:T(8,128)(2,1)S(1)} collective-permute-done((bf16[768,768]{1,0:T(8,128)(2,1)S(1)}, bf16[768,768]{1,0:T(8,128)(2,1)S(1)}, u32[]{:S(2)}, u32[]{:S(2)}) %collective-permute-start.24) | collective-permute-done | bytes 1179680 | tf_op jit(solution)/shard_map/ppermute | solution.py:29
  101.4 7.0 %gram_last.1 = f32[32,192]{1,0:T(8,128)S(1)} custom-call(s32[2]{0:T(128)S(1)} %pad_add_fusion.me_ref, bf16[384,768]{1,0:T(8,128)(2,1)S(1)} %get-tuple-element.131.refs_0_, bf16[384,768]{1,0:T(8,128)(2,1)S(1)} %get-tuple-element.57.refs_1_, bf16[384,768]{1,0:T(8,128)(2,1)S(1)} %get-tuple-element.60.refs_2_, bf16[384,768]{1,0:T(8,128)(2,1)S(1)} %get-tuple-element.119.refs_3_, ...), custom_call_target="tpu_custom_call" | custom-call | flops 3623878656 | bytes 4718592 | tf_op jit(solution)/shard_map/gram_last/pallas_call | solution.py:227
  108.5 11.5 %all_to_all.11 = f32[32,1,192]{2,1,0:T(1,128)S(1)} all-to-all(f32[32,1,192]{2,1,0:T(1,128)S(1)} %copy.3), channel_id=1, replica_groups=mesh['grp'=8,'blk'=4] {'grp','blk'}, dimensions={0} | all-to-all | bytes 49152 | tf_op jit(solution)/shard_map/all_to_all | solution.py:365
  120.6 2.3 %pick_rows.1 = f32[6,128]{1,0:T(8,128)} custom-call(s32[6,128]{1,0:T(8,128)} %bitcast.9, f32[32,192]{1,0:T(8,128)} %bitcast.12), custom_call_target="tpu_custom_call" | custom-call | tf_op jit(solution)/shard_map/pick_rows/pallas_call | solution.py:267
  (81 shorter events, 20.2 us)
Async XLA Ops:
  3.3 6.9 %collective-permute-start = (bf16[96,768]{1,0:T(8,128)(2,1)S(1)}, bf16[96,768]{1,0:T(8,128)(2,1)S(1)}, u32[]{:S(2)}, u32[]{:S(2)}) collective-permute-start(bf16[96,768]{1,0:T(8,128)(2,1)S(1)} %get-tuple-element.111), channel_id=1, source_target_pairs={{0,4},{4,0},{8,12},{12,8},{16,20},{20,16},{24,28},{28,24},{1,5},{5... | collective-permute-start | bytes 442376 | tf_op jit(solution)/shard_map/ppermute | solution.py:29
  9.0 6.8 %collective-permute-start.2 = (bf16[96,768]{1,0:T(8,128)(2,1)S(1)}, bf16[96,768]{1,0:T(8,128)(2,1)S(1)}, u32[]{:S(2)}, u32[]{:S(2)}) collective-permute-start(bf16[96,768]{1,0:T(8,128)(2,1)S(1)} %get-tuple-element.43), channel_id=1, source_target_pairs={{0,4},{4,0},{8,12},{12,8},{16,20},{20,16},{24,28},{28,24},{1,5},{5... | collective-permute-start | bytes 442376 | tf_op jit(solution)/shard_map/ppermute | solution.py:29
  10.2 23.1 %collective-permute-start.5 = (bf16[576,768]{1,0:T(8,128)(2,1)S(1)}, bf16[576,768]{1,0:T(8,128)(2,1)S(1)}, u32[]{:S(2)}, u32[]{:S(2)}) collective-permute-start(bf16[576,768]{1,0:T(8,128)(2,1)S(1)} %get-tuple-element.45), channel_id=1, source_target_pairs={{0,4},{4,0},{8,12},{12,8},{16,20},{20,16},{24,28},{28,24},{1,5},{5... | collective-permute-start | bytes 2654216 | tf_op jit(solution)/shard_map/ppermute | solution.py:29
  12.4 7.6 %collective-permute-start.1 = (bf16[96,768]{1,0:T(8,128)(2,1)S(1)}, bf16[96,768]{1,0:T(8,128)(2,1)S(1)}, u32[]{:S(2)}, u32[]{:S(2)}) collective-permute-start(bf16[96,768]{1,0:T(8,128)(2,1)S(1)} %pad_maximum_fusion.4), channel_id=1, source_target_pairs={{0,8},{4,12},{8,0},{12,4},{16,24},{20,28},{24,16},{28,20},{1,9},{5... | collective-permute-start | bytes 442376 | tf_op jit(solution)/shard_map/ppermute | solution.py:29
  15.9 11.9 %collective-permute-start.3 = (bf16[96,768]{1,0:T(8,128)(2,1)S(1)}, bf16[96,768]{1,0:T(8,128)(2,1)S(1)}, u32[]{:S(2)}, u32[]{:S(2)}) collective-permute-start(bf16[96,768]{1,0:T(8,128)(2,1)S(1)} %pad_maximum_fusion.5), channel_id=1, source_target_pairs={{0,16},{4,20},{8,24},{12,28},{16,0},{20,4},{24,8},{28,12},{1,17},{... | collective-permute-start | bytes 442376 | tf_op jit(solution)/shard_map/ppermute | solution.py:29
  18.5 9.2 %collective-permute-start.4 = (bf16[96,768]{1,0:T(8,128)(2,1)S(1)}, bf16[96,768]{1,0:T(8,128)(2,1)S(1)}, u32[]{:S(2)}, u32[]{:S(2)}) collective-permute-start(bf16[96,768]{1,0:T(8,128)(2,1)S(1)} %pad_maximum_fusion.6), channel_id=1, source_target_pairs={{0,24},{4,28},{8,16},{12,20},{16,8},{20,12},{24,0},{28,4},{1,25},{... | collective-permute-start | bytes 442376 | tf_op jit(solution)/shard_map/ppermute | solution.py:29
  27.8 20.4 %collective-permute-start.11 = (bf16[384,768]{1,0:T(8,128)(2,1)S(1)}, bf16[384,768]{1,0:T(8,128)(2,1)S(1)}, u32[]{:S(2)}, u32[]{:S(2)}) collective-permute-start(bf16[384,768]{1,0:T(8,128)(2,1)S(1)} %get-tuple-element.131.refs_0_), channel_id=1, source_target_pairs={{0,2},{1,3},{2,0},{3,1},{4,6},{5,7},{6,4},{7,5},{8,10},{9,11},{10,... | collective-permute-start | bytes 1769480 | tf_op jit(solution)/shard_map/ppermute | solution.py:29
  33.3 6.9 %collective-permute-start.6 = (bf16[96,768]{1,0:T(8,128)(2,1)S(1)}, bf16[96,768]{1,0:T(8,128)(2,1)S(1)}, u32[]{:S(2)}, u32[]{:S(2)}) collective-permute-start(bf16[96,768]{1,0:T(8,128)(2,1)S(1)} %pad_maximum_fusion.7), channel_id=1, source_target_pairs={{0,8},{4,12},{8,0},{12,4},{16,24},{20,28},{24,16},{28,20},{1,9},{5... | collective-permute-start | bytes 442376 | tf_op jit(solution)/shard_map/ppermute | solution.py:29
  35.1 13.0 %collective-permute-start.7 = (bf16[96,768]{1,0:T(8,128)(2,1)S(1)}, bf16[96,768]{1,0:T(8,128)(2,1)S(1)}, u32[]{:S(2)}, u32[]{:S(2)}) collective-permute-start(bf16[96,768]{1,0:T(8,128)(2,1)S(1)} %pad_maximum_fusion.8), channel_id=1, source_target_pairs={{0,16},{4,20},{8,24},{12,28},{16,0},{20,4},{24,8},{28,12},{1,17},{... | collective-permute-start | bytes 442376 | tf_op jit(solution)/shard_map/ppermute | solution.py:29
  37.8 10.3 %collective-permute-start.8 = (bf16[96,768]{1,0:T(8,128)(2,1)S(1)}, bf16[96,768]{1,0:T(8,128)(2,1)S(1)}, u32[]{:S(2)}, u32[]{:S(2)}) collective-permute-start(bf16[96,768]{1,0:T(8,128)(2,1)S(1)} %pad_maximum_fusion.9), channel_id=1, source_target_pairs={{0,24},{4,28},{8,16},{12,20},{16,8},{20,12},{24,0},{28,4},{1,25},{... | collective-permute-start | bytes 442376 | tf_op jit(solution)/shard_map/ppermute | solution.py:29
  48.1 10.8 %collective-permute-start.16 = (bf16[384,768]{1,0:T(8,128)(2,1)S(1)}, bf16[384,768]{1,0:T(8,128)(2,1)S(1)}, u32[]{:S(2)}, u32[]{:S(2)}) collective-permute-start(bf16[384,768]{1,0:T(8,128)(2,1)S(1)} %get-tuple-element.57.refs_1_), channel_id=1, source_target_pairs={{0,2},{1,3},{2,0},{3,1},{4,6},{5,7},{6,4},{7,5},{8,10},{9,11},{10,... | collective-permute-start | bytes 1769480 | tf_op jit(solution)/shard_map/ppermute | solution.py:29
  49.7 9.2 %collective-permute-start.12 = (bf16[96,768]{1,0:T(8,128)(2,1)S(1)}, bf16[96,768]{1,0:T(8,128)(2,1)S(1)}, u32[]{:S(2)}, u32[]{:S(2)}) collective-permute-start(bf16[96,768]{1,0:T(8,128)(2,1)S(1)} %pad_maximum_fusion.12), channel_id=1, source_target_pairs={{0,24},{4,28},{8,16},{12,20},{16,8},{20,12},{24,0},{28,4},{1,25},{... | collective-permute-start | bytes 442376 | tf_op jit(solution)/shard_map/ppermute | solution.py:29
  52.3 11.0 %collective-permute-start.10 = (bf16[96,768]{1,0:T(8,128)(2,1)S(1)}, bf16[96,768]{1,0:T(8,128)(2,1)S(1)}, u32[]{:S(2)}, u32[]{:S(2)}) collective-permute-start(bf16[96,768]{1,0:T(8,128)(2,1)S(1)} %pad_maximum_fusion.11), channel_id=1, source_target_pairs={{0,16},{4,20},{8,24},{12,28},{16,0},{20,4},{24,8},{28,12},{1,17},{... | collective-permute-start | bytes 442376 | tf_op jit(solution)/shard_map/ppermute | solution.py:29
  55.0 8.3 %collective-permute-start.9 = (bf16[96,768]{1,0:T(8,128)(2,1)S(1)}, bf16[96,768]{1,0:T(8,128)(2,1)S(1)}, u32[]{:S(2)}, u32[]{:S(2)}) collective-permute-start(bf16[96,768]{1,0:T(8,128)(2,1)S(1)} %pad_maximum_fusion.10), channel_id=1, source_target_pairs={{0,8},{4,12},{8,0},{12,4},{16,24},{20,28},{24,16},{28,20},{1,9},{5... | collective-permute-start | bytes 442376 | tf_op jit(solution)/shard_map/ppermute | solution.py:29
  55.3 8.8 %collective-permute-start.13 = (bf16[768,768]{1,0:T(8,128)(2,1)S(1)}, bf16[768,768]{1,0:T(8,128)(2,1)S(1)}, u32[]{:S(2)}, u32[]{:S(2)}) collective-permute-start(bf16[768,768]{1,0:T(8,128)(2,1)S(1)} %constant_dynamic-update-slice_fusion.15.refs_2_), channel_id=1, source_target_pairs={{0,1},{1,0},{2,3},{3,2},{4,5},{5,4},{6,7},{7,6},{8,9},{9,8},{10,11... | collective-permute-start | bytes 3538952 | tf_op jit(solution)/shard_map/ppermute | solution.py:29
  63.3 3.8 %collective-permute-start.17 = (bf16[768,768]{1,0:T(8,128)(2,1)S(1)}, bf16[768,768]{1,0:T(8,128)(2,1)S(1)}, u32[]{:S(2)}, u32[]{:S(2)}) collective-permute-start(bf16[768,768]{1,0:T(8,128)(2,1)S(1)} %constant_dynamic-update-slice_fusion.21.refs_4_), channel_id=1, source_target_pairs={{0,1},{1,0},{2,3},{3,2},{4,5},{5,4},{6,7},{7,6},{8,9},{9,8},{10,11... | collective-permute-start | bytes 3538952 | tf_op jit(solution)/shard_map/ppermute | solution.py:29
  63.4 15.8 %collective-permute-start.19 = (bf16[384,768]{1,0:T(8,128)(2,1)S(1)}, bf16[384,768]{1,0:T(8,128)(2,1)S(1)}, u32[]{:S(2)}, u32[]{:S(2)}) collective-permute-start(bf16[384,768]{1,0:T(8,128)(2,1)S(1)} %get-tuple-element.60.refs_2_), channel_id=1, source_target_pairs={{0,2},{1,3},{2,0},{3,1},{4,6},{5,7},{6,4},{7,5},{8,10},{9,11},{10,... | collective-permute-start | bytes 1769480 | tf_op jit(solution)/shard_map/ppermute | solution.py:29
  64.1 15.2 %collective-permute-start.15 = (bf16[96,768]{1,0:T(8,128)(2,1)S(1)}, bf16[96,768]{1,0:T(8,128)(2,1)S(1)}, u32[]{:S(2)}, u32[]{:S(2)}) collective-permute-start(bf16[96,768]{1,0:T(8,128)(2,1)S(1)} %pad_maximum_fusion.14), channel_id=1, source_target_pairs={{0,16},{4,20},{8,24},{12,28},{16,0},{20,4},{24,8},{28,12},{1,17},{... | collective-permute-start | bytes 442376 | tf_op jit(solution)/shard_map/ppermute | solution.py:29
  66.5 12.8 %collective-permute-start.14 = (bf16[96,768]{1,0:T(8,128)(2,1)S(1)}, bf16[96,768]{1,0:T(8,128)(2,1)S(1)}, u32[]{:S(2)}, u32[]{:S(2)}) collective-permute-start(bf16[96,768]{1,0:T(8,128)(2,1)S(1)} %pad_maximum_fusion.13), channel_id=1, source_target_pairs={{0,8},{4,12},{8,0},{12,4},{16,24},{20,28},{24,16},{28,20},{1,9},{5... | collective-permute-start | bytes 442376 | tf_op jit(solution)/shard_map/ppermute | solution.py:29
  67.1 12.2 %collective-permute-start.18 = (bf16[96,768]{1,0:T(8,128)(2,1)S(1)}, bf16[96,768]{1,0:T(8,128)(2,1)S(1)}, u32[]{:S(2)}, u32[]{:S(2)}) collective-permute-start(bf16[96,768]{1,0:T(8,128)(2,1)S(1)} %pad_maximum_fusion.15), channel_id=1, source_target_pairs={{0,24},{4,28},{8,16},{12,20},{16,8},{20,12},{24,0},{28,4},{1,25},{... | collective-permute-start | bytes 442376 | tf_op jit(solution)/shard_map/ppermute | solution.py:29
  79.3 10.1 %collective-permute-start.21 = (bf16[768,768]{1,0:T(8,128)(2,1)S(1)}, bf16[768,768]{1,0:T(8,128)(2,1)S(1)}, u32[]{:S(2)}, u32[]{:S(2)}) collective-permute-start(bf16[768,768]{1,0:T(8,128)(2,1)S(1)} %constant_dynamic-update-slice_fusion.32.refs_3_), channel_id=1, source_target_pairs={{0,1},{1,0},{2,3},{3,2},{4,5},{5,4},{6,7},{7,6},{8,9},{9,8},{10,11... | collective-permute-start | bytes 3538952 | tf_op jit(solution)/shard_map/ppermute | solution.py:29
  79.4 10.0 %collective-permute-start.20 = (bf16[208,768]{1,0:T(8,128)(2,1)S(1)}, bf16[208,768]{1,0:T(8,128)(2,1)S(1)}, u32[]{:S(2)}, u32[]{:S(2)}) collective-permute-start(bf16[208,768]{1,0:T(8,128)(2,1)S(1)} %pad_maximum_fusion), channel_id=1, source_target_pairs={{0,2},{1,3},{2,0},{3,1},{4,6},{5,7},{6,4},{7,5},{8,10},{9,11},{10,... | collective-permute-start | bytes 958472 | tf_op jit(solution)/shard_map/ppermute | solution.py:29
  89.5 7.1 %collective-permute-start.22 = (bf16[144,768]{1,0:T(8,128)(2,1)S(1)}, bf16[144,768]{1,0:T(8,128)(2,1)S(1)}, u32[]{:S(2)}, u32[]{:S(2)}) collective-permute-start(bf16[144,768]{1,0:T(8,128)(2,1)S(1)} %pad_maximum_fusion.3), channel_id=1, source_target_pairs={{0,2},{1,3},{2,0},{3,1},{4,6},{5,7},{6,4},{7,5},{8,10},{9,11},{10,... | collective-permute-start | bytes 663560 | tf_op jit(solution)/shard_map/ppermute | solution.py:29
  94.4 4.2 %collective-permute-start.23 = (bf16[32,768]{1,0:T(8,128)(2,1)S(1)}, bf16[32,768]{1,0:T(8,128)(2,1)S(1)}, u32[]{:S(2)}, u32[]{:S(2)}) collective-permute-start(bf16[32,768]{1,0:T(8,128)(2,1)S(1)} %slice.182), channel_id=1, source_target_pairs={{0,2},{1,3},{2,0},{3,1},{4,6},{5,7},{6,4},{7,5},{8,10},{9,11},{10,... | collective-permute-start | bytes 147464 | tf_op jit(solution)/shard_map/ppermute | solution.py:29
  (3 other events, 4.8 us)

commit v10 on v9

--- a/solution.py
+++ b/solution.py
@@ -57,16 +57,16 @@
 
 
 def rest_kernel(capacity, chunks, groups, me_ref, slot_ref, normed_ref, *out_refs):
-    keeps, send_ref = out_refs[:-1], out_refs[-1]
+    keeps, send_refs = out_refs[:-2], out_refs[-2:]
     slots, normed = flat(slot_ref), normed_ref[...]
     first, row = 0, 0
     for step, size in enumerate(chunks):
-        if step > 0:
-            count = groups // 2 * size
-            send_ref[row : row + count, :] = place(
-                me_ref[0], slots, normed, capacity, first, size, groups, 1
-            )
-            row += count
+        placed = place(me_ref[0], slots, normed, capacity, first, size, groups, 1) if step else None
+        if step == 1:
+            send_refs[0][...] = placed
+        elif step > 1:
+            send_refs[1][row : row + placed.shape[0], :] = placed
+            row += placed.shape[0]
         first += size
     first = 0
     for step, size in enumerate(chunks):
@@ -98,16 +98,16 @@
         cost_estimate=cost(half[0]),
         name="place_first",
     )(me, slots, embeddings)
-    *keeps, rest_send = pl.pallas_call(
+    *keeps, next_send, rest_send = pl.pallas_call(
         functools.partial(rest_kernel, capacity, chunks, groups),
         in_specs=[smem, vmem, vmem],
-        out_specs=[vmem] * (len(chunks) + 1),
-        out_shape=[shape(count) for count in half] + [shape(sum(half[1:]))],
+        out_specs=[vmem] * (len(chunks) + 2),
+        out_shape=[shape(count) for count in half + [half[1], sum(half[2:])]],
         compiler_params=params,
         cost_estimate=cost(2 * sum(half) - half[0]),
         name="place_rest",
     )(me, slots, normed)
-    return keeps, first_send, rest_send
+    return keeps, first_send, next_send, rest_send
 
 
 def lane_fold(values):
@@ -117,19 +117,14 @@
     return best
 
 
-def gram_body(own_refs, piece_refs, row_refs, col_ref, stack, tile):
+def gram_body(own_refs, piece_ref, row_refs, col_ref, col_start, holds_own):
     step = len(own_refs) - 1
-    start = 0
-    for piece_ref in piece_refs:
-        stack[start : start + piece_ref.shape[0], :] = piece_ref[...]
-        start += piece_ref.shape[0]
-    row_refs[step][...] = jnp.full(row_refs[step].shape, sentinel, jnp.float32)
+    tile = 256
     nt = (((1,), (1,)), ((), ()))
-
-    @pl.loop(0, stack.shape[0] // tile)
-    def _(n):
-        first = pl.multiple_of(n * tile, tile)
-        x = stack[pl.ds(first, tile), :]
+    if holds_own:
+        row_refs[step][...] = jnp.full(row_refs[step].shape, sentinel, jnp.float32)
+    for first in range(0, piece_ref.shape[0], tile):
+        x = piece_ref[first : first + tile, :]
         marks = x[:, :lanes].astype(jnp.float32).T[0:1, :]
         col_bias = jnp.where(marks > 1.5, dead_bias, 0.0)
         col_best = jnp.full((1, tile), sentinel, jnp.float32)
@@ -138,50 +133,54 @@
             scores = lax.dot_general(own, x, nt, preferred_element_type=jnp.float32)
             usable = scores + col_bias
             if j == step:
-                rows = lax.broadcasted_iota(jnp.int32, usable.shape, 0)
-                cols = lax.broadcasted_iota(jnp.int32, usable.shape, 1)
-                usable = jnp.where(rows - cols == first, dead_bias, usable)
+                if holds_own and first < own.shape[0]:
+                    rows = lax.broadcasted_iota(jnp.int32, usable.shape, 0)
+                    cols = lax.broadcasted_iota(jnp.int32, usable.shape, 1)
+                    usable = jnp.where(rows - cols == first, dead_bias, usable)
             else:
                 row_bias = jnp.where(own[:, 0:1].astype(jnp.float32) > 1.5, dead_bias, 0.0)
                 col_best = jnp.maximum(
                     col_best, jnp.max(scores + row_bias, axis=0, keepdims=True)
                 )
             row_refs[j][...] = jnp.maximum(row_refs[j][...], lane_fold(usable))
-        col_ref[0:1, pl.ds(first, tile)] = col_best
-
-
-def gram_kernel(first, step, tile, *refs):
+        col_ref[0:1, col_start + first : col_start + first + tile] = col_best
+
+
+def gram_kernel(first, step, pieces, *refs):
     news = step + 1 - first
     owns, refs = refs[: step + 1], refs[step + 1 :]
-    pieces, refs = refs[: 2 * news], refs[2 * news :]
+    blocks, refs = refs[: pieces * news], refs[pieces * news :]
     states, refs = refs[:first], refs[first:]
-    rows, cols, stack = refs[: step + 1], refs[step + 1 : -1], refs[-1]
+    rows, cols = refs[: step + 1], refs[step + 1 :]
     for state, row in zip(states, rows):
         row[...] = state[...]
     for k in range(news):
         now = first + k + 1
-        gram_body(owns[:now], pieces[2 * k : 2 * k + 2], rows[:now], cols[k], stack, tile)
-
-
-def gram_last_kernel(step, relatives, chunks, groups, tile, me_ref, *refs):
+        for p in range(pieces):
+            block = blocks[pieces * k + p]
+            start = p * block.shape[0]
+            gram_body(owns[:now], block, rows[:now], cols[k], start, p == 0)
+
+
+def gram_last_kernel(step, relatives, chunks, groups, me_ref, *refs):
     members = len(relatives)
-    owns, pieces, refs = refs[: step + 1], refs[step + 1 : step + 3], refs[step + 3 :]
-    states, refs = refs[:step], refs[step:]
-    cols, refs = refs[:step], refs[step:]
-    out_ref, stack, col, table = refs[:4]
-    rows = refs[4:]
+    owns, block, refs = refs[: step + 1], refs[step + 1], refs[step + 2 :]
+    states, refs = refs[: step + 1], refs[step + 1 :]
+    cols, refs = refs[: step + 1], refs[step + 1 :]
+    out_ref, col, table = refs[:3]
+    rows = refs[3:]
     for state, row in zip(states, rows):
         row[...] = state[...]
-    gram_body(owns, pieces, rows, col, stack, tile)
+    gram_body(owns, block, rows, col, 0, False)
     first = 0
     for k, size in enumerate(chunks):
-        col_k = (cols[k] if k < step else col)[0:1, :]
         row_k = jnp.max(rows[k][...].T, axis=0, keepdims=True)
         count = groups * size
         for p, relative in enumerate(relatives):
+            source, shift = (col, 2 * count) if k == step and p >= 2 else (cols[k], 0)
             for r in range(groups):
-                start = p * count + r * size
-                best = col_k[:, start : start + size]
+                start = p * count + r * size - shift
+                best = source[0:1, start : start + size]
                 if p == 0:
                     best = jnp.maximum(best, row_k[:, r * size : (r + 1) * size])
                 row = r * members + p
@@ -194,50 +193,48 @@
             out_ref[pl.ds(target, 1), :] = table[row : row + 1, :]
 
 
-def gram_step(first, me, owns, pieces, states, cols, relatives, chunks, groups):
-    step = len(owns) - 1
-    members = len(relatives)
+def gram_params(owns, blocks):
     features = owns[0].shape[1]
-    counts = [own.shape[0] for own in owns]
-    totals = [members * count for count in counts[first:]]
-    total = max(totals)
-    tile = 256
-    row_shapes = [(c, lanes) for c in counts]
-    stack = pltpu.VMEM((total, features), jnp.bfloat16)
-    params = dict(
+    mine, others = sum(own.shape[0] for own in owns), sum(block.shape[0] for block in blocks)
+    return dict(
         compiler_params=pltpu.CompilerParams(vmem_limit_bytes=24 * 2**20),
         cost_estimate=pl.CostEstimate(
-            flops=2 * sum(counts) * total * features,
-            bytes_accessed=2 * features * (sum(counts) + total),
+            flops=2 * mine * others * features,
+            bytes_accessed=2 * features * (mine + others),
             transcendentals=0,
         ),
     )
-    if step < len(chunks) - 1:
-        results = pl.pallas_call(
-            functools.partial(gram_kernel, first, step, tile),
-            in_specs=[vmem] * (step + 1 + len(pieces) + first),
-            out_specs=[vmem] * (step + 1 + len(totals)),
-            out_shape=[jax.ShapeDtypeStruct(s, jnp.float32) for s in row_shapes]
-            + [jax.ShapeDtypeStruct((1, count), jnp.float32) for count in totals],
-            scratch_shapes=[stack],
-            name="gram_step",
-            **params,
-        )(*owns, *pieces, *states)
-        return list(results[: step + 1]), cols + list(results[step + 1 :])
+
+
+def gram_step(first, owns, blocks, states, pieces):
+    step = len(owns) - 1
+    row_shapes = [(own.shape[0], lanes) for own in owns]
+    col_shapes = [(1, pieces * 2 * own.shape[0]) for own in owns[first:]]
+    results = pl.pallas_call(
+        functools.partial(gram_kernel, first, step, pieces),
+        in_specs=[vmem] * (step + 1 + len(blocks) + first),
+        out_specs=[vmem] * len(row_shapes + col_shapes),
+        out_shape=[jax.ShapeDtypeStruct(s, jnp.float32) for s in row_shapes + col_shapes],
+        name="gram_step",
+        **gram_params(owns, blocks),
+    )(*owns, *blocks, *states)
+    return list(results[: step + 1]), list(results[step + 1 :])
+
+
+def gram_last(me, owns, block, states, cols, relatives, chunks, groups):
+    step = len(owns) - 1
+    members = len(relatives)
+    shape = (groups * members, sum(chunks))
     return pl.pallas_call(
-        functools.partial(gram_last_kernel, step, relatives, chunks, groups, tile),
-        in_specs=[smem] + [vmem] * (step + 3 + 2 * step),
+        functools.partial(gram_last_kernel, step, relatives, chunks, groups),
+        in_specs=[smem] + [vmem] * (3 * step + 4),
         out_specs=vmem,
-        out_shape=jax.ShapeDtypeStruct((groups * members, sum(chunks)), jnp.float32),
-        scratch_shapes=[
-            stack,
-            pltpu.VMEM((1, total), jnp.float32),
-            pltpu.VMEM((groups * members, sum(chunks)), jnp.float32),
-        ]
-        + [pltpu.VMEM(s, jnp.float32) for s in row_shapes],
+        out_shape=jax.ShapeDtypeStruct(shape, jnp.float32),
+        scratch_shapes=[pltpu.VMEM((1, block.shape[0]), jnp.float32), pltpu.VMEM(shape, jnp.float32)]
+        + [pltpu.VMEM((own.shape[0], lanes), jnp.float32) for own in owns],
         name="gram_last",
-        **params,
-    )(me, *owns, *pieces, *states, *cols)
+        **gram_params(owns, [block]),
+    )(me, *owns, block, *states, *cols)
 
 
 def tail_kernel(capacity, members, slot_ref, part_ref, out_ref, table):
@@ -283,7 +280,7 @@
     chunks = chunk_sizes(capacity)
     me = jnp.stack([lax.axis_index("grp"), lax.axis_index("blk")]).astype(jnp.int32)
     slots = send_slot.reshape(row_count // lanes, lanes)
-    keeps, first_send, rest_send = head(me, embeddings, slots, capacity, chunks, groups)
+    keeps, first_send, next_send, rest_send = head(me, embeddings, slots, capacity, chunks, groups)
     count, high = len(chunks), groups // 2
     last = count - 1
 
@@ -294,8 +291,8 @@
 
     def block(step, z):
         size = chunks[step]
-        near = first_near if step == 0 else sent["y", 2]
-        skip = sum(chunks[1:step]) * high
+        near = first_near if step == 0 else sent["y", min(step, 2) + 1]
+        skip = sum(chunks[2:step]) * high
         return jnp.concatenate(
             [rows(keeps[step], z, size), rows(near[skip:], z, size)], axis=0
         )
@@ -312,8 +309,18 @@
             early += [("c", step - 2 if z == far[-1] else step - 3)]
         send(("z", step, z), block(step, z), "grp", groups, 2 * z, *early)
 
+    def send_near_z():
+        blocks = jnp.concatenate([block(step, 1) for step in range(1, count)], axis=0)
+        send(("n",), blocks, "grp", groups, 2, ("z", 0, 1))
+
     def collect(step):
-        parts = [block(step, 0)] + [sent["z", step, z] for z in range(1, high)]
+        parts = [block(step, 0)]
+        for z in range(1, high):
+            if z == 1 and step >= 1:
+                start = 2 * sum(chunks[1:step])
+                parts.append(sent["n",][start : start + 2 * chunks[step]])
+            else:
+                parts.append(sent["z", step, z])
         owns[step] = jnp.concatenate(parts, axis=0)
 
     def send_x(step, cuts, between):
@@ -330,38 +337,36 @@
         pairs[step] = jnp.concatenate([owns[step]] + across, axis=0)
         send(("c", step), pairs[step], "blk", members, 1, *early)
 
-    def gram(first, step, states, cols):
-        pieces = []
-        for k in range(first, step + 1):
-            pieces += [pairs[k], sent["c", k]]
-        mine = [owns[k] for k in range(step + 1)]
-        return gram_step(
-            first, me, mine, pieces, states, cols, (0, 2, 1, 3), chunks, groups
-        )
-
     far = [high // 2] + [z for z in range(1, high) if z != high // 2]
     cut = first_send.shape[0] // 32 * 16
     done["rest"] = rest_send
     send(("y", 0), first_send[:cut], "grp", groups, 1)
     send(("y", 1), first_send[cut:], "grp", groups, 1, "rest")
-    send(("y", 2), rest_send, "grp", groups, 1, ("y", 0))
+    send(("y", 2), next_send, "grp", groups, 1, ("y", 0))
+    send(("y", 3), rest_send, "grp", groups, 1, ("y", 0))
     first_near = jnp.concatenate([sent["y", 0], sent["y", 1]], axis=0)
     for z in far:
         send_z(0, z)
+    far.remove(1)
     for step in range(1, count):
         collect(step - 1)
         for z in far:
             send_z(step, z)
+        if step == 1:
+            send_near_z()
         send_x(step - 1, [], [])
         send_c(step - 1, *[("z", step, z) for z in far])
     collect(last)
-    states, cols = gram(0, last - 2, [], [])
-    done["gram", 0] = cols[-1]
-    states, cols = gram(last - 1, last - 1, states, cols)
-    done["gram", 1] = cols[-1]
-    send_x(last, [208, 352], [[("gram", 0), ("c", last - 1)], [("gram", 1)]])
+    mine = [owns[k] for k in range(count)]
+    blocks = [block for k in range(last) for block in (pairs[k], sent["c", k])]
+    states, cols = gram_step(0, mine[:last], blocks, [], 2)
+    done["gram"] = cols[-1]
+    send_x(last, [304], [["gram"]])
     send_c(last)
-    result = gram(last, last, states, cols)
+    states, half = gram_step(last, mine, [pairs[last]], states, 1)
+    result = gram_last(
+        me, mine, sent["c", last], states, cols + half, (0, 2, 1, 3), chunks, groups
+    )
     homeward = lax.all_to_all(result, ("grp", "blk"), 0, 0, tiled=True)
     return tail(homeward, slots, capacity, members).reshape(row_count)
 

time: 123 us -> 117 us (0.951)
  Pallas kernels: 23.5 us -> 17.7 us
  waiting for transfers between devices: 52.2 us -> 55.1 us
  starting transfers between devices: 31.9 us -> 29.3 us
    pallas_call x3, Pallas kernels: 17.3 us -> 11.5 us  [the longest x2 8.46 us: gram_step(): pl.pallas_call(functools.partial(gram_kernel, first, step, pieces), in_sp...]
    ppermute x25 -> x23, waiting for transfers between devices: 52.2 us -> 55.1 us  [swap(): return lax.ppermute(value, axis, [(i, i ^ bit) for i in range(size)])]
    ppermute x25 -> x23, starting transfers between devices: 31.9 us -> 29.3 us  [swap(): return lax.ppermute(value, axis, [(i, i ^ bit) for i in range(size)])]
    unnamed x23 -> x24, local copies, waits for them, and re-layouts: 3.03 us -> 3.04 us
  transfers between devices with their start and end apart: 25 -> 23, of which waited for: 13 -> 13; matrix products, arithmetic and copies ran while one was open for 1% -> 1% of each run, Pallas kernels for 10% -> 9%
where the time goes in v10:
time: 117 us
  waiting for transfers between devices  55.1 us (47%)
  starting transfers between devices  29.3 us (25%)
  Pallas kernels  17.7 us (15%)
  blocking collectives  10.7 us (9%)
  local copies, waits for them, and re-layouts  3.27 us (3%)
    ppermute x23, waiting for transfers between devices, swap(): return lax.ppermute(value, axis, [(i, i ^ bit) for i in range(size)])  55.1 us
    ppermute x23, starting transfers between devices, swap(): return lax.ppermute(value, axis, [(i, i ^ bit) for i in range(size)])  29.3 us
    all_to_all x1, blocking collectives, on_device(): homeward = lax.all_to_all(result, ('grp', 'blk'), 0, 0, tiled=True)  10.7 us
    pallas_call x2, Pallas kernels, gram_step(): pl.pallas_call(functools.partial(gram_kernel, first, step, pieces), in_sp...  8.46 us
    pallas_call x1, Pallas kernels, gram_last(): pl.pallas_call(functools.partial(gram_last_kernel, step, relatives, chunk...  3.09 us
    unnamed x24, local copies, waits for them, and re-layouts  3.04 us
    pallas_call x1, Pallas kernels, head(): pl.pallas_call(functools.partial(rest_kernel, capacity, chunks, groups),...  2.61 us
  transfers between devices with their start and end apart: 23, of which 13 were waited for; matrix products, arithmetic and copies ran while one was open for 1% of the time, Pallas kernels for 9%

profile of v10, /device:TPU:0, one launch (start us, length us, event | category | flops | bytes accessed | tf_op | source)
XLA Modules:
  0.0 116.7 jit_solution(14960779190244266423)
XLA Ops:
  3.3 3.0 %collective-permute-start = (bf16[96,768]{1,0:T(8,128)(2,1)S(1)}, bf16[96,768]{1,0:T(8,128)(2,1)S(1)}, u32[]{:S(2)}, u32[]{:S(2)}) collective-permute-start(bf16[96,768]{1,0:T(8,128)(2,1)S(1)} %get-tuple-element.118), channel_id=1, source_target_pairs={{0,4},{4,0},{8,12},{12,8},{16,20},{20,16},{24,28},{28,24},{1,5},{5... | collective-permute-start | bytes 442376 | tf_op jit(solution)/shard_map/ppermute | solution.py:29
  6.4 2.6 %place_rest.1 = (bf16[192,768]{1,0:T(8,128)(2,1)S(1)}, bf16[192,768]{1,0:T(8,128)(2,1)S(1)}, bf16[192,768]{1,0:T(8,128)(2,1)S(1)}, bf16[192,768]{1,0:T(8,128)(2,...) custom-call(s32[2]{0:T(128)S(1)} %pad_add_fusion.me_ref, s32[6,128]{1,0:T(8,128)S(1)} %bitcast.11, ...), custom_call_target="tpu_custom_call" | custom-call | flops 1585446912 | bytes 3244032 | tf_op jit(solution)/shard_map/place_rest/pallas_call | solution.py:101
  10.2 1.9 %collective-permute-start.1 = (bf16[96,768]{1,0:T(8,128)(2,1)S(1)}, bf16[96,768]{1,0:T(8,128)(2,1)S(1)}, u32[]{:S(2)}, u32[]{:S(2)}) collective-permute-start(bf16[96,768]{1,0:T(8,128)(2,1)S(1)} %pad_maximum_fusion), channel_id=1, source_target_pairs={{0,8},{4,12},{8,0},{12,4},{16,24},{20,28},{24,16},{28,20},{1,9},{5... | collective-permute-start | bytes 442376 | tf_op jit(solution)/shard_map/ppermute | solution.py:29
  12.1 1.7 %collective-permute-start.5 = (bf16[192,768]{1,0:T(8,128)(2,1)S(1)}, bf16[192,768]{1,0:T(8,128)(2,1)S(1)}, u32[]{:S(2)}, u32[]{:S(2)}) collective-permute-start(bf16[192,768]{1,0:T(8,128)(2,1)S(1)} %get-tuple-element.48), channel_id=1, source_target_pairs={{0,4},{4,0},{8,12},{12,8},{16,20},{20,16},{24,28},{28,24},{1,5},{5... | collective-permute-start | bytes 884744 | tf_op jit(solution)/shard_map/ppermute | solution.py:29
  15.4 2.6 %collective-permute-start.3 = (bf16[96,768]{1,0:T(8,128)(2,1)S(1)}, bf16[96,768]{1,0:T(8,128)(2,1)S(1)}, u32[]{:S(2)}, u32[]{:S(2)}) collective-permute-start(bf16[96,768]{1,0:T(8,128)(2,1)S(1)} %pad_maximum_fusion.1), channel_id=1, source_target_pairs={{0,16},{4,20},{8,24},{12,28},{16,0},{20,4},{24,8},{28,12},{1,17},{... | collective-permute-start | bytes 442376 | tf_op jit(solution)/shard_map/ppermute | solution.py:29
  18.0 1.9 %collective-permute-start.4 = (bf16[96,768]{1,0:T(8,128)(2,1)S(1)}, bf16[96,768]{1,0:T(8,128)(2,1)S(1)}, u32[]{:S(2)}, u32[]{:S(2)}) collective-permute-start(bf16[96,768]{1,0:T(8,128)(2,1)S(1)} %pad_maximum_fusion.2), channel_id=1, source_target_pairs={{0,24},{4,28},{8,16},{12,20},{16,8},{20,12},{24,0},{28,4},{1,25},{... | collective-permute-start | bytes 442376 | tf_op jit(solution)/shard_map/ppermute | solution.py:29
  20.5 1.6 %collective-permute-done.5 = bf16[192,768]{1,0:T(8,128)(2,1)S(1)} collective-permute-done((bf16[192,768]{1,0:T(8,128)(2,1)S(1)}, bf16[192,768]{1,0:T(8,128)(2,1)S(1)}, u32[]{:S(2)}, u32[]{:S(2)}) %collective-permute-start.5) | collective-permute-done | bytes 294944 | tf_op jit(solution)/shard_map/ppermute | solution.py:29
  22.1 11.2 %collective-permute-done.6 = bf16[384,768]{1,0:T(8,128)(2,1)S(1)} collective-permute-done((bf16[384,768]{1,0:T(8,128)(2,1)S(1)}, bf16[384,768]{1,0:T(8,128)(2,1)S(1)}, u32[]{:S(2)}, u32[]{:S(2)}) %collective-permute-start.6) | collective-permute-done | bytes 589856 | tf_op jit(solution)/shard_map/ppermute | solution.py:29
  33.4 1.6 %collective-permute-start.7 = (bf16[288,768]{1,0:T(8,128)(2,1)S(1)}, bf16[288,768]{1,0:T(8,128)(2,1)S(1)}, u32[]{:S(2)}, u32[]{:S(2)}) collective-permute-start(bf16[288,768]{1,0:T(8,128)(2,1)S(1)} %get-tuple-element.52), channel_id=1, source_target_pairs={{0,8},{4,12},{8,0},{12,4},{16,24},{20,28},{24,16},{28,20},{1,9},{5... | collective-permute-start | bytes 1327112 | tf_op jit(solution)/shard_map/ppermute | solution.py:29
  36.7 2.7 %collective-permute-start.8 = (bf16[96,768]{1,0:T(8,128)(2,1)S(1)}, bf16[96,768]{1,0:T(8,128)(2,1)S(1)}, u32[]{:S(2)}, u32[]{:S(2)}) collective-permute-start(bf16[96,768]{1,0:T(8,128)(2,1)S(1)} %pad_maximum_fusion.3), channel_id=1, source_target_pairs={{0,16},{4,20},{8,24},{12,28},{16,0},{20,4},{24,8},{28,12},{1,17},{... | collective-permute-start | bytes 442376 | tf_op jit(solution)/shard_map/ppermute | solution.py:29
  39.6 7.8 %collective-permute-done.7 = bf16[288,768]{1,0:T(8,128)(2,1)S(1)} collective-permute-done((bf16[288,768]{1,0:T(8,128)(2,1)S(1)}, bf16[288,768]{1,0:T(8,128)(2,1)S(1)}, u32[]{:S(2)}, u32[]{:S(2)}) %collective-permute-start.7) | collective-permute-done | bytes 442400 | tf_op jit(solution)/shard_map/ppermute | solution.py:29
  47.9 4.5 %collective-permute-done.9 = bf16[96,768]{1,0:T(8,128)(2,1)S(1)} collective-permute-done((bf16[96,768]{1,0:T(8,128)(2,1)S(1)}, bf16[96,768]{1,0:T(8,128)(2,1)S(1)}, u32[]{:S(2)}, u32[]{:S(2)}) %collective-permute-start.9) | collective-permute-done | bytes 147488 | tf_op jit(solution)/shard_map/ppermute | solution.py:29
  52.4 1.6 %collective-permute-start.15 = (bf16[384,768]{1,0:T(8,128)(2,1)S(1)}, bf16[384,768]{1,0:T(8,128)(2,1)S(1)}, u32[]{:S(2)}, u32[]{:S(2)}) collective-permute-start(bf16[384,768]{1,0:T(8,128)(2,1)S(1)} %get-tuple-element.59.refs_1_), channel_id=1, source_target_pairs={{0,2},{1,3},{2,0},{3,1},{4,6},{5,7},{6,4},{7,5},{8,10},{9,11},{10,... | collective-permute-start | bytes 1769480 | tf_op jit(solution)/shard_map/ppermute | solution.py:29
  54.1 1.9 %collective-permute-start.12 = (bf16[96,768]{1,0:T(8,128)(2,1)S(1)}, bf16[96,768]{1,0:T(8,128)(2,1)S(1)}, u32[]{:S(2)}, u32[]{:S(2)}) collective-permute-start(bf16[96,768]{1,0:T(8,128)(2,1)S(1)} %pad_maximum_fusion.6), channel_id=1, source_target_pairs={{0,24},{4,28},{8,16},{12,20},{16,8},{20,12},{24,0},{28,4},{1,25},{... | collective-permute-start | bytes 442376 | tf_op jit(solution)/shard_map/ppermute | solution.py:29
  56.1 8.8 %collective-permute-done.15 = bf16[384,768]{1,0:T(8,128)(2,1)S(1)} collective-permute-done((bf16[384,768]{1,0:T(8,128)(2,1)S(1)}, bf16[384,768]{1,0:T(8,128)(2,1)S(1)}, u32[]{:S(2)}, u32[]{:S(2)}) %collective-permute-start.15) | collective-permute-done | bytes 589856 | tf_op jit(solution)/shard_map/ppermute | solution.py:29
  69.7 11.3 %collective-permute-done.18 = bf16[384,768]{1,0:T(8,128)(2,1)S(1)} collective-permute-done((bf16[384,768]{1,0:T(8,128)(2,1)S(1)}, bf16[384,768]{1,0:T(8,128)(2,1)S(1)}, u32[]{:S(2)}, u32[]{:S(2)}) %collective-permute-start.18) | collective-permute-done | bytes 589856 | tf_op jit(solution)/shard_map/ppermute | solution.py:29
  83.9 6.0 %gram_step.2 = (f32[384,128]{1,0:T(8,128)S(1)}, f32[384,128]{1,0:T(8,128)S(1)}, f32[384,128]{1,0:T(8,128)S(1)}, f32[1,1536]{1,0:T(1,128)S(1)}, f32[1,1536]{1,0:T(1,128)S(1)}, /*index=5*/f32[1,1536]{1,0:T(1,128)S(1)}) custom-call(bf16[384,768]{1,0:T(8,128)(2,1)S(1)} %get-tuple-element.132.refs_0_, bf16[384,768]{1,0:T(8,128)(2,1)S(1)} %get-tuple-element.59.refs_1_, ...), custom_call_target="tpu_custom_call" | custom-call | flops 8153726976 | bytes 8847360 | tf_op jit(solution)/shard_map/gram_step/pallas_call | solution.py:213
  89.9 1.6 %collective-permute-start.21 = (bf16[80,768]{1,0:T(8,128)(2,1)S(1)}, bf16[80,768]{1,0:T(8,128)(2,1)S(1)}, u32[]{:S(2)}, u32[]{:S(2)}) collective-permute-start(bf16[80,768]{1,0:T(8,128)(2,1)S(1)} %slice.184), channel_id=1, source_target_pairs={{0,2},{1,3},{2,0},{3,1},{4,6},{5,7},{6,4},{7,5},{8,10},{9,11},{10,... | collective-permute-start | bytes 368648 | tf_op jit(solution)/shard_map/ppermute | solution.py:29
  91.5 3.2 %collective-permute-done.19 = bf16[304,768]{1,0:T(8,128)(2,1)S(1)} collective-permute-done((bf16[304,768]{1,0:T(8,128)(2,1)S(1)}, bf16[304,768]{1,0:T(8,128)(2,1)S(1)}, u32[]{:S(2)}, u32[]{:S(2)}) %collective-permute-start.19) | collective-permute-done | bytes 466976 | tf_op jit(solution)/shard_map/ppermute | solution.py:29
  94.8 2.2 %collective-permute-done.21 = bf16[80,768]{1,0:T(8,128)(2,1)S(1)} collective-permute-done((bf16[80,768]{1,0:T(8,128)(2,1)S(1)}, bf16[80,768]{1,0:T(8,128)(2,1)S(1)}, u32[]{:S(2)}, u32[]{:S(2)}) %collective-permute-start.21) | collective-permute-done | bytes 122912 | tf_op jit(solution)/shard_map/ppermute | solution.py:29
  97.1 2.4 %gram_step.3 = (f32[384,128]{1,0:T(8,128)S(1)}, f32[384,128]{1,0:T(8,128)S(1)}, f32[384,128]{1,0:T(8,128)S(1)}, f32[384,128]{1,0:T(8,128)S(1)}, f32[1,768]{1,0:T(1,128)S(1)}) custom-call(bf16[384,768]{1,0:T(8,128)(2,1)S(1)} %get-tuple-element.132.refs_0_, bf16[384,768]{1,0:T(8,128)(2,1)S(1)} %get-tuple-element.59.refs_1_, ...), custom_call_target="tpu_custom_call" | custom-call | flops 1811939328 | bytes 3538944 | tf_op jit(solution)/shard_map/gram_step/pallas_call | solution.py:213
  99.9 3.1 %gram_last.1 = f32[32,192]{1,0:T(8,128)S(1)} custom-call(s32[2]{0:T(128)S(1)} %pad_add_fusion.me_ref, bf16[384,768]{1,0:T(8,128)(2,1)S(1)} %get-tuple-element.132.refs_0_, bf16[384,768]{1,0:T(8,128)(2,1)S(1)} %get-tuple-element.59.refs_1_, bf16[384,768]{1,0:T(8,128)(2,1)S(1)} %get-tuple-element.62.refs_2_, bf16[384,768]{1,0:T(8,128)(2,1)S(1)} %get-tuple-element.124.refs_3_, ...), custom_call_target="tpu_custom_call" | custom-call | flops 1811939328 | bytes 3538944 | tf_op jit(solution)/shard_map/gram_last/pallas_call | solution.py:228
  103.0 10.7 %all_to_all.11 = f32[32,1,192]{2,1,0:T(1,128)S(1)} all-to-all(f32[32,1,192]{2,1,0:T(1,128)S(1)} %copy.3), channel_id=1, replica_groups=mesh['grp'=8,'blk'=4] {'grp','blk'}, dimensions={0} | all-to-all | bytes 49152 | tf_op jit(solution)/shard_map/all_to_all | solution.py:370
  114.4 2.3 %pick_rows.1 = f32[6,128]{1,0:T(8,128)} custom-call(s32[6,128]{1,0:T(8,128)} %bitcast.9, f32[32,192]{1,0:T(8,128)} %bitcast.12), custom_call_target="tpu_custom_call" | custom-call | tf_op jit(solution)/shard_map/pick_rows/pallas_call | solution.py:264
  (72 shorter events, 18.1 us)
Async XLA Ops:
  0.1 1.3 %copy-start = (bf16[768,768]{1,0:T(8,128)(2,1)S(1)}, bf16[768,768]{1,0:T(8,128)(2,1)}, u32[]{:S(2)}) copy-start(bf16[768,768]{1,0:T(8,128)(2,1)} %x_ref.1) | copy-start | bytes 3538948
  3.3 6.9 %collective-permute-start = (bf16[96,768]{1,0:T(8,128)(2,1)S(1)}, bf16[96,768]{1,0:T(8,128)(2,1)S(1)}, u32[]{:S(2)}, u32[]{:S(2)}) collective-permute-start(bf16[96,768]{1,0:T(8,128)(2,1)S(1)} %get-tuple-element.118), channel_id=1, source_target_pairs={{0,4},{4,0},{8,12},{12,8},{16,20},{20,16},{24,28},{28,24},{1,5},{5... | collective-permute-start | bytes 442376 | tf_op jit(solution)/shard_map/ppermute | solution.py:29
  9.0 6.4 %collective-permute-start.2 = (bf16[96,768]{1,0:T(8,128)(2,1)S(1)}, bf16[96,768]{1,0:T(8,128)(2,1)S(1)}, u32[]{:S(2)}, u32[]{:S(2)}) collective-permute-start(bf16[96,768]{1,0:T(8,128)(2,1)S(1)} %get-tuple-element.45), channel_id=1, source_target_pairs={{0,4},{4,0},{8,12},{12,8},{16,20},{20,16},{24,28},{28,24},{1,5},{5... | collective-permute-start | bytes 442376 | tf_op jit(solution)/shard_map/ppermute | solution.py:29
  10.2 10.2 %collective-permute-start.1 = (bf16[96,768]{1,0:T(8,128)(2,1)S(1)}, bf16[96,768]{1,0:T(8,128)(2,1)S(1)}, u32[]{:S(2)}, u32[]{:S(2)}) collective-permute-start(bf16[96,768]{1,0:T(8,128)(2,1)S(1)} %pad_maximum_fusion), channel_id=1, source_target_pairs={{0,8},{4,12},{8,0},{12,4},{16,24},{20,28},{24,16},{28,20},{1,9},{5... | collective-permute-start | bytes 442376 | tf_op jit(solution)/shard_map/ppermute | solution.py:29
  12.1 9.9 %collective-permute-start.5 = (bf16[192,768]{1,0:T(8,128)(2,1)S(1)}, bf16[192,768]{1,0:T(8,128)(2,1)S(1)}, u32[]{:S(2)}, u32[]{:S(2)}) collective-permute-start(bf16[192,768]{1,0:T(8,128)(2,1)S(1)} %get-tuple-element.48), channel_id=1, source_target_pairs={{0,4},{4,0},{8,12},{12,8},{16,20},{20,16},{24,28},{28,24},{1,5},{5... | collective-permute-start | bytes 884744 | tf_op jit(solution)/shard_map/ppermute | solution.py:29
  15.4 19.7 %collective-permute-start.3 = (bf16[96,768]{1,0:T(8,128)(2,1)S(1)}, bf16[96,768]{1,0:T(8,128)(2,1)S(1)}, u32[]{:S(2)}, u32[]{:S(2)}) collective-permute-start(bf16[96,768]{1,0:T(8,128)(2,1)S(1)} %pad_maximum_fusion.1), channel_id=1, source_target_pairs={{0,16},{4,20},{8,24},{12,28},{16,0},{20,4},{24,8},{28,12},{1,17},{... | collective-permute-start | bytes 442376 | tf_op jit(solution)/shard_map/ppermute | solution.py:29
  18.0 17.0 %collective-permute-start.4 = (bf16[96,768]{1,0:T(8,128)(2,1)S(1)}, bf16[96,768]{1,0:T(8,128)(2,1)S(1)}, u32[]{:S(2)}, u32[]{:S(2)}) collective-permute-start(bf16[96,768]{1,0:T(8,128)(2,1)S(1)} %pad_maximum_fusion.2), channel_id=1, source_target_pairs={{0,24},{4,28},{8,16},{12,20},{16,8},{20,12},{24,0},{28,4},{1,25},{... | collective-permute-start | bytes 442376 | tf_op jit(solution)/shard_map/ppermute | solution.py:29
  19.9 13.4 %collective-permute-start.6 = (bf16[384,768]{1,0:T(8,128)(2,1)S(1)}, bf16[384,768]{1,0:T(8,128)(2,1)S(1)}, u32[]{:S(2)}, u32[]{:S(2)}) collective-permute-start(bf16[384,768]{1,0:T(8,128)(2,1)S(1)} %get-tuple-element.50), channel_id=1, source_target_pairs={{0,4},{4,0},{8,12},{12,8},{16,20},{20,16},{24,28},{28,24},{1,5},{5... | collective-permute-start | bytes 1769480 | tf_op jit(solution)/shard_map/ppermute | solution.py:29
  33.4 14.0 %collective-permute-start.7 = (bf16[288,768]{1,0:T(8,128)(2,1)S(1)}, bf16[288,768]{1,0:T(8,128)(2,1)S(1)}, u32[]{:S(2)}, u32[]{:S(2)}) collective-permute-start(bf16[288,768]{1,0:T(8,128)(2,1)S(1)} %get-tuple-element.52), channel_id=1, source_target_pairs={{0,8},{4,12},{8,0},{12,4},{16,24},{20,28},{24,16},{28,20},{1,9},{5... | collective-permute-start | bytes 1327112 | tf_op jit(solution)/shard_map/ppermute | solution.py:29
  35.1 17.3 %collective-permute-start.11 = (bf16[384,768]{1,0:T(8,128)(2,1)S(1)}, bf16[384,768]{1,0:T(8,128)(2,1)S(1)}, u32[]{:S(2)}, u32[]{:S(2)}) collective-permute-start(bf16[384,768]{1,0:T(8,128)(2,1)S(1)} %get-tuple-element.132.refs_0_), channel_id=1, source_target_pairs={{0,2},{1,3},{2,0},{3,1},{4,6},{5,7},{6,4},{7,5},{8,10},{9,11},{10,... | collective-permute-start | bytes 1769480 | tf_op jit(solution)/shard_map/ppermute | solution.py:29
  36.7 11.2 %collective-permute-start.8 = (bf16[96,768]{1,0:T(8,128)(2,1)S(1)}, bf16[96,768]{1,0:T(8,128)(2,1)S(1)}, u32[]{:S(2)}, u32[]{:S(2)}) collective-permute-start(bf16[96,768]{1,0:T(8,128)(2,1)S(1)} %pad_maximum_fusion.3), channel_id=1, source_target_pairs={{0,16},{4,20},{8,24},{12,28},{16,0},{20,4},{24,8},{28,12},{1,17},{... | collective-permute-start | bytes 442376 | tf_op jit(solution)/shard_map/ppermute | solution.py:29
  39.3 13.0 %collective-permute-start.9 = (bf16[96,768]{1,0:T(8,128)(2,1)S(1)}, bf16[96,768]{1,0:T(8,128)(2,1)S(1)}, u32[]{:S(2)}, u32[]{:S(2)}) collective-permute-start(bf16[96,768]{1,0:T(8,128)(2,1)S(1)} %pad_maximum_fusion.4), channel_id=1, source_target_pairs={{0,24},{4,28},{8,16},{12,20},{16,8},{20,12},{24,0},{28,4},{1,25},{... | collective-permute-start | bytes 442376 | tf_op jit(solution)/shard_map/ppermute | solution.py:29
  52.4 12.6 %collective-permute-start.15 = (bf16[384,768]{1,0:T(8,128)(2,1)S(1)}, bf16[384,768]{1,0:T(8,128)(2,1)S(1)}, u32[]{:S(2)}, u32[]{:S(2)}) collective-permute-start(bf16[384,768]{1,0:T(8,128)(2,1)S(1)} %get-tuple-element.59.refs_1_), channel_id=1, source_target_pairs={{0,2},{1,3},{2,0},{3,1},{4,6},{5,7},{6,4},{7,5},{8,10},{9,11},{10,... | collective-permute-start | bytes 1769480 | tf_op jit(solution)/shard_map/ppermute | solution.py:29
  54.0 11.0 %collective-permute-start.10 = (bf16[96,768]{1,0:T(8,128)(2,1)S(1)}, bf16[96,768]{1,0:T(8,128)(2,1)S(1)}, u32[]{:S(2)}, u32[]{:S(2)}) collective-permute-start(bf16[96,768]{1,0:T(8,128)(2,1)S(1)} %pad_maximum_fusion.5), channel_id=1, source_target_pairs={{0,16},{4,20},{8,24},{12,28},{16,0},{20,4},{24,8},{28,12},{1,17},{... | collective-permute-start | bytes 442376 | tf_op jit(solution)/shard_map/ppermute | solution.py:29
  54.1 10.9 %collective-permute-start.12 = (bf16[96,768]{1,0:T(8,128)(2,1)S(1)}, bf16[96,768]{1,0:T(8,128)(2,1)S(1)}, u32[]{:S(2)}, u32[]{:S(2)}) collective-permute-start(bf16[96,768]{1,0:T(8,128)(2,1)S(1)} %pad_maximum_fusion.6), channel_id=1, source_target_pairs={{0,24},{4,28},{8,16},{12,20},{16,8},{20,12},{24,0},{28,4},{1,25},{... | collective-permute-start | bytes 442376 | tf_op jit(solution)/shard_map/ppermute | solution.py:29
  56.0 10.7 %collective-permute-start.13 = (bf16[768,768]{1,0:T(8,128)(2,1)S(1)}, bf16[768,768]{1,0:T(8,128)(2,1)S(1)}, u32[]{:S(2)}, u32[]{:S(2)}) collective-permute-start(bf16[768,768]{1,0:T(8,128)(2,1)S(1)} %constant_dynamic-update-slice_fusion.19.refs_3_), channel_id=1, source_target_pairs={{0,1},{1,0},{2,3},{3,2},{4,5},{5,4},{6,7},{7,6},{8,9},{9,8},{10,11... | collective-permute-start | bytes 3538952 | tf_op jit(solution)/shard_map/ppermute | solution.py:29
  65.0 3.2 %collective-permute-start.16 = (bf16[768,768]{1,0:T(8,128)(2,1)S(1)}, bf16[768,768]{1,0:T(8,128)(2,1)S(1)}, u32[]{:S(2)}, u32[]{:S(2)}) collective-permute-start(bf16[768,768]{1,0:T(8,128)(2,1)S(1)} %constant_dynamic-update-slice_fusion.25.refs_5_), channel_id=1, source_target_pairs={{0,1},{1,0},{2,3},{3,2},{4,5},{5,4},{6,7},{7,6},{8,9},{9,8},{10,11... | collective-permute-start | bytes 3538952 | tf_op jit(solution)/shard_map/ppermute | solution.py:29
  65.2 15.8 %collective-permute-start.18 = (bf16[384,768]{1,0:T(8,128)(2,1)S(1)}, bf16[384,768]{1,0:T(8,128)(2,1)S(1)}, u32[]{:S(2)}, u32[]{:S(2)}) collective-permute-start(bf16[384,768]{1,0:T(8,128)(2,1)S(1)} %get-tuple-element.62.refs_2_), channel_id=1, source_target_pairs={{0,2},{1,3},{2,0},{3,1},{4,6},{5,7},{6,4},{7,5},{8,10},{9,11},{10,... | collective-permute-start | bytes 1769480 | tf_op jit(solution)/shard_map/ppermute | solution.py:29
  66.8 14.2 %collective-permute-start.14 = (bf16[96,768]{1,0:T(8,128)(2,1)S(1)}, bf16[96,768]{1,0:T(8,128)(2,1)S(1)}, u32[]{:S(2)}, u32[]{:S(2)}) collective-permute-start(bf16[96,768]{1,0:T(8,128)(2,1)S(1)} %pad_maximum_fusion.7), channel_id=1, source_target_pairs={{0,16},{4,20},{8,24},{12,28},{16,0},{20,4},{24,8},{28,12},{1,17},{... | collective-permute-start | bytes 442376 | tf_op jit(solution)/shard_map/ppermute | solution.py:29
  68.2 12.8 %collective-permute-start.17 = (bf16[96,768]{1,0:T(8,128)(2,1)S(1)}, bf16[96,768]{1,0:T(8,128)(2,1)S(1)}, u32[]{:S(2)}, u32[]{:S(2)}) collective-permute-start(bf16[96,768]{1,0:T(8,128)(2,1)S(1)} %pad_maximum_fusion.8), channel_id=1, source_target_pairs={{0,24},{4,28},{8,16},{12,20},{16,8},{20,12},{24,0},{28,4},{1,25},{... | collective-permute-start | bytes 442376 | tf_op jit(solution)/shard_map/ppermute | solution.py:29
  81.0 2.9 %collective-permute-start.20 = (bf16[768,768]{1,0:T(8,128)(2,1)S(1)}, bf16[768,768]{1,0:T(8,128)(2,1)S(1)}, u32[]{:S(2)}, u32[]{:S(2)}) collective-permute-start(bf16[768,768]{1,0:T(8,128)(2,1)S(1)} %constant_dynamic-update-slice_fusion.34.refs_7_), channel_id=1, source_target_pairs={{0,1},{1,0},{2,3},{3,2},{4,5},{5,4},{6,7},{7,6},{8,9},{9,8},{10,11... | collective-permute-start | bytes 3538952 | tf_op jit(solution)/shard_map/ppermute | solution.py:29
  81.2 13.6 %collective-permute-start.19 = (bf16[304,768]{1,0:T(8,128)(2,1)S(1)}, bf16[304,768]{1,0:T(8,128)(2,1)S(1)}, u32[]{:S(2)}, u32[]{:S(2)}) collective-permute-start(bf16[304,768]{1,0:T(8,128)(2,1)S(1)} %slice.183), channel_id=1, source_target_pairs={{0,2},{1,3},{2,0},{3,1},{4,6},{5,7},{6,4},{7,5},{8,10},{9,11},{10,... | collective-permute-start | bytes 1400840 | tf_op jit(solution)/shard_map/ppermute | solution.py:29
  89.9 7.0 %collective-permute-start.21 = (bf16[80,768]{1,0:T(8,128)(2,1)S(1)}, bf16[80,768]{1,0:T(8,128)(2,1)S(1)}, u32[]{:S(2)}, u32[]{:S(2)}) collective-permute-start(bf16[80,768]{1,0:T(8,128)(2,1)S(1)} %slice.184), channel_id=1, source_target_pairs={{0,2},{1,3},{2,0},{3,1},{4,6},{5,7},{6,4},{7,5},{8,10},{9,11},{10,... | collective-permute-start | bytes 368648 | tf_op jit(solution)/shard_map/ppermute | solution.py:29
  97.0 2.9 %collective-permute-start.22 = (bf16[768,768]{1,0:T(8,128)(2,1)S(1)}, bf16[768,768]{1,0:T(8,128)(2,1)S(1)}, u32[]{:S(2)}, u32[]{:S(2)}) collective-permute-start(bf16[768,768]{1,0:T(8,128)(2,1)S(1)} %constant_dynamic-update-slice_fusion.39.refs_4_), channel_id=1, source_target_pairs={{0,1},{1,0},{2,3},{3,2},{4,5},{5,4},{6,7},{7,6},{8,9},{9,8},{10,11... | collective-permute-start | bytes 3538952 | tf_op jit(solution)/shard_map/ppermute | solution.py:29
  (1 other events, 0.7 us)

commit v11 on v10

--- a/solution.py
+++ b/solution.py
@@ -14,6 +14,7 @@
 lanes = 128
 smem = pl.BlockSpec(memory_space=pltpu.SMEM)
 vmem = pl.BlockSpec(memory_space=pltpu.VMEM)
+hbm = pl.BlockSpec(memory_space=pltpu.HBM)
 
 
 def chunk_sizes(capacity):
@@ -46,11 +47,23 @@
     return jnp.concatenate([slot_ref[q : q + 1, :] for q in range(slot_ref.shape[0])], axis=1)
 
 
-def first_kernel(capacity, chunks, groups, me_ref, slot_ref, x_ref, normed_ref, send_ref):
-    wide = x_ref[...].astype(jnp.float32)
-    normed_ref[...] = (
-        wide * lax.rsqrt(jnp.sum(wide * wide, axis=-1, keepdims=True) + epsilon)
-    ).astype(jnp.bfloat16)
+def first_kernel(
+    capacity, chunks, groups, me_ref, slots_hbm, x_hbm, normed_ref, send_ref, slot_ref, x_ref, sems
+):
+    copies = [pltpu.make_async_copy(slots_hbm, slot_ref, sems.at[0])]
+    part = x_ref.shape[0] // 3
+    for k in range(3):
+        span = pl.ds(k * part, part)
+        copies.append(pltpu.make_async_copy(x_hbm.at[span], x_ref.at[span], sems.at[k + 1]))
+    for copy in copies:
+        copy.start()
+    for k in range(3):
+        copies[k + 1].wait()
+        wide = x_ref[k * part : (k + 1) * part, :].astype(jnp.float32)
+        normed_ref[k * part : (k + 1) * part, :] = (
+            wide * lax.rsqrt(jnp.sum(wide * wide, axis=-1, keepdims=True) + epsilon)
+        ).astype(jnp.bfloat16)
+    copies[0].wait()
     send_ref[...] = place(
         me_ref[0], flat(slot_ref), normed_ref[...], capacity, 0, chunks[0], groups, 1
     )
@@ -91,9 +104,14 @@
     params = pltpu.CompilerParams(vmem_limit_bytes=24 * 2**20)
     normed, first_send = pl.pallas_call(
         functools.partial(first_kernel, capacity, chunks, groups),
-        in_specs=[smem, vmem, vmem],
+        in_specs=[smem, hbm, hbm],
         out_specs=[vmem, vmem],
         out_shape=[shape(rows), shape(half[0])],
+        scratch_shapes=[
+            pltpu.VMEM(slots.shape, jnp.int32),
+            pltpu.VMEM(embeddings.shape, embeddings.dtype),
+            pltpu.SemaphoreType.DMA((4,)),
+        ],
         compiler_params=params,
         cost_estimate=cost(half[0]),
         name="place_first",
@@ -291,10 +309,11 @@
 
     def block(step, z):
         size = chunks[step]
-        near = first_near if step == 0 else sent["y", min(step, 2) + 1]
-        skip = sum(chunks[2:step]) * high
+        near = sent["y", min(step, 2) + 1] if step else sent["y", int(z < high // 2)]
+        skip = sum(chunks[2:step]) * high if step else 0
+        index = z if step else z % (high // 2)
         return jnp.concatenate(
-            [rows(keeps[step], z, size), rows(near[skip:], z, size)], axis=0
+            [rows(keeps[step], z, size), rows(near[skip:], index, size)], axis=0
         )
 
     def send(key, value, axis, size, bit, *earlier):
@@ -306,30 +325,30 @@
         if step >= 2 and z == far[-1]:
             early += [("x", step - 2, 0)]
         if step == last and step >= 3:
-            early += [("c", step - 2 if z == far[-1] else step - 3)]
+            early += [("c", step - 3)]
         send(("z", step, z), block(step, z), "grp", groups, 2 * z, *early)
 
     def send_near_z():
-        blocks = jnp.concatenate([block(step, 1) for step in range(1, count)], axis=0)
-        send(("n",), blocks, "grp", groups, 2, ("z", 0, 1))
+        blocks = jnp.concatenate([block(step, 1) for step in range(2, count)], axis=0)
+        send(("n",), blocks, "grp", groups, 2, ("z", 1, 1), ("x", 0, 0))
 
     def collect(step):
         parts = [block(step, 0)]
         for z in range(1, high):
-            if z == 1 and step >= 1:
-                start = 2 * sum(chunks[1:step])
+            if z == 1 and step >= 2:
+                start = 2 * sum(chunks[2:step])
                 parts.append(sent["n",][start : start + 2 * chunks[step]])
             else:
                 parts.append(sent["z", step, z])
         owns[step] = jnp.concatenate(parts, axis=0)
 
-    def send_x(step, cuts, between):
+    def send_x(step, cuts, between, *earlier):
         total = owns[step].shape[0]
         cuts = [0] + [total * cut // 384 // 16 * 16 for cut in cuts] + [total]
         parts = [name for name in sent if name[:2] == ("x", step - 1)]
         for part in range(len(cuts) - 1):
             value = owns[step][cuts[part] : cuts[part + 1]]
-            early = parts if part == 0 else between[part - 1]
+            early = parts + list(earlier) if part == 0 else between[part - 1]
             send(("x", step, part), value, "blk", members, 2, *early)
 
     def send_c(step, *early):
@@ -338,30 +357,36 @@
         send(("c", step), pairs[step], "blk", members, 1, *early)
 
     far = [high // 2] + [z for z in range(1, high) if z != high // 2]
-    cut = first_send.shape[0] // 32 * 16
+    cut = first_send.shape[0] // 2
     done["rest"] = rest_send
-    send(("y", 0), first_send[:cut], "grp", groups, 1)
-    send(("y", 1), first_send[cut:], "grp", groups, 1, "rest")
+    send(("y", 0), first_send[cut:], "grp", groups, 1)
+    send(("y", 1), first_send[:cut], "grp", groups, 1, "rest")
     send(("y", 2), next_send, "grp", groups, 1, ("y", 0))
     send(("y", 3), rest_send, "grp", groups, 1, ("y", 0))
-    first_near = jnp.concatenate([sent["y", 0], sent["y", 1]], axis=0)
     for z in far:
         send_z(0, z)
-    far.remove(1)
     for step in range(1, count):
         collect(step - 1)
+        if step == 2:
+            far.remove(1)
+            send_near_z()
         for z in far:
             send_z(step, z)
-        if step == 1:
-            send_near_z()
         send_x(step - 1, [], [])
-        send_c(step - 1, *[("z", step, z) for z in far])
+        if step == last:
+            send(("o",), owns[step - 1], "blk", members, 1)
+            pairs[step - 1] = jnp.concatenate([owns[step - 1], sent["x", step - 1, 0]], axis=0)
+            early = [("z", step, z) for z in far] + [("c", step - 2)]
+            send(("p",), sent["x", step - 1, 0], "blk", members, 1, *early)
+            sent["c", step - 1] = jnp.concatenate([sent["o",], sent["p",]], axis=0)
+        else:
+            send_c(step - 1, *[("z", step, z) for z in far])
     collect(last)
     mine = [owns[k] for k in range(count)]
     blocks = [block for k in range(last) for block in (pairs[k], sent["c", k])]
     states, cols = gram_step(0, mine[:last], blocks, [], 2)
     done["gram"] = cols[-1]
-    send_x(last, [304], [["gram"]])
+    send_x(last, [304], [["gram"]], ("o",))
     send_c(last)
     states, half = gram_step(last, mine, [pairs[last]], states, 1)
     result = gram_last(

time: 117 us -> 119 us (1.017)
  waiting for transfers between devices: 55.1 us -> 51.5 us
  starting transfers between devices: 29.3 us -> 32.7 us
  blocking collectives: 10.7 us -> 12.2 us
    ppermute x23 -> x25, waiting for transfers between devices: 55.1 us -> 51.5 us  [swap(): return lax.ppermute(value, axis, [(i, i ^ bit) for i in range(size)])]
    ppermute x23 -> x25, starting transfers between devices: 29.3 us -> 32.7 us  [swap(): return lax.ppermute(value, axis, [(i, i ^ bit) for i in range(size)])]
    all_to_all x1, blocking collectives: 10.7 us -> 12.2 us  [on_device(): homeward = lax.all_to_all(result, ('grp', 'blk'), 0, 0, tiled=True)]
    unnamed x24 -> x23, local copies, waits for them, and re-layouts: 3.04 us -> 3.03 us
  transfers between devices with their start and end apart: 23 -> 25, of which waited for: 13 -> 13; matrix products, arithmetic and copies ran while one was open for 1% -> 1% of each run, Pallas kernels for 9% -> 7%
where the time goes in v11:
time: 119 us
  waiting for transfers between devices  51.5 us (43%)
  starting transfers between devices  32.7 us (27%)
  Pallas kernels  18.6 us (16%)
  blocking collectives  12.2 us (10%)
  local copies, waits for them, and re-layouts  3.27 us (3%)
    ppermute x25, waiting for transfers between devices, swap(): return lax.ppermute(value, axis, [(i, i ^ bit) for i in range(size)])  51.5 us
    ppermute x25, starting transfers between devices, swap(): return lax.ppermute(value, axis, [(i, i ^ bit) for i in range(size)])  32.7 us
    all_to_all x1, blocking collectives, on_device(): homeward = lax.all_to_all(result, ('grp', 'blk'), 0, 0, tiled=True)  12.2 us
    pallas_call x2, Pallas kernels, gram_step(): pl.pallas_call(functools.partial(gram_kernel, first, step, pieces), in_sp...  8.46 us
    pallas_call x1, Pallas kernels, gram_last(): pl.pallas_call(functools.partial(gram_last_kernel, step, relatives, chunk...  3.08 us
    unnamed x23, local copies, waits for them, and re-layouts  3.03 us
    pallas_call x1, Pallas kernels, head(): pl.pallas_call(functools.partial(rest_kernel, capacity, chunks, groups),...  2.61 us
  transfers between devices with their start and end apart: 25, of which 13 were waited for; matrix products, arithmetic and copies ran while one was open for 1% of the time, Pallas kernels for 7%

profile of v11, /device:TPU:0, one launch (start us, length us, event | category | flops | bytes accessed | tf_op | source)
XLA Modules:
  0.0 118.9 jit_solution(3248666621284782030)
XLA Ops:
  2.0 2.1 %place_first.1 = (bf16[768,768]{1,0:T(8,128)(2,1)S(1)}, bf16[192,768]{1,0:T(8,128)(2,1)S(1)}) custom-call(s32[2]{0:T(128)S(1)} %pad_add_fusion.me_ref, s32[6,128]{1,0:T(8,128)S(1)} %bitcast.10, bf16[768,768]{1,0:T(8,128)(2,1)S(1)} %copy-done), custom_call_target="tpu_custom_call" | custom-call | flops 226492416 | bytes 1474560 | tf_op jit(solution)/shard_map/place_first/pallas_call | solution.py:105
  4.2 2.6 %place_rest.1 = (bf16[192,768]{1,0:T(8,128)(2,1)S(1)}, bf16[192,768]{1,0:T(8,128)(2,1)S(1)}, bf16[192,768]{1,0:T(8,128)(2,1)S(1)}, bf16[192,768]{1,0:T(8,128)(2,...) custom-call(s32[2]{0:T(128)S(1)} %pad_add_fusion.me_ref, s32[6,128]{1,0:T(8,128)S(1)} %bitcast.11, ...), custom_call_target="tpu_custom_call" | custom-call | flops 1585446912 | bytes 3244032 | tf_op jit(solution)/shard_map/place_rest/pallas_call | solution.py:119
  6.8 3.0 %collective-permute-start = (bf16[96,768]{1,0:T(8,128)(2,1)S(1)}, bf16[96,768]{1,0:T(8,128)(2,1)S(1)}, u32[]{:S(2)}, u32[]{:S(2)}) collective-permute-start(bf16[96,768]{1,0:T(8,128)(2,1)S(1)} %get-tuple-element.46), channel_id=1, source_target_pairs={{0,4},{4,0},{8,12},{12,8},{16,20},{20,16},{24,28},{28,24},{1,5},{5... | collective-permute-start | bytes 442376 | tf_op jit(solution)/shard_map/ppermute | solution.py:30
  10.0 4.5 %collective-permute-done = bf16[96,768]{1,0:T(8,128)(2,1)S(1)} collective-permute-done((bf16[96,768]{1,0:T(8,128)(2,1)S(1)}, bf16[96,768]{1,0:T(8,128)(2,1)S(1)}, u32[]{:S(2)}, u32[]{:S(2)}) %collective-permute-start) | collective-permute-done | bytes 147488 | tf_op jit(solution)/shard_map/ppermute | solution.py:30
  14.6 2.2 %collective-permute-start.1 = (bf16[96,768]{1,0:T(8,128)(2,1)S(1)}, bf16[96,768]{1,0:T(8,128)(2,1)S(1)}, u32[]{:S(2)}, u32[]{:S(2)}) collective-permute-start(bf16[96,768]{1,0:T(8,128)(2,1)S(1)} %pad_maximum_fusion.2), channel_id=1, source_target_pairs={{0,8},{4,12},{8,0},{12,4},{16,24},{20,28},{24,16},{28,20},{1,9},{5... | collective-permute-start | bytes 442376 | tf_op jit(solution)/shard_map/ppermute | solution.py:30
  16.9 2.9 %collective-permute-start.3 = (bf16[96,768]{1,0:T(8,128)(2,1)S(1)}, bf16[96,768]{1,0:T(8,128)(2,1)S(1)}, u32[]{:S(2)}, u32[]{:S(2)}) collective-permute-start(bf16[96,768]{1,0:T(8,128)(2,1)S(1)} %pad_maximum_fusion.3), channel_id=1, source_target_pairs={{0,16},{4,20},{8,24},{12,28},{16,0},{20,4},{24,8},{28,12},{1,17},{... | collective-permute-start | bytes 442376 | tf_op jit(solution)/shard_map/ppermute | solution.py:30
  23.2 7.3 %collective-permute-done.3 = bf16[96,768]{1,0:T(8,128)(2,1)S(1)} collective-permute-done((bf16[96,768]{1,0:T(8,128)(2,1)S(1)}, bf16[96,768]{1,0:T(8,128)(2,1)S(1)}, u32[]{:S(2)}, u32[]{:S(2)}) %collective-permute-start.3) | collective-permute-done | bytes 147488 | tf_op jit(solution)/shard_map/ppermute | solution.py:30
  30.6 1.7 %collective-permute-start.10 = (bf16[384,768]{1,0:T(8,128)(2,1)S(1)}, bf16[384,768]{1,0:T(8,128)(2,1)S(1)}, u32[]{:S(2)}, u32[]{:S(2)}) collective-permute-start(bf16[384,768]{1,0:T(8,128)(2,1)S(1)} %get-tuple-element.135.refs_0_), channel_id=1, source_target_pairs={{0,2},{1,3},{2,0},{3,1},{4,6},{5,7},{6,4},{7,5},{8,10},{9,11},{10,... | collective-permute-start | bytes 1769480 | tf_op jit(solution)/shard_map/ppermute | solution.py:30
  32.3 2.4 %collective-permute-start.6 = (bf16[96,768]{1,0:T(8,128)(2,1)S(1)}, bf16[96,768]{1,0:T(8,128)(2,1)S(1)}, u32[]{:S(2)}, u32[]{:S(2)}) collective-permute-start(bf16[96,768]{1,0:T(8,128)(2,1)S(1)} %pad_maximum_fusion.5), channel_id=1, source_target_pairs={{0,8},{4,12},{8,0},{12,4},{16,24},{20,28},{24,16},{28,20},{1,9},{5... | collective-permute-start | bytes 442376 | tf_op jit(solution)/shard_map/ppermute | solution.py:30
  34.7 2.0 %collective-permute-start.7 = (bf16[96,768]{1,0:T(8,128)(2,1)S(1)}, bf16[96,768]{1,0:T(8,128)(2,1)S(1)}, u32[]{:S(2)}, u32[]{:S(2)}) collective-permute-start(bf16[96,768]{1,0:T(8,128)(2,1)S(1)} %pad_maximum_fusion.6), channel_id=1, source_target_pairs={{0,16},{4,20},{8,24},{12,28},{16,0},{20,4},{24,8},{28,12},{1,17},{... | collective-permute-start | bytes 442376 | tf_op jit(solution)/shard_map/ppermute | solution.py:30
  39.7 8.8 %collective-permute-done.7 = bf16[96,768]{1,0:T(8,128)(2,1)S(1)} collective-permute-done((bf16[96,768]{1,0:T(8,128)(2,1)S(1)}, bf16[96,768]{1,0:T(8,128)(2,1)S(1)}, u32[]{:S(2)}, u32[]{:S(2)}) %collective-permute-start.7) | collective-permute-done | bytes 147488 | tf_op jit(solution)/shard_map/ppermute | solution.py:30
  49.3 3.6 %collective-permute-start.12 = (bf16[96,768]{1,0:T(8,128)(2,1)S(1)}, bf16[96,768]{1,0:T(8,128)(2,1)S(1)}, u32[]{:S(2)}, u32[]{:S(2)}) collective-permute-start(bf16[96,768]{1,0:T(8,128)(2,1)S(1)} %pad_maximum_fusion.8), channel_id=1, source_target_pairs={{0,16},{4,20},{8,24},{12,28},{16,0},{20,4},{24,8},{28,12},{1,17},{... | collective-permute-start | bytes 442376 | tf_op jit(solution)/shard_map/ppermute | solution.py:30
  54.7 5.9 %collective-permute-done.16 = bf16[384,768]{1,0:T(8,128)(2,1)S(1)} collective-permute-done((bf16[384,768]{1,0:T(8,128)(2,1)S(1)}, bf16[384,768]{1,0:T(8,128)(2,1)S(1)}, u32[]{:S(2)}, u32[]{:S(2)}) %collective-permute-start.16) | collective-permute-done | bytes 589856 | tf_op jit(solution)/shard_map/ppermute | solution.py:30
  60.6 5.2 %collective-permute-done.13 = bf16[96,768]{1,0:T(8,128)(2,1)S(1)} collective-permute-done((bf16[96,768]{1,0:T(8,128)(2,1)S(1)}, bf16[96,768]{1,0:T(8,128)(2,1)S(1)}, u32[]{:S(2)}, u32[]{:S(2)}) %collective-permute-start.13) | collective-permute-done | bytes 147488 | tf_op jit(solution)/shard_map/ppermute | solution.py:30
  66.2 1.6 %collective-permute-start.18 = (bf16[384,768]{1,0:T(8,128)(2,1)S(1)}, bf16[384,768]{1,0:T(8,128)(2,1)S(1)}, u32[]{:S(2)}, u32[]{:S(2)}) collective-permute-start(bf16[384,768]{1,0:T(8,128)(2,1)S(1)} %get-tuple-element.63.refs_2_), channel_id=1, source_target_pairs={{0,2},{1,3},{2,0},{3,1},{4,6},{5,7},{6,4},{7,5},{8,10},{9,11},{10,... | collective-permute-start | bytes 1769480 | tf_op jit(solution)/shard_map/ppermute | solution.py:30
  67.8 2.7 %collective-permute-start.17 = (bf16[96,768]{1,0:T(8,128)(2,1)S(1)}, bf16[96,768]{1,0:T(8,128)(2,1)S(1)}, u32[]{:S(2)}, u32[]{:S(2)}) collective-permute-start(bf16[96,768]{1,0:T(8,128)(2,1)S(1)} %pad_maximum_fusion.11), channel_id=1, source_target_pairs={{0,24},{4,28},{8,16},{12,20},{16,8},{20,12},{24,0},{28,4},{1,25},{... | collective-permute-start | bytes 442376 | tf_op jit(solution)/shard_map/ppermute | solution.py:30
  70.5 11.2 %collective-permute-done.18 = bf16[384,768]{1,0:T(8,128)(2,1)S(1)} collective-permute-done((bf16[384,768]{1,0:T(8,128)(2,1)S(1)}, bf16[384,768]{1,0:T(8,128)(2,1)S(1)}, u32[]{:S(2)}, u32[]{:S(2)}) %collective-permute-start.18) | collective-permute-done | bytes 589856 | tf_op jit(solution)/shard_map/ppermute | solution.py:30
  83.9 6.0 %gram_step.2 = (f32[384,128]{1,0:T(8,128)S(1)}, f32[384,128]{1,0:T(8,128)S(1)}, f32[384,128]{1,0:T(8,128)S(1)}, f32[1,1536]{1,0:T(1,128)S(1)}, f32[1,1536]{1,0:T(1,128)S(1)}, /*index=5*/f32[1,1536]{1,0:T(1,128)S(1)}) custom-call(bf16[384,768]{1,0:T(8,128)(2,1)S(1)} %get-tuple-element.135.refs_0_, bf16[384,768]{1,0:T(8,128)(2,1)S(1)} %get-tuple-element.61.refs_1_, ...), custom_call_target="tpu_custom_call" | custom-call | flops 8153726976 | bytes 8847360 | tf_op jit(solution)/shard_map/gram_step/pallas_call | solution.py:231
  91.4 4.1 %collective-permute-done.20 = bf16[304,768]{1,0:T(8,128)(2,1)S(1)} collective-permute-done((bf16[304,768]{1,0:T(8,128)(2,1)S(1)}, bf16[304,768]{1,0:T(8,128)(2,1)S(1)}, u32[]{:S(2)}, u32[]{:S(2)}) %collective-permute-start.20) | collective-permute-done | bytes 466976 | tf_op jit(solution)/shard_map/ppermute | solution.py:30
  95.5 2.2 %collective-permute-done.23 = bf16[80,768]{1,0:T(8,128)(2,1)S(1)} collective-permute-done((bf16[80,768]{1,0:T(8,128)(2,1)S(1)}, bf16[80,768]{1,0:T(8,128)(2,1)S(1)}, u32[]{:S(2)}, u32[]{:S(2)}) %collective-permute-start.23) | collective-permute-done | bytes 122912 | tf_op jit(solution)/shard_map/ppermute | solution.py:30
  97.8 2.4 %gram_step.3 = (f32[384,128]{1,0:T(8,128)S(1)}, f32[384,128]{1,0:T(8,128)S(1)}, f32[384,128]{1,0:T(8,128)S(1)}, f32[384,128]{1,0:T(8,128)S(1)}, f32[1,768]{1,0:T(1,128)S(1)}) custom-call(bf16[384,768]{1,0:T(8,128)(2,1)S(1)} %get-tuple-element.135.refs_0_, bf16[384,768]{1,0:T(8,128)(2,1)S(1)} %get-tuple-element.61.refs_1_, ...), custom_call_target="tpu_custom_call" | custom-call | flops 1811939328 | bytes 3538944 | tf_op jit(solution)/shard_map/gram_step/pallas_call | solution.py:231
  100.7 3.1 %gram_last.1 = f32[32,192]{1,0:T(8,128)S(1)} custom-call(s32[2]{0:T(128)S(1)} %pad_add_fusion.me_ref, bf16[384,768]{1,0:T(8,128)(2,1)S(1)} %get-tuple-element.135.refs_0_, bf16[384,768]{1,0:T(8,128)(2,1)S(1)} %get-tuple-element.61.refs_1_, bf16[384,768]{1,0:T(8,128)(2,1)S(1)} %get-tuple-element.63.refs_2_, bf16[384,768]{1,0:T(8,128)(2,1)S(1)} %get-tuple-element.131.refs_3_, ...), custom_call_target="tpu_custom_call" | custom-call | flops 1811939328 | bytes 3538944 | tf_op jit(solution)/shard_map/gram_last/pallas_call | solution.py:246
  103.8 12.2 %all_to_all.11 = f32[32,1,192]{2,1,0:T(1,128)S(1)} all-to-all(f32[32,1,192]{2,1,0:T(1,128)S(1)} %copy.3), channel_id=1, replica_groups=mesh['grp'=8,'blk'=4] {'grp','blk'}, dimensions={0} | all-to-all | bytes 49152 | tf_op jit(solution)/shard_map/all_to_all | solution.py:395
  116.6 2.3 %pick_rows.1 = f32[6,128]{1,0:T(8,128)} custom-call(s32[6,128]{1,0:T(8,128)} %bitcast.9, f32[32,192]{1,0:T(8,128)} %bitcast.12), custom_call_target="tpu_custom_call" | custom-call | tf_op jit(solution)/shard_map/pick_rows/pallas_call | solution.py:282
  (78 shorter events, 16.7 us)
Async XLA Ops:
  6.8 7.7 %collective-permute-start = (bf16[96,768]{1,0:T(8,128)(2,1)S(1)}, bf16[96,768]{1,0:T(8,128)(2,1)S(1)}, u32[]{:S(2)}, u32[]{:S(2)}) collective-permute-start(bf16[96,768]{1,0:T(8,128)(2,1)S(1)} %get-tuple-element.46), channel_id=1, source_target_pairs={{0,4},{4,0},{8,12},{12,8},{16,20},{20,16},{24,28},{28,24},{1,5},{5... | collective-permute-start | bytes 442376 | tf_op jit(solution)/shard_map/ppermute | solution.py:30
  9.8 7.0 %collective-permute-start.2 = (bf16[96,768]{1,0:T(8,128)(2,1)S(1)}, bf16[96,768]{1,0:T(8,128)(2,1)S(1)}, u32[]{:S(2)}, u32[]{:S(2)}) collective-permute-start(bf16[96,768]{1,0:T(8,128)(2,1)S(1)} %get-tuple-element.118), channel_id=1, source_target_pairs={{0,4},{4,0},{8,12},{12,8},{16,20},{20,16},{24,28},{28,24},{1,5},{5... | collective-permute-start | bytes 442376 | tf_op jit(solution)/shard_map/ppermute | solution.py:30
  14.6 8.7 %collective-permute-start.1 = (bf16[96,768]{1,0:T(8,128)(2,1)S(1)}, bf16[96,768]{1,0:T(8,128)(2,1)S(1)}, u32[]{:S(2)}, u32[]{:S(2)}) collective-permute-start(bf16[96,768]{1,0:T(8,128)(2,1)S(1)} %pad_maximum_fusion.2), channel_id=1, source_target_pairs={{0,8},{4,12},{8,0},{12,4},{16,24},{20,28},{24,16},{28,20},{1,9},{5... | collective-permute-start | bytes 442376 | tf_op jit(solution)/shard_map/ppermute | solution.py:30
  16.9 13.6 %collective-permute-start.3 = (bf16[96,768]{1,0:T(8,128)(2,1)S(1)}, bf16[96,768]{1,0:T(8,128)(2,1)S(1)}, u32[]{:S(2)}, u32[]{:S(2)}) collective-permute-start(bf16[96,768]{1,0:T(8,128)(2,1)S(1)} %pad_maximum_fusion.3), channel_id=1, source_target_pairs={{0,16},{4,20},{8,24},{12,28},{16,0},{20,4},{24,8},{28,12},{1,17},{... | collective-permute-start | bytes 442376 | tf_op jit(solution)/shard_map/ppermute | solution.py:30
  19.8 10.8 %collective-permute-start.4 = (bf16[96,768]{1,0:T(8,128)(2,1)S(1)}, bf16[96,768]{1,0:T(8,128)(2,1)S(1)}, u32[]{:S(2)}, u32[]{:S(2)}) collective-permute-start(bf16[96,768]{1,0:T(8,128)(2,1)S(1)} %pad_maximum_fusion.4), channel_id=1, source_target_pairs={{0,24},{4,28},{8,16},{12,20},{16,8},{20,12},{24,0},{28,4},{1,25},{... | collective-permute-start | bytes 442376 | tf_op jit(solution)/shard_map/ppermute | solution.py:30
  21.2 11.1 %collective-permute-start.5 = (bf16[192,768]{1,0:T(8,128)(2,1)S(1)}, bf16[192,768]{1,0:T(8,128)(2,1)S(1)}, u32[]{:S(2)}, u32[]{:S(2)}) collective-permute-start(bf16[192,768]{1,0:T(8,128)(2,1)S(1)} %get-tuple-element.49), channel_id=1, source_target_pairs={{0,4},{4,0},{8,12},{12,8},{16,20},{20,16},{24,28},{28,24},{1,5},{5... | collective-permute-start | bytes 884744 | tf_op jit(solution)/shard_map/ppermute | solution.py:30
  22.7 26.5 %collective-permute-start.9 = (bf16[384,768]{1,0:T(8,128)(2,1)S(1)}, bf16[384,768]{1,0:T(8,128)(2,1)S(1)}, u32[]{:S(2)}, u32[]{:S(2)}) collective-permute-start(bf16[384,768]{1,0:T(8,128)(2,1)S(1)} %get-tuple-element.54), channel_id=1, source_target_pairs={{0,4},{4,0},{8,12},{12,8},{16,20},{20,16},{24,28},{28,24},{1,5},{5... | collective-permute-start | bytes 1769480 | tf_op jit(solution)/shard_map/ppermute | solution.py:30
  30.6 18.0 %collective-permute-start.10 = (bf16[384,768]{1,0:T(8,128)(2,1)S(1)}, bf16[384,768]{1,0:T(8,128)(2,1)S(1)}, u32[]{:S(2)}, u32[]{:S(2)}) collective-permute-start(bf16[384,768]{1,0:T(8,128)(2,1)S(1)} %get-tuple-element.135.refs_0_), channel_id=1, source_target_pairs={{0,2},{1,3},{2,0},{3,1},{4,6},{5,7},{6,4},{7,5},{8,10},{9,11},{10,... | collective-permute-start | bytes 1769480 | tf_op jit(solution)/shard_map/ppermute | solution.py:30
  32.3 7.4 %collective-permute-start.6 = (bf16[96,768]{1,0:T(8,128)(2,1)S(1)}, bf16[96,768]{1,0:T(8,128)(2,1)S(1)}, u32[]{:S(2)}, u32[]{:S(2)}) collective-permute-start(bf16[96,768]{1,0:T(8,128)(2,1)S(1)} %pad_maximum_fusion.5), channel_id=1, source_target_pairs={{0,8},{4,12},{8,0},{12,4},{16,24},{20,28},{24,16},{28,20},{1,9},{5... | collective-permute-start | bytes 442376 | tf_op jit(solution)/shard_map/ppermute | solution.py:30
  34.7 13.8 %collective-permute-start.7 = (bf16[96,768]{1,0:T(8,128)(2,1)S(1)}, bf16[96,768]{1,0:T(8,128)(2,1)S(1)}, u32[]{:S(2)}, u32[]{:S(2)}) collective-permute-start(bf16[96,768]{1,0:T(8,128)(2,1)S(1)} %pad_maximum_fusion.6), channel_id=1, source_target_pairs={{0,16},{4,20},{8,24},{12,28},{16,0},{20,4},{24,8},{28,12},{1,17},{... | collective-permute-start | bytes 442376 | tf_op jit(solution)/shard_map/ppermute | solution.py:30
  36.7 11.8 %collective-permute-start.8 = (bf16[96,768]{1,0:T(8,128)(2,1)S(1)}, bf16[96,768]{1,0:T(8,128)(2,1)S(1)}, u32[]{:S(2)}, u32[]{:S(2)}) collective-permute-start(bf16[96,768]{1,0:T(8,128)(2,1)S(1)} %pad_maximum_fusion.7), channel_id=1, source_target_pairs={{0,24},{4,28},{8,16},{12,20},{16,8},{20,12},{24,0},{28,4},{1,25},{... | collective-permute-start | bytes 442376 | tf_op jit(solution)/shard_map/ppermute | solution.py:30
  48.6 12.0 %collective-permute-start.16 = (bf16[384,768]{1,0:T(8,128)(2,1)S(1)}, bf16[384,768]{1,0:T(8,128)(2,1)S(1)}, u32[]{:S(2)}, u32[]{:S(2)}) collective-permute-start(bf16[384,768]{1,0:T(8,128)(2,1)S(1)} %get-tuple-element.61.refs_1_), channel_id=1, source_target_pairs={{0,2},{1,3},{2,0},{3,1},{4,6},{5,7},{6,4},{7,5},{8,10},{9,11},{10,... | collective-permute-start | bytes 1769480 | tf_op jit(solution)/shard_map/ppermute | solution.py:30
  49.3 11.3 %collective-permute-start.12 = (bf16[96,768]{1,0:T(8,128)(2,1)S(1)}, bf16[96,768]{1,0:T(8,128)(2,1)S(1)}, u32[]{:S(2)}, u32[]{:S(2)}) collective-permute-start(bf16[96,768]{1,0:T(8,128)(2,1)S(1)} %pad_maximum_fusion.8), channel_id=1, source_target_pairs={{0,16},{4,20},{8,24},{12,28},{16,0},{20,4},{24,8},{28,12},{1,17},{... | collective-permute-start | bytes 442376 | tf_op jit(solution)/shard_map/ppermute | solution.py:30
  52.9 13.1 %collective-permute-start.11 = (bf16[192,768]{1,0:T(8,128)(2,1)S(1)}, bf16[192,768]{1,0:T(8,128)(2,1)S(1)}, u32[]{:S(2)}, u32[]{:S(2)}) collective-permute-start(bf16[192,768]{1,0:T(8,128)(2,1)S(1)} %pad_maximum_fusion.1), channel_id=1, source_target_pairs={{0,8},{4,12},{8,0},{12,4},{16,24},{20,28},{24,16},{28,20},{1,9},{5... | collective-permute-start | bytes 884744 | tf_op jit(solution)/shard_map/ppermute | solution.py:30
  53.0 14.7 %collective-permute-start.14 = (bf16[768,768]{1,0:T(8,128)(2,1)S(1)}, bf16[768,768]{1,0:T(8,128)(2,1)S(1)}, u32[]{:S(2)}, u32[]{:S(2)}) collective-permute-start(bf16[768,768]{1,0:T(8,128)(2,1)S(1)} %constant_dynamic-update-slice_fusion.14.refs_3_), channel_id=1, source_target_pairs={{0,1},{1,0},{2,3},{3,2},{4,5},{5,4},{6,7},{7,6},{8,9},{9,8},{10,11... | collective-permute-start | bytes 3538952 | tf_op jit(solution)/shard_map/ppermute | solution.py:30
  53.1 12.6 %collective-permute-start.13 = (bf16[96,768]{1,0:T(8,128)(2,1)S(1)}, bf16[96,768]{1,0:T(8,128)(2,1)S(1)}, u32[]{:S(2)}, u32[]{:S(2)}) collective-permute-start(bf16[96,768]{1,0:T(8,128)(2,1)S(1)} %pad_maximum_fusion.9), channel_id=1, source_target_pairs={{0,24},{4,28},{8,16},{12,20},{16,8},{20,12},{24,0},{28,4},{1,25},{... | collective-permute-start | bytes 442376 | tf_op jit(solution)/shard_map/ppermute | solution.py:30
  65.8 15.9 %collective-permute-start.21 = (bf16[768,768]{1,0:T(8,128)(2,1)S(1)}, bf16[768,768]{1,0:T(8,128)(2,1)S(1)}, u32[]{:S(2)}, u32[]{:S(2)}) collective-permute-start(bf16[768,768]{1,0:T(8,128)(2,1)S(1)} %constant_dynamic-update-slice_fusion.24.refs_5_), channel_id=1, source_target_pairs={{0,1},{1,0},{2,3},{3,2},{4,5},{5,4},{6,7},{7,6},{8,9},{9,8},{10,11... | collective-permute-start | bytes 3538952 | tf_op jit(solution)/shard_map/ppermute | solution.py:30
  66.2 15.5 %collective-permute-start.18 = (bf16[384,768]{1,0:T(8,128)(2,1)S(1)}, bf16[384,768]{1,0:T(8,128)(2,1)S(1)}, u32[]{:S(2)}, u32[]{:S(2)}) collective-permute-start(bf16[384,768]{1,0:T(8,128)(2,1)S(1)} %get-tuple-element.63.refs_2_), channel_id=1, source_target_pairs={{0,2},{1,3},{2,0},{3,1},{4,6},{5,7},{6,4},{7,5},{8,10},{9,11},{10,... | collective-permute-start | bytes 1769480 | tf_op jit(solution)/shard_map/ppermute | solution.py:30
  67.8 13.9 %collective-permute-start.15 = (bf16[96,768]{1,0:T(8,128)(2,1)S(1)}, bf16[96,768]{1,0:T(8,128)(2,1)S(1)}, u32[]{:S(2)}, u32[]{:S(2)}) collective-permute-start(bf16[96,768]{1,0:T(8,128)(2,1)S(1)} %pad_maximum_fusion.10), channel_id=1, source_target_pairs={{0,16},{4,20},{8,24},{12,28},{16,0},{20,4},{24,8},{28,12},{1,17},{... | collective-permute-start | bytes 442376 | tf_op jit(solution)/shard_map/ppermute | solution.py:30
  67.8 13.8 %collective-permute-start.17 = (bf16[96,768]{1,0:T(8,128)(2,1)S(1)}, bf16[96,768]{1,0:T(8,128)(2,1)S(1)}, u32[]{:S(2)}, u32[]{:S(2)}) collective-permute-start(bf16[96,768]{1,0:T(8,128)(2,1)S(1)} %pad_maximum_fusion.11), channel_id=1, source_target_pairs={{0,24},{4,28},{8,16},{12,20},{16,8},{20,12},{24,0},{28,4},{1,25},{... | collective-permute-start | bytes 442376 | tf_op jit(solution)/shard_map/ppermute | solution.py:30
  70.5 11.4 %collective-permute-start.19 = (bf16[384,768]{1,0:T(8,128)(2,1)S(1)}, bf16[384,768]{1,0:T(8,128)(2,1)S(1)}, u32[]{:S(2)}, u32[]{:S(2)}) collective-permute-start(bf16[384,768]{1,0:T(8,128)(2,1)S(1)} %get-tuple-element.63.refs_2_), channel_id=1, source_target_pairs={{0,1},{1,0},{2,3},{3,2},{4,5},{5,4},{6,7},{7,6},{8,9},{9,8},{10,11... | collective-permute-start | bytes 1769480 | tf_op jit(solution)/shard_map/ppermute | solution.py:30
  81.9 13.6 %collective-permute-start.20 = (bf16[304,768]{1,0:T(8,128)(2,1)S(1)}, bf16[304,768]{1,0:T(8,128)(2,1)S(1)}, u32[]{:S(2)}, u32[]{:S(2)}) collective-permute-start(bf16[304,768]{1,0:T(8,128)(2,1)S(1)} %slice.178), channel_id=1, source_target_pairs={{0,2},{1,3},{2,0},{3,1},{4,6},{5,7},{6,4},{7,5},{8,10},{9,11},{10,... | collective-permute-start | bytes 1400840 | tf_op jit(solution)/shard_map/ppermute | solution.py:30
  89.9 7.9 %collective-permute-start.23 = (bf16[80,768]{1,0:T(8,128)(2,1)S(1)}, bf16[80,768]{1,0:T(8,128)(2,1)S(1)}, u32[]{:S(2)}, u32[]{:S(2)}) collective-permute-start(bf16[80,768]{1,0:T(8,128)(2,1)S(1)} %slice.179), channel_id=1, source_target_pairs={{0,2},{1,3},{2,0},{3,1},{4,6},{5,7},{6,4},{7,5},{8,10},{9,11},{10,... | collective-permute-start | bytes 368648 | tf_op jit(solution)/shard_map/ppermute | solution.py:30
  97.7 2.9 %collective-permute-start.24 = (bf16[768,768]{1,0:T(8,128)(2,1)S(1)}, bf16[768,768]{1,0:T(8,128)(2,1)S(1)}, u32[]{:S(2)}, u32[]{:S(2)}) collective-permute-start(bf16[768,768]{1,0:T(8,128)(2,1)S(1)} %constant_dynamic-update-slice_fusion.35.refs_4_), channel_id=1, source_target_pairs={{0,1},{1,0},{2,3},{3,2},{4,5},{5,4},{6,7},{7,6},{8,9},{9,8},{10,11... | collective-permute-start | bytes 3538952 | tf_op jit(solution)/shard_map/ppermute | solution.py:30
  (3 other events, 4.0 us)

commit v12 on v10

--- a/solution.py
+++ b/solution.py
@@ -29,10 +29,11 @@
     return lax.ppermute(value, axis, [(i, i ^ bit) for i in range(size)])
 
 
-def place(me, slots, normed, capacity, first, size, groups, low):
-    shape = (groups // 2, size, 1)
+def place(me, slots, normed, capacity, first, size, groups, low, turn=0):
+    high = groups // 2
+    shape = (high, size, 1)
     spot = lax.broadcasted_iota(jnp.int32, shape, 1) + first
-    group = (lax.broadcasted_iota(jnp.int32, shape, 0) * 2 + low) ^ me
+    group = ((lax.broadcasted_iota(jnp.int32, shape, 0) + turn) % high * 2 + low) ^ me
     wanted = (group * capacity + spot).reshape(groups // 2 * size, 1)
     pick = jnp.where(wanted == slots, 1.0, 0.0)
     live = jnp.max(pick, axis=1, keepdims=True)
@@ -52,7 +53,7 @@
         wide * lax.rsqrt(jnp.sum(wide * wide, axis=-1, keepdims=True) + epsilon)
     ).astype(jnp.bfloat16)
     send_ref[...] = place(
-        me_ref[0], flat(slot_ref), normed_ref[...], capacity, 0, chunks[0], groups, 1
+        me_ref[0], flat(slot_ref), normed_ref[...], capacity, 0, chunks[0], groups, 1, groups // 4
     )
 
 
@@ -190,7 +191,7 @@
         for p, relative in enumerate(relatives):
             row = r * members + p
             target = (me_ref[0] ^ r) * members + (me_ref[1] ^ relative)
-            out_ref[pl.ds(target, 1), :] = table[row : row + 1, :]
+            out_ref[target] = table[row : row + 1, :]
 
 
 def gram_params(owns, blocks):
@@ -224,13 +225,13 @@
 def gram_last(me, owns, block, states, cols, relatives, chunks, groups):
     step = len(owns) - 1
     members = len(relatives)
-    shape = (groups * members, sum(chunks))
+    shape = (groups * members, 1, sum(chunks))
     return pl.pallas_call(
         functools.partial(gram_last_kernel, step, relatives, chunks, groups),
         in_specs=[smem] + [vmem] * (3 * step + 4),
         out_specs=vmem,
         out_shape=jax.ShapeDtypeStruct(shape, jnp.float32),
-        scratch_shapes=[pltpu.VMEM((1, block.shape[0]), jnp.float32), pltpu.VMEM(shape, jnp.float32)]
+        scratch_shapes=[pltpu.VMEM((1, block.shape[0]), jnp.float32), pltpu.VMEM(shape[::2], jnp.float32)]
         + [pltpu.VMEM((own.shape[0], lanes), jnp.float32) for own in owns],
         name="gram_last",
         **gram_params(owns, [block]),
@@ -243,7 +244,7 @@
     table[...] = jnp.full(table.shape, sentinel, jnp.float32)
     for g in range(groups):
         table[g : g + 1, :capacity] = jnp.max(
-            part_ref[g * members : (g + 1) * members, :], axis=0, keepdims=True
+            part_ref[g * members : (g + 1) * members], axis=0
         )
     lane = lax.broadcasted_iota(jnp.int32, (lanes, lanes), 1)
     for q in range(out_ref.shape[0]):
@@ -291,10 +292,11 @@
 
     def block(step, z):
         size = chunks[step]
-        near = first_near if step == 0 else sent["y", min(step, 2) + 1]
-        skip = sum(chunks[2:step]) * high
+        near = sent["y", min(step, 2) + 1] if step else sent["y", int(z < high // 2)]
+        skip = sum(chunks[2:step]) * high if step else 0
+        index = z if step else z % (high // 2)
         return jnp.concatenate(
-            [rows(keeps[step], z, size), rows(near[skip:], z, size)], axis=0
+            [rows(keeps[step], z, size), rows(near[skip:], index, size)], axis=0
         )
 
     def send(key, value, axis, size, bit, *earlier):
@@ -310,14 +312,14 @@
         send(("z", step, z), block(step, z), "grp", groups, 2 * z, *early)
 
     def send_near_z():
-        blocks = jnp.concatenate([block(step, 1) for step in range(1, count)], axis=0)
-        send(("n",), blocks, "grp", groups, 2, ("z", 0, 1))
+        blocks = jnp.concatenate([block(step, 1) for step in range(2, count)], axis=0)
+        send(("n",), blocks, "grp", groups, 2, ("z", 1, 1))
 
     def collect(step):
         parts = [block(step, 0)]
         for z in range(1, high):
-            if z == 1 and step >= 1:
-                start = 2 * sum(chunks[1:step])
+            if z == 1 and step >= 2:
+                start = 2 * sum(chunks[2:step])
                 parts.append(sent["n",][start : start + 2 * chunks[step]])
             else:
                 parts.append(sent["z", step, z])
@@ -338,21 +340,20 @@
         send(("c", step), pairs[step], "blk", members, 1, *early)
 
     far = [high // 2] + [z for z in range(1, high) if z != high // 2]
-    cut = first_send.shape[0] // 32 * 16
+    cut = first_send.shape[0] // 2
     done["rest"] = rest_send
     send(("y", 0), first_send[:cut], "grp", groups, 1)
     send(("y", 1), first_send[cut:], "grp", groups, 1, "rest")
     send(("y", 2), next_send, "grp", groups, 1, ("y", 0))
     send(("y", 3), rest_send, "grp", groups, 1, ("y", 0))
-    first_near = jnp.concatenate([sent["y", 0], sent["y", 1]], axis=0)
     for z in far:
         send_z(0, z)
-    far.remove(1)
     for step in range(1, count):
         collect(step - 1)
         for z in far:
             send_z(step, z)
         if step == 1:
+            far.remove(1)
             send_near_z()
         send_x(step - 1, [], [])
         send_c(step - 1, *[("z", step, z) for z in far])

time: 117 us -> 117 us (level)
  starting transfers between devices: 29.3 us -> 32.3 us
  waiting for transfers between devices: 55.1 us -> 52.6 us
    ppermute x23 -> x24, starting transfers between devices: 29.3 us -> 32.3 us  [swap(): return lax.ppermute(value, axis, [(i, i ^ bit) for i in range(size)])]
    ppermute x23 -> x24, waiting for transfers between devices: 55.1 us -> 52.6 us  [swap(): return lax.ppermute(value, axis, [(i, i ^ bit) for i in range(size)])]
    unnamed x24 -> x22, local copies, waits for them, and re-layouts: 3.04 us -> 2.43 us
  transfers between devices with their start and end apart: 23 -> 24, of which waited for: 13 -> 13; matrix products, arithmetic and copies ran while one was open for 1% -> 1% of each run, Pallas kernels for 9% -> 7%
where the time goes in v12:
time: 117 us
  waiting for transfers between devices  52.6 us (45%)
  starting transfers between devices  32.3 us (28%)
  Pallas kernels  17.7 us (15%)
  blocking collectives  11.3 us (10%)
  local copies, waits for them, and re-layouts  2.63 us (2%)
    ppermute x24, waiting for transfers between devices, swap(): return lax.ppermute(value, axis, [(i, i ^ bit) for i in range(size)])  52.6 us
    ppermute x24, starting transfers between devices, swap(): return lax.ppermute(value, axis, [(i, i ^ bit) for i in range(size)])  32.3 us
    all_to_all x1, blocking collectives, on_device(): homeward = lax.all_to_all(result, ('grp', 'blk'), 0, 0, tiled=True)  11.3 us
    pallas_call x2, Pallas kernels, gram_step(): pl.pallas_call(functools.partial(gram_kernel, first, step, pieces), in_sp...  8.45 us
    pallas_call x1, Pallas kernels, gram_last(): pl.pallas_call(functools.partial(gram_last_kernel, step, relatives, chunk...  3.07 us
    pallas_call x1, Pallas kernels, head(): pl.pallas_call(functools.partial(rest_kernel, capacity, chunks, groups),...  2.62 us
    unnamed x22, local copies, waits for them, and re-layouts  2.43 us
  transfers between devices with their start and end apart: 24, of which 13 were waited for; matrix products, arithmetic and copies ran while one was open for 1% of the time, Pallas kernels for 7%

profile of v12, /device:TPU:0, one launch (start us, length us, event | category | flops | bytes accessed | tf_op | source)
XLA Modules:
  0.0 117.0 jit_solution(2914387838200710827)
XLA Ops:
  3.3 2.6 %place_rest.1 = (bf16[192,768]{1,0:T(8,128)(2,1)S(1)}, bf16[192,768]{1,0:T(8,128)(2,1)S(1)}, bf16[192,768]{1,0:T(8,128)(2,1)S(1)}, bf16[192,768]{1,0:T(8,128)(2,...) custom-call(s32[2]{0:T(128)S(1)} %pad_add_fusion.me_ref, s32[6,128]{1,0:T(8,128)S(1)} %bitcast.6, ...), custom_call_target="tpu_custom_call" | custom-call | flops 1585446912 | bytes 3244032 | tf_op jit(solution)/shard_map/place_rest/pallas_call | solution.py:102
  5.9 3.0 %collective-permute-start = (bf16[96,768]{1,0:T(8,128)(2,1)S(1)}, bf16[96,768]{1,0:T(8,128)(2,1)S(1)}, u32[]{:S(2)}, u32[]{:S(2)}) collective-permute-start(bf16[96,768]{1,0:T(8,128)(2,1)S(1)} %get-tuple-element.46), channel_id=1, source_target_pairs={{0,4},{4,0},{8,12},{12,8},{16,20},{20,16},{24,28},{28,24},{1,5},{5... | collective-permute-start | bytes 442376 | tf_op jit(solution)/shard_map/ppermute | solution.py:29
  9.2 4.5 %collective-permute-done = bf16[96,768]{1,0:T(8,128)(2,1)S(1)} collective-permute-done((bf16[96,768]{1,0:T(8,128)(2,1)S(1)}, bf16[96,768]{1,0:T(8,128)(2,1)S(1)}, u32[]{:S(2)}, u32[]{:S(2)}) %collective-permute-start) | collective-permute-done | bytes 147488 | tf_op jit(solution)/shard_map/ppermute | solution.py:29
  13.7 2.2 %collective-permute-start.1 = (bf16[96,768]{1,0:T(8,128)(2,1)S(1)}, bf16[96,768]{1,0:T(8,128)(2,1)S(1)}, u32[]{:S(2)}, u32[]{:S(2)}) collective-permute-start(bf16[96,768]{1,0:T(8,128)(2,1)S(1)} %pad_maximum_fusion.1), channel_id=1, source_target_pairs={{0,8},{4,12},{8,0},{12,4},{16,24},{20,28},{24,16},{28,20},{1,9},{5... | collective-permute-start | bytes 442376 | tf_op jit(solution)/shard_map/ppermute | solution.py:29
  16.0 2.9 %collective-permute-start.3 = (bf16[96,768]{1,0:T(8,128)(2,1)S(1)}, bf16[96,768]{1,0:T(8,128)(2,1)S(1)}, u32[]{:S(2)}, u32[]{:S(2)}) collective-permute-start(bf16[96,768]{1,0:T(8,128)(2,1)S(1)} %pad_maximum_fusion.2), channel_id=1, source_target_pairs={{0,16},{4,20},{8,24},{12,28},{16,0},{20,4},{24,8},{28,12},{1,17},{... | collective-permute-start | bytes 442376 | tf_op jit(solution)/shard_map/ppermute | solution.py:29
  22.4 7.3 %collective-permute-done.3 = bf16[96,768]{1,0:T(8,128)(2,1)S(1)} collective-permute-done((bf16[96,768]{1,0:T(8,128)(2,1)S(1)}, bf16[96,768]{1,0:T(8,128)(2,1)S(1)}, u32[]{:S(2)}, u32[]{:S(2)}) %collective-permute-start.3) | collective-permute-done | bytes 147488 | tf_op jit(solution)/shard_map/ppermute | solution.py:29
  29.7 1.7 %collective-permute-start.12 = (bf16[384,768]{1,0:T(8,128)(2,1)S(1)}, bf16[384,768]{1,0:T(8,128)(2,1)S(1)}, u32[]{:S(2)}, u32[]{:S(2)}) collective-permute-start(bf16[384,768]{1,0:T(8,128)(2,1)S(1)} %get-tuple-element.135.refs_0_), channel_id=1, source_target_pairs={{0,2},{1,3},{2,0},{3,1},{4,6},{5,7},{6,4},{7,5},{8,10},{9,11},{10,... | collective-permute-start | bytes 1769480 | tf_op jit(solution)/shard_map/ppermute | solution.py:29
  31.4 2.4 %collective-permute-start.6 = (bf16[96,768]{1,0:T(8,128)(2,1)S(1)}, bf16[96,768]{1,0:T(8,128)(2,1)S(1)}, u32[]{:S(2)}, u32[]{:S(2)}) collective-permute-start(bf16[96,768]{1,0:T(8,128)(2,1)S(1)} %pad_maximum_fusion.4), channel_id=1, source_target_pairs={{0,8},{4,12},{8,0},{12,4},{16,24},{20,28},{24,16},{28,20},{1,9},{5... | collective-permute-start | bytes 442376 | tf_op jit(solution)/shard_map/ppermute | solution.py:29
  33.8 2.0 %collective-permute-start.7 = (bf16[96,768]{1,0:T(8,128)(2,1)S(1)}, bf16[96,768]{1,0:T(8,128)(2,1)S(1)}, u32[]{:S(2)}, u32[]{:S(2)}) collective-permute-start(bf16[96,768]{1,0:T(8,128)(2,1)S(1)} %pad_maximum_fusion.5), channel_id=1, source_target_pairs={{0,16},{4,20},{8,24},{12,28},{16,0},{20,4},{24,8},{28,12},{1,17},{... | collective-permute-start | bytes 442376 | tf_op jit(solution)/shard_map/ppermute | solution.py:29
  38.8 8.9 %collective-permute-done.7 = bf16[96,768]{1,0:T(8,128)(2,1)S(1)} collective-permute-done((bf16[96,768]{1,0:T(8,128)(2,1)S(1)}, bf16[96,768]{1,0:T(8,128)(2,1)S(1)}, u32[]{:S(2)}, u32[]{:S(2)}) %collective-permute-start.7) | collective-permute-done | bytes 147488 | tf_op jit(solution)/shard_map/ppermute | solution.py:29
  48.4 2.3 %collective-permute-start.10 = (bf16[192,768]{1,0:T(8,128)(2,1)S(1)}, bf16[192,768]{1,0:T(8,128)(2,1)S(1)}, u32[]{:S(2)}, u32[]{:S(2)}) collective-permute-start(bf16[192,768]{1,0:T(8,128)(2,1)S(1)} %pad_maximum_fusion), channel_id=1, source_target_pairs={{0,8},{4,12},{8,0},{12,4},{16,24},{20,28},{24,16},{28,20},{1,9},{5... | collective-permute-start | bytes 884744 | tf_op jit(solution)/shard_map/ppermute | solution.py:29
  53.8 5.9 %collective-permute-done.16 = bf16[384,768]{1,0:T(8,128)(2,1)S(1)} collective-permute-done((bf16[384,768]{1,0:T(8,128)(2,1)S(1)}, bf16[384,768]{1,0:T(8,128)(2,1)S(1)}, u32[]{:S(2)}, u32[]{:S(2)}) %collective-permute-start.16) | collective-permute-done | bytes 589856 | tf_op jit(solution)/shard_map/ppermute | solution.py:29
  60.4 5.1 %collective-permute-done.13 = bf16[96,768]{1,0:T(8,128)(2,1)S(1)} collective-permute-done((bf16[96,768]{1,0:T(8,128)(2,1)S(1)}, bf16[96,768]{1,0:T(8,128)(2,1)S(1)}, u32[]{:S(2)}, u32[]{:S(2)}) %collective-permute-start.13) | collective-permute-done | bytes 147488 | tf_op jit(solution)/shard_map/ppermute | solution.py:29
  65.6 1.6 %collective-permute-start.19 = (bf16[384,768]{1,0:T(8,128)(2,1)S(1)}, bf16[384,768]{1,0:T(8,128)(2,1)S(1)}, u32[]{:S(2)}, u32[]{:S(2)}) collective-permute-start(bf16[384,768]{1,0:T(8,128)(2,1)S(1)} %get-tuple-element.64.refs_2_), channel_id=1, source_target_pairs={{0,2},{1,3},{2,0},{3,1},{4,6},{5,7},{6,4},{7,5},{8,10},{9,11},{10,... | collective-permute-start | bytes 1769480 | tf_op jit(solution)/shard_map/ppermute | solution.py:29
  67.2 1.9 %collective-permute-start.15 = (bf16[96,768]{1,0:T(8,128)(2,1)S(1)}, bf16[96,768]{1,0:T(8,128)(2,1)S(1)}, u32[]{:S(2)}, u32[]{:S(2)}) collective-permute-start(bf16[96,768]{1,0:T(8,128)(2,1)S(1)} %pad_maximum_fusion.9), channel_id=1, source_target_pairs={{0,16},{4,20},{8,24},{12,28},{16,0},{20,4},{24,8},{28,12},{1,17},{... | collective-permute-start | bytes 442376 | tf_op jit(solution)/shard_map/ppermute | solution.py:29
  69.5 11.9 %collective-permute-done.19 = bf16[384,768]{1,0:T(8,128)(2,1)S(1)} collective-permute-done((bf16[384,768]{1,0:T(8,128)(2,1)S(1)}, bf16[384,768]{1,0:T(8,128)(2,1)S(1)}, u32[]{:S(2)}, u32[]{:S(2)}) %collective-permute-start.19) | collective-permute-done | bytes 589856 | tf_op jit(solution)/shard_map/ppermute | solution.py:29
  84.4 6.0 %gram_step.2 = (f32[384,128]{1,0:T(8,128)S(1)}, f32[384,128]{1,0:T(8,128)S(1)}, f32[384,128]{1,0:T(8,128)S(1)}, f32[1,1536]{1,0:T(1,128)S(1)}, f32[1,1536]{1,0:T(1,128)S(1)}, /*index=5*/f32[1,1536]{1,0:T(1,128)S(1)}) custom-call(bf16[384,768]{1,0:T(8,128)(2,1)S(1)} %get-tuple-element.135.refs_0_, bf16[384,768]{1,0:T(8,128)(2,1)S(1)} %get-tuple-element.61.refs_1_, ...), custom_call_target="tpu_custom_call" | custom-call | flops 8153726976 | bytes 8847360 | tf_op jit(solution)/shard_map/gram_step/pallas_call | solution.py:214
  90.4 1.6 %collective-permute-start.22 = (bf16[80,768]{1,0:T(8,128)(2,1)S(1)}, bf16[80,768]{1,0:T(8,128)(2,1)S(1)}, u32[]{:S(2)}, u32[]{:S(2)}) collective-permute-start(bf16[80,768]{1,0:T(8,128)(2,1)S(1)} %slice.179), channel_id=1, source_target_pairs={{0,2},{1,3},{2,0},{3,1},{4,6},{5,7},{6,4},{7,5},{8,10},{9,11},{10,... | collective-permute-start | bytes 368648 | tf_op jit(solution)/shard_map/ppermute | solution.py:29
  91.9 3.2 %collective-permute-done.20 = bf16[304,768]{1,0:T(8,128)(2,1)S(1)} collective-permute-done((bf16[304,768]{1,0:T(8,128)(2,1)S(1)}, bf16[304,768]{1,0:T(8,128)(2,1)S(1)}, u32[]{:S(2)}, u32[]{:S(2)}) %collective-permute-start.20) | collective-permute-done | bytes 466976 | tf_op jit(solution)/shard_map/ppermute | solution.py:29
  95.2 2.2 %collective-permute-done.22 = bf16[80,768]{1,0:T(8,128)(2,1)S(1)} collective-permute-done((bf16[80,768]{1,0:T(8,128)(2,1)S(1)}, bf16[80,768]{1,0:T(8,128)(2,1)S(1)}, u32[]{:S(2)}, u32[]{:S(2)}) %collective-permute-start.22) | collective-permute-done | bytes 122912 | tf_op jit(solution)/shard_map/ppermute | solution.py:29
  97.5 2.4 %gram_step.3 = (f32[384,128]{1,0:T(8,128)S(1)}, f32[384,128]{1,0:T(8,128)S(1)}, f32[384,128]{1,0:T(8,128)S(1)}, f32[384,128]{1,0:T(8,128)S(1)}, f32[1,768]{1,0:T(1,128)S(1)}) custom-call(bf16[384,768]{1,0:T(8,128)(2,1)S(1)} %get-tuple-element.135.refs_0_, bf16[384,768]{1,0:T(8,128)(2,1)S(1)} %get-tuple-element.61.refs_1_, ...), custom_call_target="tpu_custom_call" | custom-call | flops 1811939328 | bytes 3538944 | tf_op jit(solution)/shard_map/gram_step/pallas_call | solution.py:214
  100.3 3.1 %gram_last.1 = f32[32,1,192]{2,1,0:T(1,128)S(1)} custom-call(s32[2]{0:T(128)S(1)} %pad_add_fusion.me_ref, bf16[384,768]{1,0:T(8,128)(2,1)S(1)} %get-tuple-element.135.refs_0_, bf16[384,768]{1,0:T(8,128)(2,1)S(1)} %get-tuple-element.61.refs_1_, bf16[384,768]{1,0:T(8,128)(2,1)S(1)} %get-tuple-element.64.refs_2_, ...), custom_call_target="tpu_custom_call" | custom-call | flops 1811939328 | bytes 3538944 | tf_op jit(solution)/shard_map/gram_last/pallas_call | solution.py:229
  103.4 11.3 %all_to_all.5.part_ref = f32[32,1,192]{2,1,0:T(1,128)} all-to-all(f32[32,1,192]{2,1,0:T(1,128)S(1)} %gram_last.1), channel_id=1, replica_groups=mesh['grp'=8,'blk'=4] {'grp','blk'}, dimensions={0} | all-to-all | bytes 49152 | tf_op jit(solution)/shard_map/all_to_all | solution.py:371
  114.7 2.3 %pick_rows.1 = f32[6,128]{1,0:T(8,128)} custom-call(s32[6,128]{1,0:T(8,128)} %bitcast.4, f32[32,1,192]{2,1,0:T(1,128)} %all_to_all.5.part_ref), custom_call_target="tpu_custom_call" | custom-call | tf_op jit(solution)/shard_map/pick_rows/pallas_call | solution.py:265
  (73 shorter events, 18.6 us)
Async XLA Ops:
  5.9 7.7 %collective-permute-start = (bf16[96,768]{1,0:T(8,128)(2,1)S(1)}, bf16[96,768]{1,0:T(8,128)(2,1)S(1)}, u32[]{:S(2)}, u32[]{:S(2)}) collective-permute-start(bf16[96,768]{1,0:T(8,128)(2,1)S(1)} %get-tuple-element.46), channel_id=1, source_target_pairs={{0,4},{4,0},{8,12},{12,8},{16,20},{20,16},{24,28},{28,24},{1,5},{5... | collective-permute-start | bytes 442376 | tf_op jit(solution)/shard_map/ppermute | solution.py:29
  9.0 7.0 %collective-permute-start.2 = (bf16[96,768]{1,0:T(8,128)(2,1)S(1)}, bf16[96,768]{1,0:T(8,128)(2,1)S(1)}, u32[]{:S(2)}, u32[]{:S(2)}) collective-permute-start(bf16[96,768]{1,0:T(8,128)(2,1)S(1)} %get-tuple-element.118), channel_id=1, source_target_pairs={{0,4},{4,0},{8,12},{12,8},{16,20},{20,16},{24,28},{28,24},{1,5},{5... | collective-permute-start | bytes 442376 | tf_op jit(solution)/shard_map/ppermute | solution.py:29
  13.7 8.7 %collective-permute-start.1 = (bf16[96,768]{1,0:T(8,128)(2,1)S(1)}, bf16[96,768]{1,0:T(8,128)(2,1)S(1)}, u32[]{:S(2)}, u32[]{:S(2)}) collective-permute-start(bf16[96,768]{1,0:T(8,128)(2,1)S(1)} %pad_maximum_fusion.1), channel_id=1, source_target_pairs={{0,8},{4,12},{8,0},{12,4},{16,24},{20,28},{24,16},{28,20},{1,9},{5... | collective-permute-start | bytes 442376 | tf_op jit(solution)/shard_map/ppermute | solution.py:29
  16.0 13.6 %collective-permute-start.3 = (bf16[96,768]{1,0:T(8,128)(2,1)S(1)}, bf16[96,768]{1,0:T(8,128)(2,1)S(1)}, u32[]{:S(2)}, u32[]{:S(2)}) collective-permute-start(bf16[96,768]{1,0:T(8,128)(2,1)S(1)} %pad_maximum_fusion.2), channel_id=1, source_target_pairs={{0,16},{4,20},{8,24},{12,28},{16,0},{20,4},{24,8},{28,12},{1,17},{... | collective-permute-start | bytes 442376 | tf_op jit(solution)/shard_map/ppermute | solution.py:29
  18.9 10.8 %collective-permute-start.4 = (bf16[96,768]{1,0:T(8,128)(2,1)S(1)}, bf16[96,768]{1,0:T(8,128)(2,1)S(1)}, u32[]{:S(2)}, u32[]{:S(2)}) collective-permute-start(bf16[96,768]{1,0:T(8,128)(2,1)S(1)} %pad_maximum_fusion.3), channel_id=1, source_target_pairs={{0,24},{4,28},{8,16},{12,20},{16,8},{20,12},{24,0},{28,4},{1,25},{... | collective-permute-start | bytes 442376 | tf_op jit(solution)/shard_map/ppermute | solution.py:29
  20.3 11.1 %collective-permute-start.5 = (bf16[192,768]{1,0:T(8,128)(2,1)S(1)}, bf16[192,768]{1,0:T(8,128)(2,1)S(1)}, u32[]{:S(2)}, u32[]{:S(2)}) collective-permute-start(bf16[192,768]{1,0:T(8,128)(2,1)S(1)} %get-tuple-element.49), channel_id=1, source_target_pairs={{0,4},{4,0},{8,12},{12,8},{16,20},{20,16},{24,28},{28,24},{1,5},{5... | collective-permute-start | bytes 884744 | tf_op jit(solution)/shard_map/ppermute | solution.py:29
  21.8 26.5 %collective-permute-start.9 = (bf16[384,768]{1,0:T(8,128)(2,1)S(1)}, bf16[384,768]{1,0:T(8,128)(2,1)S(1)}, u32[]{:S(2)}, u32[]{:S(2)}) collective-permute-start(bf16[384,768]{1,0:T(8,128)(2,1)S(1)} %get-tuple-element.54), channel_id=1, source_target_pairs={{0,4},{4,0},{8,12},{12,8},{16,20},{20,16},{24,28},{28,24},{1,5},{5... | collective-permute-start | bytes 1769480 | tf_op jit(solution)/shard_map/ppermute | solution.py:29
  29.7 18.0 %collective-permute-start.12 = (bf16[384,768]{1,0:T(8,128)(2,1)S(1)}, bf16[384,768]{1,0:T(8,128)(2,1)S(1)}, u32[]{:S(2)}, u32[]{:S(2)}) collective-permute-start(bf16[384,768]{1,0:T(8,128)(2,1)S(1)} %get-tuple-element.135.refs_0_), channel_id=1, source_target_pairs={{0,2},{1,3},{2,0},{3,1},{4,6},{5,7},{6,4},{7,5},{8,10},{9,11},{10,... | collective-permute-start | bytes 1769480 | tf_op jit(solution)/shard_map/ppermute | solution.py:29
  31.4 7.3 %collective-permute-start.6 = (bf16[96,768]{1,0:T(8,128)(2,1)S(1)}, bf16[96,768]{1,0:T(8,128)(2,1)S(1)}, u32[]{:S(2)}, u32[]{:S(2)}) collective-permute-start(bf16[96,768]{1,0:T(8,128)(2,1)S(1)} %pad_maximum_fusion.4), channel_id=1, source_target_pairs={{0,8},{4,12},{8,0},{12,4},{16,24},{20,28},{24,16},{28,20},{1,9},{5... | collective-permute-start | bytes 442376 | tf_op jit(solution)/shard_map/ppermute | solution.py:29
  33.8 13.8 %collective-permute-start.7 = (bf16[96,768]{1,0:T(8,128)(2,1)S(1)}, bf16[96,768]{1,0:T(8,128)(2,1)S(1)}, u32[]{:S(2)}, u32[]{:S(2)}) collective-permute-start(bf16[96,768]{1,0:T(8,128)(2,1)S(1)} %pad_maximum_fusion.5), channel_id=1, source_target_pairs={{0,16},{4,20},{8,24},{12,28},{16,0},{20,4},{24,8},{28,12},{1,17},{... | collective-permute-start | bytes 442376 | tf_op jit(solution)/shard_map/ppermute | solution.py:29
  35.9 11.8 %collective-permute-start.8 = (bf16[96,768]{1,0:T(8,128)(2,1)S(1)}, bf16[96,768]{1,0:T(8,128)(2,1)S(1)}, u32[]{:S(2)}, u32[]{:S(2)}) collective-permute-start(bf16[96,768]{1,0:T(8,128)(2,1)S(1)} %pad_maximum_fusion.6), channel_id=1, source_target_pairs={{0,24},{4,28},{8,16},{12,20},{16,8},{20,12},{24,0},{28,4},{1,25},{... | collective-permute-start | bytes 442376 | tf_op jit(solution)/shard_map/ppermute | solution.py:29
  47.7 11.9 %collective-permute-start.16 = (bf16[384,768]{1,0:T(8,128)(2,1)S(1)}, bf16[384,768]{1,0:T(8,128)(2,1)S(1)}, u32[]{:S(2)}, u32[]{:S(2)}) collective-permute-start(bf16[384,768]{1,0:T(8,128)(2,1)S(1)} %get-tuple-element.61.refs_1_), channel_id=1, source_target_pairs={{0,2},{1,3},{2,0},{3,1},{4,6},{5,7},{6,4},{7,5},{8,10},{9,11},{10,... | collective-permute-start | bytes 1769480 | tf_op jit(solution)/shard_map/ppermute | solution.py:29
  48.4 17.0 %collective-permute-start.10 = (bf16[192,768]{1,0:T(8,128)(2,1)S(1)}, bf16[192,768]{1,0:T(8,128)(2,1)S(1)}, u32[]{:S(2)}, u32[]{:S(2)}) collective-permute-start(bf16[192,768]{1,0:T(8,128)(2,1)S(1)} %pad_maximum_fusion), channel_id=1, source_target_pairs={{0,8},{4,12},{8,0},{12,4},{16,24},{20,28},{24,16},{28,20},{1,9},{5... | collective-permute-start | bytes 884744 | tf_op jit(solution)/shard_map/ppermute | solution.py:29
  50.8 9.6 %collective-permute-start.11 = (bf16[96,768]{1,0:T(8,128)(2,1)S(1)}, bf16[96,768]{1,0:T(8,128)(2,1)S(1)}, u32[]{:S(2)}, u32[]{:S(2)}) collective-permute-start(bf16[96,768]{1,0:T(8,128)(2,1)S(1)} %pad_maximum_fusion.7), channel_id=1, source_target_pairs={{0,16},{4,20},{8,24},{12,28},{16,0},{20,4},{24,8},{28,12},{1,17},{... | collective-permute-start | bytes 442376 | tf_op jit(solution)/shard_map/ppermute | solution.py:29
  52.2 13.3 %collective-permute-start.13 = (bf16[96,768]{1,0:T(8,128)(2,1)S(1)}, bf16[96,768]{1,0:T(8,128)(2,1)S(1)}, u32[]{:S(2)}, u32[]{:S(2)}) collective-permute-start(bf16[96,768]{1,0:T(8,128)(2,1)S(1)} %pad_maximum_fusion.8), channel_id=1, source_target_pairs={{0,24},{4,28},{8,16},{12,20},{16,8},{20,12},{24,0},{28,4},{1,25},{... | collective-permute-start | bytes 442376 | tf_op jit(solution)/shard_map/ppermute | solution.py:29
  53.7 13.5 %collective-permute-start.14 = (bf16[768,768]{1,0:T(8,128)(2,1)S(1)}, bf16[768,768]{1,0:T(8,128)(2,1)S(1)}, u32[]{:S(2)}, u32[]{:S(2)}) collective-permute-start(bf16[768,768]{1,0:T(8,128)(2,1)S(1)} %constant_dynamic-update-slice_fusion.14.refs_3_), channel_id=1, source_target_pairs={{0,1},{1,0},{2,3},{3,2},{4,5},{5,4},{6,7},{7,6},{8,9},{9,8},{10,11... | collective-permute-start | bytes 3538952 | tf_op jit(solution)/shard_map/ppermute | solution.py:29
  65.5 3.6 %collective-permute-start.17 = (bf16[768,768]{1,0:T(8,128)(2,1)S(1)}, bf16[768,768]{1,0:T(8,128)(2,1)S(1)}, u32[]{:S(2)}, u32[]{:S(2)}) collective-permute-start(bf16[768,768]{1,0:T(8,128)(2,1)S(1)} %constant_dynamic-update-slice_fusion.20.refs_5_), channel_id=1, source_target_pairs={{0,1},{1,0},{2,3},{3,2},{4,5},{5,4},{6,7},{7,6},{8,9},{9,8},{10,11... | collective-permute-start | bytes 3538952 | tf_op jit(solution)/shard_map/ppermute | solution.py:29
  65.6 15.8 %collective-permute-start.19 = (bf16[384,768]{1,0:T(8,128)(2,1)S(1)}, bf16[384,768]{1,0:T(8,128)(2,1)S(1)}, u32[]{:S(2)}, u32[]{:S(2)}) collective-permute-start(bf16[384,768]{1,0:T(8,128)(2,1)S(1)} %get-tuple-element.64.refs_2_), channel_id=1, source_target_pairs={{0,2},{1,3},{2,0},{3,1},{4,6},{5,7},{6,4},{7,5},{8,10},{9,11},{10,... | collective-permute-start | bytes 1769480 | tf_op jit(solution)/shard_map/ppermute | solution.py:29
  67.2 14.2 %collective-permute-start.15 = (bf16[96,768]{1,0:T(8,128)(2,1)S(1)}, bf16[96,768]{1,0:T(8,128)(2,1)S(1)}, u32[]{:S(2)}, u32[]{:S(2)}) collective-permute-start(bf16[96,768]{1,0:T(8,128)(2,1)S(1)} %pad_maximum_fusion.9), channel_id=1, source_target_pairs={{0,16},{4,20},{8,24},{12,28},{16,0},{20,4},{24,8},{28,12},{1,17},{... | collective-permute-start | bytes 442376 | tf_op jit(solution)/shard_map/ppermute | solution.py:29
  69.1 12.4 %collective-permute-start.18 = (bf16[96,768]{1,0:T(8,128)(2,1)S(1)}, bf16[96,768]{1,0:T(8,128)(2,1)S(1)}, u32[]{:S(2)}, u32[]{:S(2)}) collective-permute-start(bf16[96,768]{1,0:T(8,128)(2,1)S(1)} %pad_maximum_fusion.10), channel_id=1, source_target_pairs={{0,24},{4,28},{8,16},{12,20},{16,8},{20,12},{24,0},{28,4},{1,25},{... | collective-permute-start | bytes 442376 | tf_op jit(solution)/shard_map/ppermute | solution.py:29
  81.5 2.9 %collective-permute-start.21 = (bf16[768,768]{1,0:T(8,128)(2,1)S(1)}, bf16[768,768]{1,0:T(8,128)(2,1)S(1)}, u32[]{:S(2)}, u32[]{:S(2)}) collective-permute-start(bf16[768,768]{1,0:T(8,128)(2,1)S(1)} %constant_dynamic-update-slice_fusion.30.refs_7_), channel_id=1, source_target_pairs={{0,1},{1,0},{2,3},{3,2},{4,5},{5,4},{6,7},{7,6},{8,9},{9,8},{10,11... | collective-permute-start | bytes 3538952 | tf_op jit(solution)/shard_map/ppermute | solution.py:29
  81.6 13.6 %collective-permute-start.20 = (bf16[304,768]{1,0:T(8,128)(2,1)S(1)}, bf16[304,768]{1,0:T(8,128)(2,1)S(1)}, u32[]{:S(2)}, u32[]{:S(2)}) collective-permute-start(bf16[304,768]{1,0:T(8,128)(2,1)S(1)} %slice.178), channel_id=1, source_target_pairs={{0,2},{1,3},{2,0},{3,1},{4,6},{5,7},{6,4},{7,5},{8,10},{9,11},{10,... | collective-permute-start | bytes 1400840 | tf_op jit(solution)/shard_map/ppermute | solution.py:29
  90.4 7.0 %collective-permute-start.22 = (bf16[80,768]{1,0:T(8,128)(2,1)S(1)}, bf16[80,768]{1,0:T(8,128)(2,1)S(1)}, u32[]{:S(2)}, u32[]{:S(2)}) collective-permute-start(bf16[80,768]{1,0:T(8,128)(2,1)S(1)} %slice.179), channel_id=1, source_target_pairs={{0,2},{1,3},{2,0},{3,1},{4,6},{5,7},{6,4},{7,5},{8,10},{9,11},{10,... | collective-permute-start | bytes 368648 | tf_op jit(solution)/shard_map/ppermute | solution.py:29
  97.4 2.9 %collective-permute-start.23 = (bf16[768,768]{1,0:T(8,128)(2,1)S(1)}, bf16[768,768]{1,0:T(8,128)(2,1)S(1)}, u32[]{:S(2)}, u32[]{:S(2)}) collective-permute-start(bf16[768,768]{1,0:T(8,128)(2,1)S(1)} %constant_dynamic-update-slice_fusion.35.refs_4_), channel_id=1, source_target_pairs={{0,1},{1,0},{2,3},{3,2},{4,5},{5,4},{6,7},{7,6},{8,9},{9,8},{10,11... | collective-permute-start | bytes 3538952 | tf_op jit(solution)/shard_map/ppermute | solution.py:29
  (2 other events, 2.0 us)

commit v13 on v12

--- a/solution.py
+++ b/solution.py
@@ -305,24 +305,16 @@
 
     def send_z(step, z):
         early = [("z", step - 1, z)] if step >= 1 else []
-        if step >= 2 and z == far[-1]:
+        if step >= 2 and z == high - 1:
             early += [("x", step - 2, 0)]
-        if step == last and step >= 3:
-            early += [("c", step - 2 if z == far[-1] else step - 3)]
+        if z == 1:
+            early += [("c", step - 2)] if step >= 2 else [("y", step + 2)]
         send(("z", step, z), block(step, z), "grp", groups, 2 * z, *early)
-
-    def send_near_z():
-        blocks = jnp.concatenate([block(step, 1) for step in range(2, count)], axis=0)
-        send(("n",), blocks, "grp", groups, 2, ("z", 1, 1))
 
     def collect(step):
         parts = [block(step, 0)]
         for z in range(1, high):
-            if z == 1 and step >= 2:
-                start = 2 * sum(chunks[2:step])
-                parts.append(sent["n",][start : start + 2 * chunks[step]])
-            else:
-                parts.append(sent["z", step, z])
+            parts.append(sent["z", step, z])
         owns[step] = jnp.concatenate(parts, axis=0)
 
     def send_x(step, cuts, between):
@@ -339,7 +331,7 @@
         pairs[step] = jnp.concatenate([owns[step]] + across, axis=0)
         send(("c", step), pairs[step], "blk", members, 1, *early)
 
-    far = [high // 2] + [z for z in range(1, high) if z != high // 2]
+    far = [high // 2] + [z for z in reversed(range(1, high)) if z != high // 2]
     cut = first_send.shape[0] // 2
     done["rest"] = rest_send
     send(("y", 0), first_send[:cut], "grp", groups, 1)
@@ -352,9 +344,6 @@
         collect(step - 1)
         for z in far:
             send_z(step, z)
-        if step == 1:
-            far.remove(1)
-            send_near_z()
         send_x(step - 1, [], [])
         send_c(step - 1, *[("z", step, z) for z in far])
     collect(last)

time: 117 us -> 131 us (1.12)
  waiting for transfers between devices: 52.6 us -> 68.9 us
  starting transfers between devices: 32.3 us -> 29.8 us
    ppermute x24 -> x25, waiting for transfers between devices: 52.6 us -> 68.9 us  [swap(): return lax.ppermute(value, axis, [(i, i ^ bit) for i in range(size)])]
    ppermute x24 -> x25, starting transfers between devices: 32.3 us -> 29.8 us  [swap(): return lax.ppermute(value, axis, [(i, i ^ bit) for i in range(size)])]
  transfers between devices with their start and end apart: 24 -> 25, of which waited for: 13 -> 14; matrix products, arithmetic and copies ran while one was open for 1% -> 1% of each run, Pallas kernels for 7% -> 8%
where the time goes in v13:
time: 131 us
  waiting for transfers between devices  68.9 us (53%)
  starting transfers between devices  29.8 us (23%)
  Pallas kernels  17.7 us (14%)
  blocking collectives  11.2 us (9%)
  local copies, waits for them, and re-layouts  2.64 us (2%)
    ppermute x25, waiting for transfers between devices, swap(): return lax.ppermute(value, axis, [(i, i ^ bit) for i in range(size)])  68.9 us
    ppermute x25, starting transfers between devices, swap(): return lax.ppermute(value, axis, [(i, i ^ bit) for i in range(size)])  29.8 us
    all_to_all x1, blocking collectives, on_device(): homeward = lax.all_to_all(result, ('grp', 'blk'), 0, 0, tiled=True)  11.2 us
    pallas_call x2, Pallas kernels, gram_step(): pl.pallas_call(functools.partial(gram_kernel, first, step, pieces), in_sp...  8.45 us
    pallas_call x1, Pallas kernels, gram_last(): pl.pallas_call(functools.partial(gram_last_kernel, step, relatives, chunk...  3.07 us
  transfers between devices with their start and end apart: 25, of which 14 were waited for; matrix products, arithmetic and copies ran while one was open for 1% of the time, Pallas kernels for 8%

profile of v13, /device:TPU:0, one launch (start us, length us, event | category | flops | bytes accessed | tf_op | source)
XLA Modules:
  0.0 130.8 jit_solution(1638187850264654728)
XLA Ops:
  3.3 3.0 %collective-permute-start.1 = (bf16[96,768]{1,0:T(8,128)(2,1)S(1)}, bf16[96,768]{1,0:T(8,128)(2,1)S(1)}, u32[]{:S(2)}, u32[]{:S(2)}) collective-permute-start(bf16[96,768]{1,0:T(8,128)(2,1)S(1)} %get-tuple-element.118), channel_id=1, source_target_pairs={{0,4},{4,0},{8,12},{12,8},{16,20},{20,16},{24,28},{28,24},{1,5},{5... | collective-permute-start | bytes 442376 | tf_op jit(solution)/shard_map/ppermute | solution.py:29
  6.4 2.6 %place_rest.1 = (bf16[192,768]{1,0:T(8,128)(2,1)S(1)}, bf16[192,768]{1,0:T(8,128)(2,1)S(1)}, bf16[192,768]{1,0:T(8,128)(2,1)S(1)}, bf16[192,768]{1,0:T(8,128)(2,...) custom-call(s32[2]{0:T(128)S(1)} %pad_add_fusion.me_ref, s32[6,128]{1,0:T(8,128)S(1)} %bitcast.6, ...), custom_call_target="tpu_custom_call" | custom-call | flops 1585446912 | bytes 3244032 | tf_op jit(solution)/shard_map/place_rest/pallas_call | solution.py:102
  10.2 2.1 %collective-permute-start.6 = (bf16[384,768]{1,0:T(8,128)(2,1)S(1)}, bf16[384,768]{1,0:T(8,128)(2,1)S(1)}, u32[]{:S(2)}, u32[]{:S(2)}) collective-permute-start(bf16[384,768]{1,0:T(8,128)(2,1)S(1)} %get-tuple-element.53), channel_id=1, source_target_pairs={{0,4},{4,0},{8,12},{12,8},{16,20},{20,16},{24,28},{28,24},{1,5},{5... | collective-permute-start | bytes 1769480 | tf_op jit(solution)/shard_map/ppermute | solution.py:29
  12.4 3.5 %collective-permute-done = bf16[96,768]{1,0:T(8,128)(2,1)S(1)} collective-permute-done((bf16[96,768]{1,0:T(8,128)(2,1)S(1)}, bf16[96,768]{1,0:T(8,128)(2,1)S(1)}, u32[]{:S(2)}, u32[]{:S(2)}) %collective-permute-start) | collective-permute-done | bytes 147488 | tf_op jit(solution)/shard_map/ppermute | solution.py:29
  15.9 17.4 %collective-permute-done.2 = bf16[192,768]{1,0:T(8,128)(2,1)S(1)} collective-permute-done((bf16[192,768]{1,0:T(8,128)(2,1)S(1)}, bf16[192,768]{1,0:T(8,128)(2,1)S(1)}, u32[]{:S(2)}, u32[]{:S(2)}) %collective-permute-start.2) | collective-permute-done | bytes 294944 | tf_op jit(solution)/shard_map/ppermute | solution.py:29
  34.9 2.7 %collective-permute-start.4 = (bf16[96,768]{1,0:T(8,128)(2,1)S(1)}, bf16[96,768]{1,0:T(8,128)(2,1)S(1)}, u32[]{:S(2)}, u32[]{:S(2)}) collective-permute-start(bf16[96,768]{1,0:T(8,128)(2,1)S(1)} %pad_maximum_fusion.1), channel_id=1, source_target_pairs={{0,16},{4,20},{8,24},{12,28},{16,0},{20,4},{24,8},{28,12},{1,17},{... | collective-permute-start | bytes 442376 | tf_op jit(solution)/shard_map/ppermute | solution.py:29
  37.9 2.3 %collective-permute-done.3 = bf16[96,768]{1,0:T(8,128)(2,1)S(1)} collective-permute-done((bf16[96,768]{1,0:T(8,128)(2,1)S(1)}, bf16[96,768]{1,0:T(8,128)(2,1)S(1)}, u32[]{:S(2)}, u32[]{:S(2)}) %collective-permute-start.3) | collective-permute-done | bytes 147488 | tf_op jit(solution)/shard_map/ppermute | solution.py:29
  40.1 7.7 %collective-permute-done.4 = bf16[96,768]{1,0:T(8,128)(2,1)S(1)} collective-permute-done((bf16[96,768]{1,0:T(8,128)(2,1)S(1)}, bf16[96,768]{1,0:T(8,128)(2,1)S(1)}, u32[]{:S(2)}, u32[]{:S(2)}) %collective-permute-start.4) | collective-permute-done | bytes 147488 | tf_op jit(solution)/shard_map/ppermute | solution.py:29
  49.6 2.6 %collective-permute-start.9 = (bf16[96,768]{1,0:T(8,128)(2,1)S(1)}, bf16[96,768]{1,0:T(8,128)(2,1)S(1)}, u32[]{:S(2)}, u32[]{:S(2)}) collective-permute-start(bf16[96,768]{1,0:T(8,128)(2,1)S(1)} %pad_maximum_fusion.5), channel_id=1, source_target_pairs={{0,24},{4,28},{8,16},{12,20},{16,8},{20,12},{24,0},{28,4},{1,25},{... | collective-permute-start | bytes 442376 | tf_op jit(solution)/shard_map/ppermute | solution.py:29
  52.1 3.0 %collective-permute-start.8 = (bf16[96,768]{1,0:T(8,128)(2,1)S(1)}, bf16[96,768]{1,0:T(8,128)(2,1)S(1)}, u32[]{:S(2)}, u32[]{:S(2)}) collective-permute-start(bf16[96,768]{1,0:T(8,128)(2,1)S(1)} %pad_maximum_fusion.4), channel_id=1, source_target_pairs={{0,16},{4,20},{8,24},{12,28},{16,0},{20,4},{24,8},{28,12},{1,17},{... | collective-permute-start | bytes 442376 | tf_op jit(solution)/shard_map/ppermute | solution.py:29
  55.3 3.5 %collective-permute-done.10 = bf16[384,768]{1,0:T(8,128)(2,1)S(1)} collective-permute-done((bf16[384,768]{1,0:T(8,128)(2,1)S(1)}, bf16[384,768]{1,0:T(8,128)(2,1)S(1)}, u32[]{:S(2)}, u32[]{:S(2)}) %collective-permute-start.10) | collective-permute-done | bytes 589856 | tf_op jit(solution)/shard_map/ppermute | solution.py:29
  58.8 3.9 %collective-permute-done.8 = bf16[96,768]{1,0:T(8,128)(2,1)S(1)} collective-permute-done((bf16[96,768]{1,0:T(8,128)(2,1)S(1)}, bf16[96,768]{1,0:T(8,128)(2,1)S(1)}, u32[]{:S(2)}, u32[]{:S(2)}) %collective-permute-start.8) | collective-permute-done | bytes 147488 | tf_op jit(solution)/shard_map/ppermute | solution.py:29
  63.9 2.5 %collective-permute-start.13 = (bf16[96,768]{1,0:T(8,128)(2,1)S(1)}, bf16[96,768]{1,0:T(8,128)(2,1)S(1)}, u32[]{:S(2)}, u32[]{:S(2)}) collective-permute-start(bf16[96,768]{1,0:T(8,128)(2,1)S(1)} %pad_maximum_fusion.7), channel_id=1, source_target_pairs={{0,16},{4,20},{8,24},{12,28},{16,0},{20,4},{24,8},{28,12},{1,17},{... | collective-permute-start | bytes 442376 | tf_op jit(solution)/shard_map/ppermute | solution.py:29
  68.0 10.7 %collective-permute-done.15 = bf16[384,768]{1,0:T(8,128)(2,1)S(1)} collective-permute-done((bf16[384,768]{1,0:T(8,128)(2,1)S(1)}, bf16[384,768]{1,0:T(8,128)(2,1)S(1)}, u32[]{:S(2)}, u32[]{:S(2)}) %collective-permute-start.15) | collective-permute-done | bytes 589856 | tf_op jit(solution)/shard_map/ppermute | solution.py:29
  80.0 3.4 %collective-permute-start.18 = (bf16[96,768]{1,0:T(8,128)(2,1)S(1)}, bf16[96,768]{1,0:T(8,128)(2,1)S(1)}, u32[]{:S(2)}, u32[]{:S(2)}) collective-permute-start(bf16[96,768]{1,0:T(8,128)(2,1)S(1)} %pad_maximum_fusion.10), channel_id=1, source_target_pairs={{0,16},{4,20},{8,24},{12,28},{16,0},{20,4},{24,8},{28,12},{1,17},{... | collective-permute-start | bytes 442376 | tf_op jit(solution)/shard_map/ppermute | solution.py:29
  84.7 10.0 %collective-permute-done.20 = bf16[384,768]{1,0:T(8,128)(2,1)S(1)} collective-permute-done((bf16[384,768]{1,0:T(8,128)(2,1)S(1)}, bf16[384,768]{1,0:T(8,128)(2,1)S(1)}, u32[]{:S(2)}, u32[]{:S(2)}) %collective-permute-start.20) | collective-permute-done | bytes 589856 | tf_op jit(solution)/shard_map/ppermute | solution.py:29
  96.4 1.8 %collective-permute-done.22.refs_8_ = bf16[768,768]{1,0:T(8,128)(2,1)S(1)} collective-permute-done((bf16[768,768]{1,0:T(8,128)(2,1)S(1)}, bf16[768,768]{1,0:T(8,128)(2,1)S(1)}, u32[]{:S(2)}, u32[]{:S(2)}) %collective-permute-start.22) | collective-permute-done | bytes 1179680 | tf_op jit(solution)/shard_map/ppermute | solution.py:29
  98.2 6.0 %gram_step.2 = (f32[384,128]{1,0:T(8,128)S(1)}, f32[384,128]{1,0:T(8,128)S(1)}, f32[384,128]{1,0:T(8,128)S(1)}, f32[1,1536]{1,0:T(1,128)S(1)}, f32[1,1536]{1,0:T(1,128)S(1)}, /*index=5*/f32[1,1536]{1,0:T(1,128)S(1)}) custom-call(bf16[384,768]{1,0:T(8,128)(2,1)S(1)} %get-tuple-element.139.refs_0_, bf16[384,768]{1,0:T(8,128)(2,1)S(1)} %get-tuple-element.63.refs_1_, ...), custom_call_target="tpu_custom_call" | custom-call | flops 8153726976 | bytes 8847360 | tf_op jit(solution)/shard_map/gram_step/pallas_call | solution.py:214
  105.1 3.9 %collective-permute-done.21 = bf16[304,768]{1,0:T(8,128)(2,1)S(1)} collective-permute-done((bf16[304,768]{1,0:T(8,128)(2,1)S(1)}, bf16[304,768]{1,0:T(8,128)(2,1)S(1)}, u32[]{:S(2)}, u32[]{:S(2)}) %collective-permute-start.21) | collective-permute-done | bytes 466976 | tf_op jit(solution)/shard_map/ppermute | solution.py:29
  109.1 2.2 %collective-permute-done.23 = bf16[80,768]{1,0:T(8,128)(2,1)S(1)} collective-permute-done((bf16[80,768]{1,0:T(8,128)(2,1)S(1)}, bf16[80,768]{1,0:T(8,128)(2,1)S(1)}, u32[]{:S(2)}, u32[]{:S(2)}) %collective-permute-start.23) | collective-permute-done | bytes 122912 | tf_op jit(solution)/shard_map/ppermute | solution.py:29
  111.4 2.4 %gram_step.3 = (f32[384,128]{1,0:T(8,128)S(1)}, f32[384,128]{1,0:T(8,128)S(1)}, f32[384,128]{1,0:T(8,128)S(1)}, f32[384,128]{1,0:T(8,128)S(1)}, f32[1,768]{1,0:T(1,128)S(1)}) custom-call(bf16[384,768]{1,0:T(8,128)(2,1)S(1)} %get-tuple-element.139.refs_0_, bf16[384,768]{1,0:T(8,128)(2,1)S(1)} %get-tuple-element.63.refs_1_, ...), custom_call_target="tpu_custom_call" | custom-call | flops 1811939328 | bytes 3538944 | tf_op jit(solution)/shard_map/gram_step/pallas_call | solution.py:214
  114.2 3.1 %gram_last.1 = f32[32,1,192]{2,1,0:T(1,128)S(1)} custom-call(s32[2]{0:T(128)S(1)} %pad_add_fusion.me_ref, bf16[384,768]{1,0:T(8,128)(2,1)S(1)} %get-tuple-element.139.refs_0_, bf16[384,768]{1,0:T(8,128)(2,1)S(1)} %get-tuple-element.63.refs_1_, bf16[384,768]{1,0:T(8,128)(2,1)S(1)} %get-tuple-element.68.refs_2_, ...), custom_call_target="tpu_custom_call" | custom-call | flops 1811939328 | bytes 3538944 | tf_op jit(solution)/shard_map/gram_last/pallas_call | solution.py:229
  117.3 11.2 %all_to_all.5.part_ref = f32[32,1,192]{2,1,0:T(1,128)} all-to-all(f32[32,1,192]{2,1,0:T(1,128)S(1)} %gram_last.1), channel_id=1, replica_groups=mesh['grp'=8,'blk'=4] {'grp','blk'}, dimensions={0} | all-to-all | bytes 49152 | tf_op jit(solution)/shard_map/all_to_all | solution.py:360
  128.5 2.3 %pick_rows.1 = f32[6,128]{1,0:T(8,128)} custom-call(s32[6,128]{1,0:T(8,128)} %bitcast.4, f32[32,1,192]{2,1,0:T(1,128)} %all_to_all.5.part_ref), custom_call_target="tpu_custom_call" | custom-call | tf_op jit(solution)/shard_map/pick_rows/pallas_call | solution.py:265
  (77 shorter events, 16.7 us)
Async XLA Ops:
  3.3 6.9 %collective-permute-start.1 = (bf16[96,768]{1,0:T(8,128)(2,1)S(1)}, bf16[96,768]{1,0:T(8,128)(2,1)S(1)}, u32[]{:S(2)}, u32[]{:S(2)}) collective-permute-start(bf16[96,768]{1,0:T(8,128)(2,1)S(1)} %get-tuple-element.118), channel_id=1, source_target_pairs={{0,4},{4,0},{8,12},{12,8},{16,20},{20,16},{24,28},{28,24},{1,5},{5... | collective-permute-start | bytes 442376 | tf_op jit(solution)/shard_map/ppermute | solution.py:29
  9.0 6.8 %collective-permute-start = (bf16[96,768]{1,0:T(8,128)(2,1)S(1)}, bf16[96,768]{1,0:T(8,128)(2,1)S(1)}, u32[]{:S(2)}, u32[]{:S(2)}) collective-permute-start(bf16[96,768]{1,0:T(8,128)(2,1)S(1)} %get-tuple-element.48), channel_id=1, source_target_pairs={{0,4},{4,0},{8,12},{12,8},{16,20},{20,16},{24,28},{28,24},{1,5},{5... | collective-permute-start | bytes 442376 | tf_op jit(solution)/shard_map/ppermute | solution.py:29
  10.2 44.9 %collective-permute-start.6 = (bf16[384,768]{1,0:T(8,128)(2,1)S(1)}, bf16[384,768]{1,0:T(8,128)(2,1)S(1)}, u32[]{:S(2)}, u32[]{:S(2)}) collective-permute-start(bf16[384,768]{1,0:T(8,128)(2,1)S(1)} %get-tuple-element.53), channel_id=1, source_target_pairs={{0,4},{4,0},{8,12},{12,8},{16,20},{20,16},{24,28},{28,24},{1,5},{5... | collective-permute-start | bytes 1769480 | tf_op jit(solution)/shard_map/ppermute | solution.py:29
  12.3 21.0 %collective-permute-start.2 = (bf16[192,768]{1,0:T(8,128)(2,1)S(1)}, bf16[192,768]{1,0:T(8,128)(2,1)S(1)}, u32[]{:S(2)}, u32[]{:S(2)}) collective-permute-start(bf16[192,768]{1,0:T(8,128)(2,1)S(1)} %get-tuple-element.50), channel_id=1, source_target_pairs={{0,4},{4,0},{8,12},{12,8},{16,20},{20,16},{24,28},{28,24},{1,5},{5... | collective-permute-start | bytes 884744 | tf_op jit(solution)/shard_map/ppermute | solution.py:29
  33.3 6.8 %collective-permute-start.3 = (bf16[96,768]{1,0:T(8,128)(2,1)S(1)}, bf16[96,768]{1,0:T(8,128)(2,1)S(1)}, u32[]{:S(2)}, u32[]{:S(2)}) collective-permute-start(bf16[96,768]{1,0:T(8,128)(2,1)S(1)} %pad_maximum_fusion), channel_id=1, source_target_pairs={{0,8},{4,12},{8,0},{12,4},{16,24},{20,28},{24,16},{28,20},{1,9},{5... | collective-permute-start | bytes 442376 | tf_op jit(solution)/shard_map/ppermute | solution.py:29
  34.9 13.0 %collective-permute-start.4 = (bf16[96,768]{1,0:T(8,128)(2,1)S(1)}, bf16[96,768]{1,0:T(8,128)(2,1)S(1)}, u32[]{:S(2)}, u32[]{:S(2)}) collective-permute-start(bf16[96,768]{1,0:T(8,128)(2,1)S(1)} %pad_maximum_fusion.1), channel_id=1, source_target_pairs={{0,16},{4,20},{8,24},{12,28},{16,0},{20,4},{24,8},{28,12},{1,17},{... | collective-permute-start | bytes 442376 | tf_op jit(solution)/shard_map/ppermute | solution.py:29
  37.6 10.3 %collective-permute-start.5 = (bf16[96,768]{1,0:T(8,128)(2,1)S(1)}, bf16[96,768]{1,0:T(8,128)(2,1)S(1)}, u32[]{:S(2)}, u32[]{:S(2)}) collective-permute-start(bf16[96,768]{1,0:T(8,128)(2,1)S(1)} %pad_maximum_fusion.2), channel_id=1, source_target_pairs={{0,24},{4,28},{8,16},{12,20},{16,8},{20,12},{24,0},{28,4},{1,25},{... | collective-permute-start | bytes 442376 | tf_op jit(solution)/shard_map/ppermute | solution.py:29
  47.9 10.8 %collective-permute-start.10 = (bf16[384,768]{1,0:T(8,128)(2,1)S(1)}, bf16[384,768]{1,0:T(8,128)(2,1)S(1)}, u32[]{:S(2)}, u32[]{:S(2)}) collective-permute-start(bf16[384,768]{1,0:T(8,128)(2,1)S(1)} %get-tuple-element.139.refs_0_), channel_id=1, source_target_pairs={{0,2},{1,3},{2,0},{3,1},{4,6},{5,7},{6,4},{7,5},{8,10},{9,11},{10,... | collective-permute-start | bytes 1769480 | tf_op jit(solution)/shard_map/ppermute | solution.py:29
  49.6 9.3 %collective-permute-start.9 = (bf16[96,768]{1,0:T(8,128)(2,1)S(1)}, bf16[96,768]{1,0:T(8,128)(2,1)S(1)}, u32[]{:S(2)}, u32[]{:S(2)}) collective-permute-start(bf16[96,768]{1,0:T(8,128)(2,1)S(1)} %pad_maximum_fusion.5), channel_id=1, source_target_pairs={{0,24},{4,28},{8,16},{12,20},{16,8},{20,12},{24,0},{28,4},{1,25},{... | collective-permute-start | bytes 442376 | tf_op jit(solution)/shard_map/ppermute | solution.py:29
  52.1 10.6 %collective-permute-start.8 = (bf16[96,768]{1,0:T(8,128)(2,1)S(1)}, bf16[96,768]{1,0:T(8,128)(2,1)S(1)}, u32[]{:S(2)}, u32[]{:S(2)}) collective-permute-start(bf16[96,768]{1,0:T(8,128)(2,1)S(1)} %pad_maximum_fusion.4), channel_id=1, source_target_pairs={{0,16},{4,20},{8,24},{12,28},{16,0},{20,4},{24,8},{28,12},{1,17},{... | collective-permute-start | bytes 442376 | tf_op jit(solution)/shard_map/ppermute | solution.py:29
  55.1 7.6 %collective-permute-start.7 = (bf16[96,768]{1,0:T(8,128)(2,1)S(1)}, bf16[96,768]{1,0:T(8,128)(2,1)S(1)}, u32[]{:S(2)}, u32[]{:S(2)}) collective-permute-start(bf16[96,768]{1,0:T(8,128)(2,1)S(1)} %pad_maximum_fusion.3), channel_id=1, source_target_pairs={{0,8},{4,12},{8,0},{12,4},{16,24},{20,28},{24,16},{28,20},{1,9},{5... | collective-permute-start | bytes 442376 | tf_op jit(solution)/shard_map/ppermute | solution.py:29
  62.7 5.3 %collective-permute-start.11 = (bf16[768,768]{1,0:T(8,128)(2,1)S(1)}, bf16[768,768]{1,0:T(8,128)(2,1)S(1)}, u32[]{:S(2)}, u32[]{:S(2)}) collective-permute-start(bf16[768,768]{1,0:T(8,128)(2,1)S(1)} %constant_dynamic-update-slice_fusion.10.refs_3_), channel_id=1, source_target_pairs={{0,1},{1,0},{2,3},{3,2},{4,5},{5,4},{6,7},{7,6},{8,9},{9,8},{10,11... | collective-permute-start | bytes 3538952 | tf_op jit(solution)/shard_map/ppermute | solution.py:29
  62.9 15.8 %collective-permute-start.15 = (bf16[384,768]{1,0:T(8,128)(2,1)S(1)}, bf16[384,768]{1,0:T(8,128)(2,1)S(1)}, u32[]{:S(2)}, u32[]{:S(2)}) collective-permute-start(bf16[384,768]{1,0:T(8,128)(2,1)S(1)} %get-tuple-element.63.refs_1_), channel_id=1, source_target_pairs={{0,2},{1,3},{2,0},{3,1},{4,6},{5,7},{6,4},{7,5},{8,10},{9,11},{10,... | collective-permute-start | bytes 1769480 | tf_op jit(solution)/shard_map/ppermute | solution.py:29
  63.9 14.8 %collective-permute-start.13 = (bf16[96,768]{1,0:T(8,128)(2,1)S(1)}, bf16[96,768]{1,0:T(8,128)(2,1)S(1)}, u32[]{:S(2)}, u32[]{:S(2)}) collective-permute-start(bf16[96,768]{1,0:T(8,128)(2,1)S(1)} %pad_maximum_fusion.7), channel_id=1, source_target_pairs={{0,16},{4,20},{8,24},{12,28},{16,0},{20,4},{24,8},{28,12},{1,17},{... | collective-permute-start | bytes 442376 | tf_op jit(solution)/shard_map/ppermute | solution.py:29
  66.4 12.3 %collective-permute-start.14 = (bf16[96,768]{1,0:T(8,128)(2,1)S(1)}, bf16[96,768]{1,0:T(8,128)(2,1)S(1)}, u32[]{:S(2)}, u32[]{:S(2)}) collective-permute-start(bf16[96,768]{1,0:T(8,128)(2,1)S(1)} %pad_maximum_fusion.8), channel_id=1, source_target_pairs={{0,24},{4,28},{8,16},{12,20},{16,8},{20,12},{24,0},{28,4},{1,25},{... | collective-permute-start | bytes 442376 | tf_op jit(solution)/shard_map/ppermute | solution.py:29
  68.0 10.7 %collective-permute-start.12 = (bf16[96,768]{1,0:T(8,128)(2,1)S(1)}, bf16[96,768]{1,0:T(8,128)(2,1)S(1)}, u32[]{:S(2)}, u32[]{:S(2)}) collective-permute-start(bf16[96,768]{1,0:T(8,128)(2,1)S(1)} %pad_maximum_fusion.6), channel_id=1, source_target_pairs={{0,8},{4,12},{8,0},{12,4},{16,24},{20,28},{24,16},{28,20},{1,9},{5... | collective-permute-start | bytes 442376 | tf_op jit(solution)/shard_map/ppermute | solution.py:29
  78.8 6.0 %collective-permute-start.16 = (bf16[768,768]{1,0:T(8,128)(2,1)S(1)}, bf16[768,768]{1,0:T(8,128)(2,1)S(1)}, u32[]{:S(2)}, u32[]{:S(2)}) collective-permute-start(bf16[768,768]{1,0:T(8,128)(2,1)S(1)} %constant_dynamic-update-slice_fusion.21.refs_5_), channel_id=1, source_target_pairs={{0,1},{1,0},{2,3},{3,2},{4,5},{5,4},{6,7},{7,6},{8,9},{9,8},{10,11... | collective-permute-start | bytes 3538952 | tf_op jit(solution)/shard_map/ppermute | solution.py:29
  78.9 15.8 %collective-permute-start.20 = (bf16[384,768]{1,0:T(8,128)(2,1)S(1)}, bf16[384,768]{1,0:T(8,128)(2,1)S(1)}, u32[]{:S(2)}, u32[]{:S(2)}) collective-permute-start(bf16[384,768]{1,0:T(8,128)(2,1)S(1)} %get-tuple-element.68.refs_2_), channel_id=1, source_target_pairs={{0,2},{1,3},{2,0},{3,1},{4,6},{5,7},{6,4},{7,5},{8,10},{9,11},{10,... | collective-permute-start | bytes 1769480 | tf_op jit(solution)/shard_map/ppermute | solution.py:29
  80.0 14.8 %collective-permute-start.18 = (bf16[96,768]{1,0:T(8,128)(2,1)S(1)}, bf16[96,768]{1,0:T(8,128)(2,1)S(1)}, u32[]{:S(2)}, u32[]{:S(2)}) collective-permute-start(bf16[96,768]{1,0:T(8,128)(2,1)S(1)} %pad_maximum_fusion.10), channel_id=1, source_target_pairs={{0,16},{4,20},{8,24},{12,28},{16,0},{20,4},{24,8},{28,12},{1,17},{... | collective-permute-start | bytes 442376 | tf_op jit(solution)/shard_map/ppermute | solution.py:29
  83.4 11.4 %collective-permute-start.19 = (bf16[96,768]{1,0:T(8,128)(2,1)S(1)}, bf16[96,768]{1,0:T(8,128)(2,1)S(1)}, u32[]{:S(2)}, u32[]{:S(2)}) collective-permute-start(bf16[96,768]{1,0:T(8,128)(2,1)S(1)} %pad_maximum_fusion.11), channel_id=1, source_target_pairs={{0,24},{4,28},{8,16},{12,20},{16,8},{20,12},{24,0},{28,4},{1,25},{... | collective-permute-start | bytes 442376 | tf_op jit(solution)/shard_map/ppermute | solution.py:29
  84.7 10.6 %collective-permute-start.17 = (bf16[96,768]{1,0:T(8,128)(2,1)S(1)}, bf16[96,768]{1,0:T(8,128)(2,1)S(1)}, u32[]{:S(2)}, u32[]{:S(2)}) collective-permute-start(bf16[96,768]{1,0:T(8,128)(2,1)S(1)} %pad_maximum_fusion.9), channel_id=1, source_target_pairs={{0,8},{4,12},{8,0},{12,4},{16,24},{20,28},{24,16},{28,20},{1,9},{5... | collective-permute-start | bytes 442376 | tf_op jit(solution)/shard_map/ppermute | solution.py:29
  95.5 13.6 %collective-permute-start.21 = (bf16[304,768]{1,0:T(8,128)(2,1)S(1)}, bf16[304,768]{1,0:T(8,128)(2,1)S(1)}, u32[]{:S(2)}, u32[]{:S(2)}) collective-permute-start(bf16[304,768]{1,0:T(8,128)(2,1)S(1)} %slice.168), channel_id=1, source_target_pairs={{0,2},{1,3},{2,0},{3,1},{4,6},{5,7},{6,4},{7,5},{8,10},{9,11},{10,... | collective-permute-start | bytes 1400840 | tf_op jit(solution)/shard_map/ppermute | solution.py:29
  104.2 7.1 %collective-permute-start.23 = (bf16[80,768]{1,0:T(8,128)(2,1)S(1)}, bf16[80,768]{1,0:T(8,128)(2,1)S(1)}, u32[]{:S(2)}, u32[]{:S(2)}) collective-permute-start(bf16[80,768]{1,0:T(8,128)(2,1)S(1)} %slice.169), channel_id=1, source_target_pairs={{0,2},{1,3},{2,0},{3,1},{4,6},{5,7},{6,4},{7,5},{8,10},{9,11},{10,... | collective-permute-start | bytes 368648 | tf_op jit(solution)/shard_map/ppermute | solution.py:29
  111.3 2.9 %collective-permute-start.24 = (bf16[768,768]{1,0:T(8,128)(2,1)S(1)}, bf16[768,768]{1,0:T(8,128)(2,1)S(1)}, u32[]{:S(2)}, u32[]{:S(2)}) collective-permute-start(bf16[768,768]{1,0:T(8,128)(2,1)S(1)} %constant_dynamic-update-slice_fusion.38.refs_4_), channel_id=1, source_target_pairs={{0,1},{1,0},{2,3},{3,2},{4,5},{5,4},{6,7},{7,6},{8,9},{9,8},{10,11... | collective-permute-start | bytes 3538952 | tf_op jit(solution)/shard_map/ppermute | solution.py:29
  (3 other events, 4.8 us)

commit v14 on v13

--- a/solution.py
+++ b/solution.py
@@ -29,11 +29,11 @@
     return lax.ppermute(value, axis, [(i, i ^ bit) for i in range(size)])
 
 
-def place(me, slots, normed, capacity, first, size, groups, low, turn=0):
+def place(me, slots, normed, capacity, first, size, groups, low):
     high = groups // 2
     shape = (high, size, 1)
     spot = lax.broadcasted_iota(jnp.int32, shape, 1) + first
-    group = ((lax.broadcasted_iota(jnp.int32, shape, 0) + turn) % high * 2 + low) ^ me
+    group = (lax.broadcasted_iota(jnp.int32, shape, 0) * 2 + low) ^ me
     wanted = (group * capacity + spot).reshape(groups // 2 * size, 1)
     pick = jnp.where(wanted == slots, 1.0, 0.0)
     live = jnp.max(pick, axis=1, keepdims=True)
@@ -53,7 +53,7 @@
         wide * lax.rsqrt(jnp.sum(wide * wide, axis=-1, keepdims=True) + epsilon)
     ).astype(jnp.bfloat16)
     send_ref[...] = place(
-        me_ref[0], flat(slot_ref), normed_ref[...], capacity, 0, chunks[0], groups, 1, groups // 4
+        me_ref[0], flat(slot_ref), normed_ref[...], capacity, 0, chunks[0], groups, 1
     )
 
 
@@ -292,7 +292,7 @@
 
     def block(step, z):
         size = chunks[step]
-        near = sent["y", min(step, 2) + 1] if step else sent["y", int(z < high // 2)]
+        near = sent["y", min(step, 2) + 1] if step else sent["y", int(z >= high // 2)]
         skip = sum(chunks[2:step]) * high if step else 0
         index = z if step else z % (high // 2)
         return jnp.concatenate(
@@ -308,7 +308,7 @@
         if step >= 2 and z == high - 1:
             early += [("x", step - 2, 0)]
         if z == 1:
-            early += [("c", step - 2)] if step >= 2 else [("y", step + 2)]
+            early += [("c", step - 2)] if step >= 2 else [("y", 3)] if step else []
         send(("z", step, z), block(step, z), "grp", groups, 2 * z, *early)
 
     def collect(step):
@@ -337,7 +337,7 @@
     send(("y", 0), first_send[:cut], "grp", groups, 1)
     send(("y", 1), first_send[cut:], "grp", groups, 1, "rest")
     send(("y", 2), next_send, "grp", groups, 1, ("y", 0))
-    send(("y", 3), rest_send, "grp", groups, 1, ("y", 0))
+    send(("y", 3), rest_send, "grp", groups, 1, ("y", 1))
     for z in far:
         send_z(0, z)
     for step in range(1, count):

time: 131 us -> 119 us (0.908)
  waiting for transfers between devices: 68.9 us -> 54.7 us
    ppermute x25, waiting for transfers between devices: 68.9 us -> 54.7 us  [swap(): return lax.ppermute(value, axis, [(i, i ^ bit) for i in range(size)])]
  transfers between devices with their start and end apart: 25 -> 25, of which waited for: 14 -> 15; matrix products, arithmetic and copies ran while one was open for 1% -> 1% of each run, Pallas kernels for 8% -> 7%
where the time goes in v14:
time: 119 us
  waiting for transfers between devices  54.7 us (46%)
  starting transfers between devices  31.1 us (26%)
  Pallas kernels  17.7 us (15%)
  blocking collectives  11.9 us (10%)
  local copies, waits for them, and re-layouts  2.63 us (2%)
    ppermute x25, waiting for transfers between devices, swap(): return lax.ppermute(value, axis, [(i, i ^ bit) for i in range(size)])  54.7 us
    ppermute x25, starting transfers between devices, swap(): return lax.ppermute(value, axis, [(i, i ^ bit) for i in range(size)])  31.1 us
    all_to_all x1, blocking collectives, on_device(): homeward = lax.all_to_all(result, ('grp', 'blk'), 0, 0, tiled=True)  11.9 us
    pallas_call x2, Pallas kernels, gram_step(): pl.pallas_call(functools.partial(gram_kernel, first, step, pieces), in_sp...  8.45 us
    pallas_call x1, Pallas kernels, gram_last(): pl.pallas_call(functools.partial(gram_last_kernel, step, relatives, chunk...  3.07 us
    pallas_call x1, Pallas kernels, head(): pl.pallas_call(functools.partial(rest_kernel, capacity, chunks, groups),...  2.62 us
    unnamed x23, local copies, waits for them, and re-layouts  2.43 us
  transfers between devices with their start and end apart: 25, of which 15 were waited for; matrix products, arithmetic and copies ran while one was open for 1% of the time, Pallas kernels for 7%

profile of v14, /device:TPU:0, one launch (start us, length us, event | category | flops | bytes accessed | tf_op | source)
XLA Modules:
  0.0 118.6 jit_solution(1849055046798819008)
XLA Ops:
  3.3 2.6 %place_rest.1 = (bf16[192,768]{1,0:T(8,128)(2,1)S(1)}, bf16[192,768]{1,0:T(8,128)(2,1)S(1)}, bf16[192,768]{1,0:T(8,128)(2,1)S(1)}, bf16[192,768]{1,0:T(8,128)(2,...) custom-call(s32[2]{0:T(128)S(1)} %pad_add_fusion.me_ref, s32[6,128]{1,0:T(8,128)S(1)} %bitcast.6, ...), custom_call_target="tpu_custom_call" | custom-call | flops 1585446912 | bytes 3244032 | tf_op jit(solution)/shard_map/place_rest/pallas_call | solution.py:102
  5.9 3.0 %collective-permute-start.2 = (bf16[96,768]{1,0:T(8,128)(2,1)S(1)}, bf16[96,768]{1,0:T(8,128)(2,1)S(1)}, u32[]{:S(2)}, u32[]{:S(2)}) collective-permute-start(bf16[96,768]{1,0:T(8,128)(2,1)S(1)} %get-tuple-element.47), channel_id=1, source_target_pairs={{0,4},{4,0},{8,12},{12,8},{16,20},{20,16},{24,28},{28,24},{1,5},{5... | collective-permute-start | bytes 442376 | tf_op jit(solution)/shard_map/ppermute | solution.py:29
  9.1 4.5 %collective-permute-done.2 = bf16[96,768]{1,0:T(8,128)(2,1)S(1)} collective-permute-done((bf16[96,768]{1,0:T(8,128)(2,1)S(1)}, bf16[96,768]{1,0:T(8,128)(2,1)S(1)}, u32[]{:S(2)}, u32[]{:S(2)}) %collective-permute-start.2) | collective-permute-done | bytes 147488 | tf_op jit(solution)/shard_map/ppermute | solution.py:29
  13.7 2.1 %collective-permute-start.6 = (bf16[384,768]{1,0:T(8,128)(2,1)S(1)}, bf16[384,768]{1,0:T(8,128)(2,1)S(1)}, u32[]{:S(2)}, u32[]{:S(2)}) collective-permute-start(bf16[384,768]{1,0:T(8,128)(2,1)S(1)} %get-tuple-element.51), channel_id=1, source_target_pairs={{0,4},{4,0},{8,12},{12,8},{16,20},{20,16},{24,28},{28,24},{1,5},{5... | collective-permute-start | bytes 1769480 | tf_op jit(solution)/shard_map/ppermute | solution.py:29
  16.9 2.2 %collective-permute-start.1 = (bf16[96,768]{1,0:T(8,128)(2,1)S(1)}, bf16[96,768]{1,0:T(8,128)(2,1)S(1)}, u32[]{:S(2)}, u32[]{:S(2)}) collective-permute-start(bf16[96,768]{1,0:T(8,128)(2,1)S(1)} %pad_maximum_fusion), channel_id=1, source_target_pairs={{0,8},{4,12},{8,0},{12,4},{16,24},{20,28},{24,16},{28,20},{1,9},{5... | collective-permute-start | bytes 442376 | tf_op jit(solution)/shard_map/ppermute | solution.py:29
  19.1 2.6 %collective-permute-start.3 = (bf16[96,768]{1,0:T(8,128)(2,1)S(1)}, bf16[96,768]{1,0:T(8,128)(2,1)S(1)}, u32[]{:S(2)}, u32[]{:S(2)}) collective-permute-start(bf16[96,768]{1,0:T(8,128)(2,1)S(1)} %pad_maximum_fusion.1), channel_id=1, source_target_pairs={{0,16},{4,20},{8,24},{12,28},{16,0},{20,4},{24,8},{28,12},{1,17},{... | collective-permute-start | bytes 442376 | tf_op jit(solution)/shard_map/ppermute | solution.py:29
  21.8 1.7 %collective-permute-start.5 = (bf16[192,768]{1,0:T(8,128)(2,1)S(1)}, bf16[192,768]{1,0:T(8,128)(2,1)S(1)}, u32[]{:S(2)}, u32[]{:S(2)}) collective-permute-start(bf16[192,768]{1,0:T(8,128)(2,1)S(1)} %get-tuple-element.50), channel_id=1, source_target_pairs={{0,4},{4,0},{8,12},{12,8},{16,20},{20,16},{24,28},{28,24},{1,5},{5... | collective-permute-start | bytes 884744 | tf_op jit(solution)/shard_map/ppermute | solution.py:29
  23.6 7.6 %collective-permute-done.3 = bf16[96,768]{1,0:T(8,128)(2,1)S(1)} collective-permute-done((bf16[96,768]{1,0:T(8,128)(2,1)S(1)}, bf16[96,768]{1,0:T(8,128)(2,1)S(1)}, u32[]{:S(2)}, u32[]{:S(2)}) %collective-permute-start.3) | collective-permute-done | bytes 147488 | tf_op jit(solution)/shard_map/ppermute | solution.py:29
  32.8 2.1 %collective-permute-done.5 = bf16[192,768]{1,0:T(8,128)(2,1)S(1)} collective-permute-done((bf16[192,768]{1,0:T(8,128)(2,1)S(1)}, bf16[192,768]{1,0:T(8,128)(2,1)S(1)}, u32[]{:S(2)}, u32[]{:S(2)}) %collective-permute-start.5) | collective-permute-done | bytes 294944 | tf_op jit(solution)/shard_map/ppermute | solution.py:29
  35.0 3.9 %collective-permute-start.9 = (bf16[96,768]{1,0:T(8,128)(2,1)S(1)}, bf16[96,768]{1,0:T(8,128)(2,1)S(1)}, u32[]{:S(2)}, u32[]{:S(2)}) collective-permute-start(bf16[96,768]{1,0:T(8,128)(2,1)S(1)} %pad_maximum_fusion.5), channel_id=1, source_target_pairs={{0,24},{4,28},{8,16},{12,20},{16,8},{20,12},{24,0},{28,4},{1,25},{... | collective-permute-start | bytes 442376 | tf_op jit(solution)/shard_map/ppermute | solution.py:29
  39.6 2.0 %collective-permute-done.10 = bf16[384,768]{1,0:T(8,128)(2,1)S(1)} collective-permute-done((bf16[384,768]{1,0:T(8,128)(2,1)S(1)}, bf16[384,768]{1,0:T(8,128)(2,1)S(1)}, u32[]{:S(2)}, u32[]{:S(2)}) %collective-permute-start.10) | collective-permute-done | bytes 589856 | tf_op jit(solution)/shard_map/ppermute | solution.py:29
  41.7 1.9 %collective-permute-done.9 = bf16[96,768]{1,0:T(8,128)(2,1)S(1)} collective-permute-done((bf16[96,768]{1,0:T(8,128)(2,1)S(1)}, bf16[96,768]{1,0:T(8,128)(2,1)S(1)}, u32[]{:S(2)}, u32[]{:S(2)}) %collective-permute-start.9) | collective-permute-done | bytes 147488 | tf_op jit(solution)/shard_map/ppermute | solution.py:29
  43.6 6.4 %collective-permute-done.8 = bf16[96,768]{1,0:T(8,128)(2,1)S(1)} collective-permute-done((bf16[96,768]{1,0:T(8,128)(2,1)S(1)}, bf16[96,768]{1,0:T(8,128)(2,1)S(1)}, u32[]{:S(2)}, u32[]{:S(2)}) %collective-permute-start.8) | collective-permute-done | bytes 147488 | tf_op jit(solution)/shard_map/ppermute | solution.py:29
  51.9 2.5 %collective-permute-start.14 = (bf16[96,768]{1,0:T(8,128)(2,1)S(1)}, bf16[96,768]{1,0:T(8,128)(2,1)S(1)}, u32[]{:S(2)}, u32[]{:S(2)}) collective-permute-start(bf16[96,768]{1,0:T(8,128)(2,1)S(1)} %pad_maximum_fusion.8), channel_id=1, source_target_pairs={{0,24},{4,28},{8,16},{12,20},{16,8},{20,12},{24,0},{28,4},{1,25},{... | collective-permute-start | bytes 442376 | tf_op jit(solution)/shard_map/ppermute | solution.py:29
  55.5 10.5 %collective-permute-done.15 = bf16[384,768]{1,0:T(8,128)(2,1)S(1)} collective-permute-done((bf16[384,768]{1,0:T(8,128)(2,1)S(1)}, bf16[384,768]{1,0:T(8,128)(2,1)S(1)}, u32[]{:S(2)}, u32[]{:S(2)}) %collective-permute-start.15) | collective-permute-done | bytes 589856 | tf_op jit(solution)/shard_map/ppermute | solution.py:29
  69.4 2.5 %collective-permute-start.19 = (bf16[96,768]{1,0:T(8,128)(2,1)S(1)}, bf16[96,768]{1,0:T(8,128)(2,1)S(1)}, u32[]{:S(2)}, u32[]{:S(2)}) collective-permute-start(bf16[96,768]{1,0:T(8,128)(2,1)S(1)} %pad_maximum_fusion.11), channel_id=1, source_target_pairs={{0,24},{4,28},{8,16},{12,20},{16,8},{20,12},{24,0},{28,4},{1,25},{... | collective-permute-start | bytes 442376 | tf_op jit(solution)/shard_map/ppermute | solution.py:29
  71.9 10.4 %collective-permute-done.20 = bf16[384,768]{1,0:T(8,128)(2,1)S(1)} collective-permute-done((bf16[384,768]{1,0:T(8,128)(2,1)S(1)}, bf16[384,768]{1,0:T(8,128)(2,1)S(1)}, u32[]{:S(2)}, u32[]{:S(2)}) %collective-permute-start.20) | collective-permute-done | bytes 589856 | tf_op jit(solution)/shard_map/ppermute | solution.py:29
  85.3 6.0 %gram_step.2 = (f32[384,128]{1,0:T(8,128)S(1)}, f32[384,128]{1,0:T(8,128)S(1)}, f32[384,128]{1,0:T(8,128)S(1)}, f32[1,1536]{1,0:T(1,128)S(1)}, f32[1,1536]{1,0:T(1,128)S(1)}, /*index=5*/f32[1,1536]{1,0:T(1,128)S(1)}) custom-call(bf16[384,768]{1,0:T(8,128)(2,1)S(1)} %get-tuple-element.137.refs_0_, bf16[384,768]{1,0:T(8,128)(2,1)S(1)} %get-tuple-element.61.refs_1_, ...), custom_call_target="tpu_custom_call" | custom-call | flops 8153726976 | bytes 8847360 | tf_op jit(solution)/shard_map/gram_step/pallas_call | solution.py:214
  92.6 3.6 %collective-permute-done.21 = bf16[304,768]{1,0:T(8,128)(2,1)S(1)} collective-permute-done((bf16[304,768]{1,0:T(8,128)(2,1)S(1)}, bf16[304,768]{1,0:T(8,128)(2,1)S(1)}, u32[]{:S(2)}, u32[]{:S(2)}) %collective-permute-start.21) | collective-permute-done | bytes 466976 | tf_op jit(solution)/shard_map/ppermute | solution.py:29
  96.2 2.2 %collective-permute-done.23 = bf16[80,768]{1,0:T(8,128)(2,1)S(1)} collective-permute-done((bf16[80,768]{1,0:T(8,128)(2,1)S(1)}, bf16[80,768]{1,0:T(8,128)(2,1)S(1)}, u32[]{:S(2)}, u32[]{:S(2)}) %collective-permute-start.23) | collective-permute-done | bytes 122912 | tf_op jit(solution)/shard_map/ppermute | solution.py:29
  98.5 2.4 %gram_step.3 = (f32[384,128]{1,0:T(8,128)S(1)}, f32[384,128]{1,0:T(8,128)S(1)}, f32[384,128]{1,0:T(8,128)S(1)}, f32[384,128]{1,0:T(8,128)S(1)}, f32[1,768]{1,0:T(1,128)S(1)}) custom-call(bf16[384,768]{1,0:T(8,128)(2,1)S(1)} %get-tuple-element.137.refs_0_, bf16[384,768]{1,0:T(8,128)(2,1)S(1)} %get-tuple-element.61.refs_1_, ...), custom_call_target="tpu_custom_call" | custom-call | flops 1811939328 | bytes 3538944 | tf_op jit(solution)/shard_map/gram_step/pallas_call | solution.py:214
  101.3 3.1 %gram_last.1 = f32[32,1,192]{2,1,0:T(1,128)S(1)} custom-call(s32[2]{0:T(128)S(1)} %pad_add_fusion.me_ref, bf16[384,768]{1,0:T(8,128)(2,1)S(1)} %get-tuple-element.137.refs_0_, bf16[384,768]{1,0:T(8,128)(2,1)S(1)} %get-tuple-element.61.refs_1_, bf16[384,768]{1,0:T(8,128)(2,1)S(1)} %get-tuple-element.66.refs_2_, ...), custom_call_target="tpu_custom_call" | custom-call | flops 1811939328 | bytes 3538944 | tf_op jit(solution)/shard_map/gram_last/pallas_call | solution.py:229
  104.4 11.9 %all_to_all.5.part_ref = f32[32,1,192]{2,1,0:T(1,128)} all-to-all(f32[32,1,192]{2,1,0:T(1,128)S(1)} %gram_last.1), channel_id=1, replica_groups=mesh['grp'=8,'blk'=4] {'grp','blk'}, dimensions={0} | all-to-all | bytes 49152 | tf_op jit(solution)/shard_map/all_to_all | solution.py:360
  116.3 2.3 %pick_rows.1 = f32[6,128]{1,0:T(8,128)} custom-call(s32[6,128]{1,0:T(8,128)} %bitcast.4, f32[32,1,192]{2,1,0:T(1,128)} %all_to_all.5.part_ref), custom_call_target="tpu_custom_call" | custom-call | tf_op jit(solution)/shard_map/pick_rows/pallas_call | solution.py:265
  (77 shorter events, 18.0 us)
Async XLA Ops:
  5.9 7.7 %collective-permute-start.2 = (bf16[96,768]{1,0:T(8,128)(2,1)S(1)}, bf16[96,768]{1,0:T(8,128)(2,1)S(1)}, u32[]{:S(2)}, u32[]{:S(2)}) collective-permute-start(bf16[96,768]{1,0:T(8,128)(2,1)S(1)} %get-tuple-element.47), channel_id=1, source_target_pairs={{0,4},{4,0},{8,12},{12,8},{16,20},{20,16},{24,28},{28,24},{1,5},{5... | collective-permute-start | bytes 442376 | tf_op jit(solution)/shard_map/ppermute | solution.py:29
  9.0 7.8 %collective-permute-start = (bf16[96,768]{1,0:T(8,128)(2,1)S(1)}, bf16[96,768]{1,0:T(8,128)(2,1)S(1)}, u32[]{:S(2)}, u32[]{:S(2)}) collective-permute-start(bf16[96,768]{1,0:T(8,128)(2,1)S(1)} %get-tuple-element.117), channel_id=1, source_target_pairs={{0,4},{4,0},{8,12},{12,8},{16,20},{20,16},{24,28},{28,24},{1,5},{5... | collective-permute-start | bytes 442376 | tf_op jit(solution)/shard_map/ppermute | solution.py:29
  13.7 25.3 %collective-permute-start.6 = (bf16[384,768]{1,0:T(8,128)(2,1)S(1)}, bf16[384,768]{1,0:T(8,128)(2,1)S(1)}, u32[]{:S(2)}, u32[]{:S(2)}) collective-permute-start(bf16[384,768]{1,0:T(8,128)(2,1)S(1)} %get-tuple-element.51), channel_id=1, source_target_pairs={{0,4},{4,0},{8,12},{12,8},{16,20},{20,16},{24,28},{28,24},{1,5},{5... | collective-permute-start | bytes 1769480 | tf_op jit(solution)/shard_map/ppermute | solution.py:29
  16.9 6.7 %collective-permute-start.1 = (bf16[96,768]{1,0:T(8,128)(2,1)S(1)}, bf16[96,768]{1,0:T(8,128)(2,1)S(1)}, u32[]{:S(2)}, u32[]{:S(2)}) collective-permute-start(bf16[96,768]{1,0:T(8,128)(2,1)S(1)} %pad_maximum_fusion), channel_id=1, source_target_pairs={{0,8},{4,12},{8,0},{12,4},{16,24},{20,28},{24,16},{28,20},{1,9},{5... | collective-permute-start | bytes 442376 | tf_op jit(solution)/shard_map/ppermute | solution.py:29
  19.1 12.1 %collective-permute-start.3 = (bf16[96,768]{1,0:T(8,128)(2,1)S(1)}, bf16[96,768]{1,0:T(8,128)(2,1)S(1)}, u32[]{:S(2)}, u32[]{:S(2)}) collective-permute-start(bf16[96,768]{1,0:T(8,128)(2,1)S(1)} %pad_maximum_fusion.1), channel_id=1, source_target_pairs={{0,16},{4,20},{8,24},{12,28},{16,0},{20,4},{24,8},{28,12},{1,17},{... | collective-permute-start | bytes 442376 | tf_op jit(solution)/shard_map/ppermute | solution.py:29
  21.7 9.5 %collective-permute-start.4 = (bf16[96,768]{1,0:T(8,128)(2,1)S(1)}, bf16[96,768]{1,0:T(8,128)(2,1)S(1)}, u32[]{:S(2)}, u32[]{:S(2)}) collective-permute-start(bf16[96,768]{1,0:T(8,128)(2,1)S(1)} %pad_maximum_fusion.2), channel_id=1, source_target_pairs={{0,24},{4,28},{8,16},{12,20},{16,8},{20,12},{24,0},{28,4},{1,25},{... | collective-permute-start | bytes 442376 | tf_op jit(solution)/shard_map/ppermute | solution.py:29
  21.8 13.1 %collective-permute-start.5 = (bf16[192,768]{1,0:T(8,128)(2,1)S(1)}, bf16[192,768]{1,0:T(8,128)(2,1)S(1)}, u32[]{:S(2)}, u32[]{:S(2)}) collective-permute-start(bf16[192,768]{1,0:T(8,128)(2,1)S(1)} %get-tuple-element.50), channel_id=1, source_target_pairs={{0,4},{4,0},{8,12},{12,8},{16,20},{20,16},{24,28},{28,24},{1,5},{5... | collective-permute-start | bytes 884744 | tf_op jit(solution)/shard_map/ppermute | solution.py:29
  31.3 10.4 %collective-permute-start.10 = (bf16[384,768]{1,0:T(8,128)(2,1)S(1)}, bf16[384,768]{1,0:T(8,128)(2,1)S(1)}, u32[]{:S(2)}, u32[]{:S(2)}) collective-permute-start(bf16[384,768]{1,0:T(8,128)(2,1)S(1)} %get-tuple-element.137.refs_0_), channel_id=1, source_target_pairs={{0,2},{1,3},{2,0},{3,1},{4,6},{5,7},{6,4},{7,5},{8,10},{9,11},{10,... | collective-permute-start | bytes 1769480 | tf_op jit(solution)/shard_map/ppermute | solution.py:29
  35.0 8.7 %collective-permute-start.9 = (bf16[96,768]{1,0:T(8,128)(2,1)S(1)}, bf16[96,768]{1,0:T(8,128)(2,1)S(1)}, u32[]{:S(2)}, u32[]{:S(2)}) collective-permute-start(bf16[96,768]{1,0:T(8,128)(2,1)S(1)} %pad_maximum_fusion.5), channel_id=1, source_target_pairs={{0,24},{4,28},{8,16},{12,20},{16,8},{20,12},{24,0},{28,4},{1,25},{... | collective-permute-start | bytes 442376 | tf_op jit(solution)/shard_map/ppermute | solution.py:29
  38.9 11.1 %collective-permute-start.8 = (bf16[96,768]{1,0:T(8,128)(2,1)S(1)}, bf16[96,768]{1,0:T(8,128)(2,1)S(1)}, u32[]{:S(2)}, u32[]{:S(2)}) collective-permute-start(bf16[96,768]{1,0:T(8,128)(2,1)S(1)} %pad_maximum_fusion.4), channel_id=1, source_target_pairs={{0,16},{4,20},{8,24},{12,28},{16,0},{20,4},{24,8},{28,12},{1,17},{... | collective-permute-start | bytes 442376 | tf_op jit(solution)/shard_map/ppermute | solution.py:29
  39.0 11.0 %collective-permute-start.7 = (bf16[96,768]{1,0:T(8,128)(2,1)S(1)}, bf16[96,768]{1,0:T(8,128)(2,1)S(1)}, u32[]{:S(2)}, u32[]{:S(2)}) collective-permute-start(bf16[96,768]{1,0:T(8,128)(2,1)S(1)} %pad_maximum_fusion.3), channel_id=1, source_target_pairs={{0,8},{4,12},{8,0},{12,4},{16,24},{20,28},{24,16},{28,20},{1,9},{5... | collective-permute-start | bytes 442376 | tf_op jit(solution)/shard_map/ppermute | solution.py:29
  50.0 4.4 %collective-permute-start.11 = (bf16[768,768]{1,0:T(8,128)(2,1)S(1)}, bf16[768,768]{1,0:T(8,128)(2,1)S(1)}, u32[]{:S(2)}, u32[]{:S(2)}) collective-permute-start(bf16[768,768]{1,0:T(8,128)(2,1)S(1)} %constant_dynamic-update-slice_fusion.10.refs_3_), channel_id=1, source_target_pairs={{0,1},{1,0},{2,3},{3,2},{4,5},{5,4},{6,7},{7,6},{8,9},{9,8},{10,11... | collective-permute-start | bytes 3538952 | tf_op jit(solution)/shard_map/ppermute | solution.py:29
  50.2 15.8 %collective-permute-start.15 = (bf16[384,768]{1,0:T(8,128)(2,1)S(1)}, bf16[384,768]{1,0:T(8,128)(2,1)S(1)}, u32[]{:S(2)}, u32[]{:S(2)}) collective-permute-start(bf16[384,768]{1,0:T(8,128)(2,1)S(1)} %get-tuple-element.61.refs_1_), channel_id=1, source_target_pairs={{0,2},{1,3},{2,0},{3,1},{4,6},{5,7},{6,4},{7,5},{8,10},{9,11},{10,... | collective-permute-start | bytes 1769480 | tf_op jit(solution)/shard_map/ppermute | solution.py:29
  51.8 14.2 %collective-permute-start.13 = (bf16[96,768]{1,0:T(8,128)(2,1)S(1)}, bf16[96,768]{1,0:T(8,128)(2,1)S(1)}, u32[]{:S(2)}, u32[]{:S(2)}) collective-permute-start(bf16[96,768]{1,0:T(8,128)(2,1)S(1)} %pad_maximum_fusion.7), channel_id=1, source_target_pairs={{0,16},{4,20},{8,24},{12,28},{16,0},{20,4},{24,8},{28,12},{1,17},{... | collective-permute-start | bytes 442376 | tf_op jit(solution)/shard_map/ppermute | solution.py:29
  51.9 14.1 %collective-permute-start.14 = (bf16[96,768]{1,0:T(8,128)(2,1)S(1)}, bf16[96,768]{1,0:T(8,128)(2,1)S(1)}, u32[]{:S(2)}, u32[]{:S(2)}) collective-permute-start(bf16[96,768]{1,0:T(8,128)(2,1)S(1)} %pad_maximum_fusion.8), channel_id=1, source_target_pairs={{0,24},{4,28},{8,16},{12,20},{16,8},{20,12},{24,0},{28,4},{1,25},{... | collective-permute-start | bytes 442376 | tf_op jit(solution)/shard_map/ppermute | solution.py:29
  54.5 11.9 %collective-permute-start.12 = (bf16[96,768]{1,0:T(8,128)(2,1)S(1)}, bf16[96,768]{1,0:T(8,128)(2,1)S(1)}, u32[]{:S(2)}, u32[]{:S(2)}) collective-permute-start(bf16[96,768]{1,0:T(8,128)(2,1)S(1)} %pad_maximum_fusion.6), channel_id=1, source_target_pairs={{0,8},{4,12},{8,0},{12,4},{16,24},{20,28},{24,16},{28,20},{1,9},{5... | collective-permute-start | bytes 442376 | tf_op jit(solution)/shard_map/ppermute | solution.py:29
  66.4 5.5 %collective-permute-start.16 = (bf16[768,768]{1,0:T(8,128)(2,1)S(1)}, bf16[768,768]{1,0:T(8,128)(2,1)S(1)}, u32[]{:S(2)}, u32[]{:S(2)}) collective-permute-start(bf16[768,768]{1,0:T(8,128)(2,1)S(1)} %constant_dynamic-update-slice_fusion.21.refs_5_), channel_id=1, source_target_pairs={{0,1},{1,0},{2,3},{3,2},{4,5},{5,4},{6,7},{7,6},{8,9},{9,8},{10,11... | collective-permute-start | bytes 3538952 | tf_op jit(solution)/shard_map/ppermute | solution.py:29
  66.5 15.8 %collective-permute-start.20 = (bf16[384,768]{1,0:T(8,128)(2,1)S(1)}, bf16[384,768]{1,0:T(8,128)(2,1)S(1)}, u32[]{:S(2)}, u32[]{:S(2)}) collective-permute-start(bf16[384,768]{1,0:T(8,128)(2,1)S(1)} %get-tuple-element.66.refs_2_), channel_id=1, source_target_pairs={{0,2},{1,3},{2,0},{3,1},{4,6},{5,7},{6,4},{7,5},{8,10},{9,11},{10,... | collective-permute-start | bytes 1769480 | tf_op jit(solution)/shard_map/ppermute | solution.py:29
  67.8 14.5 %collective-permute-start.18 = (bf16[96,768]{1,0:T(8,128)(2,1)S(1)}, bf16[96,768]{1,0:T(8,128)(2,1)S(1)}, u32[]{:S(2)}, u32[]{:S(2)}) collective-permute-start(bf16[96,768]{1,0:T(8,128)(2,1)S(1)} %pad_maximum_fusion.10), channel_id=1, source_target_pairs={{0,16},{4,20},{8,24},{12,28},{16,0},{20,4},{24,8},{28,12},{1,17},{... | collective-permute-start | bytes 442376 | tf_op jit(solution)/shard_map/ppermute | solution.py:29
  69.4 12.9 %collective-permute-start.19 = (bf16[96,768]{1,0:T(8,128)(2,1)S(1)}, bf16[96,768]{1,0:T(8,128)(2,1)S(1)}, u32[]{:S(2)}, u32[]{:S(2)}) collective-permute-start(bf16[96,768]{1,0:T(8,128)(2,1)S(1)} %pad_maximum_fusion.11), channel_id=1, source_target_pairs={{0,24},{4,28},{8,16},{12,20},{16,8},{20,12},{24,0},{28,4},{1,25},{... | collective-permute-start | bytes 442376 | tf_op jit(solution)/shard_map/ppermute | solution.py:29
  71.9 10.6 %collective-permute-start.17 = (bf16[96,768]{1,0:T(8,128)(2,1)S(1)}, bf16[96,768]{1,0:T(8,128)(2,1)S(1)}, u32[]{:S(2)}, u32[]{:S(2)}) collective-permute-start(bf16[96,768]{1,0:T(8,128)(2,1)S(1)} %pad_maximum_fusion.9), channel_id=1, source_target_pairs={{0,8},{4,12},{8,0},{12,4},{16,24},{20,28},{24,16},{28,20},{1,9},{5... | collective-permute-start | bytes 442376 | tf_op jit(solution)/shard_map/ppermute | solution.py:29
  82.6 13.6 %collective-permute-start.21 = (bf16[304,768]{1,0:T(8,128)(2,1)S(1)}, bf16[304,768]{1,0:T(8,128)(2,1)S(1)}, u32[]{:S(2)}, u32[]{:S(2)}) collective-permute-start(bf16[304,768]{1,0:T(8,128)(2,1)S(1)} %slice.168), channel_id=1, source_target_pairs={{0,2},{1,3},{2,0},{3,1},{4,6},{5,7},{6,4},{7,5},{8,10},{9,11},{10,... | collective-permute-start | bytes 1400840 | tf_op jit(solution)/shard_map/ppermute | solution.py:29
  91.3 7.1 %collective-permute-start.23 = (bf16[80,768]{1,0:T(8,128)(2,1)S(1)}, bf16[80,768]{1,0:T(8,128)(2,1)S(1)}, u32[]{:S(2)}, u32[]{:S(2)}) collective-permute-start(bf16[80,768]{1,0:T(8,128)(2,1)S(1)} %slice.169), channel_id=1, source_target_pairs={{0,2},{1,3},{2,0},{3,1},{4,6},{5,7},{6,4},{7,5},{8,10},{9,11},{10,... | collective-permute-start | bytes 368648 | tf_op jit(solution)/shard_map/ppermute | solution.py:29
  98.4 2.9 %collective-permute-start.24 = (bf16[768,768]{1,0:T(8,128)(2,1)S(1)}, bf16[768,768]{1,0:T(8,128)(2,1)S(1)}, u32[]{:S(2)}, u32[]{:S(2)}) collective-permute-start(bf16[768,768]{1,0:T(8,128)(2,1)S(1)} %constant_dynamic-update-slice_fusion.38.refs_4_), channel_id=1, source_target_pairs={{0,1},{1,0},{2,3},{3,2},{4,5},{5,4},{6,7},{7,6},{8,9},{9,8},{10,11... | collective-permute-start | bytes 3538952 | tf_op jit(solution)/shard_map/ppermute | solution.py:29
  (3 other events, 4.8 us)

commit v15 on v10

--- a/solution.py
+++ b/solution.py
@@ -190,7 +190,7 @@
         for p, relative in enumerate(relatives):
             row = r * members + p
             target = (me_ref[0] ^ r) * members + (me_ref[1] ^ relative)
-            out_ref[pl.ds(target, 1), :] = table[row : row + 1, :]
+            out_ref[target] = table[row : row + 1, :]
 
 
 def gram_params(owns, blocks):
@@ -224,13 +224,13 @@
 def gram_last(me, owns, block, states, cols, relatives, chunks, groups):
     step = len(owns) - 1
     members = len(relatives)
-    shape = (groups * members, sum(chunks))
+    shape = (groups * members, 1, sum(chunks))
     return pl.pallas_call(
         functools.partial(gram_last_kernel, step, relatives, chunks, groups),
         in_specs=[smem] + [vmem] * (3 * step + 4),
         out_specs=vmem,
         out_shape=jax.ShapeDtypeStruct(shape, jnp.float32),
-        scratch_shapes=[pltpu.VMEM((1, block.shape[0]), jnp.float32), pltpu.VMEM(shape, jnp.float32)]
+        scratch_shapes=[pltpu.VMEM((1, block.shape[0]), jnp.float32), pltpu.VMEM(shape[::2], jnp.float32)]
         + [pltpu.VMEM((own.shape[0], lanes), jnp.float32) for own in owns],
         name="gram_last",
         **gram_params(owns, [block]),
@@ -243,7 +243,7 @@
     table[...] = jnp.full(table.shape, sentinel, jnp.float32)
     for g in range(groups):
         table[g : g + 1, :capacity] = jnp.max(
-            part_ref[g * members : (g + 1) * members, :], axis=0, keepdims=True
+            part_ref[g * members : (g + 1) * members], axis=0
         )
     lane = lax.broadcasted_iota(jnp.int32, (lanes, lanes), 1)
     for q in range(out_ref.shape[0]):
@@ -309,18 +309,10 @@
             early += [("c", step - 2 if z == far[-1] else step - 3)]
         send(("z", step, z), block(step, z), "grp", groups, 2 * z, *early)
 
-    def send_near_z():
-        blocks = jnp.concatenate([block(step, 1) for step in range(1, count)], axis=0)
-        send(("n",), blocks, "grp", groups, 2, ("z", 0, 1))
-
     def collect(step):
         parts = [block(step, 0)]
         for z in range(1, high):
-            if z == 1 and step >= 1:
-                start = 2 * sum(chunks[1:step])
-                parts.append(sent["n",][start : start + 2 * chunks[step]])
-            else:
-                parts.append(sent["z", step, z])
+            parts.append(sent["z", step, z])
         owns[step] = jnp.concatenate(parts, axis=0)
 
     def send_x(step, cuts, between):
@@ -347,13 +339,10 @@
     first_near = jnp.concatenate([sent["y", 0], sent["y", 1]], axis=0)
     for z in far:
         send_z(0, z)
-    far.remove(1)
     for step in range(1, count):
         collect(step - 1)
         for z in far:
             send_z(step, z)
-        if step == 1:
-            send_near_z()
         send_x(step - 1, [], [])
         send_c(step - 1, *[("z", step, z) for z in far])
     collect(last)

time: 117 us -> 117 us (level)
  waiting for transfers between devices: 55.1 us -> 50.6 us
  starting transfers between devices: 29.3 us -> 33.1 us
    ppermute x23 -> x25, waiting for transfers between devices: 55.1 us -> 50.6 us  [swap(): return lax.ppermute(value, axis, [(i, i ^ bit) for i in range(size)])]
    ppermute x23 -> x25, starting transfers between devices: 29.3 us -> 33.1 us  [swap(): return lax.ppermute(value, axis, [(i, i ^ bit) for i in range(size)])]
    unnamed x24 -> x23, local copies, waits for them, and re-layouts: 3.04 us -> 2.43 us
  transfers between devices with their start and end apart: 23 -> 25, of which waited for: 13 -> 13; matrix products, arithmetic and copies ran while one was open for 1% -> 1% of each run, Pallas kernels for 9% -> 10%
where the time goes in v15:
time: 117 us; the launch traced here: 116 us
  waiting for transfers between devices  50.6 us (43%)
  starting transfers between devices  33.1 us (28%)
  Pallas kernels  17.7 us (15%)
  blocking collectives  11.8 us (10%)
  local copies, waits for them, and re-layouts  2.63 us (2%)
    ppermute x25, waiting for transfers between devices, swap(): return lax.ppermute(value, axis, [(i, i ^ bit) for i in range(size)])  50.6 us
    ppermute x25, starting transfers between devices, swap(): return lax.ppermute(value, axis, [(i, i ^ bit) for i in range(size)])  33.1 us
    all_to_all x1, blocking collectives, on_device(): homeward = lax.all_to_all(result, ('grp', 'blk'), 0, 0, tiled=True)  11.8 us
    pallas_call x2, Pallas kernels, gram_step(): pl.pallas_call(functools.partial(gram_kernel, first, step, pieces), in_sp...  8.45 us
    pallas_call x1, Pallas kernels, gram_last(): pl.pallas_call(functools.partial(gram_last_kernel, step, relatives, chunk...  3.08 us
    pallas_call x1, Pallas kernels, head(): pl.pallas_call(functools.partial(rest_kernel, capacity, chunks, groups),...  2.61 us
    unnamed x23, local copies, waits for them, and re-layouts  2.43 us
  transfers between devices with their start and end apart: 25, of which 13 were waited for; matrix products, arithmetic and copies ran while one was open for 1% of the time, Pallas kernels for 10%

profile of v15, /device:TPU:0, one launch (start us, length us, event | category | flops | bytes accessed | tf_op | source)
XLA Modules:
  0.0 116.4 jit_solution(3556140428658584402)
XLA Ops:
  3.3 3.0 %collective-permute-start = (bf16[96,768]{1,0:T(8,128)(2,1)S(1)}, bf16[96,768]{1,0:T(8,128)(2,1)S(1)}, u32[]{:S(2)}, u32[]{:S(2)}) collective-permute-start(bf16[96,768]{1,0:T(8,128)(2,1)S(1)} %get-tuple-element.117), channel_id=1, source_target_pairs={{0,4},{4,0},{8,12},{12,8},{16,20},{20,16},{24,28},{28,24},{1,5},{5... | collective-permute-start | bytes 442376 | tf_op jit(solution)/shard_map/ppermute | solution.py:29
  6.4 2.6 %place_rest.1 = (bf16[192,768]{1,0:T(8,128)(2,1)S(1)}, bf16[192,768]{1,0:T(8,128)(2,1)S(1)}, bf16[192,768]{1,0:T(8,128)(2,1)S(1)}, bf16[192,768]{1,0:T(8,128)(2,...) custom-call(s32[2]{0:T(128)S(1)} %pad_add_fusion.me_ref, s32[6,128]{1,0:T(8,128)S(1)} %bitcast.6, ...), custom_call_target="tpu_custom_call" | custom-call | flops 1585446912 | bytes 3244032 | tf_op jit(solution)/shard_map/place_rest/pallas_call | solution.py:101
  10.2 1.9 %collective-permute-start.1 = (bf16[96,768]{1,0:T(8,128)(2,1)S(1)}, bf16[96,768]{1,0:T(8,128)(2,1)S(1)}, u32[]{:S(2)}, u32[]{:S(2)}) collective-permute-start(bf16[96,768]{1,0:T(8,128)(2,1)S(1)} %pad_maximum_fusion), channel_id=1, source_target_pairs={{0,8},{4,12},{8,0},{12,4},{16,24},{20,28},{24,16},{28,20},{1,9},{5... | collective-permute-start | bytes 442376 | tf_op jit(solution)/shard_map/ppermute | solution.py:29
  12.1 2.2 %collective-permute-done.2 = bf16[96,768]{1,0:T(8,128)(2,1)S(1)} collective-permute-done((bf16[96,768]{1,0:T(8,128)(2,1)S(1)}, bf16[96,768]{1,0:T(8,128)(2,1)S(1)}, u32[]{:S(2)}, u32[]{:S(2)}) %collective-permute-start.2) | collective-permute-done | bytes 147488 | tf_op jit(solution)/shard_map/ppermute | solution.py:29
  14.4 2.7 %collective-permute-start.3 = (bf16[96,768]{1,0:T(8,128)(2,1)S(1)}, bf16[96,768]{1,0:T(8,128)(2,1)S(1)}, u32[]{:S(2)}, u32[]{:S(2)}) collective-permute-start(bf16[96,768]{1,0:T(8,128)(2,1)S(1)} %pad_maximum_fusion.1), channel_id=1, source_target_pairs={{0,16},{4,20},{8,24},{12,28},{16,0},{20,4},{24,8},{28,12},{1,17},{... | collective-permute-start | bytes 442376 | tf_op jit(solution)/shard_map/ppermute | solution.py:29
  20.5 6.8 %collective-permute-done.3 = bf16[96,768]{1,0:T(8,128)(2,1)S(1)} collective-permute-done((bf16[96,768]{1,0:T(8,128)(2,1)S(1)}, bf16[96,768]{1,0:T(8,128)(2,1)S(1)}, u32[]{:S(2)}, u32[]{:S(2)}) %collective-permute-start.3) | collective-permute-done | bytes 147488 | tf_op jit(solution)/shard_map/ppermute | solution.py:29
  29.0 2.6 %collective-permute-start.6 = (bf16[96,768]{1,0:T(8,128)(2,1)S(1)}, bf16[96,768]{1,0:T(8,128)(2,1)S(1)}, u32[]{:S(2)}, u32[]{:S(2)}) collective-permute-start(bf16[96,768]{1,0:T(8,128)(2,1)S(1)} %pad_maximum_fusion.3), channel_id=1, source_target_pairs={{0,8},{4,12},{8,0},{12,4},{16,24},{20,28},{24,16},{28,20},{1,9},{5... | collective-permute-start | bytes 442376 | tf_op jit(solution)/shard_map/ppermute | solution.py:29
  31.6 2.0 %collective-permute-start.7 = (bf16[96,768]{1,0:T(8,128)(2,1)S(1)}, bf16[96,768]{1,0:T(8,128)(2,1)S(1)}, u32[]{:S(2)}, u32[]{:S(2)}) collective-permute-start(bf16[96,768]{1,0:T(8,128)(2,1)S(1)} %pad_maximum_fusion.4), channel_id=1, source_target_pairs={{0,16},{4,20},{8,24},{12,28},{16,0},{20,4},{24,8},{28,12},{1,17},{... | collective-permute-start | bytes 442376 | tf_op jit(solution)/shard_map/ppermute | solution.py:29
  35.1 2.7 %collective-permute-done.6 = bf16[96,768]{1,0:T(8,128)(2,1)S(1)} collective-permute-done((bf16[96,768]{1,0:T(8,128)(2,1)S(1)}, bf16[96,768]{1,0:T(8,128)(2,1)S(1)}, u32[]{:S(2)}, u32[]{:S(2)}) %collective-permute-start.6) | collective-permute-done | bytes 147488 | tf_op jit(solution)/shard_map/ppermute | solution.py:29
  37.9 7.2 %collective-permute-done.7 = bf16[96,768]{1,0:T(8,128)(2,1)S(1)} collective-permute-done((bf16[96,768]{1,0:T(8,128)(2,1)S(1)}, bf16[96,768]{1,0:T(8,128)(2,1)S(1)}, u32[]{:S(2)}, u32[]{:S(2)}) %collective-permute-start.7) | collective-permute-done | bytes 147488 | tf_op jit(solution)/shard_map/ppermute | solution.py:29
  45.9 2.8 %collective-permute-start.10 = (bf16[96,768]{1,0:T(8,128)(2,1)S(1)}, bf16[96,768]{1,0:T(8,128)(2,1)S(1)}, u32[]{:S(2)}, u32[]{:S(2)}) collective-permute-start(bf16[96,768]{1,0:T(8,128)(2,1)S(1)} %pad_maximum_fusion.6), channel_id=1, source_target_pairs={{0,8},{4,12},{8,0},{12,4},{16,24},{20,28},{24,16},{28,20},{1,9},{5... | collective-permute-start | bytes 442376 | tf_op jit(solution)/shard_map/ppermute | solution.py:29
  52.1 6.9 %collective-permute-done.17 = bf16[384,768]{1,0:T(8,128)(2,1)S(1)} collective-permute-done((bf16[384,768]{1,0:T(8,128)(2,1)S(1)}, bf16[384,768]{1,0:T(8,128)(2,1)S(1)}, u32[]{:S(2)}, u32[]{:S(2)}) %collective-permute-start.17) | collective-permute-done | bytes 589856 | tf_op jit(solution)/shard_map/ppermute | solution.py:29
  59.0 3.4 %collective-permute-done.11 = bf16[96,768]{1,0:T(8,128)(2,1)S(1)} collective-permute-done((bf16[96,768]{1,0:T(8,128)(2,1)S(1)}, bf16[96,768]{1,0:T(8,128)(2,1)S(1)}, u32[]{:S(2)}, u32[]{:S(2)}) %collective-permute-start.11) | collective-permute-done | bytes 147488 | tf_op jit(solution)/shard_map/ppermute | solution.py:29
  64.2 2.2 %collective-permute-start.15 = (bf16[96,768]{1,0:T(8,128)(2,1)S(1)}, bf16[96,768]{1,0:T(8,128)(2,1)S(1)}, u32[]{:S(2)}, u32[]{:S(2)}) collective-permute-start(bf16[96,768]{1,0:T(8,128)(2,1)S(1)} %pad_maximum_fusion.9), channel_id=1, source_target_pairs={{0,8},{4,12},{8,0},{12,4},{16,24},{20,28},{24,16},{28,20},{1,9},{5... | collective-permute-start | bytes 442376 | tf_op jit(solution)/shard_map/ppermute | solution.py:29
  68.9 9.4 %collective-permute-done.20 = bf16[384,768]{1,0:T(8,128)(2,1)S(1)} collective-permute-done((bf16[384,768]{1,0:T(8,128)(2,1)S(1)}, bf16[384,768]{1,0:T(8,128)(2,1)S(1)}, u32[]{:S(2)}, u32[]{:S(2)}) %collective-permute-start.20) | collective-permute-done | bytes 589856 | tf_op jit(solution)/shard_map/ppermute | solution.py:29
  78.4 1.9 %collective-permute-done.16 = bf16[96,768]{1,0:T(8,128)(2,1)S(1)} collective-permute-done((bf16[96,768]{1,0:T(8,128)(2,1)S(1)}, bf16[96,768]{1,0:T(8,128)(2,1)S(1)}, u32[]{:S(2)}, u32[]{:S(2)}) %collective-permute-start.16) | collective-permute-done | bytes 147488 | tf_op jit(solution)/shard_map/ppermute | solution.py:29
  81.1 2.1 %collective-permute-done.22.refs_8_ = bf16[768,768]{1,0:T(8,128)(2,1)S(1)} collective-permute-done((bf16[768,768]{1,0:T(8,128)(2,1)S(1)}, bf16[768,768]{1,0:T(8,128)(2,1)S(1)}, u32[]{:S(2)}, u32[]{:S(2)}) %collective-permute-start.22) | collective-permute-done | bytes 1179680 | tf_op jit(solution)/shard_map/ppermute | solution.py:29
  83.2 6.0 %gram_step.2 = (f32[384,128]{1,0:T(8,128)S(1)}, f32[384,128]{1,0:T(8,128)S(1)}, f32[384,128]{1,0:T(8,128)S(1)}, f32[1,1536]{1,0:T(1,128)S(1)}, f32[1,1536]{1,0:T(1,128)S(1)}, /*index=5*/f32[1,1536]{1,0:T(1,128)S(1)}) custom-call(bf16[384,768]{1,0:T(8,128)(2,1)S(1)} %get-tuple-element.137.refs_0_, bf16[384,768]{1,0:T(8,128)(2,1)S(1)} %get-tuple-element.63.refs_1_, ...), custom_call_target="tpu_custom_call" | custom-call | flops 8153726976 | bytes 8847360 | tf_op jit(solution)/shard_map/gram_step/pallas_call | solution.py:213
  89.8 4.2 %collective-permute-done.21 = bf16[304,768]{1,0:T(8,128)(2,1)S(1)} collective-permute-done((bf16[304,768]{1,0:T(8,128)(2,1)S(1)}, bf16[304,768]{1,0:T(8,128)(2,1)S(1)}, u32[]{:S(2)}, u32[]{:S(2)}) %collective-permute-start.21) | collective-permute-done | bytes 466976 | tf_op jit(solution)/shard_map/ppermute | solution.py:29
  94.0 2.2 %collective-permute-done.23 = bf16[80,768]{1,0:T(8,128)(2,1)S(1)} collective-permute-done((bf16[80,768]{1,0:T(8,128)(2,1)S(1)}, bf16[80,768]{1,0:T(8,128)(2,1)S(1)}, u32[]{:S(2)}, u32[]{:S(2)}) %collective-permute-start.23) | collective-permute-done | bytes 122912 | tf_op jit(solution)/shard_map/ppermute | solution.py:29
  96.4 2.4 %gram_step.3 = (f32[384,128]{1,0:T(8,128)S(1)}, f32[384,128]{1,0:T(8,128)S(1)}, f32[384,128]{1,0:T(8,128)S(1)}, f32[384,128]{1,0:T(8,128)S(1)}, f32[1,768]{1,0:T(1,128)S(1)}) custom-call(bf16[384,768]{1,0:T(8,128)(2,1)S(1)} %get-tuple-element.137.refs_0_, bf16[384,768]{1,0:T(8,128)(2,1)S(1)} %get-tuple-element.63.refs_1_, ...), custom_call_target="tpu_custom_call" | custom-call | flops 1811939328 | bytes 3538944 | tf_op jit(solution)/shard_map/gram_step/pallas_call | solution.py:213
  99.2 3.1 %gram_last.1 = f32[32,1,192]{2,1,0:T(1,128)S(1)} custom-call(s32[2]{0:T(128)S(1)} %pad_add_fusion.me_ref, bf16[384,768]{1,0:T(8,128)(2,1)S(1)} %get-tuple-element.137.refs_0_, bf16[384,768]{1,0:T(8,128)(2,1)S(1)} %get-tuple-element.63.refs_1_, bf16[384,768]{1,0:T(8,128)(2,1)S(1)} %get-tuple-element.66.refs_2_, ...), custom_call_target="tpu_custom_call" | custom-call | flops 1811939328 | bytes 3538944 | tf_op jit(solution)/shard_map/gram_last/pallas_call | solution.py:228
  102.3 11.8 %all_to_all.5.part_ref = f32[32,1,192]{2,1,0:T(1,128)} all-to-all(f32[32,1,192]{2,1,0:T(1,128)S(1)} %gram_last.1), channel_id=1, replica_groups=mesh['grp'=8,'blk'=4] {'grp','blk'}, dimensions={0} | all-to-all | bytes 49152 | tf_op jit(solution)/shard_map/all_to_all | solution.py:359
  114.0 2.3 %pick_rows.1 = f32[6,128]{1,0:T(8,128)} custom-call(s32[6,128]{1,0:T(8,128)} %bitcast.4, f32[32,1,192]{2,1,0:T(1,128)} %all_to_all.5.part_ref), custom_call_target="tpu_custom_call" | custom-call | tf_op jit(solution)/shard_map/pick_rows/pallas_call | solution.py:264
  (77 shorter events, 21.5 us)
Async XLA Ops:
  3.3 6.9 %collective-permute-start = (bf16[96,768]{1,0:T(8,128)(2,1)S(1)}, bf16[96,768]{1,0:T(8,128)(2,1)S(1)}, u32[]{:S(2)}, u32[]{:S(2)}) collective-permute-start(bf16[96,768]{1,0:T(8,128)(2,1)S(1)} %get-tuple-element.117), channel_id=1, source_target_pairs={{0,4},{4,0},{8,12},{12,8},{16,20},{20,16},{24,28},{28,24},{1,5},{5... | collective-permute-start | bytes 442376 | tf_op jit(solution)/shard_map/ppermute | solution.py:29
  9.0 5.4 %collective-permute-start.2 = (bf16[96,768]{1,0:T(8,128)(2,1)S(1)}, bf16[96,768]{1,0:T(8,128)(2,1)S(1)}, u32[]{:S(2)}, u32[]{:S(2)}) collective-permute-start(bf16[96,768]{1,0:T(8,128)(2,1)S(1)} %get-tuple-element.47), channel_id=1, source_target_pairs={{0,4},{4,0},{8,12},{12,8},{16,20},{20,16},{24,28},{28,24},{1,5},{5... | collective-permute-start | bytes 442376 | tf_op jit(solution)/shard_map/ppermute | solution.py:29
  10.2 10.3 %collective-permute-start.1 = (bf16[96,768]{1,0:T(8,128)(2,1)S(1)}, bf16[96,768]{1,0:T(8,128)(2,1)S(1)}, u32[]{:S(2)}, u32[]{:S(2)}) collective-permute-start(bf16[96,768]{1,0:T(8,128)(2,1)S(1)} %pad_maximum_fusion), channel_id=1, source_target_pairs={{0,8},{4,12},{8,0},{12,4},{16,24},{20,28},{24,16},{28,20},{1,9},{5... | collective-permute-start | bytes 442376 | tf_op jit(solution)/shard_map/ppermute | solution.py:29
  14.4 13.0 %collective-permute-start.3 = (bf16[96,768]{1,0:T(8,128)(2,1)S(1)}, bf16[96,768]{1,0:T(8,128)(2,1)S(1)}, u32[]{:S(2)}, u32[]{:S(2)}) collective-permute-start(bf16[96,768]{1,0:T(8,128)(2,1)S(1)} %pad_maximum_fusion.1), channel_id=1, source_target_pairs={{0,16},{4,20},{8,24},{12,28},{16,0},{20,4},{24,8},{28,12},{1,17},{... | collective-permute-start | bytes 442376 | tf_op jit(solution)/shard_map/ppermute | solution.py:29
  17.1 10.3 %collective-permute-start.4 = (bf16[96,768]{1,0:T(8,128)(2,1)S(1)}, bf16[96,768]{1,0:T(8,128)(2,1)S(1)}, u32[]{:S(2)}, u32[]{:S(2)}) collective-permute-start(bf16[96,768]{1,0:T(8,128)(2,1)S(1)} %pad_maximum_fusion.2), channel_id=1, source_target_pairs={{0,24},{4,28},{8,16},{12,20},{16,8},{20,12},{24,0},{28,4},{1,25},{... | collective-permute-start | bytes 442376 | tf_op jit(solution)/shard_map/ppermute | solution.py:29
  18.5 10.5 %collective-permute-start.5 = (bf16[192,768]{1,0:T(8,128)(2,1)S(1)}, bf16[192,768]{1,0:T(8,128)(2,1)S(1)}, u32[]{:S(2)}, u32[]{:S(2)}) collective-permute-start(bf16[192,768]{1,0:T(8,128)(2,1)S(1)} %get-tuple-element.50), channel_id=1, source_target_pairs={{0,4},{4,0},{8,12},{12,8},{16,20},{20,16},{24,28},{28,24},{1,5},{5... | collective-permute-start | bytes 884744 | tf_op jit(solution)/shard_map/ppermute | solution.py:29
  19.2 26.6 %collective-permute-start.9 = (bf16[384,768]{1,0:T(8,128)(2,1)S(1)}, bf16[384,768]{1,0:T(8,128)(2,1)S(1)}, u32[]{:S(2)}, u32[]{:S(2)}) collective-permute-start(bf16[384,768]{1,0:T(8,128)(2,1)S(1)} %get-tuple-element.55), channel_id=1, source_target_pairs={{0,4},{4,0},{8,12},{12,8},{16,20},{20,16},{24,28},{28,24},{1,5},{5... | collective-permute-start | bytes 1769480 | tf_op jit(solution)/shard_map/ppermute | solution.py:29
  27.4 17.8 %collective-permute-start.12 = (bf16[384,768]{1,0:T(8,128)(2,1)S(1)}, bf16[384,768]{1,0:T(8,128)(2,1)S(1)}, u32[]{:S(2)}, u32[]{:S(2)}) collective-permute-start(bf16[384,768]{1,0:T(8,128)(2,1)S(1)} %get-tuple-element.137.refs_0_), channel_id=1, source_target_pairs={{0,2},{1,3},{2,0},{3,1},{4,6},{5,7},{6,4},{7,5},{8,10},{9,11},{10,... | collective-permute-start | bytes 1769480 | tf_op jit(solution)/shard_map/ppermute | solution.py:29
  29.0 8.9 %collective-permute-start.6 = (bf16[96,768]{1,0:T(8,128)(2,1)S(1)}, bf16[96,768]{1,0:T(8,128)(2,1)S(1)}, u32[]{:S(2)}, u32[]{:S(2)}) collective-permute-start(bf16[96,768]{1,0:T(8,128)(2,1)S(1)} %pad_maximum_fusion.3), channel_id=1, source_target_pairs={{0,8},{4,12},{8,0},{12,4},{16,24},{20,28},{24,16},{28,20},{1,9},{5... | collective-permute-start | bytes 442376 | tf_op jit(solution)/shard_map/ppermute | solution.py:29
  31.6 13.5 %collective-permute-start.7 = (bf16[96,768]{1,0:T(8,128)(2,1)S(1)}, bf16[96,768]{1,0:T(8,128)(2,1)S(1)}, u32[]{:S(2)}, u32[]{:S(2)}) collective-permute-start(bf16[96,768]{1,0:T(8,128)(2,1)S(1)} %pad_maximum_fusion.4), channel_id=1, source_target_pairs={{0,16},{4,20},{8,24},{12,28},{16,0},{20,4},{24,8},{28,12},{1,17},{... | collective-permute-start | bytes 442376 | tf_op jit(solution)/shard_map/ppermute | solution.py:29
  33.6 11.5 %collective-permute-start.8 = (bf16[96,768]{1,0:T(8,128)(2,1)S(1)}, bf16[96,768]{1,0:T(8,128)(2,1)S(1)}, u32[]{:S(2)}, u32[]{:S(2)}) collective-permute-start(bf16[96,768]{1,0:T(8,128)(2,1)S(1)} %pad_maximum_fusion.5), channel_id=1, source_target_pairs={{0,24},{4,28},{8,16},{12,20},{16,8},{20,12},{24,0},{28,4},{1,25},{... | collective-permute-start | bytes 442376 | tf_op jit(solution)/shard_map/ppermute | solution.py:29
  45.2 13.8 %collective-permute-start.17 = (bf16[384,768]{1,0:T(8,128)(2,1)S(1)}, bf16[384,768]{1,0:T(8,128)(2,1)S(1)}, u32[]{:S(2)}, u32[]{:S(2)}) collective-permute-start(bf16[384,768]{1,0:T(8,128)(2,1)S(1)} %get-tuple-element.63.refs_1_), channel_id=1, source_target_pairs={{0,2},{1,3},{2,0},{3,1},{4,6},{5,7},{6,4},{7,5},{8,10},{9,11},{10,... | collective-permute-start | bytes 1769480 | tf_op jit(solution)/shard_map/ppermute | solution.py:29
  45.9 13.2 %collective-permute-start.10 = (bf16[96,768]{1,0:T(8,128)(2,1)S(1)}, bf16[96,768]{1,0:T(8,128)(2,1)S(1)}, u32[]{:S(2)}, u32[]{:S(2)}) collective-permute-start(bf16[96,768]{1,0:T(8,128)(2,1)S(1)} %pad_maximum_fusion.6), channel_id=1, source_target_pairs={{0,8},{4,12},{8,0},{12,4},{16,24},{20,28},{24,16},{28,20},{1,9},{5... | collective-permute-start | bytes 442376 | tf_op jit(solution)/shard_map/ppermute | solution.py:29
  48.7 13.8 %collective-permute-start.11 = (bf16[96,768]{1,0:T(8,128)(2,1)S(1)}, bf16[96,768]{1,0:T(8,128)(2,1)S(1)}, u32[]{:S(2)}, u32[]{:S(2)}) collective-permute-start(bf16[96,768]{1,0:T(8,128)(2,1)S(1)} %pad_maximum_fusion.7), channel_id=1, source_target_pairs={{0,16},{4,20},{8,24},{12,28},{16,0},{20,4},{24,8},{28,12},{1,17},{... | collective-permute-start | bytes 442376 | tf_op jit(solution)/shard_map/ppermute | solution.py:29
  50.5 12.0 %collective-permute-start.13 = (bf16[96,768]{1,0:T(8,128)(2,1)S(1)}, bf16[96,768]{1,0:T(8,128)(2,1)S(1)}, u32[]{:S(2)}, u32[]{:S(2)}) collective-permute-start(bf16[96,768]{1,0:T(8,128)(2,1)S(1)} %pad_maximum_fusion.8), channel_id=1, source_target_pairs={{0,24},{4,28},{8,16},{12,20},{16,8},{20,12},{24,0},{28,4},{1,25},{... | collective-permute-start | bytes 442376 | tf_op jit(solution)/shard_map/ppermute | solution.py:29
  52.0 12.1 %collective-permute-start.14 = (bf16[768,768]{1,0:T(8,128)(2,1)S(1)}, bf16[768,768]{1,0:T(8,128)(2,1)S(1)}, u32[]{:S(2)}, u32[]{:S(2)}) collective-permute-start(bf16[768,768]{1,0:T(8,128)(2,1)S(1)} %constant_dynamic-update-slice_fusion.15.refs_3_), channel_id=1, source_target_pairs={{0,1},{1,0},{2,3},{3,2},{4,5},{5,4},{6,7},{7,6},{8,9},{9,8},{10,11... | collective-permute-start | bytes 3538952 | tf_op jit(solution)/shard_map/ppermute | solution.py:29
  62.5 5.1 %collective-permute-start.18 = (bf16[768,768]{1,0:T(8,128)(2,1)S(1)}, bf16[768,768]{1,0:T(8,128)(2,1)S(1)}, u32[]{:S(2)}, u32[]{:S(2)}) collective-permute-start(bf16[768,768]{1,0:T(8,128)(2,1)S(1)} %constant_dynamic-update-slice_fusion.21.refs_5_), channel_id=1, source_target_pairs={{0,1},{1,0},{2,3},{3,2},{4,5},{5,4},{6,7},{7,6},{8,9},{9,8},{10,11... | collective-permute-start | bytes 3538952 | tf_op jit(solution)/shard_map/ppermute | solution.py:29
  62.6 15.8 %collective-permute-start.20 = (bf16[384,768]{1,0:T(8,128)(2,1)S(1)}, bf16[384,768]{1,0:T(8,128)(2,1)S(1)}, u32[]{:S(2)}, u32[]{:S(2)}) collective-permute-start(bf16[384,768]{1,0:T(8,128)(2,1)S(1)} %get-tuple-element.66.refs_2_), channel_id=1, source_target_pairs={{0,2},{1,3},{2,0},{3,1},{4,6},{5,7},{6,4},{7,5},{8,10},{9,11},{10,... | collective-permute-start | bytes 1769480 | tf_op jit(solution)/shard_map/ppermute | solution.py:29
  64.2 14.2 %collective-permute-start.15 = (bf16[96,768]{1,0:T(8,128)(2,1)S(1)}, bf16[96,768]{1,0:T(8,128)(2,1)S(1)}, u32[]{:S(2)}, u32[]{:S(2)}) collective-permute-start(bf16[96,768]{1,0:T(8,128)(2,1)S(1)} %pad_maximum_fusion.9), channel_id=1, source_target_pairs={{0,8},{4,12},{8,0},{12,4},{16,24},{20,28},{24,16},{28,20},{1,9},{5... | collective-permute-start | bytes 442376 | tf_op jit(solution)/shard_map/ppermute | solution.py:29
  66.4 13.9 %collective-permute-start.16 = (bf16[96,768]{1,0:T(8,128)(2,1)S(1)}, bf16[96,768]{1,0:T(8,128)(2,1)S(1)}, u32[]{:S(2)}, u32[]{:S(2)}) collective-permute-start(bf16[96,768]{1,0:T(8,128)(2,1)S(1)} %pad_maximum_fusion.10), channel_id=1, source_target_pairs={{0,16},{4,20},{8,24},{12,28},{16,0},{20,4},{24,8},{28,12},{1,17},{... | collective-permute-start | bytes 442376 | tf_op jit(solution)/shard_map/ppermute | solution.py:29
  67.5 12.8 %collective-permute-start.19 = (bf16[96,768]{1,0:T(8,128)(2,1)S(1)}, bf16[96,768]{1,0:T(8,128)(2,1)S(1)}, u32[]{:S(2)}, u32[]{:S(2)}) collective-permute-start(bf16[96,768]{1,0:T(8,128)(2,1)S(1)} %pad_maximum_fusion.11), channel_id=1, source_target_pairs={{0,24},{4,28},{8,16},{12,20},{16,8},{20,12},{24,0},{28,4},{1,25},{... | collective-permute-start | bytes 442376 | tf_op jit(solution)/shard_map/ppermute | solution.py:29
  80.5 13.6 %collective-permute-start.21 = (bf16[304,768]{1,0:T(8,128)(2,1)S(1)}, bf16[304,768]{1,0:T(8,128)(2,1)S(1)}, u32[]{:S(2)}, u32[]{:S(2)}) collective-permute-start(bf16[304,768]{1,0:T(8,128)(2,1)S(1)} %slice.168), channel_id=1, source_target_pairs={{0,2},{1,3},{2,0},{3,1},{4,6},{5,7},{6,4},{7,5},{8,10},{9,11},{10,... | collective-permute-start | bytes 1400840 | tf_op jit(solution)/shard_map/ppermute | solution.py:29
  89.2 7.1 %collective-permute-start.23 = (bf16[80,768]{1,0:T(8,128)(2,1)S(1)}, bf16[80,768]{1,0:T(8,128)(2,1)S(1)}, u32[]{:S(2)}, u32[]{:S(2)}) collective-permute-start(bf16[80,768]{1,0:T(8,128)(2,1)S(1)} %slice.169), channel_id=1, source_target_pairs={{0,2},{1,3},{2,0},{3,1},{4,6},{5,7},{6,4},{7,5},{8,10},{9,11},{10,... | collective-permute-start | bytes 368648 | tf_op jit(solution)/shard_map/ppermute | solution.py:29
  96.3 2.9 %collective-permute-start.24 = (bf16[768,768]{1,0:T(8,128)(2,1)S(1)}, bf16[768,768]{1,0:T(8,128)(2,1)S(1)}, u32[]{:S(2)}, u32[]{:S(2)}) collective-permute-start(bf16[768,768]{1,0:T(8,128)(2,1)S(1)} %constant_dynamic-update-slice_fusion.38.refs_4_), channel_id=1, source_target_pairs={{0,1},{1,0},{2,3},{3,2},{4,5},{5,4},{6,7},{7,6},{8,9},{9,8},{10,11... | collective-permute-start | bytes 3538952 | tf_op jit(solution)/shard_map/ppermute | solution.py:29
  (3 other events, 4.8 us)

commit v16 on v15

--- a/solution.py
+++ b/solution.py
@@ -305,8 +305,8 @@
         early = [("z", step - 1, z)] if step >= 1 else []
         if step >= 2 and z == far[-1]:
             early += [("x", step - 2, 0)]
-        if step == last and step >= 3:
-            early += [("c", step - 2 if z == far[-1] else step - 3)]
+        if step >= 2 and z == 1:
+            early += [("c", step - 2)]
         send(("z", step, z), block(step, z), "grp", groups, 2 * z, *early)
 
     def collect(step):

time: 117 us -> 114 us (0.974)
  starting transfers between devices: 33.1 us -> 29.5 us
  waiting for transfers between devices: 50.6 us -> 52 us
    ppermute x25, starting transfers between devices: 33.1 us -> 29.5 us  [swap(): return lax.ppermute(value, axis, [(i, i ^ bit) for i in range(size)])]
    ppermute x25, waiting for transfers between devices: 50.6 us -> 52 us  [swap(): return lax.ppermute(value, axis, [(i, i ^ bit) for i in range(size)])]
  transfers between devices with their start and end apart: 25 -> 25, of which waited for: 13 -> 15; matrix products, arithmetic and copies ran while one was open for 1% -> 1% of each run, Pallas kernels for 10% -> 10%
where the time goes in v16:
time: 114 us
  waiting for transfers between devices  52 us (46%)
  starting transfers between devices  29.5 us (26%)
  Pallas kernels  17.7 us (16%)
  blocking collectives  11.2 us (10%)
  local copies, waits for them, and re-layouts  2.63 us (2%)
    ppermute x25, waiting for transfers between devices, swap(): return lax.ppermute(value, axis, [(i, i ^ bit) for i in range(size)])  52 us
    ppermute x25, starting transfers between devices, swap(): return lax.ppermute(value, axis, [(i, i ^ bit) for i in range(size)])  29.5 us
    all_to_all x1, blocking collectives, on_device(): homeward = lax.all_to_all(result, ('grp', 'blk'), 0, 0, tiled=True)  11.2 us
    pallas_call x2, Pallas kernels, gram_step(): pl.pallas_call(functools.partial(gram_kernel, first, step, pieces), in_sp...  8.45 us
    pallas_call x1, Pallas kernels, gram_last(): pl.pallas_call(functools.partial(gram_last_kernel, step, relatives, chunk...  3.08 us
    pallas_call x1, Pallas kernels, head(): pl.pallas_call(functools.partial(rest_kernel, capacity, chunks, groups),...  2.61 us
    unnamed x23, local copies, waits for them, and re-layouts  2.43 us
    pallas_call x1, Pallas kernels, tail(): pl.pallas_call(functools.partial(tail_kernel, capacity, members), in_spec...  2.33 us
  transfers between devices with their start and end apart: 25, of which 15 were waited for; matrix products, arithmetic and copies ran while one was open for 1% of the time, Pallas kernels for 10%

profile of v16, /device:TPU:0, one launch (start us, length us, event | category | flops | bytes accessed | tf_op | source)
XLA Modules:
  0.0 113.7 jit_solution(2712645099925872485)
XLA Ops:
  3.3 3.0 %collective-permute-start = (bf16[96,768]{1,0:T(8,128)(2,1)S(1)}, bf16[96,768]{1,0:T(8,128)(2,1)S(1)}, u32[]{:S(2)}, u32[]{:S(2)}) collective-permute-start(bf16[96,768]{1,0:T(8,128)(2,1)S(1)} %get-tuple-element.117), channel_id=1, source_target_pairs={{0,4},{4,0},{8,12},{12,8},{16,20},{20,16},{24,28},{28,24},{1,5},{5... | collective-permute-start | bytes 442376 | tf_op jit(solution)/shard_map/ppermute | solution.py:29
  6.4 2.6 %place_rest.1 = (bf16[192,768]{1,0:T(8,128)(2,1)S(1)}, bf16[192,768]{1,0:T(8,128)(2,1)S(1)}, bf16[192,768]{1,0:T(8,128)(2,1)S(1)}, bf16[192,768]{1,0:T(8,128)(2,...) custom-call(s32[2]{0:T(128)S(1)} %pad_add_fusion.me_ref, s32[6,128]{1,0:T(8,128)S(1)} %bitcast.6, ...), custom_call_target="tpu_custom_call" | custom-call | flops 1585446912 | bytes 3244032 | tf_op jit(solution)/shard_map/place_rest/pallas_call | solution.py:101
  10.2 1.9 %collective-permute-start.1 = (bf16[96,768]{1,0:T(8,128)(2,1)S(1)}, bf16[96,768]{1,0:T(8,128)(2,1)S(1)}, u32[]{:S(2)}, u32[]{:S(2)}) collective-permute-start(bf16[96,768]{1,0:T(8,128)(2,1)S(1)} %pad_maximum_fusion), channel_id=1, source_target_pairs={{0,8},{4,12},{8,0},{12,4},{16,24},{20,28},{24,16},{28,20},{1,9},{5... | collective-permute-start | bytes 442376 | tf_op jit(solution)/shard_map/ppermute | solution.py:29
  12.1 2.2 %collective-permute-done.2 = bf16[96,768]{1,0:T(8,128)(2,1)S(1)} collective-permute-done((bf16[96,768]{1,0:T(8,128)(2,1)S(1)}, bf16[96,768]{1,0:T(8,128)(2,1)S(1)}, u32[]{:S(2)}, u32[]{:S(2)}) %collective-permute-start.2) | collective-permute-done | bytes 147488 | tf_op jit(solution)/shard_map/ppermute | solution.py:29
  14.4 2.7 %collective-permute-start.3 = (bf16[96,768]{1,0:T(8,128)(2,1)S(1)}, bf16[96,768]{1,0:T(8,128)(2,1)S(1)}, u32[]{:S(2)}, u32[]{:S(2)}) collective-permute-start(bf16[96,768]{1,0:T(8,128)(2,1)S(1)} %pad_maximum_fusion.1), channel_id=1, source_target_pairs={{0,16},{4,20},{8,24},{12,28},{16,0},{20,4},{24,8},{28,12},{1,17},{... | collective-permute-start | bytes 442376 | tf_op jit(solution)/shard_map/ppermute | solution.py:29
  19.2 8.1 %collective-permute-done.3 = bf16[96,768]{1,0:T(8,128)(2,1)S(1)} collective-permute-done((bf16[96,768]{1,0:T(8,128)(2,1)S(1)}, bf16[96,768]{1,0:T(8,128)(2,1)S(1)}, u32[]{:S(2)}, u32[]{:S(2)}) %collective-permute-start.3) | collective-permute-done | bytes 147488 | tf_op jit(solution)/shard_map/ppermute | solution.py:29
  27.4 1.6 %collective-permute-start.10 = (bf16[384,768]{1,0:T(8,128)(2,1)S(1)}, bf16[384,768]{1,0:T(8,128)(2,1)S(1)}, u32[]{:S(2)}, u32[]{:S(2)}) collective-permute-start(bf16[384,768]{1,0:T(8,128)(2,1)S(1)} %get-tuple-element.137.refs_0_), channel_id=1, source_target_pairs={{0,2},{1,3},{2,0},{3,1},{4,6},{5,7},{6,4},{7,5},{8,10},{9,11},{10,... | collective-permute-start | bytes 1769480 | tf_op jit(solution)/shard_map/ppermute | solution.py:29
  29.0 2.4 %collective-permute-start.8 = (bf16[96,768]{1,0:T(8,128)(2,1)S(1)}, bf16[96,768]{1,0:T(8,128)(2,1)S(1)}, u32[]{:S(2)}, u32[]{:S(2)}) collective-permute-start(bf16[96,768]{1,0:T(8,128)(2,1)S(1)} %pad_maximum_fusion.5), channel_id=1, source_target_pairs={{0,24},{4,28},{8,16},{12,20},{16,8},{20,12},{24,0},{28,4},{1,25},{... | collective-permute-start | bytes 442376 | tf_op jit(solution)/shard_map/ppermute | solution.py:29
  31.4 2.2 %collective-permute-start.7 = (bf16[96,768]{1,0:T(8,128)(2,1)S(1)}, bf16[96,768]{1,0:T(8,128)(2,1)S(1)}, u32[]{:S(2)}, u32[]{:S(2)}) collective-permute-start(bf16[96,768]{1,0:T(8,128)(2,1)S(1)} %pad_maximum_fusion.4), channel_id=1, source_target_pairs={{0,16},{4,20},{8,24},{12,28},{16,0},{20,4},{24,8},{28,12},{1,17},{... | collective-permute-start | bytes 442376 | tf_op jit(solution)/shard_map/ppermute | solution.py:29
  35.3 5.0 %collective-permute-done.10 = bf16[384,768]{1,0:T(8,128)(2,1)S(1)} collective-permute-done((bf16[384,768]{1,0:T(8,128)(2,1)S(1)}, bf16[384,768]{1,0:T(8,128)(2,1)S(1)}, u32[]{:S(2)}, u32[]{:S(2)}) %collective-permute-start.10) | collective-permute-done | bytes 589856 | tf_op jit(solution)/shard_map/ppermute | solution.py:29
  40.3 4.8 %collective-permute-done.7 = bf16[96,768]{1,0:T(8,128)(2,1)S(1)} collective-permute-done((bf16[96,768]{1,0:T(8,128)(2,1)S(1)}, bf16[96,768]{1,0:T(8,128)(2,1)S(1)}, u32[]{:S(2)}, u32[]{:S(2)}) %collective-permute-start.7) | collective-permute-done | bytes 147488 | tf_op jit(solution)/shard_map/ppermute | solution.py:29
  45.9 2.8 %collective-permute-done.9 = bf16[384,768]{1,0:T(8,128)(2,1)S(1)} collective-permute-done((bf16[384,768]{1,0:T(8,128)(2,1)S(1)}, bf16[384,768]{1,0:T(8,128)(2,1)S(1)}, u32[]{:S(2)}, u32[]{:S(2)}) %collective-permute-start.9) | collective-permute-done | bytes 589856 | tf_op jit(solution)/shard_map/ppermute | solution.py:29
  48.7 2.7 %collective-permute-start.13 = (bf16[96,768]{1,0:T(8,128)(2,1)S(1)}, bf16[96,768]{1,0:T(8,128)(2,1)S(1)}, u32[]{:S(2)}, u32[]{:S(2)}) collective-permute-start(bf16[96,768]{1,0:T(8,128)(2,1)S(1)} %pad_maximum_fusion.7), channel_id=1, source_target_pairs={{0,16},{4,20},{8,24},{12,28},{16,0},{20,4},{24,8},{28,12},{1,17},{... | collective-permute-start | bytes 442376 | tf_op jit(solution)/shard_map/ppermute | solution.py:29
  52.7 8.4 %collective-permute-done.15 = bf16[384,768]{1,0:T(8,128)(2,1)S(1)} collective-permute-done((bf16[384,768]{1,0:T(8,128)(2,1)S(1)}, bf16[384,768]{1,0:T(8,128)(2,1)S(1)}, u32[]{:S(2)}, u32[]{:S(2)}) %collective-permute-start.15) | collective-permute-done | bytes 589856 | tf_op jit(solution)/shard_map/ppermute | solution.py:29
  62.4 3.8 %collective-permute-start.18 = (bf16[96,768]{1,0:T(8,128)(2,1)S(1)}, bf16[96,768]{1,0:T(8,128)(2,1)S(1)}, u32[]{:S(2)}, u32[]{:S(2)}) collective-permute-start(bf16[96,768]{1,0:T(8,128)(2,1)S(1)} %pad_maximum_fusion.10), channel_id=1, source_target_pairs={{0,16},{4,20},{8,24},{12,28},{16,0},{20,4},{24,8},{28,12},{1,17},{... | collective-permute-start | bytes 442376 | tf_op jit(solution)/shard_map/ppermute | solution.py:29
  67.2 10.2 %collective-permute-done.20 = bf16[384,768]{1,0:T(8,128)(2,1)S(1)} collective-permute-done((bf16[384,768]{1,0:T(8,128)(2,1)S(1)}, bf16[384,768]{1,0:T(8,128)(2,1)S(1)}, u32[]{:S(2)}, u32[]{:S(2)}) %collective-permute-start.20) | collective-permute-done | bytes 589856 | tf_op jit(solution)/shard_map/ppermute | solution.py:29
  79.2 1.8 %collective-permute-done.22.refs_8_ = bf16[768,768]{1,0:T(8,128)(2,1)S(1)} collective-permute-done((bf16[768,768]{1,0:T(8,128)(2,1)S(1)}, bf16[768,768]{1,0:T(8,128)(2,1)S(1)}, u32[]{:S(2)}, u32[]{:S(2)}) %collective-permute-start.22) | collective-permute-done | bytes 1179680 | tf_op jit(solution)/shard_map/ppermute | solution.py:29
  81.0 6.0 %gram_step.2 = (f32[384,128]{1,0:T(8,128)S(1)}, f32[384,128]{1,0:T(8,128)S(1)}, f32[384,128]{1,0:T(8,128)S(1)}, f32[1,1536]{1,0:T(1,128)S(1)}, f32[1,1536]{1,0:T(1,128)S(1)}, /*index=5*/f32[1,1536]{1,0:T(1,128)S(1)}) custom-call(bf16[384,768]{1,0:T(8,128)(2,1)S(1)} %get-tuple-element.137.refs_0_, bf16[384,768]{1,0:T(8,128)(2,1)S(1)} %get-tuple-element.61.refs_1_, ...), custom_call_target="tpu_custom_call" | custom-call | flops 8153726976 | bytes 8847360 | tf_op jit(solution)/shard_map/gram_step/pallas_call | solution.py:213
  87.9 3.9 %collective-permute-done.21 = bf16[304,768]{1,0:T(8,128)(2,1)S(1)} collective-permute-done((bf16[304,768]{1,0:T(8,128)(2,1)S(1)}, bf16[304,768]{1,0:T(8,128)(2,1)S(1)}, u32[]{:S(2)}, u32[]{:S(2)}) %collective-permute-start.21) | collective-permute-done | bytes 466976 | tf_op jit(solution)/shard_map/ppermute | solution.py:29
  91.9 2.2 %collective-permute-done.23 = bf16[80,768]{1,0:T(8,128)(2,1)S(1)} collective-permute-done((bf16[80,768]{1,0:T(8,128)(2,1)S(1)}, bf16[80,768]{1,0:T(8,128)(2,1)S(1)}, u32[]{:S(2)}, u32[]{:S(2)}) %collective-permute-start.23) | collective-permute-done | bytes 122912 | tf_op jit(solution)/shard_map/ppermute | solution.py:29
  94.2 2.4 %gram_step.3 = (f32[384,128]{1,0:T(8,128)S(1)}, f32[384,128]{1,0:T(8,128)S(1)}, f32[384,128]{1,0:T(8,128)S(1)}, f32[384,128]{1,0:T(8,128)S(1)}, f32[1,768]{1,0:T(1,128)S(1)}) custom-call(bf16[384,768]{1,0:T(8,128)(2,1)S(1)} %get-tuple-element.137.refs_0_, bf16[384,768]{1,0:T(8,128)(2,1)S(1)} %get-tuple-element.61.refs_1_, ...), custom_call_target="tpu_custom_call" | custom-call | flops 1811939328 | bytes 3538944 | tf_op jit(solution)/shard_map/gram_step/pallas_call | solution.py:213
  97.0 3.1 %gram_last.1 = f32[32,1,192]{2,1,0:T(1,128)S(1)} custom-call(s32[2]{0:T(128)S(1)} %pad_add_fusion.me_ref, bf16[384,768]{1,0:T(8,128)(2,1)S(1)} %get-tuple-element.137.refs_0_, bf16[384,768]{1,0:T(8,128)(2,1)S(1)} %get-tuple-element.61.refs_1_, bf16[384,768]{1,0:T(8,128)(2,1)S(1)} %get-tuple-element.66.refs_2_, ...), custom_call_target="tpu_custom_call" | custom-call | flops 1811939328 | bytes 3538944 | tf_op jit(solution)/shard_map/gram_last/pallas_call | solution.py:228
  100.1 11.2 %all_to_all.5.part_ref = f32[32,1,192]{2,1,0:T(1,128)} all-to-all(f32[32,1,192]{2,1,0:T(1,128)S(1)} %gram_last.1), channel_id=1, replica_groups=mesh['grp'=8,'blk'=4] {'grp','blk'}, dimensions={0} | all-to-all | bytes 49152 | tf_op jit(solution)/shard_map/all_to_all | solution.py:359
  111.3 2.3 %pick_rows.1 = f32[6,128]{1,0:T(8,128)} custom-call(s32[6,128]{1,0:T(8,128)} %bitcast.4, f32[32,1,192]{2,1,0:T(1,128)} %all_to_all.5.part_ref), custom_call_target="tpu_custom_call" | custom-call | tf_op jit(solution)/shard_map/pick_rows/pallas_call | solution.py:264
  (77 shorter events, 16.0 us)
Async XLA Ops:
  3.3 6.9 %collective-permute-start = (bf16[96,768]{1,0:T(8,128)(2,1)S(1)}, bf16[96,768]{1,0:T(8,128)(2,1)S(1)}, u32[]{:S(2)}, u32[]{:S(2)}) collective-permute-start(bf16[96,768]{1,0:T(8,128)(2,1)S(1)} %get-tuple-element.117), channel_id=1, source_target_pairs={{0,4},{4,0},{8,12},{12,8},{16,20},{20,16},{24,28},{28,24},{1,5},{5... | collective-permute-start | bytes 442376 | tf_op jit(solution)/shard_map/ppermute | solution.py:29
  9.0 5.4 %collective-permute-start.2 = (bf16[96,768]{1,0:T(8,128)(2,1)S(1)}, bf16[96,768]{1,0:T(8,128)(2,1)S(1)}, u32[]{:S(2)}, u32[]{:S(2)}) collective-permute-start(bf16[96,768]{1,0:T(8,128)(2,1)S(1)} %get-tuple-element.47), channel_id=1, source_target_pairs={{0,4},{4,0},{8,12},{12,8},{16,20},{20,16},{24,28},{28,24},{1,5},{5... | collective-permute-start | bytes 442376 | tf_op jit(solution)/shard_map/ppermute | solution.py:29
  10.2 9.0 %collective-permute-start.1 = (bf16[96,768]{1,0:T(8,128)(2,1)S(1)}, bf16[96,768]{1,0:T(8,128)(2,1)S(1)}, u32[]{:S(2)}, u32[]{:S(2)}) collective-permute-start(bf16[96,768]{1,0:T(8,128)(2,1)S(1)} %pad_maximum_fusion), channel_id=1, source_target_pairs={{0,8},{4,12},{8,0},{12,4},{16,24},{20,28},{24,16},{28,20},{1,9},{5... | collective-permute-start | bytes 442376 | tf_op jit(solution)/shard_map/ppermute | solution.py:29
  14.4 13.0 %collective-permute-start.3 = (bf16[96,768]{1,0:T(8,128)(2,1)S(1)}, bf16[96,768]{1,0:T(8,128)(2,1)S(1)}, u32[]{:S(2)}, u32[]{:S(2)}) collective-permute-start(bf16[96,768]{1,0:T(8,128)(2,1)S(1)} %pad_maximum_fusion.1), channel_id=1, source_target_pairs={{0,16},{4,20},{8,24},{12,28},{16,0},{20,4},{24,8},{28,12},{1,17},{... | collective-permute-start | bytes 442376 | tf_op jit(solution)/shard_map/ppermute | solution.py:29
  17.1 10.3 %collective-permute-start.4 = (bf16[96,768]{1,0:T(8,128)(2,1)S(1)}, bf16[96,768]{1,0:T(8,128)(2,1)S(1)}, u32[]{:S(2)}, u32[]{:S(2)}) collective-permute-start(bf16[96,768]{1,0:T(8,128)(2,1)S(1)} %pad_maximum_fusion.2), channel_id=1, source_target_pairs={{0,24},{4,28},{8,16},{12,20},{16,8},{20,12},{24,0},{28,4},{1,25},{... | collective-permute-start | bytes 442376 | tf_op jit(solution)/shard_map/ppermute | solution.py:29
  18.5 10.5 %collective-permute-start.5 = (bf16[192,768]{1,0:T(8,128)(2,1)S(1)}, bf16[192,768]{1,0:T(8,128)(2,1)S(1)}, u32[]{:S(2)}, u32[]{:S(2)}) collective-permute-start(bf16[192,768]{1,0:T(8,128)(2,1)S(1)} %get-tuple-element.50), channel_id=1, source_target_pairs={{0,4},{4,0},{8,12},{12,8},{16,20},{20,16},{24,28},{28,24},{1,5},{5... | collective-permute-start | bytes 884744 | tf_op jit(solution)/shard_map/ppermute | solution.py:29
  27.4 12.9 %collective-permute-start.10 = (bf16[384,768]{1,0:T(8,128)(2,1)S(1)}, bf16[384,768]{1,0:T(8,128)(2,1)S(1)}, u32[]{:S(2)}, u32[]{:S(2)}) collective-permute-start(bf16[384,768]{1,0:T(8,128)(2,1)S(1)} %get-tuple-element.137.refs_0_), channel_id=1, source_target_pairs={{0,2},{1,3},{2,0},{3,1},{4,6},{5,7},{6,4},{7,5},{8,10},{9,11},{10,... | collective-permute-start | bytes 1769480 | tf_op jit(solution)/shard_map/ppermute | solution.py:29
  29.0 11.3 %collective-permute-start.8 = (bf16[96,768]{1,0:T(8,128)(2,1)S(1)}, bf16[96,768]{1,0:T(8,128)(2,1)S(1)}, u32[]{:S(2)}, u32[]{:S(2)}) collective-permute-start(bf16[96,768]{1,0:T(8,128)(2,1)S(1)} %pad_maximum_fusion.5), channel_id=1, source_target_pairs={{0,24},{4,28},{8,16},{12,20},{16,8},{20,12},{24,0},{28,4},{1,25},{... | collective-permute-start | bytes 442376 | tf_op jit(solution)/shard_map/ppermute | solution.py:29
  31.4 13.8 %collective-permute-start.7 = (bf16[96,768]{1,0:T(8,128)(2,1)S(1)}, bf16[96,768]{1,0:T(8,128)(2,1)S(1)}, u32[]{:S(2)}, u32[]{:S(2)}) collective-permute-start(bf16[96,768]{1,0:T(8,128)(2,1)S(1)} %pad_maximum_fusion.4), channel_id=1, source_target_pairs={{0,16},{4,20},{8,24},{12,28},{16,0},{20,4},{24,8},{28,12},{1,17},{... | collective-permute-start | bytes 442376 | tf_op jit(solution)/shard_map/ppermute | solution.py:29
  33.6 11.5 %collective-permute-start.6 = (bf16[96,768]{1,0:T(8,128)(2,1)S(1)}, bf16[96,768]{1,0:T(8,128)(2,1)S(1)}, u32[]{:S(2)}, u32[]{:S(2)}) collective-permute-start(bf16[96,768]{1,0:T(8,128)(2,1)S(1)} %pad_maximum_fusion.3), channel_id=1, source_target_pairs={{0,8},{4,12},{8,0},{12,4},{16,24},{20,28},{24,16},{28,20},{1,9},{5... | collective-permute-start | bytes 442376 | tf_op jit(solution)/shard_map/ppermute | solution.py:29
  34.3 14.4 %collective-permute-start.9 = (bf16[384,768]{1,0:T(8,128)(2,1)S(1)}, bf16[384,768]{1,0:T(8,128)(2,1)S(1)}, u32[]{:S(2)}, u32[]{:S(2)}) collective-permute-start(bf16[384,768]{1,0:T(8,128)(2,1)S(1)} %get-tuple-element.55), channel_id=1, source_target_pairs={{0,4},{4,0},{8,12},{12,8},{16,20},{20,16},{24,28},{28,24},{1,5},{5... | collective-permute-start | bytes 1769480 | tf_op jit(solution)/shard_map/ppermute | solution.py:29
  45.2 7.6 %collective-permute-start.11 = (bf16[768,768]{1,0:T(8,128)(2,1)S(1)}, bf16[768,768]{1,0:T(8,128)(2,1)S(1)}, u32[]{:S(2)}, u32[]{:S(2)}) collective-permute-start(bf16[768,768]{1,0:T(8,128)(2,1)S(1)} %constant_dynamic-update-slice_fusion.10.refs_3_), channel_id=1, source_target_pairs={{0,1},{1,0},{2,3},{3,2},{4,5},{5,4},{6,7},{7,6},{8,9},{9,8},{10,11... | collective-permute-start | bytes 3538952 | tf_op jit(solution)/shard_map/ppermute | solution.py:29
  45.3 15.8 %collective-permute-start.15 = (bf16[384,768]{1,0:T(8,128)(2,1)S(1)}, bf16[384,768]{1,0:T(8,128)(2,1)S(1)}, u32[]{:S(2)}, u32[]{:S(2)}) collective-permute-start(bf16[384,768]{1,0:T(8,128)(2,1)S(1)} %get-tuple-element.61.refs_1_), channel_id=1, source_target_pairs={{0,2},{1,3},{2,0},{3,1},{4,6},{5,7},{6,4},{7,5},{8,10},{9,11},{10,... | collective-permute-start | bytes 1769480 | tf_op jit(solution)/shard_map/ppermute | solution.py:29
  48.7 12.5 %collective-permute-start.13 = (bf16[96,768]{1,0:T(8,128)(2,1)S(1)}, bf16[96,768]{1,0:T(8,128)(2,1)S(1)}, u32[]{:S(2)}, u32[]{:S(2)}) collective-permute-start(bf16[96,768]{1,0:T(8,128)(2,1)S(1)} %pad_maximum_fusion.7), channel_id=1, source_target_pairs={{0,16},{4,20},{8,24},{12,28},{16,0},{20,4},{24,8},{28,12},{1,17},{... | collective-permute-start | bytes 442376 | tf_op jit(solution)/shard_map/ppermute | solution.py:29
  51.5 9.8 %collective-permute-start.14 = (bf16[96,768]{1,0:T(8,128)(2,1)S(1)}, bf16[96,768]{1,0:T(8,128)(2,1)S(1)}, u32[]{:S(2)}, u32[]{:S(2)}) collective-permute-start(bf16[96,768]{1,0:T(8,128)(2,1)S(1)} %pad_maximum_fusion.8), channel_id=1, source_target_pairs={{0,24},{4,28},{8,16},{12,20},{16,8},{20,12},{24,0},{28,4},{1,25},{... | collective-permute-start | bytes 442376 | tf_op jit(solution)/shard_map/ppermute | solution.py:29
  52.7 8.8 %collective-permute-start.12 = (bf16[96,768]{1,0:T(8,128)(2,1)S(1)}, bf16[96,768]{1,0:T(8,128)(2,1)S(1)}, u32[]{:S(2)}, u32[]{:S(2)}) collective-permute-start(bf16[96,768]{1,0:T(8,128)(2,1)S(1)} %pad_maximum_fusion.6), channel_id=1, source_target_pairs={{0,8},{4,12},{8,0},{12,4},{16,24},{20,28},{24,16},{28,20},{1,9},{5... | collective-permute-start | bytes 442376 | tf_op jit(solution)/shard_map/ppermute | solution.py:29
  61.5 5.7 %collective-permute-start.16 = (bf16[768,768]{1,0:T(8,128)(2,1)S(1)}, bf16[768,768]{1,0:T(8,128)(2,1)S(1)}, u32[]{:S(2)}, u32[]{:S(2)}) collective-permute-start(bf16[768,768]{1,0:T(8,128)(2,1)S(1)} %constant_dynamic-update-slice_fusion.21.refs_5_), channel_id=1, source_target_pairs={{0,1},{1,0},{2,3},{3,2},{4,5},{5,4},{6,7},{7,6},{8,9},{9,8},{10,11... | collective-permute-start | bytes 3538952 | tf_op jit(solution)/shard_map/ppermute | solution.py:29
  61.6 15.8 %collective-permute-start.20 = (bf16[384,768]{1,0:T(8,128)(2,1)S(1)}, bf16[384,768]{1,0:T(8,128)(2,1)S(1)}, u32[]{:S(2)}, u32[]{:S(2)}) collective-permute-start(bf16[384,768]{1,0:T(8,128)(2,1)S(1)} %get-tuple-element.66.refs_2_), channel_id=1, source_target_pairs={{0,2},{1,3},{2,0},{3,1},{4,6},{5,7},{6,4},{7,5},{8,10},{9,11},{10,... | collective-permute-start | bytes 1769480 | tf_op jit(solution)/shard_map/ppermute | solution.py:29
  62.4 15.0 %collective-permute-start.18 = (bf16[96,768]{1,0:T(8,128)(2,1)S(1)}, bf16[96,768]{1,0:T(8,128)(2,1)S(1)}, u32[]{:S(2)}, u32[]{:S(2)}) collective-permute-start(bf16[96,768]{1,0:T(8,128)(2,1)S(1)} %pad_maximum_fusion.10), channel_id=1, source_target_pairs={{0,16},{4,20},{8,24},{12,28},{16,0},{20,4},{24,8},{28,12},{1,17},{... | collective-permute-start | bytes 442376 | tf_op jit(solution)/shard_map/ppermute | solution.py:29
  66.2 11.2 %collective-permute-start.19 = (bf16[96,768]{1,0:T(8,128)(2,1)S(1)}, bf16[96,768]{1,0:T(8,128)(2,1)S(1)}, u32[]{:S(2)}, u32[]{:S(2)}) collective-permute-start(bf16[96,768]{1,0:T(8,128)(2,1)S(1)} %pad_maximum_fusion.11), channel_id=1, source_target_pairs={{0,24},{4,28},{8,16},{12,20},{16,8},{20,12},{24,0},{28,4},{1,25},{... | collective-permute-start | bytes 442376 | tf_op jit(solution)/shard_map/ppermute | solution.py:29
  67.1 11.0 %collective-permute-start.17 = (bf16[96,768]{1,0:T(8,128)(2,1)S(1)}, bf16[96,768]{1,0:T(8,128)(2,1)S(1)}, u32[]{:S(2)}, u32[]{:S(2)}) collective-permute-start(bf16[96,768]{1,0:T(8,128)(2,1)S(1)} %pad_maximum_fusion.9), channel_id=1, source_target_pairs={{0,8},{4,12},{8,0},{12,4},{16,24},{20,28},{24,16},{28,20},{1,9},{5... | collective-permute-start | bytes 442376 | tf_op jit(solution)/shard_map/ppermute | solution.py:29
  78.3 13.6 %collective-permute-start.21 = (bf16[304,768]{1,0:T(8,128)(2,1)S(1)}, bf16[304,768]{1,0:T(8,128)(2,1)S(1)}, u32[]{:S(2)}, u32[]{:S(2)}) collective-permute-start(bf16[304,768]{1,0:T(8,128)(2,1)S(1)} %slice.168), channel_id=1, source_target_pairs={{0,2},{1,3},{2,0},{3,1},{4,6},{5,7},{6,4},{7,5},{8,10},{9,11},{10,... | collective-permute-start | bytes 1400840 | tf_op jit(solution)/shard_map/ppermute | solution.py:29
  87.0 7.1 %collective-permute-start.23 = (bf16[80,768]{1,0:T(8,128)(2,1)S(1)}, bf16[80,768]{1,0:T(8,128)(2,1)S(1)}, u32[]{:S(2)}, u32[]{:S(2)}) collective-permute-start(bf16[80,768]{1,0:T(8,128)(2,1)S(1)} %slice.169), channel_id=1, source_target_pairs={{0,2},{1,3},{2,0},{3,1},{4,6},{5,7},{6,4},{7,5},{8,10},{9,11},{10,... | collective-permute-start | bytes 368648 | tf_op jit(solution)/shard_map/ppermute | solution.py:29
  94.1 2.9 %collective-permute-start.24 = (bf16[768,768]{1,0:T(8,128)(2,1)S(1)}, bf16[768,768]{1,0:T(8,128)(2,1)S(1)}, u32[]{:S(2)}, u32[]{:S(2)}) collective-permute-start(bf16[768,768]{1,0:T(8,128)(2,1)S(1)} %constant_dynamic-update-slice_fusion.38.refs_4_), channel_id=1, source_target_pairs={{0,1},{1,0},{2,3},{3,2},{4,5},{5,4},{6,7},{7,6},{8,9},{9,8},{10,11... | collective-permute-start | bytes 3538952 | tf_op jit(solution)/shard_map/ppermute | solution.py:29
  (3 other events, 4.8 us)

commit v17 on v16

--- a/solution.py
+++ b/solution.py
@@ -57,16 +57,14 @@
 
 
 def rest_kernel(capacity, chunks, groups, me_ref, slot_ref, normed_ref, *out_refs):
-    keeps, send_refs = out_refs[:-2], out_refs[-2:]
+    keeps, send_refs = out_refs[: len(chunks)], out_refs[len(chunks) :]
     slots, normed = flat(slot_ref), normed_ref[...]
-    first, row = 0, 0
+    first = 0
     for step, size in enumerate(chunks):
-        placed = place(me_ref[0], slots, normed, capacity, first, size, groups, 1) if step else None
-        if step == 1:
-            send_refs[0][...] = placed
-        elif step > 1:
-            send_refs[1][row : row + placed.shape[0], :] = placed
-            row += placed.shape[0]
+        if step > 0:
+            send_refs[step - 1][...] = place(
+                me_ref[0], slots, normed, capacity, first, size, groups, 1
+            )
         first += size
     first = 0
     for step, size in enumerate(chunks):
@@ -98,16 +96,16 @@
         cost_estimate=cost(half[0]),
         name="place_first",
     )(me, slots, embeddings)
-    *keeps, next_send, rest_send = pl.pallas_call(
+    *placed, = pl.pallas_call(
         functools.partial(rest_kernel, capacity, chunks, groups),
         in_specs=[smem, vmem, vmem],
-        out_specs=[vmem] * (len(chunks) + 2),
-        out_shape=[shape(count) for count in half + [half[1], sum(half[2:])]],
+        out_specs=[vmem] * (2 * len(chunks) - 1),
+        out_shape=[shape(count) for count in half + half[1:]],
         compiler_params=params,
         cost_estimate=cost(2 * sum(half) - half[0]),
         name="place_rest",
     )(me, slots, normed)
-    return keeps, first_send, next_send, rest_send
+    return placed[: len(chunks)], [first_send] + placed[len(chunks) :]
 
 
 def lane_fold(values):
@@ -280,7 +278,7 @@
     chunks = chunk_sizes(capacity)
     me = jnp.stack([lax.axis_index("grp"), lax.axis_index("blk")]).astype(jnp.int32)
     slots = send_slot.reshape(row_count // lanes, lanes)
-    keeps, first_send, next_send, rest_send = head(me, embeddings, slots, capacity, chunks, groups)
+    keeps, sends = head(me, embeddings, slots, capacity, chunks, groups)
     count, high = len(chunks), groups // 2
     last = count - 1
 
@@ -291,11 +289,8 @@
 
     def block(step, z):
         size = chunks[step]
-        near = first_near if step == 0 else sent["y", min(step, 2) + 1]
-        skip = sum(chunks[2:step]) * high
-        return jnp.concatenate(
-            [rows(keeps[step], z, size), rows(near[skip:], z, size)], axis=0
-        )
+        near = first_near if step == 0 else sent["y", step + 1]
+        return jnp.concatenate([rows(keeps[step], z, size), rows(near, z, size)], axis=0)
 
     def send(key, value, axis, size, bit, *earlier):
         held = [done[name] if name in done else sent[name] for name in earlier]
@@ -330,12 +325,14 @@
         send(("c", step), pairs[step], "blk", members, 1, *early)
 
     far = [high // 2] + [z for z in range(1, high) if z != high // 2]
-    cut = first_send.shape[0] // 32 * 16
-    done["rest"] = rest_send
-    send(("y", 0), first_send[:cut], "grp", groups, 1)
-    send(("y", 1), first_send[cut:], "grp", groups, 1, "rest")
-    send(("y", 2), next_send, "grp", groups, 1, ("y", 0))
-    send(("y", 3), rest_send, "grp", groups, 1, ("y", 0))
+    cut = sends[0].shape[0] // 32 * 16
+    done["rest"] = sends[1]
+    send(("y", 0), sends[0][:cut], "grp", groups, 1)
+    send(("y", 1), sends[0][cut:], "grp", groups, 1, "rest")
+    send(("y", 2), sends[1], "grp", groups, 1, ("y", 0))
+    for step in range(2, count):
+        early = ("y", 0) if step == 2 else ("y", step)
+        send(("y", step + 1), sends[step], "grp", groups, 1, early)
     first_near = jnp.concatenate([sent["y", 0], sent["y", 1]], axis=0)
     for z in far:
         send_z(0, z)

time: 114 us -> 130 us (1.14)
  waiting for transfers between devices: 52 us -> 64.3 us
  starting transfers between devices: 29.5 us -> 32.9 us
    ppermute x25 -> x26, waiting for transfers between devices: 52 us -> 64.3 us  [swap(): return lax.ppermute(value, axis, [(i, i ^ bit) for i in range(size)])]
    ppermute x25 -> x26, starting transfers between devices: 29.5 us -> 32.9 us  [swap(): return lax.ppermute(value, axis, [(i, i ^ bit) for i in range(size)])]
  transfers between devices with their start and end apart: 25 -> 26, of which waited for: 15 -> 17; matrix products, arithmetic and copies ran while one was open for 1% -> 1% of each run, Pallas kernels for 10% -> 9%
where the time goes in v17:
time: 130 us
  waiting for transfers between devices  64.3 us (49%)
  starting transfers between devices  32.9 us (25%)
  Pallas kernels  17.8 us (14%)
  blocking collectives  11.5 us (9%)
  local copies, waits for them, and re-layouts  2.63 us (2%)
    ppermute x26, waiting for transfers between devices, swap(): return lax.ppermute(value, axis, [(i, i ^ bit) for i in range(size)])  64.3 us
    ppermute x26, starting transfers between devices, swap(): return lax.ppermute(value, axis, [(i, i ^ bit) for i in range(size)])  32.9 us
    all_to_all x1, blocking collectives, on_device(): homeward = lax.all_to_all(result, ('grp', 'blk'), 0, 0, tiled=True)  11.5 us
    pallas_call x2, Pallas kernels, gram_step(): pl.pallas_call(functools.partial(gram_kernel, first, step, pieces), in_sp...  8.48 us
    pallas_call x1, Pallas kernels, gram_last(): pl.pallas_call(functools.partial(gram_last_kernel, step, relatives, chunk...  3.08 us
    pallas_call x1, Pallas kernels, head(): pl.pallas_call(functools.partial(rest_kernel, capacity, chunks, groups),...  2.61 us
  transfers between devices with their start and end apart: 26, of which 17 were waited for; matrix products, arithmetic and copies ran while one was open for 1% of the time, Pallas kernels for 9%

profile of v17, /device:TPU:0, one launch (start us, length us, event | category | flops | bytes accessed | tf_op | source)
XLA Modules:
  0.0 129.7 jit_solution(3389557885472465536)
XLA Ops:
  3.3 3.0 %collective-permute-start = (bf16[96,768]{1,0:T(8,128)(2,1)S(1)}, bf16[96,768]{1,0:T(8,128)(2,1)S(1)}, u32[]{:S(2)}, u32[]{:S(2)}) collective-permute-start(bf16[96,768]{1,0:T(8,128)(2,1)S(1)} %get-tuple-element.121), channel_id=1, source_target_pairs={{0,4},{4,0},{8,12},{12,8},{16,20},{20,16},{24,28},{28,24},{1,5},{5... | collective-permute-start | bytes 442376 | tf_op jit(solution)/shard_map/ppermute | solution.py:29
  6.4 2.6 %place_rest.1 = (bf16[192,768]{1,0:T(8,128)(2,1)S(1)}, bf16[192,768]{1,0:T(8,128)(2,1)S(1)}, bf16[192,768]{1,0:T(8,128)(2,1)S(1)}, bf16[192,768]{1,0:T(8,128)(2,...) custom-call(s32[2]{0:T(128)S(1)} %pad_add_fusion.me_ref, ...), custom_call_target="tpu_custom_call" | custom-call | flops 1585446912 | bytes 3244032 | tf_op jit(solution)/shard_map/place_rest/pallas_call | solution.py:99
  10.2 2.1 %collective-permute-start.5 = (bf16[192,768]{1,0:T(8,128)(2,1)S(1)}, bf16[192,768]{1,0:T(8,128)(2,1)S(1)}, u32[]{:S(2)}, u32[]{:S(2)}) collective-permute-start(bf16[192,768]{1,0:T(8,128)(2,1)S(1)} %get-tuple-element.51), channel_id=1, source_target_pairs={{0,4},{4,0},{8,12},{12,8},{16,20},{20,16},{24,28},{28,24},{1,5},{5... | collective-permute-start | bytes 884744 | tf_op jit(solution)/shard_map/ppermute | solution.py:29
  15.9 2.7 %collective-permute-start.3 = (bf16[96,768]{1,0:T(8,128)(2,1)S(1)}, bf16[96,768]{1,0:T(8,128)(2,1)S(1)}, u32[]{:S(2)}, u32[]{:S(2)}) collective-permute-start(bf16[96,768]{1,0:T(8,128)(2,1)S(1)} %pad_maximum_fusion.1), channel_id=1, source_target_pairs={{0,16},{4,20},{8,24},{12,28},{16,0},{20,4},{24,8},{28,12},{1,17},{... | collective-permute-start | bytes 442376 | tf_op jit(solution)/shard_map/ppermute | solution.py:29
  20.0 7.8 %collective-permute-done.3 = bf16[96,768]{1,0:T(8,128)(2,1)S(1)} collective-permute-done((bf16[96,768]{1,0:T(8,128)(2,1)S(1)}, bf16[96,768]{1,0:T(8,128)(2,1)S(1)}, u32[]{:S(2)}, u32[]{:S(2)}) %collective-permute-start.3) | collective-permute-done | bytes 147488 | tf_op jit(solution)/shard_map/ppermute | solution.py:29
  29.4 2.3 %collective-permute-start.6 = (bf16[96,768]{1,0:T(8,128)(2,1)S(1)}, bf16[96,768]{1,0:T(8,128)(2,1)S(1)}, u32[]{:S(2)}, u32[]{:S(2)}) collective-permute-start(bf16[96,768]{1,0:T(8,128)(2,1)S(1)} %pad_maximum_fusion.3), channel_id=1, source_target_pairs={{0,8},{4,12},{8,0},{12,4},{16,24},{20,28},{24,16},{28,20},{1,9},{5... | collective-permute-start | bytes 442376 | tf_op jit(solution)/shard_map/ppermute | solution.py:29
  35.2 3.2 %collective-permute-done.10 = bf16[384,768]{1,0:T(8,128)(2,1)S(1)} collective-permute-done((bf16[384,768]{1,0:T(8,128)(2,1)S(1)}, bf16[384,768]{1,0:T(8,128)(2,1)S(1)}, u32[]{:S(2)}, u32[]{:S(2)}) %collective-permute-start.10) | collective-permute-done | bytes 589856 | tf_op jit(solution)/shard_map/ppermute | solution.py:29
  38.4 7.2 %collective-permute-done.7 = bf16[96,768]{1,0:T(8,128)(2,1)S(1)} collective-permute-done((bf16[96,768]{1,0:T(8,128)(2,1)S(1)}, bf16[96,768]{1,0:T(8,128)(2,1)S(1)}, u32[]{:S(2)}, u32[]{:S(2)}) %collective-permute-start.7) | collective-permute-done | bytes 147488 | tf_op jit(solution)/shard_map/ppermute | solution.py:29
  47.5 7.6 %collective-permute-done.9 = bf16[192,768]{1,0:T(8,128)(2,1)S(1)} collective-permute-done((bf16[192,768]{1,0:T(8,128)(2,1)S(1)}, bf16[192,768]{1,0:T(8,128)(2,1)S(1)}, u32[]{:S(2)}, u32[]{:S(2)}) %collective-permute-start.9) | collective-permute-done | bytes 294944 | tf_op jit(solution)/shard_map/ppermute | solution.py:29
  55.2 3.4 %collective-permute-start.13 = (bf16[96,768]{1,0:T(8,128)(2,1)S(1)}, bf16[96,768]{1,0:T(8,128)(2,1)S(1)}, u32[]{:S(2)}, u32[]{:S(2)}) collective-permute-start(bf16[96,768]{1,0:T(8,128)(2,1)S(1)} %pad_maximum_fusion.7), channel_id=1, source_target_pairs={{0,16},{4,20},{8,24},{12,28},{16,0},{20,4},{24,8},{28,12},{1,17},{... | collective-permute-start | bytes 442376 | tf_op jit(solution)/shard_map/ppermute | solution.py:29
  61.8 7.9 %collective-permute-done.13 = bf16[96,768]{1,0:T(8,128)(2,1)S(1)} collective-permute-done((bf16[96,768]{1,0:T(8,128)(2,1)S(1)}, bf16[96,768]{1,0:T(8,128)(2,1)S(1)}, u32[]{:S(2)}, u32[]{:S(2)}) %collective-permute-start.13) | collective-permute-done | bytes 147488 | tf_op jit(solution)/shard_map/ppermute | solution.py:29
  72.5 7.1 %collective-permute-done.15 = bf16[192,768]{1,0:T(8,128)(2,1)S(1)} collective-permute-done((bf16[192,768]{1,0:T(8,128)(2,1)S(1)}, bf16[192,768]{1,0:T(8,128)(2,1)S(1)}, u32[]{:S(2)}, u32[]{:S(2)}) %collective-permute-start.15) | collective-permute-done | bytes 294944 | tf_op jit(solution)/shard_map/ppermute | solution.py:29
  79.6 2.5 %collective-permute-start.19 = (bf16[96,768]{1,0:T(8,128)(2,1)S(1)}, bf16[96,768]{1,0:T(8,128)(2,1)S(1)}, u32[]{:S(2)}, u32[]{:S(2)}) collective-permute-start(bf16[96,768]{1,0:T(8,128)(2,1)S(1)} %pad_maximum_fusion.10), channel_id=1, source_target_pairs={{0,16},{4,20},{8,24},{12,28},{16,0},{20,4},{24,8},{28,12},{1,17},{... | collective-permute-start | bytes 442376 | tf_op jit(solution)/shard_map/ppermute | solution.py:29
  82.2 2.4 %collective-permute-start.20 = (bf16[96,768]{1,0:T(8,128)(2,1)S(1)}, bf16[96,768]{1,0:T(8,128)(2,1)S(1)}, u32[]{:S(2)}, u32[]{:S(2)}) collective-permute-start(bf16[96,768]{1,0:T(8,128)(2,1)S(1)} %pad_maximum_fusion.11), channel_id=1, source_target_pairs={{0,24},{4,28},{8,16},{12,20},{16,8},{20,12},{24,0},{28,4},{1,25},{... | collective-permute-start | bytes 442376 | tf_op jit(solution)/shard_map/ppermute | solution.py:29
  84.6 2.9 %collective-permute-done.21 = bf16[384,768]{1,0:T(8,128)(2,1)S(1)} collective-permute-done((bf16[384,768]{1,0:T(8,128)(2,1)S(1)}, bf16[384,768]{1,0:T(8,128)(2,1)S(1)}, u32[]{:S(2)}, u32[]{:S(2)}) %collective-permute-start.21) | collective-permute-done | bytes 589856 | tf_op jit(solution)/shard_map/ppermute | solution.py:29
  87.5 6.2 %collective-permute-done.19 = bf16[96,768]{1,0:T(8,128)(2,1)S(1)} collective-permute-done((bf16[96,768]{1,0:T(8,128)(2,1)S(1)}, bf16[96,768]{1,0:T(8,128)(2,1)S(1)}, u32[]{:S(2)}, u32[]{:S(2)}) %collective-permute-start.19) | collective-permute-done | bytes 147488 | tf_op jit(solution)/shard_map/ppermute | solution.py:29
  94.6 2.1 %collective-permute-done.23.refs_8_ = bf16[768,768]{1,0:T(8,128)(2,1)S(1)} collective-permute-done((bf16[768,768]{1,0:T(8,128)(2,1)S(1)}, bf16[768,768]{1,0:T(8,128)(2,1)S(1)}, u32[]{:S(2)}, u32[]{:S(2)}) %collective-permute-start.23) | collective-permute-done | bytes 1179680 | tf_op jit(solution)/shard_map/ppermute | solution.py:29
  96.7 6.1 %gram_step.2 = (f32[384,128]{1,0:T(8,128)S(1)}, f32[384,128]{1,0:T(8,128)S(1)}, f32[384,128]{1,0:T(8,128)S(1)}, f32[1,1536]{1,0:T(1,128)S(1)}, f32[1,1536]{1,0:T(1,128)S(1)}, /*index=5*/f32[1,1536]{1,0:T(1,128)S(1)}) custom-call(bf16[384,768]{1,0:T(8,128)(2,1)S(1)} %get-tuple-element.141.refs_0_, bf16[384,768]{1,0:T(8,128)(2,1)S(1)} %get-tuple-element.65.refs_1_, ...), custom_call_target="tpu_custom_call" | custom-call | flops 8153726976 | bytes 8847360 | tf_op jit(solution)/shard_map/gram_step/pallas_call | solution.py:211
  103.4 4.2 %collective-permute-done.22 = bf16[304,768]{1,0:T(8,128)(2,1)S(1)} collective-permute-done((bf16[304,768]{1,0:T(8,128)(2,1)S(1)}, bf16[304,768]{1,0:T(8,128)(2,1)S(1)}, u32[]{:S(2)}, u32[]{:S(2)}) %collective-permute-start.22) | collective-permute-done | bytes 466976 | tf_op jit(solution)/shard_map/ppermute | solution.py:29
  107.6 2.2 %collective-permute-done.24 = bf16[80,768]{1,0:T(8,128)(2,1)S(1)} collective-permute-done((bf16[80,768]{1,0:T(8,128)(2,1)S(1)}, bf16[80,768]{1,0:T(8,128)(2,1)S(1)}, u32[]{:S(2)}, u32[]{:S(2)}) %collective-permute-start.24) | collective-permute-done | bytes 122912 | tf_op jit(solution)/shard_map/ppermute | solution.py:29
  109.9 2.4 %gram_step.3 = (f32[384,128]{1,0:T(8,128)S(1)}, f32[384,128]{1,0:T(8,128)S(1)}, f32[384,128]{1,0:T(8,128)S(1)}, f32[384,128]{1,0:T(8,128)S(1)}, f32[1,768]{1,0:T(1,128)S(1)}) custom-call(bf16[384,768]{1,0:T(8,128)(2,1)S(1)} %get-tuple-element.141.refs_0_, bf16[384,768]{1,0:T(8,128)(2,1)S(1)} %get-tuple-element.65.refs_1_, ...), custom_call_target="tpu_custom_call" | custom-call | flops 1811939328 | bytes 3538944 | tf_op jit(solution)/shard_map/gram_step/pallas_call | solution.py:211
  112.8 3.1 %gram_last.1 = f32[32,1,192]{2,1,0:T(1,128)S(1)} custom-call(s32[2]{0:T(128)S(1)} %pad_add_fusion.me_ref, bf16[384,768]{1,0:T(8,128)(2,1)S(1)} %get-tuple-element.141.refs_0_, bf16[384,768]{1,0:T(8,128)(2,1)S(1)} %get-tuple-element.65.refs_1_, bf16[384,768]{1,0:T(8,128)(2,1)S(1)} %get-tuple-element.70.refs_2_, ...), custom_call_target="tpu_custom_call" | custom-call | flops 1811939328 | bytes 3538944 | tf_op jit(solution)/shard_map/gram_last/pallas_call | solution.py:226
  115.8 11.5 %all_to_all.5.part_ref = f32[32,1,192]{2,1,0:T(1,128)} all-to-all(f32[32,1,192]{2,1,0:T(1,128)S(1)} %gram_last.1), channel_id=1, replica_groups=mesh['grp'=8,'blk'=4] {'grp','blk'}, dimensions={0} | all-to-all | bytes 49152 | tf_op jit(solution)/shard_map/all_to_all | solution.py:356
  127.3 2.3 %pick_rows.1 = f32[6,128]{1,0:T(8,128)} custom-call(s32[6,128]{1,0:T(8,128)} %bitcast.4, f32[32,1,192]{2,1,0:T(1,128)} %all_to_all.5.part_ref), custom_call_target="tpu_custom_call" | custom-call | tf_op jit(solution)/shard_map/pick_rows/pallas_call | solution.py:262
  (81 shorter events, 24.7 us)
Async XLA Ops:
  3.3 6.9 %collective-permute-start = (bf16[96,768]{1,0:T(8,128)(2,1)S(1)}, bf16[96,768]{1,0:T(8,128)(2,1)S(1)}, u32[]{:S(2)}, u32[]{:S(2)}) collective-permute-start(bf16[96,768]{1,0:T(8,128)(2,1)S(1)} %get-tuple-element.121), channel_id=1, source_target_pairs={{0,4},{4,0},{8,12},{12,8},{16,20},{20,16},{24,28},{28,24},{1,5},{5... | collective-permute-start | bytes 442376 | tf_op jit(solution)/shard_map/ppermute | solution.py:29
  9.0 6.8 %collective-permute-start.2 = (bf16[96,768]{1,0:T(8,128)(2,1)S(1)}, bf16[96,768]{1,0:T(8,128)(2,1)S(1)}, u32[]{:S(2)}, u32[]{:S(2)}) collective-permute-start(bf16[96,768]{1,0:T(8,128)(2,1)S(1)} %get-tuple-element.49), channel_id=1, source_target_pairs={{0,4},{4,0},{8,12},{12,8},{16,20},{20,16},{24,28},{28,24},{1,5},{5... | collective-permute-start | bytes 442376 | tf_op jit(solution)/shard_map/ppermute | solution.py:29
  10.2 19.1 %collective-permute-start.5 = (bf16[192,768]{1,0:T(8,128)(2,1)S(1)}, bf16[192,768]{1,0:T(8,128)(2,1)S(1)}, u32[]{:S(2)}, u32[]{:S(2)}) collective-permute-start(bf16[192,768]{1,0:T(8,128)(2,1)S(1)} %get-tuple-element.51), channel_id=1, source_target_pairs={{0,4},{4,0},{8,12},{12,8},{16,20},{20,16},{24,28},{28,24},{1,5},{5... | collective-permute-start | bytes 884744 | tf_op jit(solution)/shard_map/ppermute | solution.py:29
  12.4 7.6 %collective-permute-start.1 = (bf16[96,768]{1,0:T(8,128)(2,1)S(1)}, bf16[96,768]{1,0:T(8,128)(2,1)S(1)}, u32[]{:S(2)}, u32[]{:S(2)}) collective-permute-start(bf16[96,768]{1,0:T(8,128)(2,1)S(1)} %pad_maximum_fusion), channel_id=1, source_target_pairs={{0,8},{4,12},{8,0},{12,4},{16,24},{20,28},{24,16},{28,20},{1,9},{5... | collective-permute-start | bytes 442376 | tf_op jit(solution)/shard_map/ppermute | solution.py:29
  15.9 11.9 %collective-permute-start.3 = (bf16[96,768]{1,0:T(8,128)(2,1)S(1)}, bf16[96,768]{1,0:T(8,128)(2,1)S(1)}, u32[]{:S(2)}, u32[]{:S(2)}) collective-permute-start(bf16[96,768]{1,0:T(8,128)(2,1)S(1)} %pad_maximum_fusion.1), channel_id=1, source_target_pairs={{0,16},{4,20},{8,24},{12,28},{16,0},{20,4},{24,8},{28,12},{1,17},{... | collective-permute-start | bytes 442376 | tf_op jit(solution)/shard_map/ppermute | solution.py:29
  18.5 9.2 %collective-permute-start.4 = (bf16[96,768]{1,0:T(8,128)(2,1)S(1)}, bf16[96,768]{1,0:T(8,128)(2,1)S(1)}, u32[]{:S(2)}, u32[]{:S(2)}) collective-permute-start(bf16[96,768]{1,0:T(8,128)(2,1)S(1)} %pad_maximum_fusion.2), channel_id=1, source_target_pairs={{0,24},{4,28},{8,16},{12,20},{16,8},{20,12},{24,0},{28,4},{1,25},{... | collective-permute-start | bytes 442376 | tf_op jit(solution)/shard_map/ppermute | solution.py:29
  27.8 10.6 %collective-permute-start.10 = (bf16[384,768]{1,0:T(8,128)(2,1)S(1)}, bf16[384,768]{1,0:T(8,128)(2,1)S(1)}, u32[]{:S(2)}, u32[]{:S(2)}) collective-permute-start(bf16[384,768]{1,0:T(8,128)(2,1)S(1)} %get-tuple-element.141.refs_0_), channel_id=1, source_target_pairs={{0,2},{1,3},{2,0},{3,1},{4,6},{5,7},{6,4},{7,5},{8,10},{9,11},{10,... | collective-permute-start | bytes 1769480 | tf_op jit(solution)/shard_map/ppermute | solution.py:29
  29.4 9.0 %collective-permute-start.6 = (bf16[96,768]{1,0:T(8,128)(2,1)S(1)}, bf16[96,768]{1,0:T(8,128)(2,1)S(1)}, u32[]{:S(2)}, u32[]{:S(2)}) collective-permute-start(bf16[96,768]{1,0:T(8,128)(2,1)S(1)} %pad_maximum_fusion.3), channel_id=1, source_target_pairs={{0,8},{4,12},{8,0},{12,4},{16,24},{20,28},{24,16},{28,20},{1,9},{5... | collective-permute-start | bytes 442376 | tf_op jit(solution)/shard_map/ppermute | solution.py:29
  31.7 13.9 %collective-permute-start.7 = (bf16[96,768]{1,0:T(8,128)(2,1)S(1)}, bf16[96,768]{1,0:T(8,128)(2,1)S(1)}, u32[]{:S(2)}, u32[]{:S(2)}) collective-permute-start(bf16[96,768]{1,0:T(8,128)(2,1)S(1)} %pad_maximum_fusion.4), channel_id=1, source_target_pairs={{0,16},{4,20},{8,24},{12,28},{16,0},{20,4},{24,8},{28,12},{1,17},{... | collective-permute-start | bytes 442376 | tf_op jit(solution)/shard_map/ppermute | solution.py:29
  33.7 11.9 %collective-permute-start.8 = (bf16[96,768]{1,0:T(8,128)(2,1)S(1)}, bf16[96,768]{1,0:T(8,128)(2,1)S(1)}, u32[]{:S(2)}, u32[]{:S(2)}) collective-permute-start(bf16[96,768]{1,0:T(8,128)(2,1)S(1)} %pad_maximum_fusion.5), channel_id=1, source_target_pairs={{0,24},{4,28},{8,16},{12,20},{16,8},{20,12},{24,0},{28,4},{1,25},{... | collective-permute-start | bytes 442376 | tf_op jit(solution)/shard_map/ppermute | solution.py:29
  45.6 14.2 %collective-permute-start.11 = (bf16[768,768]{1,0:T(8,128)(2,1)S(1)}, bf16[768,768]{1,0:T(8,128)(2,1)S(1)}, u32[]{:S(2)}, u32[]{:S(2)}) collective-permute-start(bf16[768,768]{1,0:T(8,128)(2,1)S(1)} %constant_dynamic-update-slice_fusion.10.refs_3_), channel_id=1, source_target_pairs={{0,1},{1,0},{2,3},{3,2},{4,5},{5,4},{6,7},{7,6},{8,9},{9,8},{10,11... | collective-permute-start | bytes 3538952 | tf_op jit(solution)/shard_map/ppermute | solution.py:29
  45.6 9.5 %collective-permute-start.9 = (bf16[192,768]{1,0:T(8,128)(2,1)S(1)}, bf16[192,768]{1,0:T(8,128)(2,1)S(1)}, u32[]{:S(2)}, u32[]{:S(2)}) collective-permute-start(bf16[192,768]{1,0:T(8,128)(2,1)S(1)} %get-tuple-element.57), channel_id=1, source_target_pairs={{0,4},{4,0},{8,12},{12,8},{16,20},{20,16},{24,28},{28,24},{1,5},{5... | collective-permute-start | bytes 884744 | tf_op jit(solution)/shard_map/ppermute | solution.py:29
  46.3 15.5 %collective-permute-start.16 = (bf16[384,768]{1,0:T(8,128)(2,1)S(1)}, bf16[384,768]{1,0:T(8,128)(2,1)S(1)}, u32[]{:S(2)}, u32[]{:S(2)}) collective-permute-start(bf16[384,768]{1,0:T(8,128)(2,1)S(1)} %get-tuple-element.65.refs_1_), channel_id=1, source_target_pairs={{0,2},{1,3},{2,0},{3,1},{4,6},{5,7},{6,4},{7,5},{8,10},{9,11},{10,... | collective-permute-start | bytes 1769480 | tf_op jit(solution)/shard_map/ppermute | solution.py:29
  55.2 14.5 %collective-permute-start.13 = (bf16[96,768]{1,0:T(8,128)(2,1)S(1)}, bf16[96,768]{1,0:T(8,128)(2,1)S(1)}, u32[]{:S(2)}, u32[]{:S(2)}) collective-permute-start(bf16[96,768]{1,0:T(8,128)(2,1)S(1)} %pad_maximum_fusion.7), channel_id=1, source_target_pairs={{0,16},{4,20},{8,24},{12,28},{16,0},{20,4},{24,8},{28,12},{1,17},{... | collective-permute-start | bytes 442376 | tf_op jit(solution)/shard_map/ppermute | solution.py:29
  58.6 11.1 %collective-permute-start.14 = (bf16[96,768]{1,0:T(8,128)(2,1)S(1)}, bf16[96,768]{1,0:T(8,128)(2,1)S(1)}, u32[]{:S(2)}, u32[]{:S(2)}) collective-permute-start(bf16[96,768]{1,0:T(8,128)(2,1)S(1)} %pad_maximum_fusion.8), channel_id=1, source_target_pairs={{0,24},{4,28},{8,16},{12,20},{16,8},{20,12},{24,0},{28,4},{1,25},{... | collective-permute-start | bytes 442376 | tf_op jit(solution)/shard_map/ppermute | solution.py:29
  59.8 10.2 %collective-permute-start.12 = (bf16[96,768]{1,0:T(8,128)(2,1)S(1)}, bf16[96,768]{1,0:T(8,128)(2,1)S(1)}, u32[]{:S(2)}, u32[]{:S(2)}) collective-permute-start(bf16[96,768]{1,0:T(8,128)(2,1)S(1)} %pad_maximum_fusion.6), channel_id=1, source_target_pairs={{0,8},{4,12},{8,0},{12,4},{16,24},{20,28},{24,16},{28,20},{1,9},{5... | collective-permute-start | bytes 442376 | tf_op jit(solution)/shard_map/ppermute | solution.py:29
  70.1 14.5 %collective-permute-start.17 = (bf16[768,768]{1,0:T(8,128)(2,1)S(1)}, bf16[768,768]{1,0:T(8,128)(2,1)S(1)}, u32[]{:S(2)}, u32[]{:S(2)}) collective-permute-start(bf16[768,768]{1,0:T(8,128)(2,1)S(1)} %constant_dynamic-update-slice_fusion.21.refs_5_), channel_id=1, source_target_pairs={{0,1},{1,0},{2,3},{3,2},{4,5},{5,4},{6,7},{7,6},{8,9},{9,8},{10,11... | collective-permute-start | bytes 3538952 | tf_op jit(solution)/shard_map/ppermute | solution.py:29
  70.1 9.5 %collective-permute-start.15 = (bf16[192,768]{1,0:T(8,128)(2,1)S(1)}, bf16[192,768]{1,0:T(8,128)(2,1)S(1)}, u32[]{:S(2)}, u32[]{:S(2)}) collective-permute-start(bf16[192,768]{1,0:T(8,128)(2,1)S(1)} %get-tuple-element.64), channel_id=1, source_target_pairs={{0,4},{4,0},{8,12},{12,8},{16,20},{20,16},{24,28},{28,24},{1,5},{5... | collective-permute-start | bytes 884744 | tf_op jit(solution)/shard_map/ppermute | solution.py:29
  71.9 15.5 %collective-permute-start.21 = (bf16[384,768]{1,0:T(8,128)(2,1)S(1)}, bf16[384,768]{1,0:T(8,128)(2,1)S(1)}, u32[]{:S(2)}, u32[]{:S(2)}) collective-permute-start(bf16[384,768]{1,0:T(8,128)(2,1)S(1)} %get-tuple-element.70.refs_2_), channel_id=1, source_target_pairs={{0,2},{1,3},{2,0},{3,1},{4,6},{5,7},{6,4},{7,5},{8,10},{9,11},{10,... | collective-permute-start | bytes 1769480 | tf_op jit(solution)/shard_map/ppermute | solution.py:29
  79.6 14.0 %collective-permute-start.19 = (bf16[96,768]{1,0:T(8,128)(2,1)S(1)}, bf16[96,768]{1,0:T(8,128)(2,1)S(1)}, u32[]{:S(2)}, u32[]{:S(2)}) collective-permute-start(bf16[96,768]{1,0:T(8,128)(2,1)S(1)} %pad_maximum_fusion.10), channel_id=1, source_target_pairs={{0,16},{4,20},{8,24},{12,28},{16,0},{20,4},{24,8},{28,12},{1,17},{... | collective-permute-start | bytes 442376 | tf_op jit(solution)/shard_map/ppermute | solution.py:29
  82.2 11.5 %collective-permute-start.20 = (bf16[96,768]{1,0:T(8,128)(2,1)S(1)}, bf16[96,768]{1,0:T(8,128)(2,1)S(1)}, u32[]{:S(2)}, u32[]{:S(2)}) collective-permute-start(bf16[96,768]{1,0:T(8,128)(2,1)S(1)} %pad_maximum_fusion.11), channel_id=1, source_target_pairs={{0,24},{4,28},{8,16},{12,20},{16,8},{20,12},{24,0},{28,4},{1,25},{... | collective-permute-start | bytes 442376 | tf_op jit(solution)/shard_map/ppermute | solution.py:29
  84.6 9.3 %collective-permute-start.18 = (bf16[96,768]{1,0:T(8,128)(2,1)S(1)}, bf16[96,768]{1,0:T(8,128)(2,1)S(1)}, u32[]{:S(2)}, u32[]{:S(2)}) collective-permute-start(bf16[96,768]{1,0:T(8,128)(2,1)S(1)} %pad_maximum_fusion.9), channel_id=1, source_target_pairs={{0,8},{4,12},{8,0},{12,4},{16,24},{20,28},{24,16},{28,20},{1,9},{5... | collective-permute-start | bytes 442376 | tf_op jit(solution)/shard_map/ppermute | solution.py:29
  94.0 13.6 %collective-permute-start.22 = (bf16[304,768]{1,0:T(8,128)(2,1)S(1)}, bf16[304,768]{1,0:T(8,128)(2,1)S(1)}, u32[]{:S(2)}, u32[]{:S(2)}) collective-permute-start(bf16[304,768]{1,0:T(8,128)(2,1)S(1)} %slice.160), channel_id=1, source_target_pairs={{0,2},{1,3},{2,0},{3,1},{4,6},{5,7},{6,4},{7,5},{8,10},{9,11},{10,... | collective-permute-start | bytes 1400840 | tf_op jit(solution)/shard_map/ppermute | solution.py:29
  102.8 7.0 %collective-permute-start.24 = (bf16[80,768]{1,0:T(8,128)(2,1)S(1)}, bf16[80,768]{1,0:T(8,128)(2,1)S(1)}, u32[]{:S(2)}, u32[]{:S(2)}) collective-permute-start(bf16[80,768]{1,0:T(8,128)(2,1)S(1)} %slice.161), channel_id=1, source_target_pairs={{0,2},{1,3},{2,0},{3,1},{4,6},{5,7},{6,4},{7,5},{8,10},{9,11},{10,... | collective-permute-start | bytes 368648 | tf_op jit(solution)/shard_map/ppermute | solution.py:29
  (4 other events, 7.7 us)

commit v18 on v17

--- a/solution.py
+++ b/solution.py
@@ -302,6 +302,8 @@
             early += [("x", step - 2, 0)]
         if step >= 2 and z == 1:
             early += [("c", step - 2)]
+        if 1 <= step < last and z == 1:
+            early += [("y", step + 2)]
         send(("z", step, z), block(step, z), "grp", groups, 2 * z, *early)
 
     def collect(step):

time: 130 us -> 116 us (0.89)
  waiting for transfers between devices: 64.3 us -> 49.9 us
  starting transfers between devices: 32.9 us -> 34.9 us
  blocking collectives: 11.5 us -> 9.83 us
    ppermute x26, waiting for transfers between devices: 64.3 us -> 49.9 us  [swap(): return lax.ppermute(value, axis, [(i, i ^ bit) for i in range(size)])]
    ppermute x26, starting transfers between devices: 32.9 us -> 34.9 us  [swap(): return lax.ppermute(value, axis, [(i, i ^ bit) for i in range(size)])]
    all_to_all x1, blocking collectives: 11.5 us -> 9.83 us  [on_device(): homeward = lax.all_to_all(result, ('grp', 'blk'), 0, 0, tiled=True)]
  transfers between devices with their start and end apart: 26 -> 26, of which waited for: 17 -> 15; matrix products, arithmetic and copies ran while one was open for 1% -> 1% of each run, Pallas kernels for 9% -> 10%
where the time goes in v18:
time: 116 us
  waiting for transfers between devices  49.9 us (43%)
  starting transfers between devices  34.9 us (30%)
  Pallas kernels  17.8 us (15%)
  blocking collectives  9.83 us (8%)
  local copies, waits for them, and re-layouts  2.64 us (2%)
    ppermute x26, waiting for transfers between devices, swap(): return lax.ppermute(value, axis, [(i, i ^ bit) for i in range(size)])  49.9 us
    ppermute x26, starting transfers between devices, swap(): return lax.ppermute(value, axis, [(i, i ^ bit) for i in range(size)])  34.9 us
    all_to_all x1, blocking collectives, on_device(): homeward = lax.all_to_all(result, ('grp', 'blk'), 0, 0, tiled=True)  9.83 us
    pallas_call x2, Pallas kernels, gram_step(): pl.pallas_call(functools.partial(gram_kernel, first, step, pieces), in_sp...  8.48 us
    pallas_call x1, Pallas kernels, gram_last(): pl.pallas_call(functools.partial(gram_last_kernel, step, relatives, chunk...  3.09 us
    pallas_call x1, Pallas kernels, head(): pl.pallas_call(functools.partial(rest_kernel, capacity, chunks, groups),...  2.61 us
    unnamed x25, local copies, waits for them, and re-layouts  2.44 us
    pallas_call x1, Pallas kernels, tail(): pl.pallas_call(functools.partial(tail_kernel, capacity, members), in_spec...  2.33 us
  transfers between devices with their start and end apart: 26, of which 15 were waited for; matrix products, arithmetic and copies ran while one was open for 1% of the time, Pallas kernels for 10%

profile of v18, /device:TPU:0, one launch (start us, length us, event | category | flops | bytes accessed | tf_op | source)
XLA Modules:
  0.0 115.5 jit_solution(3262812537652332042)
XLA Ops:
  3.3 3.0 %collective-permute-start = (bf16[96,768]{1,0:T(8,128)(2,1)S(1)}, bf16[96,768]{1,0:T(8,128)(2,1)S(1)}, u32[]{:S(2)}, u32[]{:S(2)}) collective-permute-start(bf16[96,768]{1,0:T(8,128)(2,1)S(1)} %get-tuple-element.121), channel_id=1, source_target_pairs={{0,4},{4,0},{8,12},{12,8},{16,20},{20,16},{24,28},{28,24},{1,5},{5... | collective-permute-start | bytes 442376 | tf_op jit(solution)/shard_map/ppermute | solution.py:29
  6.4 2.6 %place_rest.1 = (bf16[192,768]{1,0:T(8,128)(2,1)S(1)}, bf16[192,768]{1,0:T(8,128)(2,1)S(1)}, bf16[192,768]{1,0:T(8,128)(2,1)S(1)}, bf16[192,768]{1,0:T(8,128)(2,...) custom-call(s32[2]{0:T(128)S(1)} %pad_add_fusion.me_ref, ...), custom_call_target="tpu_custom_call" | custom-call | flops 1585446912 | bytes 3244032 | tf_op jit(solution)/shard_map/place_rest/pallas_call | solution.py:99
  10.2 2.1 %collective-permute-start.5 = (bf16[192,768]{1,0:T(8,128)(2,1)S(1)}, bf16[192,768]{1,0:T(8,128)(2,1)S(1)}, u32[]{:S(2)}, u32[]{:S(2)}) collective-permute-start(bf16[192,768]{1,0:T(8,128)(2,1)S(1)} %get-tuple-element.51), channel_id=1, source_target_pairs={{0,4},{4,0},{8,12},{12,8},{16,20},{20,16},{24,28},{28,24},{1,5},{5... | collective-permute-start | bytes 884744 | tf_op jit(solution)/shard_map/ppermute | solution.py:29
  14.1 1.7 %collective-permute-done.2 = bf16[96,768]{1,0:T(8,128)(2,1)S(1)} collective-permute-done((bf16[96,768]{1,0:T(8,128)(2,1)S(1)}, bf16[96,768]{1,0:T(8,128)(2,1)S(1)}, u32[]{:S(2)}, u32[]{:S(2)}) %collective-permute-start.2) | collective-permute-done | bytes 147488 | tf_op jit(solution)/shard_map/ppermute | solution.py:29
  15.9 2.7 %collective-permute-start.3 = (bf16[96,768]{1,0:T(8,128)(2,1)S(1)}, bf16[96,768]{1,0:T(8,128)(2,1)S(1)}, u32[]{:S(2)}, u32[]{:S(2)}) collective-permute-start(bf16[96,768]{1,0:T(8,128)(2,1)S(1)} %pad_maximum_fusion.1), channel_id=1, source_target_pairs={{0,16},{4,20},{8,24},{12,28},{16,0},{20,4},{24,8},{28,12},{1,17},{... | collective-permute-start | bytes 442376 | tf_op jit(solution)/shard_map/ppermute | solution.py:29
  20.0 7.8 %collective-permute-done.3 = bf16[96,768]{1,0:T(8,128)(2,1)S(1)} collective-permute-done((bf16[96,768]{1,0:T(8,128)(2,1)S(1)}, bf16[96,768]{1,0:T(8,128)(2,1)S(1)}, u32[]{:S(2)}, u32[]{:S(2)}) %collective-permute-start.3) | collective-permute-done | bytes 147488 | tf_op jit(solution)/shard_map/ppermute | solution.py:29
  29.4 2.3 %collective-permute-start.7 = (bf16[96,768]{1,0:T(8,128)(2,1)S(1)}, bf16[96,768]{1,0:T(8,128)(2,1)S(1)}, u32[]{:S(2)}, u32[]{:S(2)}) collective-permute-start(bf16[96,768]{1,0:T(8,128)(2,1)S(1)} %pad_maximum_fusion.3), channel_id=1, source_target_pairs={{0,8},{4,12},{8,0},{12,4},{16,24},{20,28},{24,16},{28,20},{1,9},{5... | collective-permute-start | bytes 442376 | tf_op jit(solution)/shard_map/ppermute | solution.py:29
  31.7 2.0 %collective-permute-start.8 = (bf16[96,768]{1,0:T(8,128)(2,1)S(1)}, bf16[96,768]{1,0:T(8,128)(2,1)S(1)}, u32[]{:S(2)}, u32[]{:S(2)}) collective-permute-start(bf16[96,768]{1,0:T(8,128)(2,1)S(1)} %pad_maximum_fusion.4), channel_id=1, source_target_pairs={{0,16},{4,20},{8,24},{12,28},{16,0},{20,4},{24,8},{28,12},{1,17},{... | collective-permute-start | bytes 442376 | tf_op jit(solution)/shard_map/ppermute | solution.py:29
  35.2 3.2 %collective-permute-done.10 = bf16[384,768]{1,0:T(8,128)(2,1)S(1)} collective-permute-done((bf16[384,768]{1,0:T(8,128)(2,1)S(1)}, bf16[384,768]{1,0:T(8,128)(2,1)S(1)}, u32[]{:S(2)}, u32[]{:S(2)}) %collective-permute-start.10) | collective-permute-done | bytes 589856 | tf_op jit(solution)/shard_map/ppermute | solution.py:29
  38.4 7.2 %collective-permute-done.8 = bf16[96,768]{1,0:T(8,128)(2,1)S(1)} collective-permute-done((bf16[96,768]{1,0:T(8,128)(2,1)S(1)}, bf16[96,768]{1,0:T(8,128)(2,1)S(1)}, u32[]{:S(2)}, u32[]{:S(2)}) %collective-permute-start.8) | collective-permute-done | bytes 147488 | tf_op jit(solution)/shard_map/ppermute | solution.py:29
  47.6 3.9 %collective-permute-start.14 = (bf16[96,768]{1,0:T(8,128)(2,1)S(1)}, bf16[96,768]{1,0:T(8,128)(2,1)S(1)}, u32[]{:S(2)}, u32[]{:S(2)}) collective-permute-start(bf16[96,768]{1,0:T(8,128)(2,1)S(1)} %pad_maximum_fusion.7), channel_id=1, source_target_pairs={{0,16},{4,20},{8,24},{12,28},{16,0},{20,4},{24,8},{28,12},{1,17},{... | collective-permute-start | bytes 442376 | tf_op jit(solution)/shard_map/ppermute | solution.py:29
  52.5 2.6 %collective-permute-done.12 = bf16[192,768]{1,0:T(8,128)(2,1)S(1)} collective-permute-done((bf16[192,768]{1,0:T(8,128)(2,1)S(1)}, bf16[192,768]{1,0:T(8,128)(2,1)S(1)}, u32[]{:S(2)}, u32[]{:S(2)}) %collective-permute-start.12) | collective-permute-done | bytes 294944 | tf_op jit(solution)/shard_map/ppermute | solution.py:29
  55.1 2.2 %collective-permute-start.13 = (bf16[96,768]{1,0:T(8,128)(2,1)S(1)}, bf16[96,768]{1,0:T(8,128)(2,1)S(1)}, u32[]{:S(2)}, u32[]{:S(2)}) collective-permute-start(bf16[96,768]{1,0:T(8,128)(2,1)S(1)} %pad_maximum_fusion.6), channel_id=1, source_target_pairs={{0,8},{4,12},{8,0},{12,4},{16,24},{20,28},{24,16},{28,20},{1,9},{5... | collective-permute-start | bytes 442376 | tf_op jit(solution)/shard_map/ppermute | solution.py:29
  57.3 4.5 %collective-permute-done.16 = bf16[384,768]{1,0:T(8,128)(2,1)S(1)} collective-permute-done((bf16[384,768]{1,0:T(8,128)(2,1)S(1)}, bf16[384,768]{1,0:T(8,128)(2,1)S(1)}, u32[]{:S(2)}, u32[]{:S(2)}) %collective-permute-start.16) | collective-permute-done | bytes 589856 | tf_op jit(solution)/shard_map/ppermute | solution.py:29
  62.5 2.4 %collective-permute-done.13 = bf16[96,768]{1,0:T(8,128)(2,1)S(1)} collective-permute-done((bf16[96,768]{1,0:T(8,128)(2,1)S(1)}, bf16[96,768]{1,0:T(8,128)(2,1)S(1)}, u32[]{:S(2)}, u32[]{:S(2)}) %collective-permute-start.13) | collective-permute-done | bytes 147488 | tf_op jit(solution)/shard_map/ppermute | solution.py:29
  67.3 2.5 %collective-permute-start.20 = (bf16[96,768]{1,0:T(8,128)(2,1)S(1)}, bf16[96,768]{1,0:T(8,128)(2,1)S(1)}, u32[]{:S(2)}, u32[]{:S(2)}) collective-permute-start(bf16[96,768]{1,0:T(8,128)(2,1)S(1)} %pad_maximum_fusion.11), channel_id=1, source_target_pairs={{0,24},{4,28},{8,16},{12,20},{16,8},{20,12},{24,0},{28,4},{1,25},{... | collective-permute-start | bytes 442376 | tf_op jit(solution)/shard_map/ppermute | solution.py:29
  70.3 10.5 %collective-permute-done.21 = bf16[384,768]{1,0:T(8,128)(2,1)S(1)} collective-permute-done((bf16[384,768]{1,0:T(8,128)(2,1)S(1)}, bf16[384,768]{1,0:T(8,128)(2,1)S(1)}, u32[]{:S(2)}, u32[]{:S(2)}) %collective-permute-start.21) | collective-permute-done | bytes 589856 | tf_op jit(solution)/shard_map/ppermute | solution.py:29
  84.2 6.1 %gram_step.2 = (f32[384,128]{1,0:T(8,128)S(1)}, f32[384,128]{1,0:T(8,128)S(1)}, f32[384,128]{1,0:T(8,128)S(1)}, f32[1,1536]{1,0:T(1,128)S(1)}, f32[1,1536]{1,0:T(1,128)S(1)}, /*index=5*/f32[1,1536]{1,0:T(1,128)S(1)}) custom-call(bf16[384,768]{1,0:T(8,128)(2,1)S(1)} %get-tuple-element.141.refs_0_, bf16[384,768]{1,0:T(8,128)(2,1)S(1)} %get-tuple-element.65.refs_1_, ...), custom_call_target="tpu_custom_call" | custom-call | flops 8153726976 | bytes 8847360 | tf_op jit(solution)/shard_map/gram_step/pallas_call | solution.py:211
  91.5 3.6 %collective-permute-done.22 = bf16[304,768]{1,0:T(8,128)(2,1)S(1)} collective-permute-done((bf16[304,768]{1,0:T(8,128)(2,1)S(1)}, bf16[304,768]{1,0:T(8,128)(2,1)S(1)}, u32[]{:S(2)}, u32[]{:S(2)}) %collective-permute-start.22) | collective-permute-done | bytes 466976 | tf_op jit(solution)/shard_map/ppermute | solution.py:29
  95.1 2.2 %collective-permute-done.24 = bf16[80,768]{1,0:T(8,128)(2,1)S(1)} collective-permute-done((bf16[80,768]{1,0:T(8,128)(2,1)S(1)}, bf16[80,768]{1,0:T(8,128)(2,1)S(1)}, u32[]{:S(2)}, u32[]{:S(2)}) %collective-permute-start.24) | collective-permute-done | bytes 122912 | tf_op jit(solution)/shard_map/ppermute | solution.py:29
  97.4 2.4 %gram_step.3 = (f32[384,128]{1,0:T(8,128)S(1)}, f32[384,128]{1,0:T(8,128)S(1)}, f32[384,128]{1,0:T(8,128)S(1)}, f32[384,128]{1,0:T(8,128)S(1)}, f32[1,768]{1,0:T(1,128)S(1)}) custom-call(bf16[384,768]{1,0:T(8,128)(2,1)S(1)} %get-tuple-element.141.refs_0_, bf16[384,768]{1,0:T(8,128)(2,1)S(1)} %get-tuple-element.65.refs_1_, ...), custom_call_target="tpu_custom_call" | custom-call | flops 1811939328 | bytes 3538944 | tf_op jit(solution)/shard_map/gram_step/pallas_call | solution.py:211
  100.3 3.1 %gram_last.1 = f32[32,1,192]{2,1,0:T(1,128)S(1)} custom-call(s32[2]{0:T(128)S(1)} %pad_add_fusion.me_ref, bf16[384,768]{1,0:T(8,128)(2,1)S(1)} %get-tuple-element.141.refs_0_, bf16[384,768]{1,0:T(8,128)(2,1)S(1)} %get-tuple-element.65.refs_1_, bf16[384,768]{1,0:T(8,128)(2,1)S(1)} %get-tuple-element.70.refs_2_, ...), custom_call_target="tpu_custom_call" | custom-call | flops 1811939328 | bytes 3538944 | tf_op jit(solution)/shard_map/gram_last/pallas_call | solution.py:226
  103.4 9.8 %all_to_all.5.part_ref = f32[32,1,192]{2,1,0:T(1,128)} all-to-all(f32[32,1,192]{2,1,0:T(1,128)S(1)} %gram_last.1), channel_id=1, replica_groups=mesh['grp'=8,'blk'=4] {'grp','blk'}, dimensions={0} | all-to-all | bytes 49152 | tf_op jit(solution)/shard_map/all_to_all | solution.py:358
  113.2 2.3 %pick_rows.1 = f32[6,128]{1,0:T(8,128)} custom-call(s32[6,128]{1,0:T(8,128)} %bitcast.4, f32[32,1,192]{2,1,0:T(1,128)} %all_to_all.5.part_ref), custom_call_target="tpu_custom_call" | custom-call | tf_op jit(solution)/shard_map/pick_rows/pallas_call | solution.py:262
  (81 shorter events, 22.5 us)
Async XLA Ops:
  3.3 6.9 %collective-permute-start = (bf16[96,768]{1,0:T(8,128)(2,1)S(1)}, bf16[96,768]{1,0:T(8,128)(2,1)S(1)}, u32[]{:S(2)}, u32[]{:S(2)}) collective-permute-start(bf16[96,768]{1,0:T(8,128)(2,1)S(1)} %get-tuple-element.121), channel_id=1, source_target_pairs={{0,4},{4,0},{8,12},{12,8},{16,20},{20,16},{24,28},{28,24},{1,5},{5... | collective-permute-start | bytes 442376 | tf_op jit(solution)/shard_map/ppermute | solution.py:29
  9.0 6.8 %collective-permute-start.2 = (bf16[96,768]{1,0:T(8,128)(2,1)S(1)}, bf16[96,768]{1,0:T(8,128)(2,1)S(1)}, u32[]{:S(2)}, u32[]{:S(2)}) collective-permute-start(bf16[96,768]{1,0:T(8,128)(2,1)S(1)} %get-tuple-element.49), channel_id=1, source_target_pairs={{0,4},{4,0},{8,12},{12,8},{16,20},{20,16},{24,28},{28,24},{1,5},{5... | collective-permute-start | bytes 442376 | tf_op jit(solution)/shard_map/ppermute | solution.py:29
  10.2 19.1 %collective-permute-start.5 = (bf16[192,768]{1,0:T(8,128)(2,1)S(1)}, bf16[192,768]{1,0:T(8,128)(2,1)S(1)}, u32[]{:S(2)}, u32[]{:S(2)}) collective-permute-start(bf16[192,768]{1,0:T(8,128)(2,1)S(1)} %get-tuple-element.51), channel_id=1, source_target_pairs={{0,4},{4,0},{8,12},{12,8},{16,20},{20,16},{24,28},{28,24},{1,5},{5... | collective-permute-start | bytes 884744 | tf_op jit(solution)/shard_map/ppermute | solution.py:29
  12.4 7.6 %collective-permute-start.1 = (bf16[96,768]{1,0:T(8,128)(2,1)S(1)}, bf16[96,768]{1,0:T(8,128)(2,1)S(1)}, u32[]{:S(2)}, u32[]{:S(2)}) collective-permute-start(bf16[96,768]{1,0:T(8,128)(2,1)S(1)} %pad_maximum_fusion), channel_id=1, source_target_pairs={{0,8},{4,12},{8,0},{12,4},{16,24},{20,28},{24,16},{28,20},{1,9},{5... | collective-permute-start | bytes 442376 | tf_op jit(solution)/shard_map/ppermute | solution.py:29
  13.8 15.6 %collective-permute-start.6 = (bf16[192,768]{1,0:T(8,128)(2,1)S(1)}, bf16[192,768]{1,0:T(8,128)(2,1)S(1)}, u32[]{:S(2)}, u32[]{:S(2)}) collective-permute-start(bf16[192,768]{1,0:T(8,128)(2,1)S(1)} %get-tuple-element.53), channel_id=1, source_target_pairs={{0,4},{4,0},{8,12},{12,8},{16,20},{20,16},{24,28},{28,24},{1,5},{5... | collective-permute-start | bytes 884744 | tf_op jit(solution)/shard_map/ppermute | solution.py:29
  15.9 11.9 %collective-permute-start.3 = (bf16[96,768]{1,0:T(8,128)(2,1)S(1)}, bf16[96,768]{1,0:T(8,128)(2,1)S(1)}, u32[]{:S(2)}, u32[]{:S(2)}) collective-permute-start(bf16[96,768]{1,0:T(8,128)(2,1)S(1)} %pad_maximum_fusion.1), channel_id=1, source_target_pairs={{0,16},{4,20},{8,24},{12,28},{16,0},{20,4},{24,8},{28,12},{1,17},{... | collective-permute-start | bytes 442376 | tf_op jit(solution)/shard_map/ppermute | solution.py:29
  18.5 9.2 %collective-permute-start.4 = (bf16[96,768]{1,0:T(8,128)(2,1)S(1)}, bf16[96,768]{1,0:T(8,128)(2,1)S(1)}, u32[]{:S(2)}, u32[]{:S(2)}) collective-permute-start(bf16[96,768]{1,0:T(8,128)(2,1)S(1)} %pad_maximum_fusion.2), channel_id=1, source_target_pairs={{0,24},{4,28},{8,16},{12,20},{16,8},{20,12},{24,0},{28,4},{1,25},{... | collective-permute-start | bytes 442376 | tf_op jit(solution)/shard_map/ppermute | solution.py:29
  27.8 10.6 %collective-permute-start.10 = (bf16[384,768]{1,0:T(8,128)(2,1)S(1)}, bf16[384,768]{1,0:T(8,128)(2,1)S(1)}, u32[]{:S(2)}, u32[]{:S(2)}) collective-permute-start(bf16[384,768]{1,0:T(8,128)(2,1)S(1)} %get-tuple-element.141.refs_0_), channel_id=1, source_target_pairs={{0,2},{1,3},{2,0},{3,1},{4,6},{5,7},{6,4},{7,5},{8,10},{9,11},{10,... | collective-permute-start | bytes 1769480 | tf_op jit(solution)/shard_map/ppermute | solution.py:29
  29.4 9.0 %collective-permute-start.7 = (bf16[96,768]{1,0:T(8,128)(2,1)S(1)}, bf16[96,768]{1,0:T(8,128)(2,1)S(1)}, u32[]{:S(2)}, u32[]{:S(2)}) collective-permute-start(bf16[96,768]{1,0:T(8,128)(2,1)S(1)} %pad_maximum_fusion.3), channel_id=1, source_target_pairs={{0,8},{4,12},{8,0},{12,4},{16,24},{20,28},{24,16},{28,20},{1,9},{5... | collective-permute-start | bytes 442376 | tf_op jit(solution)/shard_map/ppermute | solution.py:29
  31.7 13.9 %collective-permute-start.8 = (bf16[96,768]{1,0:T(8,128)(2,1)S(1)}, bf16[96,768]{1,0:T(8,128)(2,1)S(1)}, u32[]{:S(2)}, u32[]{:S(2)}) collective-permute-start(bf16[96,768]{1,0:T(8,128)(2,1)S(1)} %pad_maximum_fusion.4), channel_id=1, source_target_pairs={{0,16},{4,20},{8,24},{12,28},{16,0},{20,4},{24,8},{28,12},{1,17},{... | collective-permute-start | bytes 442376 | tf_op jit(solution)/shard_map/ppermute | solution.py:29
  33.7 11.9 %collective-permute-start.9 = (bf16[96,768]{1,0:T(8,128)(2,1)S(1)}, bf16[96,768]{1,0:T(8,128)(2,1)S(1)}, u32[]{:S(2)}, u32[]{:S(2)}) collective-permute-start(bf16[96,768]{1,0:T(8,128)(2,1)S(1)} %pad_maximum_fusion.5), channel_id=1, source_target_pairs={{0,24},{4,28},{8,16},{12,20},{16,8},{20,12},{24,0},{28,4},{1,25},{... | collective-permute-start | bytes 442376 | tf_op jit(solution)/shard_map/ppermute | solution.py:29
  45.6 9.5 %collective-permute-start.11 = (bf16[768,768]{1,0:T(8,128)(2,1)S(1)}, bf16[768,768]{1,0:T(8,128)(2,1)S(1)}, u32[]{:S(2)}, u32[]{:S(2)}) collective-permute-start(bf16[768,768]{1,0:T(8,128)(2,1)S(1)} %constant_dynamic-update-slice_fusion.10.refs_3_), channel_id=1, source_target_pairs={{0,1},{1,0},{2,3},{3,2},{4,5},{5,4},{6,7},{7,6},{8,9},{9,8},{10,11... | collective-permute-start | bytes 3538952 | tf_op jit(solution)/shard_map/ppermute | solution.py:29
  45.7 9.5 %collective-permute-start.12 = (bf16[192,768]{1,0:T(8,128)(2,1)S(1)}, bf16[192,768]{1,0:T(8,128)(2,1)S(1)}, u32[]{:S(2)}, u32[]{:S(2)}) collective-permute-start(bf16[192,768]{1,0:T(8,128)(2,1)S(1)} %get-tuple-element.60), channel_id=1, source_target_pairs={{0,4},{4,0},{8,12},{12,8},{16,20},{20,16},{24,28},{28,24},{1,5},{5... | collective-permute-start | bytes 884744 | tf_op jit(solution)/shard_map/ppermute | solution.py:29
  46.3 15.5 %collective-permute-start.16 = (bf16[384,768]{1,0:T(8,128)(2,1)S(1)}, bf16[384,768]{1,0:T(8,128)(2,1)S(1)}, u32[]{:S(2)}, u32[]{:S(2)}) collective-permute-start(bf16[384,768]{1,0:T(8,128)(2,1)S(1)} %get-tuple-element.65.refs_1_), channel_id=1, source_target_pairs={{0,2},{1,3},{2,0},{3,1},{4,6},{5,7},{6,4},{7,5},{8,10},{9,11},{10,... | collective-permute-start | bytes 1769480 | tf_op jit(solution)/shard_map/ppermute | solution.py:29
  47.6 14.9 %collective-permute-start.14 = (bf16[96,768]{1,0:T(8,128)(2,1)S(1)}, bf16[96,768]{1,0:T(8,128)(2,1)S(1)}, u32[]{:S(2)}, u32[]{:S(2)}) collective-permute-start(bf16[96,768]{1,0:T(8,128)(2,1)S(1)} %pad_maximum_fusion.7), channel_id=1, source_target_pairs={{0,16},{4,20},{8,24},{12,28},{16,0},{20,4},{24,8},{28,12},{1,17},{... | collective-permute-start | bytes 442376 | tf_op jit(solution)/shard_map/ppermute | solution.py:29
  51.5 11.0 %collective-permute-start.15 = (bf16[96,768]{1,0:T(8,128)(2,1)S(1)}, bf16[96,768]{1,0:T(8,128)(2,1)S(1)}, u32[]{:S(2)}, u32[]{:S(2)}) collective-permute-start(bf16[96,768]{1,0:T(8,128)(2,1)S(1)} %pad_maximum_fusion.8), channel_id=1, source_target_pairs={{0,24},{4,28},{8,16},{12,20},{16,8},{20,12},{24,0},{28,4},{1,25},{... | collective-permute-start | bytes 442376 | tf_op jit(solution)/shard_map/ppermute | solution.py:29
  55.1 9.8 %collective-permute-start.13 = (bf16[96,768]{1,0:T(8,128)(2,1)S(1)}, bf16[96,768]{1,0:T(8,128)(2,1)S(1)}, u32[]{:S(2)}, u32[]{:S(2)}) collective-permute-start(bf16[96,768]{1,0:T(8,128)(2,1)S(1)} %pad_maximum_fusion.6), channel_id=1, source_target_pairs={{0,8},{4,12},{8,0},{12,4},{16,24},{20,28},{24,16},{28,20},{1,9},{5... | collective-permute-start | bytes 442376 | tf_op jit(solution)/shard_map/ppermute | solution.py:29
  65.0 4.8 %collective-permute-start.17 = (bf16[768,768]{1,0:T(8,128)(2,1)S(1)}, bf16[768,768]{1,0:T(8,128)(2,1)S(1)}, u32[]{:S(2)}, u32[]{:S(2)}) collective-permute-start(bf16[768,768]{1,0:T(8,128)(2,1)S(1)} %constant_dynamic-update-slice_fusion.21.refs_5_), channel_id=1, source_target_pairs={{0,1},{1,0},{2,3},{3,2},{4,5},{5,4},{6,7},{7,6},{8,9},{9,8},{10,11... | collective-permute-start | bytes 3538952 | tf_op jit(solution)/shard_map/ppermute | solution.py:29
  65.1 15.8 %collective-permute-start.21 = (bf16[384,768]{1,0:T(8,128)(2,1)S(1)}, bf16[384,768]{1,0:T(8,128)(2,1)S(1)}, u32[]{:S(2)}, u32[]{:S(2)}) collective-permute-start(bf16[384,768]{1,0:T(8,128)(2,1)S(1)} %get-tuple-element.70.refs_2_), channel_id=1, source_target_pairs={{0,2},{1,3},{2,0},{3,1},{4,6},{5,7},{6,4},{7,5},{8,10},{9,11},{10,... | collective-permute-start | bytes 1769480 | tf_op jit(solution)/shard_map/ppermute | solution.py:29
  66.7 14.2 %collective-permute-start.19 = (bf16[96,768]{1,0:T(8,128)(2,1)S(1)}, bf16[96,768]{1,0:T(8,128)(2,1)S(1)}, u32[]{:S(2)}, u32[]{:S(2)}) collective-permute-start(bf16[96,768]{1,0:T(8,128)(2,1)S(1)} %pad_maximum_fusion.10), channel_id=1, source_target_pairs={{0,16},{4,20},{8,24},{12,28},{16,0},{20,4},{24,8},{28,12},{1,17},{... | collective-permute-start | bytes 442376 | tf_op jit(solution)/shard_map/ppermute | solution.py:29
  67.3 13.6 %collective-permute-start.20 = (bf16[96,768]{1,0:T(8,128)(2,1)S(1)}, bf16[96,768]{1,0:T(8,128)(2,1)S(1)}, u32[]{:S(2)}, u32[]{:S(2)}) collective-permute-start(bf16[96,768]{1,0:T(8,128)(2,1)S(1)} %pad_maximum_fusion.11), channel_id=1, source_target_pairs={{0,24},{4,28},{8,16},{12,20},{16,8},{20,12},{24,0},{28,4},{1,25},{... | collective-permute-start | bytes 442376 | tf_op jit(solution)/shard_map/ppermute | solution.py:29
  69.8 11.6 %collective-permute-start.18 = (bf16[96,768]{1,0:T(8,128)(2,1)S(1)}, bf16[96,768]{1,0:T(8,128)(2,1)S(1)}, u32[]{:S(2)}, u32[]{:S(2)}) collective-permute-start(bf16[96,768]{1,0:T(8,128)(2,1)S(1)} %pad_maximum_fusion.9), channel_id=1, source_target_pairs={{0,8},{4,12},{8,0},{12,4},{16,24},{20,28},{24,16},{28,20},{1,9},{5... | collective-permute-start | bytes 442376 | tf_op jit(solution)/shard_map/ppermute | solution.py:29
  81.5 13.6 %collective-permute-start.22 = (bf16[304,768]{1,0:T(8,128)(2,1)S(1)}, bf16[304,768]{1,0:T(8,128)(2,1)S(1)}, u32[]{:S(2)}, u32[]{:S(2)}) collective-permute-start(bf16[304,768]{1,0:T(8,128)(2,1)S(1)} %slice.160), channel_id=1, source_target_pairs={{0,2},{1,3},{2,0},{3,1},{4,6},{5,7},{6,4},{7,5},{8,10},{9,11},{10,... | collective-permute-start | bytes 1400840 | tf_op jit(solution)/shard_map/ppermute | solution.py:29
  90.3 7.0 %collective-permute-start.24 = (bf16[80,768]{1,0:T(8,128)(2,1)S(1)}, bf16[80,768]{1,0:T(8,128)(2,1)S(1)}, u32[]{:S(2)}, u32[]{:S(2)}) collective-permute-start(bf16[80,768]{1,0:T(8,128)(2,1)S(1)} %slice.161), channel_id=1, source_target_pairs={{0,2},{1,3},{2,0},{3,1},{4,6},{5,7},{6,4},{7,5},{8,10},{9,11},{10,... | collective-permute-start | bytes 368648 | tf_op jit(solution)/shard_map/ppermute | solution.py:29
  (4 other events, 7.7 us)

commit v19 on v17

--- a/solution.py
+++ b/solution.py
@@ -302,6 +302,8 @@
             early += [("x", step - 2, 0)]
         if step >= 2 and z == 1:
             early += [("c", step - 2)]
+        if step == 1 and z == 1:
+            early += [("y", k + 1) for k in range(2, count)]
         send(("z", step, z), block(step, z), "grp", groups, 2 * z, *early)
 
     def collect(step):

time: 130 us -> 115 us (0.88)
  waiting for transfers between devices: 64.3 us -> 49.2 us
    ppermute x26, waiting for transfers between devices: 64.3 us -> 49.2 us  [swap(): return lax.ppermute(value, axis, [(i, i ^ bit) for i in range(size)])]
  transfers between devices with their start and end apart: 26 -> 26, of which waited for: 17 -> 12; matrix products, arithmetic and copies ran while one was open for 1% -> 1% of each run, Pallas kernels for 9% -> 10%
where the time goes in v19:
time: 115 us; the launch traced here: 114 us
  waiting for transfers between devices  49.2 us (43%)
  starting transfers between devices  33.7 us (29%)
  Pallas kernels  17.8 us (15%)
  blocking collectives  10.5 us (9%)
  local copies, waits for them, and re-layouts  2.64 us (2%)
    ppermute x26, waiting for transfers between devices, swap(): return lax.ppermute(value, axis, [(i, i ^ bit) for i in range(size)])  49.2 us
    ppermute x26, starting transfers between devices, swap(): return lax.ppermute(value, axis, [(i, i ^ bit) for i in range(size)])  33.7 us
    all_to_all x1, blocking collectives, on_device(): homeward = lax.all_to_all(result, ('grp', 'blk'), 0, 0, tiled=True)  10.5 us
    pallas_call x2, Pallas kernels, gram_step(): pl.pallas_call(functools.partial(gram_kernel, first, step, pieces), in_sp...  8.48 us
    pallas_call x1, Pallas kernels, gram_last(): pl.pallas_call(functools.partial(gram_last_kernel, step, relatives, chunk...  3.09 us
    pallas_call x1, Pallas kernels, head(): pl.pallas_call(functools.partial(rest_kernel, capacity, chunks, groups),...  2.61 us
    unnamed x25, local copies, waits for them, and re-layouts  2.44 us
    pallas_call x1, Pallas kernels, tail(): pl.pallas_call(functools.partial(tail_kernel, capacity, members), in_spec...  2.33 us
  transfers between devices with their start and end apart: 26, of which 12 were waited for; matrix products, arithmetic and copies ran while one was open for 1% of the time, Pallas kernels for 10%

profile of v19, /device:TPU:0, one launch (start us, length us, event | category | flops | bytes accessed | tf_op | source)
XLA Modules:
  0.0 114.4 jit_solution(1473500242145787400)
XLA Ops:
  3.3 3.0 %collective-permute-start = (bf16[96,768]{1,0:T(8,128)(2,1)S(1)}, bf16[96,768]{1,0:T(8,128)(2,1)S(1)}, u32[]{:S(2)}, u32[]{:S(2)}) collective-permute-start(bf16[96,768]{1,0:T(8,128)(2,1)S(1)} %get-tuple-element.121), channel_id=1, source_target_pairs={{0,4},{4,0},{8,12},{12,8},{16,20},{20,16},{24,28},{28,24},{1,5},{5... | collective-permute-start | bytes 442376 | tf_op jit(solution)/shard_map/ppermute | solution.py:29
  6.4 2.6 %place_rest.1 = (bf16[192,768]{1,0:T(8,128)(2,1)S(1)}, bf16[192,768]{1,0:T(8,128)(2,1)S(1)}, bf16[192,768]{1,0:T(8,128)(2,1)S(1)}, bf16[192,768]{1,0:T(8,128)(2,...) custom-call(s32[2]{0:T(128)S(1)} %pad_add_fusion.me_ref, ...), custom_call_target="tpu_custom_call" | custom-call | flops 1585446912 | bytes 3244032 | tf_op jit(solution)/shard_map/place_rest/pallas_call | solution.py:99
  10.2 2.1 %collective-permute-start.5 = (bf16[192,768]{1,0:T(8,128)(2,1)S(1)}, bf16[192,768]{1,0:T(8,128)(2,1)S(1)}, u32[]{:S(2)}, u32[]{:S(2)}) collective-permute-start(bf16[192,768]{1,0:T(8,128)(2,1)S(1)} %get-tuple-element.51), channel_id=1, source_target_pairs={{0,4},{4,0},{8,12},{12,8},{16,20},{20,16},{24,28},{28,24},{1,5},{5... | collective-permute-start | bytes 884744 | tf_op jit(solution)/shard_map/ppermute | solution.py:29
  14.1 1.7 %collective-permute-done.2 = bf16[96,768]{1,0:T(8,128)(2,1)S(1)} collective-permute-done((bf16[96,768]{1,0:T(8,128)(2,1)S(1)}, bf16[96,768]{1,0:T(8,128)(2,1)S(1)}, u32[]{:S(2)}, u32[]{:S(2)}) %collective-permute-start.2) | collective-permute-done | bytes 147488 | tf_op jit(solution)/shard_map/ppermute | solution.py:29
  15.9 2.7 %collective-permute-start.3 = (bf16[96,768]{1,0:T(8,128)(2,1)S(1)}, bf16[96,768]{1,0:T(8,128)(2,1)S(1)}, u32[]{:S(2)}, u32[]{:S(2)}) collective-permute-start(bf16[96,768]{1,0:T(8,128)(2,1)S(1)} %pad_maximum_fusion.1), channel_id=1, source_target_pairs={{0,16},{4,20},{8,24},{12,28},{16,0},{20,4},{24,8},{28,12},{1,17},{... | collective-permute-start | bytes 442376 | tf_op jit(solution)/shard_map/ppermute | solution.py:29
  20.0 7.8 %collective-permute-done.3 = bf16[96,768]{1,0:T(8,128)(2,1)S(1)} collective-permute-done((bf16[96,768]{1,0:T(8,128)(2,1)S(1)}, bf16[96,768]{1,0:T(8,128)(2,1)S(1)}, u32[]{:S(2)}, u32[]{:S(2)}) %collective-permute-start.3) | collective-permute-done | bytes 147488 | tf_op jit(solution)/shard_map/ppermute | solution.py:29
  27.8 1.6 %collective-permute-start.11 = (bf16[384,768]{1,0:T(8,128)(2,1)S(1)}, bf16[384,768]{1,0:T(8,128)(2,1)S(1)}, u32[]{:S(2)}, u32[]{:S(2)}) collective-permute-start(bf16[384,768]{1,0:T(8,128)(2,1)S(1)} %get-tuple-element.141.refs_0_), channel_id=1, source_target_pairs={{0,2},{1,3},{2,0},{3,1},{4,6},{5,7},{6,4},{7,5},{8,10},{9,11},{10,... | collective-permute-start | bytes 1769480 | tf_op jit(solution)/shard_map/ppermute | solution.py:29
  30.5 4.1 %collective-permute-start.9 = (bf16[96,768]{1,0:T(8,128)(2,1)S(1)}, bf16[96,768]{1,0:T(8,128)(2,1)S(1)}, u32[]{:S(2)}, u32[]{:S(2)}) collective-permute-start(bf16[96,768]{1,0:T(8,128)(2,1)S(1)} %pad_maximum_fusion.4), channel_id=1, source_target_pairs={{0,16},{4,20},{8,24},{12,28},{16,0},{20,4},{24,8},{28,12},{1,17},{... | collective-permute-start | bytes 442376 | tf_op jit(solution)/shard_map/ppermute | solution.py:29
  36.1 3.4 %collective-permute-start.8 = (bf16[96,768]{1,0:T(8,128)(2,1)S(1)}, bf16[96,768]{1,0:T(8,128)(2,1)S(1)}, u32[]{:S(2)}, u32[]{:S(2)}) collective-permute-start(bf16[96,768]{1,0:T(8,128)(2,1)S(1)} %pad_maximum_fusion.3), channel_id=1, source_target_pairs={{0,8},{4,12},{8,0},{12,4},{16,24},{20,28},{24,16},{28,20},{1,9},{5... | collective-permute-start | bytes 442376 | tf_op jit(solution)/shard_map/ppermute | solution.py:29
  39.5 5.0 %collective-permute-done.9 = bf16[96,768]{1,0:T(8,128)(2,1)S(1)} collective-permute-done((bf16[96,768]{1,0:T(8,128)(2,1)S(1)}, bf16[96,768]{1,0:T(8,128)(2,1)S(1)}, u32[]{:S(2)}, u32[]{:S(2)}) %collective-permute-start.9) | collective-permute-done | bytes 147488 | tf_op jit(solution)/shard_map/ppermute | solution.py:29
  44.6 2.9 %collective-permute-done.8 = bf16[96,768]{1,0:T(8,128)(2,1)S(1)} collective-permute-done((bf16[96,768]{1,0:T(8,128)(2,1)S(1)}, bf16[96,768]{1,0:T(8,128)(2,1)S(1)}, u32[]{:S(2)}, u32[]{:S(2)}) %collective-permute-start.8) | collective-permute-done | bytes 147488 | tf_op jit(solution)/shard_map/ppermute | solution.py:29
  48.5 2.8 %collective-permute-start.15 = (bf16[96,768]{1,0:T(8,128)(2,1)S(1)}, bf16[96,768]{1,0:T(8,128)(2,1)S(1)}, u32[]{:S(2)}, u32[]{:S(2)}) collective-permute-start(bf16[96,768]{1,0:T(8,128)(2,1)S(1)} %pad_maximum_fusion.8), channel_id=1, source_target_pairs={{0,24},{4,28},{8,16},{12,20},{16,8},{20,12},{24,0},{28,4},{1,25},{... | collective-permute-start | bytes 442376 | tf_op jit(solution)/shard_map/ppermute | solution.py:29
  51.6 11.8 %collective-permute-done.16 = bf16[384,768]{1,0:T(8,128)(2,1)S(1)} collective-permute-done((bf16[384,768]{1,0:T(8,128)(2,1)S(1)}, bf16[384,768]{1,0:T(8,128)(2,1)S(1)}, u32[]{:S(2)}, u32[]{:S(2)}) %collective-permute-start.16) | collective-permute-done | bytes 589856 | tf_op jit(solution)/shard_map/ppermute | solution.py:29
  64.6 1.5 %collective-permute-start.19 = (bf16[96,768]{1,0:T(8,128)(2,1)S(1)}, bf16[96,768]{1,0:T(8,128)(2,1)S(1)}, u32[]{:S(2)}, u32[]{:S(2)}) collective-permute-start(bf16[96,768]{1,0:T(8,128)(2,1)S(1)} %pad_maximum_fusion.10), channel_id=1, source_target_pairs={{0,16},{4,20},{8,24},{12,28},{16,0},{20,4},{24,8},{28,12},{1,17},{... | collective-permute-start | bytes 442376 | tf_op jit(solution)/shard_map/ppermute | solution.py:29
  66.1 3.4 %collective-permute-start.20 = (bf16[96,768]{1,0:T(8,128)(2,1)S(1)}, bf16[96,768]{1,0:T(8,128)(2,1)S(1)}, u32[]{:S(2)}, u32[]{:S(2)}) collective-permute-start(bf16[96,768]{1,0:T(8,128)(2,1)S(1)} %pad_maximum_fusion.11), channel_id=1, source_target_pairs={{0,24},{4,28},{8,16},{12,20},{16,8},{20,12},{24,0},{28,4},{1,25},{... | collective-permute-start | bytes 442376 | tf_op jit(solution)/shard_map/ppermute | solution.py:29
  69.5 9.9 %collective-permute-done.21 = bf16[384,768]{1,0:T(8,128)(2,1)S(1)} collective-permute-done((bf16[384,768]{1,0:T(8,128)(2,1)S(1)}, bf16[384,768]{1,0:T(8,128)(2,1)S(1)}, u32[]{:S(2)}, u32[]{:S(2)}) %collective-permute-start.21) | collective-permute-done | bytes 589856 | tf_op jit(solution)/shard_map/ppermute | solution.py:29
  80.7 1.7 %collective-permute-done.23.refs_8_ = bf16[768,768]{1,0:T(8,128)(2,1)S(1)} collective-permute-done((bf16[768,768]{1,0:T(8,128)(2,1)S(1)}, bf16[768,768]{1,0:T(8,128)(2,1)S(1)}, u32[]{:S(2)}, u32[]{:S(2)}) %collective-permute-start.23) | collective-permute-done | bytes 1179680 | tf_op jit(solution)/shard_map/ppermute | solution.py:29
  82.4 6.1 %gram_step.2 = (f32[384,128]{1,0:T(8,128)S(1)}, f32[384,128]{1,0:T(8,128)S(1)}, f32[384,128]{1,0:T(8,128)S(1)}, f32[1,1536]{1,0:T(1,128)S(1)}, f32[1,1536]{1,0:T(1,128)S(1)}, /*index=5*/f32[1,1536]{1,0:T(1,128)S(1)}) custom-call(bf16[384,768]{1,0:T(8,128)(2,1)S(1)} %get-tuple-element.141.refs_0_, bf16[384,768]{1,0:T(8,128)(2,1)S(1)} %get-tuple-element.65.refs_1_, ...), custom_call_target="tpu_custom_call" | custom-call | flops 8153726976 | bytes 8847360 | tf_op jit(solution)/shard_map/gram_step/pallas_call | solution.py:211
  89.5 3.8 %collective-permute-done.22 = bf16[304,768]{1,0:T(8,128)(2,1)S(1)} collective-permute-done((bf16[304,768]{1,0:T(8,128)(2,1)S(1)}, bf16[304,768]{1,0:T(8,128)(2,1)S(1)}, u32[]{:S(2)}, u32[]{:S(2)}) %collective-permute-start.22) | collective-permute-done | bytes 466976 | tf_op jit(solution)/shard_map/ppermute | solution.py:29
  93.3 2.2 %collective-permute-done.24 = bf16[80,768]{1,0:T(8,128)(2,1)S(1)} collective-permute-done((bf16[80,768]{1,0:T(8,128)(2,1)S(1)}, bf16[80,768]{1,0:T(8,128)(2,1)S(1)}, u32[]{:S(2)}, u32[]{:S(2)}) %collective-permute-start.24) | collective-permute-done | bytes 122912 | tf_op jit(solution)/shard_map/ppermute | solution.py:29
  95.6 2.4 %gram_step.3 = (f32[384,128]{1,0:T(8,128)S(1)}, f32[384,128]{1,0:T(8,128)S(1)}, f32[384,128]{1,0:T(8,128)S(1)}, f32[384,128]{1,0:T(8,128)S(1)}, f32[1,768]{1,0:T(1,128)S(1)}) custom-call(bf16[384,768]{1,0:T(8,128)(2,1)S(1)} %get-tuple-element.141.refs_0_, bf16[384,768]{1,0:T(8,128)(2,1)S(1)} %get-tuple-element.65.refs_1_, ...), custom_call_target="tpu_custom_call" | custom-call | flops 1811939328 | bytes 3538944 | tf_op jit(solution)/shard_map/gram_step/pallas_call | solution.py:211
  98.4 3.1 %gram_last.1 = f32[32,1,192]{2,1,0:T(1,128)S(1)} custom-call(s32[2]{0:T(128)S(1)} %pad_add_fusion.me_ref, bf16[384,768]{1,0:T(8,128)(2,1)S(1)} %get-tuple-element.141.refs_0_, bf16[384,768]{1,0:T(8,128)(2,1)S(1)} %get-tuple-element.65.refs_1_, bf16[384,768]{1,0:T(8,128)(2,1)S(1)} %get-tuple-element.70.refs_2_, ...), custom_call_target="tpu_custom_call" | custom-call | flops 1811939328 | bytes 3538944 | tf_op jit(solution)/shard_map/gram_last/pallas_call | solution.py:226
  101.5 10.5 %all_to_all.5.part_ref = f32[32,1,192]{2,1,0:T(1,128)} all-to-all(f32[32,1,192]{2,1,0:T(1,128)S(1)} %gram_last.1), channel_id=1, replica_groups=mesh['grp'=8,'blk'=4] {'grp','blk'}, dimensions={0} | all-to-all | bytes 49152 | tf_op jit(solution)/shard_map/all_to_all | solution.py:358
  112.0 2.3 %pick_rows.1 = f32[6,128]{1,0:T(8,128)} custom-call(s32[6,128]{1,0:T(8,128)} %bitcast.4, f32[32,1,192]{2,1,0:T(1,128)} %all_to_all.5.part_ref), custom_call_target="tpu_custom_call" | custom-call | tf_op jit(solution)/shard_map/pick_rows/pallas_call | solution.py:262
  (81 shorter events, 15.8 us)
Async XLA Ops:
  3.3 6.9 %collective-permute-start = (bf16[96,768]{1,0:T(8,128)(2,1)S(1)}, bf16[96,768]{1,0:T(8,128)(2,1)S(1)}, u32[]{:S(2)}, u32[]{:S(2)}) collective-permute-start(bf16[96,768]{1,0:T(8,128)(2,1)S(1)} %get-tuple-element.121), channel_id=1, source_target_pairs={{0,4},{4,0},{8,12},{12,8},{16,20},{20,16},{24,28},{28,24},{1,5},{5... | collective-permute-start | bytes 442376 | tf_op jit(solution)/shard_map/ppermute | solution.py:29
  9.0 6.8 %collective-permute-start.2 = (bf16[96,768]{1,0:T(8,128)(2,1)S(1)}, bf16[96,768]{1,0:T(8,128)(2,1)S(1)}, u32[]{:S(2)}, u32[]{:S(2)}) collective-permute-start(bf16[96,768]{1,0:T(8,128)(2,1)S(1)} %get-tuple-element.49), channel_id=1, source_target_pairs={{0,4},{4,0},{8,12},{12,8},{16,20},{20,16},{24,28},{28,24},{1,5},{5... | collective-permute-start | bytes 442376 | tf_op jit(solution)/shard_map/ppermute | solution.py:29
  10.2 20.2 %collective-permute-start.5 = (bf16[192,768]{1,0:T(8,128)(2,1)S(1)}, bf16[192,768]{1,0:T(8,128)(2,1)S(1)}, u32[]{:S(2)}, u32[]{:S(2)}) collective-permute-start(bf16[192,768]{1,0:T(8,128)(2,1)S(1)} %get-tuple-element.51), channel_id=1, source_target_pairs={{0,4},{4,0},{8,12},{12,8},{16,20},{20,16},{24,28},{28,24},{1,5},{5... | collective-permute-start | bytes 884744 | tf_op jit(solution)/shard_map/ppermute | solution.py:29
  12.4 7.6 %collective-permute-start.1 = (bf16[96,768]{1,0:T(8,128)(2,1)S(1)}, bf16[96,768]{1,0:T(8,128)(2,1)S(1)}, u32[]{:S(2)}, u32[]{:S(2)}) collective-permute-start(bf16[96,768]{1,0:T(8,128)(2,1)S(1)} %pad_maximum_fusion), channel_id=1, source_target_pairs={{0,8},{4,12},{8,0},{12,4},{16,24},{20,28},{24,16},{28,20},{1,9},{5... | collective-permute-start | bytes 442376 | tf_op jit(solution)/shard_map/ppermute | solution.py:29
  13.8 15.5 %collective-permute-start.6 = (bf16[192,768]{1,0:T(8,128)(2,1)S(1)}, bf16[192,768]{1,0:T(8,128)(2,1)S(1)}, u32[]{:S(2)}, u32[]{:S(2)}) collective-permute-start(bf16[192,768]{1,0:T(8,128)(2,1)S(1)} %get-tuple-element.53), channel_id=1, source_target_pairs={{0,4},{4,0},{8,12},{12,8},{16,20},{20,16},{24,28},{28,24},{1,5},{5... | collective-permute-start | bytes 884744 | tf_op jit(solution)/shard_map/ppermute | solution.py:29
  15.9 11.9 %collective-permute-start.3 = (bf16[96,768]{1,0:T(8,128)(2,1)S(1)}, bf16[96,768]{1,0:T(8,128)(2,1)S(1)}, u32[]{:S(2)}, u32[]{:S(2)}) collective-permute-start(bf16[96,768]{1,0:T(8,128)(2,1)S(1)} %pad_maximum_fusion.1), channel_id=1, source_target_pairs={{0,16},{4,20},{8,24},{12,28},{16,0},{20,4},{24,8},{28,12},{1,17},{... | collective-permute-start | bytes 442376 | tf_op jit(solution)/shard_map/ppermute | solution.py:29
  18.5 9.2 %collective-permute-start.4 = (bf16[96,768]{1,0:T(8,128)(2,1)S(1)}, bf16[96,768]{1,0:T(8,128)(2,1)S(1)}, u32[]{:S(2)}, u32[]{:S(2)}) collective-permute-start(bf16[96,768]{1,0:T(8,128)(2,1)S(1)} %pad_maximum_fusion.2), channel_id=1, source_target_pairs={{0,24},{4,28},{8,16},{12,20},{16,8},{20,12},{24,0},{28,4},{1,25},{... | collective-permute-start | bytes 442376 | tf_op jit(solution)/shard_map/ppermute | solution.py:29
  27.8 11.7 %collective-permute-start.11 = (bf16[384,768]{1,0:T(8,128)(2,1)S(1)}, bf16[384,768]{1,0:T(8,128)(2,1)S(1)}, u32[]{:S(2)}, u32[]{:S(2)}) collective-permute-start(bf16[384,768]{1,0:T(8,128)(2,1)S(1)} %get-tuple-element.141.refs_0_), channel_id=1, source_target_pairs={{0,2},{1,3},{2,0},{3,1},{4,6},{5,7},{6,4},{7,5},{8,10},{9,11},{10,... | collective-permute-start | bytes 1769480 | tf_op jit(solution)/shard_map/ppermute | solution.py:29
  29.3 6.7 %collective-permute-start.7 = (bf16[192,768]{1,0:T(8,128)(2,1)S(1)}, bf16[192,768]{1,0:T(8,128)(2,1)S(1)}, u32[]{:S(2)}, u32[]{:S(2)}) collective-permute-start(bf16[192,768]{1,0:T(8,128)(2,1)S(1)} %get-tuple-element.55), channel_id=1, source_target_pairs={{0,4},{4,0},{8,12},{12,8},{16,20},{20,16},{24,28},{28,24},{1,5},{5... | collective-permute-start | bytes 884744 | tf_op jit(solution)/shard_map/ppermute | solution.py:29
  30.5 14.1 %collective-permute-start.9 = (bf16[96,768]{1,0:T(8,128)(2,1)S(1)}, bf16[96,768]{1,0:T(8,128)(2,1)S(1)}, u32[]{:S(2)}, u32[]{:S(2)}) collective-permute-start(bf16[96,768]{1,0:T(8,128)(2,1)S(1)} %pad_maximum_fusion.4), channel_id=1, source_target_pairs={{0,16},{4,20},{8,24},{12,28},{16,0},{20,4},{24,8},{28,12},{1,17},{... | collective-permute-start | bytes 442376 | tf_op jit(solution)/shard_map/ppermute | solution.py:29
  34.5 10.0 %collective-permute-start.10 = (bf16[96,768]{1,0:T(8,128)(2,1)S(1)}, bf16[96,768]{1,0:T(8,128)(2,1)S(1)}, u32[]{:S(2)}, u32[]{:S(2)}) collective-permute-start(bf16[96,768]{1,0:T(8,128)(2,1)S(1)} %pad_maximum_fusion.5), channel_id=1, source_target_pairs={{0,24},{4,28},{8,16},{12,20},{16,8},{20,12},{24,0},{28,4},{1,25},{... | collective-permute-start | bytes 442376 | tf_op jit(solution)/shard_map/ppermute | solution.py:29
  36.1 11.4 %collective-permute-start.8 = (bf16[96,768]{1,0:T(8,128)(2,1)S(1)}, bf16[96,768]{1,0:T(8,128)(2,1)S(1)}, u32[]{:S(2)}, u32[]{:S(2)}) collective-permute-start(bf16[96,768]{1,0:T(8,128)(2,1)S(1)} %pad_maximum_fusion.3), channel_id=1, source_target_pairs={{0,8},{4,12},{8,0},{12,4},{16,24},{20,28},{24,16},{28,20},{1,9},{5... | collective-permute-start | bytes 442376 | tf_op jit(solution)/shard_map/ppermute | solution.py:29
  47.4 3.9 %collective-permute-start.12 = (bf16[768,768]{1,0:T(8,128)(2,1)S(1)}, bf16[768,768]{1,0:T(8,128)(2,1)S(1)}, u32[]{:S(2)}, u32[]{:S(2)}) collective-permute-start(bf16[768,768]{1,0:T(8,128)(2,1)S(1)} %constant_dynamic-update-slice_fusion.10.refs_3_), channel_id=1, source_target_pairs={{0,1},{1,0},{2,3},{3,2},{4,5},{5,4},{6,7},{7,6},{8,9},{9,8},{10,11... | collective-permute-start | bytes 3538952 | tf_op jit(solution)/shard_map/ppermute | solution.py:29
  47.6 15.8 %collective-permute-start.16 = (bf16[384,768]{1,0:T(8,128)(2,1)S(1)}, bf16[384,768]{1,0:T(8,128)(2,1)S(1)}, u32[]{:S(2)}, u32[]{:S(2)}) collective-permute-start(bf16[384,768]{1,0:T(8,128)(2,1)S(1)} %get-tuple-element.65.refs_1_), channel_id=1, source_target_pairs={{0,2},{1,3},{2,0},{3,1},{4,6},{5,7},{6,4},{7,5},{8,10},{9,11},{10,... | collective-permute-start | bytes 1769480 | tf_op jit(solution)/shard_map/ppermute | solution.py:29
  48.0 15.4 %collective-permute-start.14 = (bf16[96,768]{1,0:T(8,128)(2,1)S(1)}, bf16[96,768]{1,0:T(8,128)(2,1)S(1)}, u32[]{:S(2)}, u32[]{:S(2)}) collective-permute-start(bf16[96,768]{1,0:T(8,128)(2,1)S(1)} %pad_maximum_fusion.7), channel_id=1, source_target_pairs={{0,16},{4,20},{8,24},{12,28},{16,0},{20,4},{24,8},{28,12},{1,17},{... | collective-permute-start | bytes 442376 | tf_op jit(solution)/shard_map/ppermute | solution.py:29
  48.5 14.9 %collective-permute-start.15 = (bf16[96,768]{1,0:T(8,128)(2,1)S(1)}, bf16[96,768]{1,0:T(8,128)(2,1)S(1)}, u32[]{:S(2)}, u32[]{:S(2)}) collective-permute-start(bf16[96,768]{1,0:T(8,128)(2,1)S(1)} %pad_maximum_fusion.8), channel_id=1, source_target_pairs={{0,24},{4,28},{8,16},{12,20},{16,8},{20,12},{24,0},{28,4},{1,25},{... | collective-permute-start | bytes 442376 | tf_op jit(solution)/shard_map/ppermute | solution.py:29
  51.3 12.1 %collective-permute-start.13 = (bf16[96,768]{1,0:T(8,128)(2,1)S(1)}, bf16[96,768]{1,0:T(8,128)(2,1)S(1)}, u32[]{:S(2)}, u32[]{:S(2)}) collective-permute-start(bf16[96,768]{1,0:T(8,128)(2,1)S(1)} %pad_maximum_fusion.6), channel_id=1, source_target_pairs={{0,8},{4,12},{8,0},{12,4},{16,24},{20,28},{24,16},{28,20},{1,9},{5... | collective-permute-start | bytes 442376 | tf_op jit(solution)/shard_map/ppermute | solution.py:29
  63.4 6.1 %collective-permute-start.17 = (bf16[768,768]{1,0:T(8,128)(2,1)S(1)}, bf16[768,768]{1,0:T(8,128)(2,1)S(1)}, u32[]{:S(2)}, u32[]{:S(2)}) collective-permute-start(bf16[768,768]{1,0:T(8,128)(2,1)S(1)} %constant_dynamic-update-slice_fusion.21.refs_5_), channel_id=1, source_target_pairs={{0,1},{1,0},{2,3},{3,2},{4,5},{5,4},{6,7},{7,6},{8,9},{9,8},{10,11... | collective-permute-start | bytes 3538952 | tf_op jit(solution)/shard_map/ppermute | solution.py:29
  63.6 15.8 %collective-permute-start.21 = (bf16[384,768]{1,0:T(8,128)(2,1)S(1)}, bf16[384,768]{1,0:T(8,128)(2,1)S(1)}, u32[]{:S(2)}, u32[]{:S(2)}) collective-permute-start(bf16[384,768]{1,0:T(8,128)(2,1)S(1)} %get-tuple-element.70.refs_2_), channel_id=1, source_target_pairs={{0,2},{1,3},{2,0},{3,1},{4,6},{5,7},{6,4},{7,5},{8,10},{9,11},{10,... | collective-permute-start | bytes 1769480 | tf_op jit(solution)/shard_map/ppermute | solution.py:29
  64.6 14.9 %collective-permute-start.19 = (bf16[96,768]{1,0:T(8,128)(2,1)S(1)}, bf16[96,768]{1,0:T(8,128)(2,1)S(1)}, u32[]{:S(2)}, u32[]{:S(2)}) collective-permute-start(bf16[96,768]{1,0:T(8,128)(2,1)S(1)} %pad_maximum_fusion.10), channel_id=1, source_target_pairs={{0,16},{4,20},{8,24},{12,28},{16,0},{20,4},{24,8},{28,12},{1,17},{... | collective-permute-start | bytes 442376 | tf_op jit(solution)/shard_map/ppermute | solution.py:29
  66.1 13.4 %collective-permute-start.20 = (bf16[96,768]{1,0:T(8,128)(2,1)S(1)}, bf16[96,768]{1,0:T(8,128)(2,1)S(1)}, u32[]{:S(2)}, u32[]{:S(2)}) collective-permute-start(bf16[96,768]{1,0:T(8,128)(2,1)S(1)} %pad_maximum_fusion.11), channel_id=1, source_target_pairs={{0,24},{4,28},{8,16},{12,20},{16,8},{20,12},{24,0},{28,4},{1,25},{... | collective-permute-start | bytes 442376 | tf_op jit(solution)/shard_map/ppermute | solution.py:29
  69.5 10.0 %collective-permute-start.18 = (bf16[96,768]{1,0:T(8,128)(2,1)S(1)}, bf16[96,768]{1,0:T(8,128)(2,1)S(1)}, u32[]{:S(2)}, u32[]{:S(2)}) collective-permute-start(bf16[96,768]{1,0:T(8,128)(2,1)S(1)} %pad_maximum_fusion.9), channel_id=1, source_target_pairs={{0,8},{4,12},{8,0},{12,4},{16,24},{20,28},{24,16},{28,20},{1,9},{5... | collective-permute-start | bytes 442376 | tf_op jit(solution)/shard_map/ppermute | solution.py:29
  79.7 13.6 %collective-permute-start.22 = (bf16[304,768]{1,0:T(8,128)(2,1)S(1)}, bf16[304,768]{1,0:T(8,128)(2,1)S(1)}, u32[]{:S(2)}, u32[]{:S(2)}) collective-permute-start(bf16[304,768]{1,0:T(8,128)(2,1)S(1)} %slice.160), channel_id=1, source_target_pairs={{0,2},{1,3},{2,0},{3,1},{4,6},{5,7},{6,4},{7,5},{8,10},{9,11},{10,... | collective-permute-start | bytes 1400840 | tf_op jit(solution)/shard_map/ppermute | solution.py:29
  88.5 7.0 %collective-permute-start.24 = (bf16[80,768]{1,0:T(8,128)(2,1)S(1)}, bf16[80,768]{1,0:T(8,128)(2,1)S(1)}, u32[]{:S(2)}, u32[]{:S(2)}) collective-permute-start(bf16[80,768]{1,0:T(8,128)(2,1)S(1)} %slice.161), channel_id=1, source_target_pairs={{0,2},{1,3},{2,0},{3,1},{4,6},{5,7},{6,4},{7,5},{8,10},{9,11},{10,... | collective-permute-start | bytes 368648 | tf_op jit(solution)/shard_map/ppermute | solution.py:29
  (4 other events, 7.8 us)

commit v20 on v19

--- a/solution.py
+++ b/solution.py
@@ -303,7 +303,7 @@
         if step >= 2 and z == 1:
             early += [("c", step - 2)]
         if step == 1 and z == 1:
-            early += [("y", k + 1) for k in range(2, count)]
+            early += [("y", 3)]
         send(("z", step, z), block(step, z), "grp", groups, 2 * z, *early)
 
     def collect(step):
@@ -319,6 +319,8 @@
         for part in range(len(cuts) - 1):
             value = owns[step][cuts[part] : cuts[part + 1]]
             early = parts if part == 0 else between[part - 1]
+            if step == 1 and part == 0:
+                early = early + [("y", count)]
             send(("x", step, part), value, "blk", members, 2, *early)
 
     def send_c(step, *early):

time: 115 us -> 123 us (1.070)
  waiting for transfers between devices: 49.2 us -> 57.1 us
    ppermute x26, waiting for transfers between devices: 49.2 us -> 57.1 us  [swap(): return lax.ppermute(value, axis, [(i, i ^ bit) for i in range(size)])]
  transfers between devices with their start and end apart: 26 -> 26, of which waited for: 12 -> 14; matrix products, arithmetic and copies ran while one was open for 1% -> 1% of each run, Pallas kernels for 10% -> 9%
where the time goes in v20:
time: 123 us
  waiting for transfers between devices  57.1 us (46%)
  starting transfers between devices  33.1 us (27%)
  Pallas kernels  17.8 us (14%)
  blocking collectives  11.5 us (9%)
  local copies, waits for them, and re-layouts  2.64 us (2%)
    ppermute x26, waiting for transfers between devices, swap(): return lax.ppermute(value, axis, [(i, i ^ bit) for i in range(size)])  57.1 us
    ppermute x26, starting transfers between devices, swap(): return lax.ppermute(value, axis, [(i, i ^ bit) for i in range(size)])  33.1 us
    all_to_all x1, blocking collectives, on_device(): homeward = lax.all_to_all(result, ('grp', 'blk'), 0, 0, tiled=True)  11.5 us
    pallas_call x2, Pallas kernels, gram_step(): pl.pallas_call(functools.partial(gram_kernel, first, step, pieces), in_sp...  8.48 us
    pallas_call x1, Pallas kernels, gram_last(): pl.pallas_call(functools.partial(gram_last_kernel, step, relatives, chunk...  3.09 us
    pallas_call x1, Pallas kernels, head(): pl.pallas_call(functools.partial(rest_kernel, capacity, chunks, groups),...  2.61 us
  transfers between devices with their start and end apart: 26, of which 14 were waited for; matrix products, arithmetic and copies ran while one was open for 1% of the time, Pallas kernels for 9%

profile of v20, /device:TPU:0, one launch (start us, length us, event | category | flops | bytes accessed | tf_op | source)
XLA Modules:
  0.0 122.6 jit_solution(3282858699307547667)
XLA Ops:
  3.3 3.0 %collective-permute-start = (bf16[96,768]{1,0:T(8,128)(2,1)S(1)}, bf16[96,768]{1,0:T(8,128)(2,1)S(1)}, u32[]{:S(2)}, u32[]{:S(2)}) collective-permute-start(bf16[96,768]{1,0:T(8,128)(2,1)S(1)} %get-tuple-element.121), channel_id=1, source_target_pairs={{0,4},{4,0},{8,12},{12,8},{16,20},{20,16},{24,28},{28,24},{1,5},{5... | collective-permute-start | bytes 442376 | tf_op jit(solution)/shard_map/ppermute | solution.py:29
  6.4 2.6 %place_rest.1 = (bf16[192,768]{1,0:T(8,128)(2,1)S(1)}, bf16[192,768]{1,0:T(8,128)(2,1)S(1)}, bf16[192,768]{1,0:T(8,128)(2,1)S(1)}, bf16[192,768]{1,0:T(8,128)(2,...) custom-call(s32[2]{0:T(128)S(1)} %pad_add_fusion.me_ref, ...), custom_call_target="tpu_custom_call" | custom-call | flops 1585446912 | bytes 3244032 | tf_op jit(solution)/shard_map/place_rest/pallas_call | solution.py:99
  10.2 2.1 %collective-permute-start.5 = (bf16[192,768]{1,0:T(8,128)(2,1)S(1)}, bf16[192,768]{1,0:T(8,128)(2,1)S(1)}, u32[]{:S(2)}, u32[]{:S(2)}) collective-permute-start(bf16[192,768]{1,0:T(8,128)(2,1)S(1)} %get-tuple-element.51), channel_id=1, source_target_pairs={{0,4},{4,0},{8,12},{12,8},{16,20},{20,16},{24,28},{28,24},{1,5},{5... | collective-permute-start | bytes 884744 | tf_op jit(solution)/shard_map/ppermute | solution.py:29
  14.1 1.7 %collective-permute-done.2 = bf16[96,768]{1,0:T(8,128)(2,1)S(1)} collective-permute-done((bf16[96,768]{1,0:T(8,128)(2,1)S(1)}, bf16[96,768]{1,0:T(8,128)(2,1)S(1)}, u32[]{:S(2)}, u32[]{:S(2)}) %collective-permute-start.2) | collective-permute-done | bytes 147488 | tf_op jit(solution)/shard_map/ppermute | solution.py:29
  15.9 2.7 %collective-permute-start.3 = (bf16[96,768]{1,0:T(8,128)(2,1)S(1)}, bf16[96,768]{1,0:T(8,128)(2,1)S(1)}, u32[]{:S(2)}, u32[]{:S(2)}) collective-permute-start(bf16[96,768]{1,0:T(8,128)(2,1)S(1)} %pad_maximum_fusion.1), channel_id=1, source_target_pairs={{0,16},{4,20},{8,24},{12,28},{16,0},{20,4},{24,8},{28,12},{1,17},{... | collective-permute-start | bytes 442376 | tf_op jit(solution)/shard_map/ppermute | solution.py:29
  20.0 7.8 %collective-permute-done.3 = bf16[96,768]{1,0:T(8,128)(2,1)S(1)} collective-permute-done((bf16[96,768]{1,0:T(8,128)(2,1)S(1)}, bf16[96,768]{1,0:T(8,128)(2,1)S(1)}, u32[]{:S(2)}, u32[]{:S(2)}) %collective-permute-start.3) | collective-permute-done | bytes 147488 | tf_op jit(solution)/shard_map/ppermute | solution.py:29
  29.4 2.3 %collective-permute-start.7 = (bf16[96,768]{1,0:T(8,128)(2,1)S(1)}, bf16[96,768]{1,0:T(8,128)(2,1)S(1)}, u32[]{:S(2)}, u32[]{:S(2)}) collective-permute-start(bf16[96,768]{1,0:T(8,128)(2,1)S(1)} %pad_maximum_fusion.3), channel_id=1, source_target_pairs={{0,8},{4,12},{8,0},{12,4},{16,24},{20,28},{24,16},{28,20},{1,9},{5... | collective-permute-start | bytes 442376 | tf_op jit(solution)/shard_map/ppermute | solution.py:29
  31.7 2.0 %collective-permute-start.8 = (bf16[96,768]{1,0:T(8,128)(2,1)S(1)}, bf16[96,768]{1,0:T(8,128)(2,1)S(1)}, u32[]{:S(2)}, u32[]{:S(2)}) collective-permute-start(bf16[96,768]{1,0:T(8,128)(2,1)S(1)} %pad_maximum_fusion.4), channel_id=1, source_target_pairs={{0,16},{4,20},{8,24},{12,28},{16,0},{20,4},{24,8},{28,12},{1,17},{... | collective-permute-start | bytes 442376 | tf_op jit(solution)/shard_map/ppermute | solution.py:29
  35.2 3.2 %collective-permute-done.10 = bf16[384,768]{1,0:T(8,128)(2,1)S(1)} collective-permute-done((bf16[384,768]{1,0:T(8,128)(2,1)S(1)}, bf16[384,768]{1,0:T(8,128)(2,1)S(1)}, u32[]{:S(2)}, u32[]{:S(2)}) %collective-permute-start.10) | collective-permute-done | bytes 589856 | tf_op jit(solution)/shard_map/ppermute | solution.py:29
  38.4 7.2 %collective-permute-done.8 = bf16[96,768]{1,0:T(8,128)(2,1)S(1)} collective-permute-done((bf16[96,768]{1,0:T(8,128)(2,1)S(1)}, bf16[96,768]{1,0:T(8,128)(2,1)S(1)}, u32[]{:S(2)}, u32[]{:S(2)}) %collective-permute-start.8) | collective-permute-done | bytes 147488 | tf_op jit(solution)/shard_map/ppermute | solution.py:29
  46.3 8.9 %collective-permute-done.15 = bf16[192,768]{1,0:T(8,128)(2,1)S(1)} collective-permute-done((bf16[192,768]{1,0:T(8,128)(2,1)S(1)}, bf16[192,768]{1,0:T(8,128)(2,1)S(1)}, u32[]{:S(2)}, u32[]{:S(2)}) %collective-permute-start.15) | collective-permute-done | bytes 294944 | tf_op jit(solution)/shard_map/ppermute | solution.py:29
  55.8 3.4 %collective-permute-start.13 = (bf16[96,768]{1,0:T(8,128)(2,1)S(1)}, bf16[96,768]{1,0:T(8,128)(2,1)S(1)}, u32[]{:S(2)}, u32[]{:S(2)}) collective-permute-start(bf16[96,768]{1,0:T(8,128)(2,1)S(1)} %pad_maximum_fusion.7), channel_id=1, source_target_pairs={{0,16},{4,20},{8,24},{12,28},{16,0},{20,4},{24,8},{28,12},{1,17},{... | collective-permute-start | bytes 442376 | tf_op jit(solution)/shard_map/ppermute | solution.py:29
  60.4 9.7 %collective-permute-done.16 = bf16[384,768]{1,0:T(8,128)(2,1)S(1)} collective-permute-done((bf16[384,768]{1,0:T(8,128)(2,1)S(1)}, bf16[384,768]{1,0:T(8,128)(2,1)S(1)}, u32[]{:S(2)}, u32[]{:S(2)}) %collective-permute-start.16) | collective-permute-done | bytes 589856 | tf_op jit(solution)/shard_map/ppermute | solution.py:29
  70.4 1.6 %collective-permute-start.21 = (bf16[384,768]{1,0:T(8,128)(2,1)S(1)}, bf16[384,768]{1,0:T(8,128)(2,1)S(1)}, u32[]{:S(2)}, u32[]{:S(2)}) collective-permute-start(bf16[384,768]{1,0:T(8,128)(2,1)S(1)} %get-tuple-element.70.refs_2_), channel_id=1, source_target_pairs={{0,2},{1,3},{2,0},{3,1},{4,6},{5,7},{6,4},{7,5},{8,10},{9,11},{10,... | collective-permute-start | bytes 1769480 | tf_op jit(solution)/shard_map/ppermute | solution.py:29
  72.1 2.5 %collective-permute-start.19 = (bf16[96,768]{1,0:T(8,128)(2,1)S(1)}, bf16[96,768]{1,0:T(8,128)(2,1)S(1)}, u32[]{:S(2)}, u32[]{:S(2)}) collective-permute-start(bf16[96,768]{1,0:T(8,128)(2,1)S(1)} %pad_maximum_fusion.10), channel_id=1, source_target_pairs={{0,16},{4,20},{8,24},{12,28},{16,0},{20,4},{24,8},{28,12},{1,17},{... | collective-permute-start | bytes 442376 | tf_op jit(solution)/shard_map/ppermute | solution.py:29
  74.6 2.3 %collective-permute-start.20 = (bf16[96,768]{1,0:T(8,128)(2,1)S(1)}, bf16[96,768]{1,0:T(8,128)(2,1)S(1)}, u32[]{:S(2)}, u32[]{:S(2)}) collective-permute-start(bf16[96,768]{1,0:T(8,128)(2,1)S(1)} %pad_maximum_fusion.11), channel_id=1, source_target_pairs={{0,24},{4,28},{8,16},{12,20},{16,8},{20,12},{24,0},{28,4},{1,25},{... | collective-permute-start | bytes 442376 | tf_op jit(solution)/shard_map/ppermute | solution.py:29
  76.9 9.3 %collective-permute-done.21 = bf16[384,768]{1,0:T(8,128)(2,1)S(1)} collective-permute-done((bf16[384,768]{1,0:T(8,128)(2,1)S(1)}, bf16[384,768]{1,0:T(8,128)(2,1)S(1)}, u32[]{:S(2)}, u32[]{:S(2)}) %collective-permute-start.21) | collective-permute-done | bytes 589856 | tf_op jit(solution)/shard_map/ppermute | solution.py:29
  89.6 6.1 %gram_step.2 = (f32[384,128]{1,0:T(8,128)S(1)}, f32[384,128]{1,0:T(8,128)S(1)}, f32[384,128]{1,0:T(8,128)S(1)}, f32[1,1536]{1,0:T(1,128)S(1)}, f32[1,1536]{1,0:T(1,128)S(1)}, /*index=5*/f32[1,1536]{1,0:T(1,128)S(1)}) custom-call(bf16[384,768]{1,0:T(8,128)(2,1)S(1)} %get-tuple-element.141.refs_0_, bf16[384,768]{1,0:T(8,128)(2,1)S(1)} %get-tuple-element.65.refs_1_, ...), custom_call_target="tpu_custom_call" | custom-call | flops 8153726976 | bytes 8847360 | tf_op jit(solution)/shard_map/gram_step/pallas_call | solution.py:211
  96.9 3.6 %collective-permute-done.22 = bf16[304,768]{1,0:T(8,128)(2,1)S(1)} collective-permute-done((bf16[304,768]{1,0:T(8,128)(2,1)S(1)}, bf16[304,768]{1,0:T(8,128)(2,1)S(1)}, u32[]{:S(2)}, u32[]{:S(2)}) %collective-permute-start.22) | collective-permute-done | bytes 466976 | tf_op jit(solution)/shard_map/ppermute | solution.py:29
  100.5 2.2 %collective-permute-done.24 = bf16[80,768]{1,0:T(8,128)(2,1)S(1)} collective-permute-done((bf16[80,768]{1,0:T(8,128)(2,1)S(1)}, bf16[80,768]{1,0:T(8,128)(2,1)S(1)}, u32[]{:S(2)}, u32[]{:S(2)}) %collective-permute-start.24) | collective-permute-done | bytes 122912 | tf_op jit(solution)/shard_map/ppermute | solution.py:29
  102.8 2.4 %gram_step.3 = (f32[384,128]{1,0:T(8,128)S(1)}, f32[384,128]{1,0:T(8,128)S(1)}, f32[384,128]{1,0:T(8,128)S(1)}, f32[384,128]{1,0:T(8,128)S(1)}, f32[1,768]{1,0:T(1,128)S(1)}) custom-call(bf16[384,768]{1,0:T(8,128)(2,1)S(1)} %get-tuple-element.141.refs_0_, bf16[384,768]{1,0:T(8,128)(2,1)S(1)} %get-tuple-element.65.refs_1_, ...), custom_call_target="tpu_custom_call" | custom-call | flops 1811939328 | bytes 3538944 | tf_op jit(solution)/shard_map/gram_step/pallas_call | solution.py:211
  105.7 3.1 %gram_last.1 = f32[32,1,192]{2,1,0:T(1,128)S(1)} custom-call(s32[2]{0:T(128)S(1)} %pad_add_fusion.me_ref, bf16[384,768]{1,0:T(8,128)(2,1)S(1)} %get-tuple-element.141.refs_0_, bf16[384,768]{1,0:T(8,128)(2,1)S(1)} %get-tuple-element.65.refs_1_, bf16[384,768]{1,0:T(8,128)(2,1)S(1)} %get-tuple-element.70.refs_2_, ...), custom_call_target="tpu_custom_call" | custom-call | flops 1811939328 | bytes 3538944 | tf_op jit(solution)/shard_map/gram_last/pallas_call | solution.py:226
  108.8 11.5 %all_to_all.5.part_ref = f32[32,1,192]{2,1,0:T(1,128)} all-to-all(f32[32,1,192]{2,1,0:T(1,128)S(1)} %gram_last.1), channel_id=1, replica_groups=mesh['grp'=8,'blk'=4] {'grp','blk'}, dimensions={0} | all-to-all | bytes 49152 | tf_op jit(solution)/shard_map/all_to_all | solution.py:360
  120.3 2.3 %pick_rows.1 = f32[6,128]{1,0:T(8,128)} custom-call(s32[6,128]{1,0:T(8,128)} %bitcast.4, f32[32,1,192]{2,1,0:T(1,128)} %all_to_all.5.part_ref), custom_call_target="tpu_custom_call" | custom-call | tf_op jit(solution)/shard_map/pick_rows/pallas_call | solution.py:262
  (81 shorter events, 18.9 us)
Async XLA Ops:
  3.3 6.9 %collective-permute-start = (bf16[96,768]{1,0:T(8,128)(2,1)S(1)}, bf16[96,768]{1,0:T(8,128)(2,1)S(1)}, u32[]{:S(2)}, u32[]{:S(2)}) collective-permute-start(bf16[96,768]{1,0:T(8,128)(2,1)S(1)} %get-tuple-element.121), channel_id=1, source_target_pairs={{0,4},{4,0},{8,12},{12,8},{16,20},{20,16},{24,28},{28,24},{1,5},{5... | collective-permute-start | bytes 442376 | tf_op jit(solution)/shard_map/ppermute | solution.py:29
  9.0 6.8 %collective-permute-start.2 = (bf16[96,768]{1,0:T(8,128)(2,1)S(1)}, bf16[96,768]{1,0:T(8,128)(2,1)S(1)}, u32[]{:S(2)}, u32[]{:S(2)}) collective-permute-start(bf16[96,768]{1,0:T(8,128)(2,1)S(1)} %get-tuple-element.49), channel_id=1, source_target_pairs={{0,4},{4,0},{8,12},{12,8},{16,20},{20,16},{24,28},{28,24},{1,5},{5... | collective-permute-start | bytes 442376 | tf_op jit(solution)/shard_map/ppermute | solution.py:29
  10.2 19.1 %collective-permute-start.5 = (bf16[192,768]{1,0:T(8,128)(2,1)S(1)}, bf16[192,768]{1,0:T(8,128)(2,1)S(1)}, u32[]{:S(2)}, u32[]{:S(2)}) collective-permute-start(bf16[192,768]{1,0:T(8,128)(2,1)S(1)} %get-tuple-element.51), channel_id=1, source_target_pairs={{0,4},{4,0},{8,12},{12,8},{16,20},{20,16},{24,28},{28,24},{1,5},{5... | collective-permute-start | bytes 884744 | tf_op jit(solution)/shard_map/ppermute | solution.py:29
  12.4 7.6 %collective-permute-start.1 = (bf16[96,768]{1,0:T(8,128)(2,1)S(1)}, bf16[96,768]{1,0:T(8,128)(2,1)S(1)}, u32[]{:S(2)}, u32[]{:S(2)}) collective-permute-start(bf16[96,768]{1,0:T(8,128)(2,1)S(1)} %pad_maximum_fusion), channel_id=1, source_target_pairs={{0,8},{4,12},{8,0},{12,4},{16,24},{20,28},{24,16},{28,20},{1,9},{5... | collective-permute-start | bytes 442376 | tf_op jit(solution)/shard_map/ppermute | solution.py:29
  13.8 15.6 %collective-permute-start.6 = (bf16[192,768]{1,0:T(8,128)(2,1)S(1)}, bf16[192,768]{1,0:T(8,128)(2,1)S(1)}, u32[]{:S(2)}, u32[]{:S(2)}) collective-permute-start(bf16[192,768]{1,0:T(8,128)(2,1)S(1)} %get-tuple-element.53), channel_id=1, source_target_pairs={{0,4},{4,0},{8,12},{12,8},{16,20},{20,16},{24,28},{28,24},{1,5},{5... | collective-permute-start | bytes 884744 | tf_op jit(solution)/shard_map/ppermute | solution.py:29
  15.9 11.9 %collective-permute-start.3 = (bf16[96,768]{1,0:T(8,128)(2,1)S(1)}, bf16[96,768]{1,0:T(8,128)(2,1)S(1)}, u32[]{:S(2)}, u32[]{:S(2)}) collective-permute-start(bf16[96,768]{1,0:T(8,128)(2,1)S(1)} %pad_maximum_fusion.1), channel_id=1, source_target_pairs={{0,16},{4,20},{8,24},{12,28},{16,0},{20,4},{24,8},{28,12},{1,17},{... | collective-permute-start | bytes 442376 | tf_op jit(solution)/shard_map/ppermute | solution.py:29
  18.5 9.2 %collective-permute-start.4 = (bf16[96,768]{1,0:T(8,128)(2,1)S(1)}, bf16[96,768]{1,0:T(8,128)(2,1)S(1)}, u32[]{:S(2)}, u32[]{:S(2)}) collective-permute-start(bf16[96,768]{1,0:T(8,128)(2,1)S(1)} %pad_maximum_fusion.2), channel_id=1, source_target_pairs={{0,24},{4,28},{8,16},{12,20},{16,8},{20,12},{24,0},{28,4},{1,25},{... | collective-permute-start | bytes 442376 | tf_op jit(solution)/shard_map/ppermute | solution.py:29
  27.8 10.6 %collective-permute-start.10 = (bf16[384,768]{1,0:T(8,128)(2,1)S(1)}, bf16[384,768]{1,0:T(8,128)(2,1)S(1)}, u32[]{:S(2)}, u32[]{:S(2)}) collective-permute-start(bf16[384,768]{1,0:T(8,128)(2,1)S(1)} %get-tuple-element.141.refs_0_), channel_id=1, source_target_pairs={{0,2},{1,3},{2,0},{3,1},{4,6},{5,7},{6,4},{7,5},{8,10},{9,11},{10,... | collective-permute-start | bytes 1769480 | tf_op jit(solution)/shard_map/ppermute | solution.py:29
  29.4 9.0 %collective-permute-start.7 = (bf16[96,768]{1,0:T(8,128)(2,1)S(1)}, bf16[96,768]{1,0:T(8,128)(2,1)S(1)}, u32[]{:S(2)}, u32[]{:S(2)}) collective-permute-start(bf16[96,768]{1,0:T(8,128)(2,1)S(1)} %pad_maximum_fusion.3), channel_id=1, source_target_pairs={{0,8},{4,12},{8,0},{12,4},{16,24},{20,28},{24,16},{28,20},{1,9},{5... | collective-permute-start | bytes 442376 | tf_op jit(solution)/shard_map/ppermute | solution.py:29
  31.7 13.9 %collective-permute-start.8 = (bf16[96,768]{1,0:T(8,128)(2,1)S(1)}, bf16[96,768]{1,0:T(8,128)(2,1)S(1)}, u32[]{:S(2)}, u32[]{:S(2)}) collective-permute-start(bf16[96,768]{1,0:T(8,128)(2,1)S(1)} %pad_maximum_fusion.4), channel_id=1, source_target_pairs={{0,16},{4,20},{8,24},{12,28},{16,0},{20,4},{24,8},{28,12},{1,17},{... | collective-permute-start | bytes 442376 | tf_op jit(solution)/shard_map/ppermute | solution.py:29
  33.7 11.9 %collective-permute-start.9 = (bf16[96,768]{1,0:T(8,128)(2,1)S(1)}, bf16[96,768]{1,0:T(8,128)(2,1)S(1)}, u32[]{:S(2)}, u32[]{:S(2)}) collective-permute-start(bf16[96,768]{1,0:T(8,128)(2,1)S(1)} %pad_maximum_fusion.5), channel_id=1, source_target_pairs={{0,24},{4,28},{8,16},{12,20},{16,8},{20,12},{24,0},{28,4},{1,25},{... | collective-permute-start | bytes 442376 | tf_op jit(solution)/shard_map/ppermute | solution.py:29
  45.6 14.8 %collective-permute-start.11 = (bf16[768,768]{1,0:T(8,128)(2,1)S(1)}, bf16[768,768]{1,0:T(8,128)(2,1)S(1)}, u32[]{:S(2)}, u32[]{:S(2)}) collective-permute-start(bf16[768,768]{1,0:T(8,128)(2,1)S(1)} %constant_dynamic-update-slice_fusion.10.refs_3_), channel_id=1, source_target_pairs={{0,1},{1,0},{2,3},{3,2},{4,5},{5,4},{6,7},{7,6},{8,9},{9,8},{10,11... | collective-permute-start | bytes 3538952 | tf_op jit(solution)/shard_map/ppermute | solution.py:29
  45.7 9.5 %collective-permute-start.15 = (bf16[192,768]{1,0:T(8,128)(2,1)S(1)}, bf16[192,768]{1,0:T(8,128)(2,1)S(1)}, u32[]{:S(2)}, u32[]{:S(2)}) collective-permute-start(bf16[192,768]{1,0:T(8,128)(2,1)S(1)} %get-tuple-element.64), channel_id=1, source_target_pairs={{0,4},{4,0},{8,12},{12,8},{16,20},{20,16},{24,28},{28,24},{1,5},{5... | collective-permute-start | bytes 884744 | tf_op jit(solution)/shard_map/ppermute | solution.py:29
  55.1 15.0 %collective-permute-start.16 = (bf16[384,768]{1,0:T(8,128)(2,1)S(1)}, bf16[384,768]{1,0:T(8,128)(2,1)S(1)}, u32[]{:S(2)}, u32[]{:S(2)}) collective-permute-start(bf16[384,768]{1,0:T(8,128)(2,1)S(1)} %get-tuple-element.65.refs_1_), channel_id=1, source_target_pairs={{0,2},{1,3},{2,0},{3,1},{4,6},{5,7},{6,4},{7,5},{8,10},{9,11},{10,... | collective-permute-start | bytes 1769480 | tf_op jit(solution)/shard_map/ppermute | solution.py:29
  55.8 14.4 %collective-permute-start.13 = (bf16[96,768]{1,0:T(8,128)(2,1)S(1)}, bf16[96,768]{1,0:T(8,128)(2,1)S(1)}, u32[]{:S(2)}, u32[]{:S(2)}) collective-permute-start(bf16[96,768]{1,0:T(8,128)(2,1)S(1)} %pad_maximum_fusion.7), channel_id=1, source_target_pairs={{0,16},{4,20},{8,24},{12,28},{16,0},{20,4},{24,8},{28,12},{1,17},{... | collective-permute-start | bytes 442376 | tf_op jit(solution)/shard_map/ppermute | solution.py:29
  59.2 11.0 %collective-permute-start.14 = (bf16[96,768]{1,0:T(8,128)(2,1)S(1)}, bf16[96,768]{1,0:T(8,128)(2,1)S(1)}, u32[]{:S(2)}, u32[]{:S(2)}) collective-permute-start(bf16[96,768]{1,0:T(8,128)(2,1)S(1)} %pad_maximum_fusion.8), channel_id=1, source_target_pairs={{0,24},{4,28},{8,16},{12,20},{16,8},{20,12},{24,0},{28,4},{1,25},{... | collective-permute-start | bytes 442376 | tf_op jit(solution)/shard_map/ppermute | solution.py:29
  60.4 9.9 %collective-permute-start.12 = (bf16[96,768]{1,0:T(8,128)(2,1)S(1)}, bf16[96,768]{1,0:T(8,128)(2,1)S(1)}, u32[]{:S(2)}, u32[]{:S(2)}) collective-permute-start(bf16[96,768]{1,0:T(8,128)(2,1)S(1)} %pad_maximum_fusion.6), channel_id=1, source_target_pairs={{0,8},{4,12},{8,0},{12,4},{16,24},{20,28},{24,16},{28,20},{1,9},{5... | collective-permute-start | bytes 442376 | tf_op jit(solution)/shard_map/ppermute | solution.py:29
  70.3 6.6 %collective-permute-start.17 = (bf16[768,768]{1,0:T(8,128)(2,1)S(1)}, bf16[768,768]{1,0:T(8,128)(2,1)S(1)}, u32[]{:S(2)}, u32[]{:S(2)}) collective-permute-start(bf16[768,768]{1,0:T(8,128)(2,1)S(1)} %constant_dynamic-update-slice_fusion.21.refs_5_), channel_id=1, source_target_pairs={{0,1},{1,0},{2,3},{3,2},{4,5},{5,4},{6,7},{7,6},{8,9},{9,8},{10,11... | collective-permute-start | bytes 3538952 | tf_op jit(solution)/shard_map/ppermute | solution.py:29
  70.4 15.8 %collective-permute-start.21 = (bf16[384,768]{1,0:T(8,128)(2,1)S(1)}, bf16[384,768]{1,0:T(8,128)(2,1)S(1)}, u32[]{:S(2)}, u32[]{:S(2)}) collective-permute-start(bf16[384,768]{1,0:T(8,128)(2,1)S(1)} %get-tuple-element.70.refs_2_), channel_id=1, source_target_pairs={{0,2},{1,3},{2,0},{3,1},{4,6},{5,7},{6,4},{7,5},{8,10},{9,11},{10,... | collective-permute-start | bytes 1769480 | tf_op jit(solution)/shard_map/ppermute | solution.py:29
  72.1 14.2 %collective-permute-start.19 = (bf16[96,768]{1,0:T(8,128)(2,1)S(1)}, bf16[96,768]{1,0:T(8,128)(2,1)S(1)}, u32[]{:S(2)}, u32[]{:S(2)}) collective-permute-start(bf16[96,768]{1,0:T(8,128)(2,1)S(1)} %pad_maximum_fusion.10), channel_id=1, source_target_pairs={{0,16},{4,20},{8,24},{12,28},{16,0},{20,4},{24,8},{28,12},{1,17},{... | collective-permute-start | bytes 442376 | tf_op jit(solution)/shard_map/ppermute | solution.py:29
  74.6 11.7 %collective-permute-start.20 = (bf16[96,768]{1,0:T(8,128)(2,1)S(1)}, bf16[96,768]{1,0:T(8,128)(2,1)S(1)}, u32[]{:S(2)}, u32[]{:S(2)}) collective-permute-start(bf16[96,768]{1,0:T(8,128)(2,1)S(1)} %pad_maximum_fusion.11), channel_id=1, source_target_pairs={{0,24},{4,28},{8,16},{12,20},{16,8},{20,12},{24,0},{28,4},{1,25},{... | collective-permute-start | bytes 442376 | tf_op jit(solution)/shard_map/ppermute | solution.py:29
  76.9 9.8 %collective-permute-start.18 = (bf16[96,768]{1,0:T(8,128)(2,1)S(1)}, bf16[96,768]{1,0:T(8,128)(2,1)S(1)}, u32[]{:S(2)}, u32[]{:S(2)}) collective-permute-start(bf16[96,768]{1,0:T(8,128)(2,1)S(1)} %pad_maximum_fusion.9), channel_id=1, source_target_pairs={{0,8},{4,12},{8,0},{12,4},{16,24},{20,28},{24,16},{28,20},{1,9},{5... | collective-permute-start | bytes 442376 | tf_op jit(solution)/shard_map/ppermute | solution.py:29
  86.9 13.6 %collective-permute-start.22 = (bf16[304,768]{1,0:T(8,128)(2,1)S(1)}, bf16[304,768]{1,0:T(8,128)(2,1)S(1)}, u32[]{:S(2)}, u32[]{:S(2)}) collective-permute-start(bf16[304,768]{1,0:T(8,128)(2,1)S(1)} %slice.160), channel_id=1, source_target_pairs={{0,2},{1,3},{2,0},{3,1},{4,6},{5,7},{6,4},{7,5},{8,10},{9,11},{10,... | collective-permute-start | bytes 1400840 | tf_op jit(solution)/shard_map/ppermute | solution.py:29
  95.7 7.0 %collective-permute-start.24 = (bf16[80,768]{1,0:T(8,128)(2,1)S(1)}, bf16[80,768]{1,0:T(8,128)(2,1)S(1)}, u32[]{:S(2)}, u32[]{:S(2)}) collective-permute-start(bf16[80,768]{1,0:T(8,128)(2,1)S(1)} %slice.161), channel_id=1, source_target_pairs={{0,2},{1,3},{2,0},{3,1},{4,6},{5,7},{6,4},{7,5},{8,10},{9,11},{10,... | collective-permute-start | bytes 368648 | tf_op jit(solution)/shard_map/ppermute | solution.py:29
  (4 other events, 7.7 us)

commit v21 on v16

--- a/solution.py
+++ b/solution.py
@@ -307,6 +307,8 @@
             early += [("x", step - 2, 0)]
         if step >= 2 and z == 1:
             early += [("c", step - 2)]
+        if step == 1 and z == 1:
+            early += [("y", 3)]
         send(("z", step, z), block(step, z), "grp", groups, 2 * z, *early)
 
     def collect(step):

time: 114 us -> 117 us (1.026)
  waiting for transfers between devices: 52 us -> 53.6 us
    ppermute x25, waiting for transfers between devices: 52 us -> 53.6 us  [swap(): return lax.ppermute(value, axis, [(i, i ^ bit) for i in range(size)])]
where the time goes in v21:
time: 117 us; the launch traced here: 116 us
  waiting for transfers between devices  53.6 us (46%)
  starting transfers between devices  30.5 us (26%)
  Pallas kernels  17.7 us (15%)
  blocking collectives  11.4 us (10%)
  local copies, waits for them, and re-layouts  2.63 us (2%)
    ppermute x25, waiting for transfers between devices, swap(): return lax.ppermute(value, axis, [(i, i ^ bit) for i in range(size)])  53.6 us
    ppermute x25, starting transfers between devices, swap(): return lax.ppermute(value, axis, [(i, i ^ bit) for i in range(size)])  30.5 us
    all_to_all x1, blocking collectives, on_device(): homeward = lax.all_to_all(result, ('grp', 'blk'), 0, 0, tiled=True)  11.4 us
    pallas_call x2, Pallas kernels, gram_step(): pl.pallas_call(functools.partial(gram_kernel, first, step, pieces), in_sp...  8.45 us
    pallas_call x1, Pallas kernels, gram_last(): pl.pallas_call(functools.partial(gram_last_kernel, step, relatives, chunk...  3.07 us
    pallas_call x1, Pallas kernels, head(): pl.pallas_call(functools.partial(rest_kernel, capacity, chunks, groups),...  2.61 us
    unnamed x23, local copies, waits for them, and re-layouts  2.43 us
  transfers between devices with their start and end apart: 25, of which 15 were waited for; matrix products, arithmetic and copies ran while one was open for 1% of the time, Pallas kernels for 10%

profile of v21, /device:TPU:0, one launch (start us, length us, event | category | flops | bytes accessed | tf_op | source)
XLA Modules:
  0.0 116.4 jit_solution(16497043753784806366)
XLA Ops:
  3.3 3.0 %collective-permute-start = (bf16[96,768]{1,0:T(8,128)(2,1)S(1)}, bf16[96,768]{1,0:T(8,128)(2,1)S(1)}, u32[]{:S(2)}, u32[]{:S(2)}) collective-permute-start(bf16[96,768]{1,0:T(8,128)(2,1)S(1)} %get-tuple-element.117), channel_id=1, source_target_pairs={{0,4},{4,0},{8,12},{12,8},{16,20},{20,16},{24,28},{28,24},{1,5},{5... | collective-permute-start | bytes 442376 | tf_op jit(solution)/shard_map/ppermute | solution.py:29
  6.4 2.6 %place_rest.1 = (bf16[192,768]{1,0:T(8,128)(2,1)S(1)}, bf16[192,768]{1,0:T(8,128)(2,1)S(1)}, bf16[192,768]{1,0:T(8,128)(2,1)S(1)}, bf16[192,768]{1,0:T(8,128)(2,...) custom-call(s32[2]{0:T(128)S(1)} %pad_add_fusion.me_ref, s32[6,128]{1,0:T(8,128)S(1)} %bitcast.6, ...), custom_call_target="tpu_custom_call" | custom-call | flops 1585446912 | bytes 3244032 | tf_op jit(solution)/shard_map/place_rest/pallas_call | solution.py:101
  10.2 2.1 %collective-permute-start.6 = (bf16[384,768]{1,0:T(8,128)(2,1)S(1)}, bf16[384,768]{1,0:T(8,128)(2,1)S(1)}, u32[]{:S(2)}, u32[]{:S(2)}) collective-permute-start(bf16[384,768]{1,0:T(8,128)(2,1)S(1)} %get-tuple-element.51), channel_id=1, source_target_pairs={{0,4},{4,0},{8,12},{12,8},{16,20},{20,16},{24,28},{28,24},{1,5},{5... | collective-permute-start | bytes 1769480 | tf_op jit(solution)/shard_map/ppermute | solution.py:29
  13.8 2.0 %collective-permute-done.2 = bf16[96,768]{1,0:T(8,128)(2,1)S(1)} collective-permute-done((bf16[96,768]{1,0:T(8,128)(2,1)S(1)}, bf16[96,768]{1,0:T(8,128)(2,1)S(1)}, u32[]{:S(2)}, u32[]{:S(2)}) %collective-permute-start.2) | collective-permute-done | bytes 147488 | tf_op jit(solution)/shard_map/ppermute | solution.py:29
  15.9 2.7 %collective-permute-start.3 = (bf16[96,768]{1,0:T(8,128)(2,1)S(1)}, bf16[96,768]{1,0:T(8,128)(2,1)S(1)}, u32[]{:S(2)}, u32[]{:S(2)}) collective-permute-start(bf16[96,768]{1,0:T(8,128)(2,1)S(1)} %pad_maximum_fusion.1), channel_id=1, source_target_pairs={{0,16},{4,20},{8,24},{12,28},{16,0},{20,4},{24,8},{28,12},{1,17},{... | collective-permute-start | bytes 442376 | tf_op jit(solution)/shard_map/ppermute | solution.py:29
  20.5 7.2 %collective-permute-done.3 = bf16[96,768]{1,0:T(8,128)(2,1)S(1)} collective-permute-done((bf16[96,768]{1,0:T(8,128)(2,1)S(1)}, bf16[96,768]{1,0:T(8,128)(2,1)S(1)}, u32[]{:S(2)}, u32[]{:S(2)}) %collective-permute-start.3) | collective-permute-done | bytes 147488 | tf_op jit(solution)/shard_map/ppermute | solution.py:29
  27.8 1.6 %collective-permute-start.10 = (bf16[384,768]{1,0:T(8,128)(2,1)S(1)}, bf16[384,768]{1,0:T(8,128)(2,1)S(1)}, u32[]{:S(2)}, u32[]{:S(2)}) collective-permute-start(bf16[384,768]{1,0:T(8,128)(2,1)S(1)} %get-tuple-element.137.refs_0_), channel_id=1, source_target_pairs={{0,2},{1,3},{2,0},{3,1},{4,6},{5,7},{6,4},{7,5},{8,10},{9,11},{10,... | collective-permute-start | bytes 1769480 | tf_op jit(solution)/shard_map/ppermute | solution.py:29
  29.3 4.0 %collective-permute-done.5 = bf16[192,768]{1,0:T(8,128)(2,1)S(1)} collective-permute-done((bf16[192,768]{1,0:T(8,128)(2,1)S(1)}, bf16[192,768]{1,0:T(8,128)(2,1)S(1)}, u32[]{:S(2)}, u32[]{:S(2)}) %collective-permute-start.5) | collective-permute-done | bytes 294944 | tf_op jit(solution)/shard_map/ppermute | solution.py:29
  33.4 3.7 %collective-permute-start.9 = (bf16[96,768]{1,0:T(8,128)(2,1)S(1)}, bf16[96,768]{1,0:T(8,128)(2,1)S(1)}, u32[]{:S(2)}, u32[]{:S(2)}) collective-permute-start(bf16[96,768]{1,0:T(8,128)(2,1)S(1)} %pad_maximum_fusion.5), channel_id=1, source_target_pairs={{0,24},{4,28},{8,16},{12,20},{16,8},{20,12},{24,0},{28,4},{1,25},{... | collective-permute-start | bytes 442376 | tf_op jit(solution)/shard_map/ppermute | solution.py:29
  38.4 3.6 %collective-permute-done.9 = bf16[96,768]{1,0:T(8,128)(2,1)S(1)} collective-permute-done((bf16[96,768]{1,0:T(8,128)(2,1)S(1)}, bf16[96,768]{1,0:T(8,128)(2,1)S(1)}, u32[]{:S(2)}, u32[]{:S(2)}) %collective-permute-start.9) | collective-permute-done | bytes 147488 | tf_op jit(solution)/shard_map/ppermute | solution.py:29
  42.0 6.3 %collective-permute-done.8 = bf16[96,768]{1,0:T(8,128)(2,1)S(1)} collective-permute-done((bf16[96,768]{1,0:T(8,128)(2,1)S(1)}, bf16[96,768]{1,0:T(8,128)(2,1)S(1)}, u32[]{:S(2)}, u32[]{:S(2)}) %collective-permute-start.8) | collective-permute-done | bytes 147488 | tf_op jit(solution)/shard_map/ppermute | solution.py:29
  48.5 1.6 %collective-permute-start.15 = (bf16[384,768]{1,0:T(8,128)(2,1)S(1)}, bf16[384,768]{1,0:T(8,128)(2,1)S(1)}, u32[]{:S(2)}, u32[]{:S(2)}) collective-permute-start(bf16[384,768]{1,0:T(8,128)(2,1)S(1)} %get-tuple-element.61.refs_1_), channel_id=1, source_target_pairs={{0,2},{1,3},{2,0},{3,1},{4,6},{5,7},{6,4},{7,5},{8,10},{9,11},{10,... | collective-permute-start | bytes 1769480 | tf_op jit(solution)/shard_map/ppermute | solution.py:29
  50.2 2.5 %collective-permute-start.14 = (bf16[96,768]{1,0:T(8,128)(2,1)S(1)}, bf16[96,768]{1,0:T(8,128)(2,1)S(1)}, u32[]{:S(2)}, u32[]{:S(2)}) collective-permute-start(bf16[96,768]{1,0:T(8,128)(2,1)S(1)} %pad_maximum_fusion.8), channel_id=1, source_target_pairs={{0,24},{4,28},{8,16},{12,20},{16,8},{20,12},{24,0},{28,4},{1,25},{... | collective-permute-start | bytes 442376 | tf_op jit(solution)/shard_map/ppermute | solution.py:29
  53.8 10.5 %collective-permute-done.15 = bf16[384,768]{1,0:T(8,128)(2,1)S(1)} collective-permute-done((bf16[384,768]{1,0:T(8,128)(2,1)S(1)}, bf16[384,768]{1,0:T(8,128)(2,1)S(1)}, u32[]{:S(2)}, u32[]{:S(2)}) %collective-permute-start.15) | collective-permute-done | bytes 589856 | tf_op jit(solution)/shard_map/ppermute | solution.py:29
  66.1 1.6 %collective-permute-start.18 = (bf16[96,768]{1,0:T(8,128)(2,1)S(1)}, bf16[96,768]{1,0:T(8,128)(2,1)S(1)}, u32[]{:S(2)}, u32[]{:S(2)}) collective-permute-start(bf16[96,768]{1,0:T(8,128)(2,1)S(1)} %pad_maximum_fusion.10), channel_id=1, source_target_pairs={{0,16},{4,20},{8,24},{12,28},{16,0},{20,4},{24,8},{28,12},{1,17},{... | collective-permute-start | bytes 442376 | tf_op jit(solution)/shard_map/ppermute | solution.py:29
  67.7 2.5 %collective-permute-start.19 = (bf16[96,768]{1,0:T(8,128)(2,1)S(1)}, bf16[96,768]{1,0:T(8,128)(2,1)S(1)}, u32[]{:S(2)}, u32[]{:S(2)}) collective-permute-start(bf16[96,768]{1,0:T(8,128)(2,1)S(1)} %pad_maximum_fusion.11), channel_id=1, source_target_pairs={{0,24},{4,28},{8,16},{12,20},{16,8},{20,12},{24,0},{28,4},{1,25},{... | collective-permute-start | bytes 442376 | tf_op jit(solution)/shard_map/ppermute | solution.py:29
  70.2 10.4 %collective-permute-done.20 = bf16[384,768]{1,0:T(8,128)(2,1)S(1)} collective-permute-done((bf16[384,768]{1,0:T(8,128)(2,1)S(1)}, bf16[384,768]{1,0:T(8,128)(2,1)S(1)}, u32[]{:S(2)}, u32[]{:S(2)}) %collective-permute-start.20) | collective-permute-done | bytes 589856 | tf_op jit(solution)/shard_map/ppermute | solution.py:29
  83.6 6.0 %gram_step.2 = (f32[384,128]{1,0:T(8,128)S(1)}, f32[384,128]{1,0:T(8,128)S(1)}, f32[384,128]{1,0:T(8,128)S(1)}, f32[1,1536]{1,0:T(1,128)S(1)}, f32[1,1536]{1,0:T(1,128)S(1)}, /*index=5*/f32[1,1536]{1,0:T(1,128)S(1)}) custom-call(bf16[384,768]{1,0:T(8,128)(2,1)S(1)} %get-tuple-element.137.refs_0_, bf16[384,768]{1,0:T(8,128)(2,1)S(1)} %get-tuple-element.61.refs_1_, ...), custom_call_target="tpu_custom_call" | custom-call | flops 8153726976 | bytes 8847360 | tf_op jit(solution)/shard_map/gram_step/pallas_call | solution.py:213
  90.9 3.6 %collective-permute-done.21 = bf16[304,768]{1,0:T(8,128)(2,1)S(1)} collective-permute-done((bf16[304,768]{1,0:T(8,128)(2,1)S(1)}, bf16[304,768]{1,0:T(8,128)(2,1)S(1)}, u32[]{:S(2)}, u32[]{:S(2)}) %collective-permute-start.21) | collective-permute-done | bytes 466976 | tf_op jit(solution)/shard_map/ppermute | solution.py:29
  94.5 2.2 %collective-permute-done.23 = bf16[80,768]{1,0:T(8,128)(2,1)S(1)} collective-permute-done((bf16[80,768]{1,0:T(8,128)(2,1)S(1)}, bf16[80,768]{1,0:T(8,128)(2,1)S(1)}, u32[]{:S(2)}, u32[]{:S(2)}) %collective-permute-start.23) | collective-permute-done | bytes 122912 | tf_op jit(solution)/shard_map/ppermute | solution.py:29
  96.8 2.4 %gram_step.3 = (f32[384,128]{1,0:T(8,128)S(1)}, f32[384,128]{1,0:T(8,128)S(1)}, f32[384,128]{1,0:T(8,128)S(1)}, f32[384,128]{1,0:T(8,128)S(1)}, f32[1,768]{1,0:T(1,128)S(1)}) custom-call(bf16[384,768]{1,0:T(8,128)(2,1)S(1)} %get-tuple-element.137.refs_0_, bf16[384,768]{1,0:T(8,128)(2,1)S(1)} %get-tuple-element.61.refs_1_, ...), custom_call_target="tpu_custom_call" | custom-call | flops 1811939328 | bytes 3538944 | tf_op jit(solution)/shard_map/gram_step/pallas_call | solution.py:213
  99.6 3.1 %gram_last.1 = f32[32,1,192]{2,1,0:T(1,128)S(1)} custom-call(s32[2]{0:T(128)S(1)} %pad_add_fusion.me_ref, bf16[384,768]{1,0:T(8,128)(2,1)S(1)} %get-tuple-element.137.refs_0_, bf16[384,768]{1,0:T(8,128)(2,1)S(1)} %get-tuple-element.61.refs_1_, bf16[384,768]{1,0:T(8,128)(2,1)S(1)} %get-tuple-element.66.refs_2_, ...), custom_call_target="tpu_custom_call" | custom-call | flops 1811939328 | bytes 3538944 | tf_op jit(solution)/shard_map/gram_last/pallas_call | solution.py:228
  102.7 11.4 %all_to_all.5.part_ref = f32[32,1,192]{2,1,0:T(1,128)} all-to-all(f32[32,1,192]{2,1,0:T(1,128)S(1)} %gram_last.1), channel_id=1, replica_groups=mesh['grp'=8,'blk'=4] {'grp','blk'}, dimensions={0} | all-to-all | bytes 49152 | tf_op jit(solution)/shard_map/all_to_all | solution.py:361
  114.0 2.3 %pick_rows.1 = f32[6,128]{1,0:T(8,128)} custom-call(s32[6,128]{1,0:T(8,128)} %bitcast.4, f32[32,1,192]{2,1,0:T(1,128)} %all_to_all.5.part_ref), custom_call_target="tpu_custom_call" | custom-call | tf_op jit(solution)/shard_map/pick_rows/pallas_call | solution.py:264
  (77 shorter events, 17.2 us)
Async XLA Ops:
  3.3 6.9 %collective-permute-start = (bf16[96,768]{1,0:T(8,128)(2,1)S(1)}, bf16[96,768]{1,0:T(8,128)(2,1)S(1)}, u32[]{:S(2)}, u32[]{:S(2)}) collective-permute-start(bf16[96,768]{1,0:T(8,128)(2,1)S(1)} %get-tuple-element.117), channel_id=1, source_target_pairs={{0,4},{4,0},{8,12},{12,8},{16,20},{20,16},{24,28},{28,24},{1,5},{5... | collective-permute-start | bytes 442376 | tf_op jit(solution)/shard_map/ppermute | solution.py:29
  9.0 6.8 %collective-permute-start.2 = (bf16[96,768]{1,0:T(8,128)(2,1)S(1)}, bf16[96,768]{1,0:T(8,128)(2,1)S(1)}, u32[]{:S(2)}, u32[]{:S(2)}) collective-permute-start(bf16[96,768]{1,0:T(8,128)(2,1)S(1)} %get-tuple-element.47), channel_id=1, source_target_pairs={{0,4},{4,0},{8,12},{12,8},{16,20},{20,16},{24,28},{28,24},{1,5},{5... | collective-permute-start | bytes 442376 | tf_op jit(solution)/shard_map/ppermute | solution.py:29
  10.2 26.9 %collective-permute-start.6 = (bf16[384,768]{1,0:T(8,128)(2,1)S(1)}, bf16[384,768]{1,0:T(8,128)(2,1)S(1)}, u32[]{:S(2)}, u32[]{:S(2)}) collective-permute-start(bf16[384,768]{1,0:T(8,128)(2,1)S(1)} %get-tuple-element.51), channel_id=1, source_target_pairs={{0,4},{4,0},{8,12},{12,8},{16,20},{20,16},{24,28},{28,24},{1,5},{5... | collective-permute-start | bytes 1769480 | tf_op jit(solution)/shard_map/ppermute | solution.py:29
  12.4 8.1 %collective-permute-start.1 = (bf16[96,768]{1,0:T(8,128)(2,1)S(1)}, bf16[96,768]{1,0:T(8,128)(2,1)S(1)}, u32[]{:S(2)}, u32[]{:S(2)}) collective-permute-start(bf16[96,768]{1,0:T(8,128)(2,1)S(1)} %pad_maximum_fusion), channel_id=1, source_target_pairs={{0,8},{4,12},{8,0},{12,4},{16,24},{20,28},{24,16},{28,20},{1,9},{5... | collective-permute-start | bytes 442376 | tf_op jit(solution)/shard_map/ppermute | solution.py:29
  15.9 11.9 %collective-permute-start.3 = (bf16[96,768]{1,0:T(8,128)(2,1)S(1)}, bf16[96,768]{1,0:T(8,128)(2,1)S(1)}, u32[]{:S(2)}, u32[]{:S(2)}) collective-permute-start(bf16[96,768]{1,0:T(8,128)(2,1)S(1)} %pad_maximum_fusion.1), channel_id=1, source_target_pairs={{0,16},{4,20},{8,24},{12,28},{16,0},{20,4},{24,8},{28,12},{1,17},{... | collective-permute-start | bytes 442376 | tf_op jit(solution)/shard_map/ppermute | solution.py:29
  18.5 9.2 %collective-permute-start.4 = (bf16[96,768]{1,0:T(8,128)(2,1)S(1)}, bf16[96,768]{1,0:T(8,128)(2,1)S(1)}, u32[]{:S(2)}, u32[]{:S(2)}) collective-permute-start(bf16[96,768]{1,0:T(8,128)(2,1)S(1)} %pad_maximum_fusion.2), channel_id=1, source_target_pairs={{0,24},{4,28},{8,16},{12,20},{16,8},{20,12},{24,0},{28,4},{1,25},{... | collective-permute-start | bytes 442376 | tf_op jit(solution)/shard_map/ppermute | solution.py:29
  19.9 13.4 %collective-permute-start.5 = (bf16[192,768]{1,0:T(8,128)(2,1)S(1)}, bf16[192,768]{1,0:T(8,128)(2,1)S(1)}, u32[]{:S(2)}, u32[]{:S(2)}) collective-permute-start(bf16[192,768]{1,0:T(8,128)(2,1)S(1)} %get-tuple-element.50), channel_id=1, source_target_pairs={{0,4},{4,0},{8,12},{12,8},{16,20},{20,16},{24,28},{28,24},{1,5},{5... | collective-permute-start | bytes 884744 | tf_op jit(solution)/shard_map/ppermute | solution.py:29
  27.8 10.6 %collective-permute-start.10 = (bf16[384,768]{1,0:T(8,128)(2,1)S(1)}, bf16[384,768]{1,0:T(8,128)(2,1)S(1)}, u32[]{:S(2)}, u32[]{:S(2)}) collective-permute-start(bf16[384,768]{1,0:T(8,128)(2,1)S(1)} %get-tuple-element.137.refs_0_), channel_id=1, source_target_pairs={{0,2},{1,3},{2,0},{3,1},{4,6},{5,7},{6,4},{7,5},{8,10},{9,11},{10,... | collective-permute-start | bytes 1769480 | tf_op jit(solution)/shard_map/ppermute | solution.py:29
  33.4 8.7 %collective-permute-start.9 = (bf16[96,768]{1,0:T(8,128)(2,1)S(1)}, bf16[96,768]{1,0:T(8,128)(2,1)S(1)}, u32[]{:S(2)}, u32[]{:S(2)}) collective-permute-start(bf16[96,768]{1,0:T(8,128)(2,1)S(1)} %pad_maximum_fusion.5), channel_id=1, source_target_pairs={{0,24},{4,28},{8,16},{12,20},{16,8},{20,12},{24,0},{28,4},{1,25},{... | collective-permute-start | bytes 442376 | tf_op jit(solution)/shard_map/ppermute | solution.py:29
  37.0 11.3 %collective-permute-start.8 = (bf16[96,768]{1,0:T(8,128)(2,1)S(1)}, bf16[96,768]{1,0:T(8,128)(2,1)S(1)}, u32[]{:S(2)}, u32[]{:S(2)}) collective-permute-start(bf16[96,768]{1,0:T(8,128)(2,1)S(1)} %pad_maximum_fusion.4), channel_id=1, source_target_pairs={{0,16},{4,20},{8,24},{12,28},{16,0},{20,4},{24,8},{28,12},{1,17},{... | collective-permute-start | bytes 442376 | tf_op jit(solution)/shard_map/ppermute | solution.py:29
  37.1 11.2 %collective-permute-start.7 = (bf16[96,768]{1,0:T(8,128)(2,1)S(1)}, bf16[96,768]{1,0:T(8,128)(2,1)S(1)}, u32[]{:S(2)}, u32[]{:S(2)}) collective-permute-start(bf16[96,768]{1,0:T(8,128)(2,1)S(1)} %pad_maximum_fusion.3), channel_id=1, source_target_pairs={{0,8},{4,12},{8,0},{12,4},{16,24},{20,28},{24,16},{28,20},{1,9},{5... | collective-permute-start | bytes 442376 | tf_op jit(solution)/shard_map/ppermute | solution.py:29
  48.3 4.4 %collective-permute-start.11 = (bf16[768,768]{1,0:T(8,128)(2,1)S(1)}, bf16[768,768]{1,0:T(8,128)(2,1)S(1)}, u32[]{:S(2)}, u32[]{:S(2)}) collective-permute-start(bf16[768,768]{1,0:T(8,128)(2,1)S(1)} %constant_dynamic-update-slice_fusion.10.refs_3_), channel_id=1, source_target_pairs={{0,1},{1,0},{2,3},{3,2},{4,5},{5,4},{6,7},{7,6},{8,9},{9,8},{10,11... | collective-permute-start | bytes 3538952 | tf_op jit(solution)/shard_map/ppermute | solution.py:29
  48.5 15.8 %collective-permute-start.15 = (bf16[384,768]{1,0:T(8,128)(2,1)S(1)}, bf16[384,768]{1,0:T(8,128)(2,1)S(1)}, u32[]{:S(2)}, u32[]{:S(2)}) collective-permute-start(bf16[384,768]{1,0:T(8,128)(2,1)S(1)} %get-tuple-element.61.refs_1_), channel_id=1, source_target_pairs={{0,2},{1,3},{2,0},{3,1},{4,6},{5,7},{6,4},{7,5},{8,10},{9,11},{10,... | collective-permute-start | bytes 1769480 | tf_op jit(solution)/shard_map/ppermute | solution.py:29
  50.1 14.2 %collective-permute-start.13 = (bf16[96,768]{1,0:T(8,128)(2,1)S(1)}, bf16[96,768]{1,0:T(8,128)(2,1)S(1)}, u32[]{:S(2)}, u32[]{:S(2)}) collective-permute-start(bf16[96,768]{1,0:T(8,128)(2,1)S(1)} %pad_maximum_fusion.7), channel_id=1, source_target_pairs={{0,16},{4,20},{8,24},{12,28},{16,0},{20,4},{24,8},{28,12},{1,17},{... | collective-permute-start | bytes 442376 | tf_op jit(solution)/shard_map/ppermute | solution.py:29
  50.2 14.1 %collective-permute-start.14 = (bf16[96,768]{1,0:T(8,128)(2,1)S(1)}, bf16[96,768]{1,0:T(8,128)(2,1)S(1)}, u32[]{:S(2)}, u32[]{:S(2)}) collective-permute-start(bf16[96,768]{1,0:T(8,128)(2,1)S(1)} %pad_maximum_fusion.8), channel_id=1, source_target_pairs={{0,24},{4,28},{8,16},{12,20},{16,8},{20,12},{24,0},{28,4},{1,25},{... | collective-permute-start | bytes 442376 | tf_op jit(solution)/shard_map/ppermute | solution.py:29
  52.8 11.9 %collective-permute-start.12 = (bf16[96,768]{1,0:T(8,128)(2,1)S(1)}, bf16[96,768]{1,0:T(8,128)(2,1)S(1)}, u32[]{:S(2)}, u32[]{:S(2)}) collective-permute-start(bf16[96,768]{1,0:T(8,128)(2,1)S(1)} %pad_maximum_fusion.6), channel_id=1, source_target_pairs={{0,8},{4,12},{8,0},{12,4},{16,24},{20,28},{24,16},{28,20},{1,9},{5... | collective-permute-start | bytes 442376 | tf_op jit(solution)/shard_map/ppermute | solution.py:29
  64.7 5.5 %collective-permute-start.16 = (bf16[768,768]{1,0:T(8,128)(2,1)S(1)}, bf16[768,768]{1,0:T(8,128)(2,1)S(1)}, u32[]{:S(2)}, u32[]{:S(2)}) collective-permute-start(bf16[768,768]{1,0:T(8,128)(2,1)S(1)} %constant_dynamic-update-slice_fusion.21.refs_5_), channel_id=1, source_target_pairs={{0,1},{1,0},{2,3},{3,2},{4,5},{5,4},{6,7},{7,6},{8,9},{9,8},{10,11... | collective-permute-start | bytes 3538952 | tf_op jit(solution)/shard_map/ppermute | solution.py:29
  64.8 15.8 %collective-permute-start.20 = (bf16[384,768]{1,0:T(8,128)(2,1)S(1)}, bf16[384,768]{1,0:T(8,128)(2,1)S(1)}, u32[]{:S(2)}, u32[]{:S(2)}) collective-permute-start(bf16[384,768]{1,0:T(8,128)(2,1)S(1)} %get-tuple-element.66.refs_2_), channel_id=1, source_target_pairs={{0,2},{1,3},{2,0},{3,1},{4,6},{5,7},{6,4},{7,5},{8,10},{9,11},{10,... | collective-permute-start | bytes 1769480 | tf_op jit(solution)/shard_map/ppermute | solution.py:29
  66.1 14.5 %collective-permute-start.18 = (bf16[96,768]{1,0:T(8,128)(2,1)S(1)}, bf16[96,768]{1,0:T(8,128)(2,1)S(1)}, u32[]{:S(2)}, u32[]{:S(2)}) collective-permute-start(bf16[96,768]{1,0:T(8,128)(2,1)S(1)} %pad_maximum_fusion.10), channel_id=1, source_target_pairs={{0,16},{4,20},{8,24},{12,28},{16,0},{20,4},{24,8},{28,12},{1,17},{... | collective-permute-start | bytes 442376 | tf_op jit(solution)/shard_map/ppermute | solution.py:29
  67.7 12.9 %collective-permute-start.19 = (bf16[96,768]{1,0:T(8,128)(2,1)S(1)}, bf16[96,768]{1,0:T(8,128)(2,1)S(1)}, u32[]{:S(2)}, u32[]{:S(2)}) collective-permute-start(bf16[96,768]{1,0:T(8,128)(2,1)S(1)} %pad_maximum_fusion.11), channel_id=1, source_target_pairs={{0,24},{4,28},{8,16},{12,20},{16,8},{20,12},{24,0},{28,4},{1,25},{... | collective-permute-start | bytes 442376 | tf_op jit(solution)/shard_map/ppermute | solution.py:29
  70.2 10.6 %collective-permute-start.17 = (bf16[96,768]{1,0:T(8,128)(2,1)S(1)}, bf16[96,768]{1,0:T(8,128)(2,1)S(1)}, u32[]{:S(2)}, u32[]{:S(2)}) collective-permute-start(bf16[96,768]{1,0:T(8,128)(2,1)S(1)} %pad_maximum_fusion.9), channel_id=1, source_target_pairs={{0,8},{4,12},{8,0},{12,4},{16,24},{20,28},{24,16},{28,20},{1,9},{5... | collective-permute-start | bytes 442376 | tf_op jit(solution)/shard_map/ppermute | solution.py:29
  80.9 13.6 %collective-permute-start.21 = (bf16[304,768]{1,0:T(8,128)(2,1)S(1)}, bf16[304,768]{1,0:T(8,128)(2,1)S(1)}, u32[]{:S(2)}, u32[]{:S(2)}) collective-permute-start(bf16[304,768]{1,0:T(8,128)(2,1)S(1)} %slice.168), channel_id=1, source_target_pairs={{0,2},{1,3},{2,0},{3,1},{4,6},{5,7},{6,4},{7,5},{8,10},{9,11},{10,... | collective-permute-start | bytes 1400840 | tf_op jit(solution)/shard_map/ppermute | solution.py:29
  89.6 7.1 %collective-permute-start.23 = (bf16[80,768]{1,0:T(8,128)(2,1)S(1)}, bf16[80,768]{1,0:T(8,128)(2,1)S(1)}, u32[]{:S(2)}, u32[]{:S(2)}) collective-permute-start(bf16[80,768]{1,0:T(8,128)(2,1)S(1)} %slice.169), channel_id=1, source_target_pairs={{0,2},{1,3},{2,0},{3,1},{4,6},{5,7},{6,4},{7,5},{8,10},{9,11},{10,... | collective-permute-start | bytes 368648 | tf_op jit(solution)/shard_map/ppermute | solution.py:29
  96.7 2.9 %collective-permute-start.24 = (bf16[768,768]{1,0:T(8,128)(2,1)S(1)}, bf16[768,768]{1,0:T(8,128)(2,1)S(1)}, u32[]{:S(2)}, u32[]{:S(2)}) collective-permute-start(bf16[768,768]{1,0:T(8,128)(2,1)S(1)} %constant_dynamic-update-slice_fusion.38.refs_4_), channel_id=1, source_target_pairs={{0,1},{1,0},{2,3},{3,2},{4,5},{5,4},{6,7},{7,6},{8,9},{9,8},{10,11... | collective-permute-start | bytes 3538952 | tf_op jit(solution)/shard_map/ppermute | solution.py:29
  (3 other events, 4.8 us)
